TPU v7x, 32 devices: a whole 2x2x4 slice. The times are simulated.
32 devices in a mesh: grp: 2 (over y), dp: 8 (over z, x), head: 2 (over core).
Axes of the slice: x: 2, y: 2, z: 4, core: 2. Of those that a mesh axis runs over, the one named last changes fastest.
Arguments:
- tokens: bfloat16 [2, 896, 4096], P(None, ('grp', 'dp'), 'head'), parts along dimension 1, may hold values from -6 to 6
- inner_weight: bfloat16 [4096, 256], P(None, 'head'), may hold values from -0.09375 to 0.09375
- gate_weight: bfloat16 [4096, 256], P(None, 'head'), may hold values from -0.09375 to 0.09375
- group_weight: bfloat16 [4096, 128], P(None, 'head'), may hold values from -0.09375 to 0.09375
- delta_weight: bfloat16 [4096, 2], P(None, 'head'), may hold values from -0.09375 to 0.09375
- inner_taps: float32 [4, 256], P(None, 'head'), may hold values from -1 to 1
- inner_offset: float32 [256], P('head'), may hold values from -0.5 to 0.5
- group_taps: float32 [4, 128], P(None, 'head'), may hold values from -1 to 1
- group_offset: float32 [128], P('head'), may hold values from -0.5 to 0.5
- decay_log: float32 [2], P('head'), may hold values from -2.3 to 0.5
- delta_bias: float32 [2], P('head'), may hold values from -1 to 1
- skip_gain: float32 [2], P('head'), may hold values from 0.5 to 2
- inner_window: bfloat16 [896, 3, 256], P(('grp', 'dp'), None, 'head'), parts along dimension 0, may hold values from -6 to 6
- group_window: bfloat16 [896, 3, 128], P(('grp', 'dp'), None, 'head'), parts along dimension 0, may hold values from -6 to 6
- scan_state: bfloat16 [896, 256, 64], P(('grp', 'dp'), 'head'), parts along dimension 0, may hold values from -6 to 6
- send_list: int32 [16, 56], P(('grp', 'dp')), parts along dimension 0, may hold values from -1 to 55, as said below
- receive_list: int32 [16, 56], P(('grp', 'dp')), parts along dimension 0, may hold values from -1 to 55, as said below
- live_count: int32 [16], P(('grp', 'dp')), parts along dimension 0, may hold values from 1 to 56, as said below
Outputs:
- gated_output: bfloat16 [2, 896, 256], P(None, ('grp', 'dp'), 'head'), parts along dimension 1
- inner_next: bfloat16 [896, 3, 256], P(('grp', 'dp'), None, 'head'), parts along dimension 0
- group_next: bfloat16 [896, 3, 128], P(('grp', 'dp'), None, 'head'), parts along dimension 0
- scan_next: bfloat16 [896, 256, 64], P(('grp', 'dp'), 'head'), parts along dimension 0
There are 2 independent parts, one for each index of `grp`. A program takes and returns all parts, laid end to end along the dimension named above; an argument that names none is the same for every part. Nothing has to cross between parts.
Inputs may be any that keep to these rules, and one draw needn't show every extreme that they name: `send_list`: row s lists, at position d * 7 + c, the local slot of old replica s whose states become the c-th arrival at replica d, or -1; each replica sends exactly 28 distinct slots, exactly 7 to each of 4 other replicas and none to itself. `receive_list`: entry d, k is -1 when new slot k of replica d keeps the state of old slot k of the same replica, else s * 7 * 7 + c (7 = 1) where the c-th state that replica s sends to replica d is the one it takes; a slot takes an arrival exactly when replica d sends its own old slot k away; it agrees with send_list. `live_count`: some replica is full and some holds a single live request.
All inputs are finite; a program needn't handle non-finite values.
Results may differ from a plain program's by a relative error of at most 0.008.
Values may be sent and summed in bfloat16 or wider, within the bound.
No kernel may reach another device: no remote copies, remote signals or barrier semaphores. Data moves between devices by JAX's collectives and lax.ppermute only.
A program may use at most 64 MiB of HBM per device.

v0:
```python
import functools

import jax
import jax.numpy as jnp
from jax import lax
from jax.experimental import pallas as pl
from jax.experimental.pallas import tpu as pltpu
from jax.sharding import PartitionSpec as P

F32 = jnp.float32
BF16 = jnp.bfloat16
SMALL_LIMIT = 8 * 1024 * 1024
LARGE_LIMIT = 60 * 1024 * 1024
MAX_ROUNDS = 16
EARLIER = 2
LANES = 128
ROWS = 8
MAX_SETS = 64

VMEM = pl.BlockSpec(memory_space=pltpu.VMEM)
SMEM = pl.BlockSpec(memory_space=pltpu.SMEM)
HBM = pl.BlockSpec(memory_space=pl.ANY)


def round_up(value, step):
    return -(-value // step) * step


def silu(value):
    return value * jax.nn.sigmoid(value)


def rounded(value):
    return value.astype(BF16).astype(F32)


def rounds_of(replicas):
    if replicas > MAX_ROUNDS or replicas & (replicas - 1):
        return []
    light = list(range(1, replicas // 2))
    heavy = list(range(replicas // 2, replicas))
    order = []
    while light or heavy:
        order += light[:1] + heavy[:1] if len(order) < 4 else heavy[:1] or light[:1]
        light = [mask for mask in light if mask not in order]
        heavy = [mask for mask in heavy if mask not in order]
    return order


def partner(replicas, mask):
    return jnp.bitwise_xor(lax.axis_index("dp"), mask)


def both_halves(mine, theirs):
    first = lax.axis_index("head") == 0
    return jnp.concatenate(
        [jnp.where(first, mine, theirs), jnp.where(first, theirs, mine)], axis=-1
    )


def pack_kernel(replicas, cap, scan, send, inner, group, group_other, *refs):
    rounds = rounds_of(replicas)
    count = max(1, len(rounds))
    outs = refs[:count]
    (indices, inner_in, mine_in, theirs_in, held, table, picked, cast) = refs[count : count + 8]
    load_sem, in_sem, out_sem, window_sem = refs[count + 8 :]
    loads = [
        pltpu.make_async_copy(source, target, load_sem.at[place])
        for place, (source, target) in enumerate(
            [(send, indices), (inner, inner_in), (group, mine_in), (group_other, theirs_in)]
        )
    ]
    for load in loads:
        load.start()
    taps = inner_in.shape[0]
    state_rows = scan.shape[1]
    blocks = []
    if rounds:
        for ref, mask in zip(outs, rounds):
            blocks.append((ref.at[0], partner(replicas, mask)))
    else:
        blocks = [(outs[0].at[target], target) for target in range(replicas)]
    loads[0].wait()

    plan = []
    for block, (ref, target) in enumerate(blocks):
        for c in range(cap):
            plan.append((block, ref, c, indices[0, target * cap + c]))

    def fetch(place, index):
        return pltpu.make_async_copy(scan.at[index], held.at[place], in_sem.at[place])

    def store(place, ref, c):
        return pltpu.make_async_copy(
            held.at[place], ref.at[pl.ds(c * state_rows, state_rows)], out_sem.at[place]
        )

    for place, (_, _, _, index) in enumerate(plan):

        @pl.when(index >= 0)
        def _():
            fetch(place, index).start()

    for load in loads[1:]:
        load.wait()
    for tap in range(taps):
        table[:, tap * LANES : (tap + 1) * LANES] = inner_in[tap].astype(F32)
        table[:, (taps + tap) * LANES : (taps + tap + 1) * LANES] = both_halves(
            mine_in[tap].astype(F32), theirs_in[tap].astype(F32)
        )
    picked[...] = jnp.zeros_like(picked)
    for place, (block, _, c, index) in enumerate(plan):
        row = table[pl.ds(jnp.maximum(index, 0), 1), :]
        for kind in range(2 * taps):
            picked[block, kind * ROWS + c : kind * ROWS + c + 1, :] = row[
                :, kind * LANES : (kind + 1) * LANES
            ]
    windows = []
    for block, (ref, _) in enumerate(blocks):
        cast[block] = picked[block].astype(BF16)
        windows.append(
            pltpu.make_async_copy(
                cast.at[block],
                ref.at[pl.ds(cap * state_rows, cast.shape[1])],
                window_sem.at[block],
            )
        )
        windows[-1].start()

    for place, (_, ref, c, index) in enumerate(plan):

        @pl.when(index >= 0)
        def _():
            fetch(place, index).wait()
            store(place, ref, c).start()

    for place, (_, ref, c, index) in enumerate(plan):

        @pl.when(index >= 0)
        def _():
            store(place, ref, c).wait()

    for window in windows:
        window.wait()


def pack(replicas, cap, send_list, scan, inner, group, group_other):
    rounds = rounds_of(replicas)
    count = max(1, len(rounds))
    per_block = 1 if rounds else replicas
    taps, slots, _ = inner.shape
    window_rows = 2 * taps * ROWS
    rows = cap * scan.shape[1] + window_rows
    blocks = count * per_block
    places = blocks * cap
    return pl.pallas_call(
        functools.partial(pack_kernel, replicas, cap),
        out_shape=[jax.ShapeDtypeStruct((per_block, rows, LANES), BF16)] * count,
        in_specs=[HBM] * 5,
        out_specs=[HBM] * count,
        scratch_shapes=[
            pltpu.SMEM(send_list.shape, jnp.int32),
            pltpu.VMEM(inner.shape, BF16),
            pltpu.VMEM(group.shape, BF16),
            pltpu.VMEM(group.shape, BF16),
            pltpu.VMEM((places,) + scan.shape[1:], BF16),
            pltpu.VMEM((slots, 2 * taps * LANES), F32),
            pltpu.VMEM((blocks, window_rows, LANES), F32),
            pltpu.VMEM((blocks, window_rows, LANES), BF16),
            pltpu.SemaphoreType.DMA((4,)),
            pltpu.SemaphoreType.DMA((places,)),
            pltpu.SemaphoreType.DMA((places,)),
            pltpu.SemaphoreType.DMA((blocks,)),
        ],
        compiler_params=pltpu.CompilerParams(vmem_limit_bytes=LARGE_LIMIT),
        cost_estimate=pl.CostEstimate(flops=0, bytes_accessed=2_000_000, transcendentals=0),
        name="pack_leaving",
    )(scan, send_list, inner, group, group_other)


def sources_of(replicas):
    rounds = rounds_of(replicas)
    if rounds:
        return [partner(replicas, mask) for mask in rounds]
    return list(range(replicas))


def make_plan(replicas, cap, receive, slots, plan, inverse):
    moving = slots // 2
    kept = 0
    for entry in range(replicas * cap):
        inverse[entry] = -1
    for slot in range(slots):
        entry = receive[0, slot]
        stays = entry < 0
        plan[0, jnp.where(stays, kept, moving)] = slot
        inverse[jnp.where(stays, replicas * cap, entry)] = slot
        kept = kept + jnp.where(stays, 1, 0)
    for block, source in enumerate(sources_of(replicas)):
        for c in range(cap):
            plan[0, moving + block * cap + c] = inverse[source * cap + c]


def convolve(carried, raw, weights, offset):
    joined = carried + raw
    results = []
    for step in range(len(raw)):
        summed = offset
        for tap in range(len(carried) + 1):
            summed = summed + joined[step + tap] * weights[tap : tap + 1, :]
        results.append(rounded(silu(summed)))
    return results


def transposed(rows, scratch, stride):
    scratch[...] = jnp.zeros_like(scratch)
    for step, value in enumerate(rows):
        scratch[step * stride : step * stride + value.shape[0], :] = value
    return [scratch[first : first + LANES].T for first in range(0, scratch.shape[0], LANES)]


def advance_slot(state, rows, driven, decay, sums, maps, lanes):
    hidden = state.astype(F32)
    width = state.shape[0]
    for row, lane in zip(rows, lanes):
        piece = maps[lane // LANES]
        column = piece[:, lane % LANES : lane % LANES + 1]
        hidden = decay[row, :] * hidden + driven[row, :] * column[:width]
        sums[row, :] = jnp.sum(hidden * column[width:], axis=0, keepdims=True)
        result = hidden.astype(BF16)
        hidden = result.astype(F32)
    return result


def stay_kernel(
    replicas,
    cap,
    receive_hbm,
    live_hbm,
    decay_log_hbm,
    delta_bias_hbm,
    skip_gain_hbm,
    own_hbm,
    other_hbm,
    inner_weight,
    gate_weight,
    group_weight,
    group_weight_other,
    delta_weight,
    inner_taps_hbm,
    inner_offset_hbm,
    group_taps_hbm,
    group_taps_other_hbm,
    inner_hbm,
    group_hbm,
    group_other_hbm,
    scan_hbm,
    *refs,
):
    (
        plan,
        gated,
        group_weights,
        inner_raw,
        both,
        inner_moved,
        group_moved,
        gate_moved,
        delta_moved,
        decay_moved,
        scan_next,
        receive,
        live,
        decay_log,
        delta_bias,
        skip_gain,
        own,
        other,
        wide,
        tall,
        delta_row,
        inner_taps,
        inner_offset,
        group_taps,
        group_taps_other,
        inner,
        group,
        group_other,
        scan,
        inverse,
        gate,
        delta,
        decay,
        driven,
        skipped,
        sums,
        maps_in,
        ordered,
        done,
        sem,
        load_sem,
    ) = refs[-41:]
    taps, slots, _ = inner.shape
    rows, half = own.shape
    steps = rows // slots
    moving = slots // 2
    moved_rows = inner_moved.shape[0] // steps
    width = group.shape[2]
    head = lax.axis_index("head")

    def band(place):
        return tall.at[pl.ds(pl.multiple_of(place * width, width), width)]

    pairs = [
        (receive_hbm, receive),
        (delta_weight, delta_row),
        (own_hbm, own),
        (inner_weight, wide.at[:, pl.ds(0, LANES)]),
        (gate_weight, wide.at[:, pl.ds(LANES, LANES)]),
        (other_hbm, other),
        (group_weight, band(head)),
        (group_weight_other, band(1 - head)),
        (live_hbm, live),
        (decay_log_hbm, decay_log),
        (delta_bias_hbm, delta_bias),
        (skip_gain_hbm, skip_gain),
        (inner_taps_hbm, inner_taps),
        (inner_offset_hbm, inner_offset),
        (group_taps_hbm, group_taps),
        (group_taps_other_hbm, group_taps_other),
        (inner_hbm, inner),
        (group_hbm, group),
        (group_other_hbm, group_other),
        (scan_hbm, scan),
    ]
    loads = [
        pltpu.make_async_copy(source, target, load_sem.at[place])
        for place, (source, target) in enumerate(pairs)
    ]
    for load in loads:
        load.start()
    loads[0].wait()
    make_plan(replicas, cap, receive, slots, plan, inverse)
    loads[1].wait()
    first = 2 * width
    tall[first:, :] = jnp.broadcast_to(delta_row[...], (tall.shape[0] - first, 2 * half))
    for load in loads[2:]:
        load.wait()
    mine = pl.ds(pl.multiple_of(head * half, half), half)
    theirs = pl.ds(pl.multiple_of((1 - head) * half, half), half)
    flat = jnp.dot(own[...], wide[mine, :], preferred_element_type=F32) + jnp.dot(
        other[...], wide[theirs, :], preferred_element_type=F32
    )

    def across(tokens, part):
        return lax.dot_general(
            tokens, tall[:, part], (((1,), (1,)), ((), ())), preferred_element_type=F32
        )

    deep = across(own[...], mine) + across(other[...], theirs)
    inner_raw[...] = rounded(flat[:, :LANES])
    gate[...] = silu(rounded(flat[:, LANES:]))
    both[...] = rounded(deep[:, :first])
    shifted = rounded(jnp.broadcast_to(deep[:, first : first + 1], (rows, LANES))) + delta_bias[0]
    rate = jnp.maximum(shifted, 0.0) + jnp.log1p(jnp.exp(-jnp.abs(shifted)))
    delta[...] = rate
    decay[...] = jnp.exp(-rate * jnp.exp(jnp.full((1, LANES), decay_log[0], F32)))
    group_weights[: taps + 2, :] = both_halves(group_taps[...], group_taps_other[...])

    def parts(ref):
        return [ref[step * slots : (step + 1) * slots, :] for step in range(steps)]

    inner_conv = convolve(
        [inner[tap].astype(F32) for tap in range(taps)],
        parts(inner_raw),
        inner_taps[...],
        inner_offset[...],
    )
    group_conv = convolve(
        [both_halves(group[tap].astype(F32), group_other[tap].astype(F32)) for tap in range(taps)],
        parts(both),
        group_weights[: taps + 1, :],
        group_weights[taps + 1 : taps + 2, :],
    )
    for step in range(steps):
        part = slice(step * slots, (step + 1) * slots)
        driven[part, :] = delta[part, :] * inner_conv[step]
        skipped[part, :] = inner_conv[step] * skip_gain[0]
        maps_in[part, :] = group_conv[step]
    sums[...] = jnp.zeros_like(sums)
    stride = ordered.shape[0] // steps
    ordered[...] = jnp.zeros_like(ordered)
    for position in range(moving):
        slot = plan[0, position]
        for step in range(steps):
            ordered[step * stride + position : step * stride + position + 1, :] = maps_in[
                pl.ds(step * slots + slot, 1), :
            ]
    maps = [ordered[first : first + LANES].T for first in range(0, ordered.shape[0], LANES)]
    copies = []
    for position in range(moving):
        slot = plan[0, position]
        result = advance_slot(
            scan[slot],
            [pl.ds(step * slots + slot, 1) for step in range(steps)],
            driven,
            decay,
            sums,
            maps,
            [step * stride + position for step in range(steps)],
        )
        done[position] = jnp.where(slot < live[0], result, jnp.zeros_like(result))
        copies.append(
            pltpu.make_async_copy(done.at[position], scan_next.at[slot], sem.at[position])
        )
        copies[-1].start()
    gated[...] = (sums[...] + skipped[...]) * gate[...]
    pairs = (
        (inner_raw, inner_moved),
        (both, group_moved),
        (gate, gate_moved),
        (delta, delta_moved),
        (decay, decay_moved),
    )
    for _, target in pairs:
        target[...] = jnp.zeros_like(target)
    for block in range(moved_rows // ROWS):

        @pl.when(plan[0, moving + block * cap] >= 0)
        def _():
            for c in range(cap):
                slot = plan[0, moving + block * cap + c]
                for step in range(steps):
                    row = step * moved_rows + block * ROWS + c
                    for source, target in pairs:
                        target[row : row + 1, :] = source[pl.ds(step * slots + slot, 1), :]

    for copy in copies:
        copy.wait()


def stay(replicas, cap, operands, earlier):
    scalars, arrays = operands[:5], operands[5:]
    own, inner_weight, group_weight, delta_weight = arrays[0], arrays[2], arrays[4], arrays[6]
    inner, scan = arrays[-4], arrays[-1]
    taps, slots, _ = inner.shape
    rows = own.shape[0]
    steps = rows // slots
    moving = slots // 2
    blocks = len(sources_of(replicas))
    moved_rows = blocks * ROWS
    width, features = group_weight.shape
    full = jax.ShapeDtypeStruct((rows, LANES), F32)
    moved = jax.ShapeDtypeStruct((steps * moved_rows, LANES), F32)

    def like(value):
        return pltpu.VMEM(value.shape, value.dtype)

    return pl.pallas_call(
        functools.partial(stay_kernel, replicas, cap),
        out_shape=[
            jax.ShapeDtypeStruct((1, round_up(moving + blocks * cap, LANES)), jnp.int32),
            full,
            jax.ShapeDtypeStruct((round_up(taps + 2, ROWS), LANES), F32),
            full,
            full,
        ]
        + [moved] * 5
        + [jax.ShapeDtypeStruct(scan.shape, BF16)],
        in_specs=[HBM] * (len(operands) + len(earlier)),
        out_specs=[SMEM] + [VMEM] * 9 + [HBM],
        scratch_shapes=[pltpu.SMEM(value.shape, value.dtype) for value in scalars]
        + [
            like(own),
            like(own),
            pltpu.VMEM((features, 2 * LANES), BF16),
            pltpu.VMEM((2 * width + 2 * ROWS, features), BF16),
            like(delta_weight),
        ]
        + [like(value) for value in arrays[7:]]
        + [pltpu.SMEM((replicas * cap + 1,), jnp.int32)]
        + [pltpu.VMEM((rows, LANES), F32)] * 7
        + [
            pltpu.VMEM((round_up(rows, LANES), LANES), F32),
            pltpu.VMEM((moving,) + scan.shape[1:], BF16),
            pltpu.SemaphoreType.DMA((moving,)),
            pltpu.SemaphoreType.DMA((20,)),
        ],
        compiler_params=pltpu.CompilerParams(vmem_limit_bytes=LARGE_LIMIT),
        cost_estimate=pl.CostEstimate(
            flops=300_000_000, bytes_accessed=6_000_000, transcendentals=100_000
        ),
        name="advance_staying",
    )(*operands, *earlier)


def arrive_kernel(
    replicas,
    cap,
    plan_hbm,
    live_hbm,
    skip_gain_hbm,
    gated_in,
    group_weights,
    inner_moved,
    group_moved,
    gate_moved,
    delta_moved,
    decay_moved,
    inner_raw,
    both,
    inner_taps,
    inner_offset,
    inner,
    group,
    scan_in,
    *refs,
):
    del scan_in
    arrived = refs[:-18]
    gated_out, inner_next, group_next, scan_next = refs[-18:-14]
    plan, live, skip_gain = refs[-14:-11]
    (driven, sums, ordered, table, gated, gated_cast, inner_out, group_out) = refs[-11:-3]
    done, sem, out_sem = refs[-3:]
    taps, slots, _ = inner.shape
    moving = slots // 2
    state_rows = scan_next.shape[1]
    steps = inner_raw.shape[0] // slots
    width = group.shape[2]
    head = lax.axis_index("head")
    loads = [
        pltpu.make_async_copy(source, target, out_sem.at[place])
        for place, (source, target) in enumerate(
            [(plan_hbm, plan), (live_hbm, live), (skip_gain_hbm, skip_gain)]
        )
    ]
    for load in loads:
        load.start()
    if rounds_of(replicas):
        blocks = [ref.at[0] for ref in arrived]
    else:
        blocks = [arrived[0].at[source] for source in range(replicas)]
    moved_rows = len(blocks) * ROWS

    kinds = [[] for _ in range(2 * taps)]
    for ref in blocks:
        block = ref[cap * state_rows :, :].astype(F32)
        for kind in range(2 * taps):
            kinds[kind].append(block[kind * ROWS : (kind + 1) * ROWS])
    windows = [jnp.concatenate(kind, axis=0) for kind in kinds]

    def parts(ref):
        return [ref[step * moved_rows : (step + 1) * moved_rows, :] for step in range(steps)]

    inner_conv = convolve(
        windows[:taps], parts(inner_moved), inner_taps[...], inner_offset[...]
    )
    group_conv = convolve(
        windows[taps:],
        parts(group_moved),
        group_weights[: taps + 1, :],
        group_weights[taps + 1 : taps + 2, :],
    )
    for step, delta in enumerate(parts(delta_moved)):
        driven[step * moved_rows : (step + 1) * moved_rows, :] = delta * inner_conv[step]
    stride = ordered.shape[0] // steps
    maps = transposed(group_conv, ordered, stride)
    sums[...] = jnp.zeros_like(sums)
    for load in loads:
        load.wait()

    def each(act):
        for block in range(len(blocks)):

            @pl.when(plan[0, moving + block * cap] >= 0)
            def _():
                for c in range(cap):
                    act(block, c, plan[0, moving + block * cap + c])

    def store(block, c, slot):
        place = block * cap + c
        return pltpu.make_async_copy(done.at[place], scan_next.at[slot], sem.at[place])

    def advance(block, c, slot):
        place = block * ROWS + c
        result = advance_slot(
            blocks[block][c * state_rows : (c + 1) * state_rows, :],
            [
                slice(step * moved_rows + place, step * moved_rows + place + 1)
                for step in range(steps)
            ],
            driven,
            decay_moved,
            sums,
            maps,
            [step * stride + place for step in range(steps)],
        )
        done[block * cap + c] = jnp.where(slot < live[0], result, jnp.zeros_like(result))
        store(block, c, slot).start()

    each(advance)
    living = lax.broadcasted_iota(jnp.int32, (slots, LANES), 0) < live[0]
    for step in range(steps):
        part = slice(step * slots, (step + 1) * slots)
        tap = taps - steps + step
        inner_out[tap] = jnp.where(living, inner_raw[part, :], 0.0).astype(BF16)
        raw = jnp.where(head == 0, both[part, :width], both[part, width:])
        group_out[tap] = jnp.where(living[:, :width], raw, 0.0).astype(BF16)
    table[:, :LANES] = inner[steps].astype(F32)
    group_own = group[steps].astype(F32)
    table[:, LANES:] = jnp.concatenate([group_own, group_own], axis=1)
    gated[...] = gated_in[...]
    for step in range(steps):
        part = slice(step * moved_rows, (step + 1) * moved_rows)
        skipped = inner_conv[step] * skip_gain[0]
        sums[part, :] = (sums[part, :] + skipped) * gate_moved[part, :]
    driven[:moved_rows, :] = windows[steps]
    driven[moved_rows : 2 * moved_rows, :] = windows[taps + steps]

    def scatter(block, c, slot):
        place = block * ROWS + c
        for step in range(steps):
            row = step * moved_rows + place
            gated[pl.ds(step * slots + slot, 1), :] = sums[row : row + 1, :]
        table[pl.ds(slot, 1), :] = jnp.concatenate(
            [driven[place : place + 1, :], driven[moved_rows + place : moved_rows + place + 1, :]],
            axis=1,
        )

    each(scatter)
    for step in range(steps):
        part = slice(step * slots, (step + 1) * slots)
        gated_cast[step] = jnp.where(living, gated[part, :], 0.0).astype(BF16)
    inner_out[0] = jnp.where(living, table[:, :LANES], 0.0).astype(BF16)
    carried = jnp.where(head == 0, table[:, LANES : LANES + width], table[:, LANES + width :])
    group_out[0] = jnp.where(living[:, :width], carried, 0.0).astype(BF16)
    copies = [
        pltpu.make_async_copy(source, target, out_sem.at[place])
        for place, (source, target) in enumerate(
            [(inner_out, inner_next), (gated_cast, gated_out), (group_out, group_next)]
        )
    ]
    for copy in copies:
        copy.start()
    each(lambda block, c, slot: store(block, c, slot).wait())
    for copy in copies:
        copy.wait()


def arrive(replicas, cap, scalars, operands, scan_next, arrived):
    inner_moved, inner_raw, inner, group = operands[2], operands[7], operands[-2], operands[-1]
    taps, slots, _ = inner.shape
    rows = inner_raw.shape[0]
    steps = rows // slots
    places = len(sources_of(replicas)) * cap
    gated = jax.ShapeDtypeStruct((steps, slots, LANES), BF16)
    limit = SMALL_LIMIT if rounds_of(replicas) else LARGE_LIMIT
    return pl.pallas_call(
        functools.partial(arrive_kernel, replicas, cap),
        out_shape=[
            gated,
            jax.ShapeDtypeStruct(inner.shape, BF16),
            jax.ShapeDtypeStruct(group.shape, BF16),
            jax.ShapeDtypeStruct(scan_next.shape, BF16),
        ],
        in_specs=[HBM] * len(scalars) + [VMEM] * len(operands) + [HBM] + [VMEM] * len(arrived),
        out_specs=[HBM] * 4,
        scratch_shapes=[pltpu.SMEM(value.shape, value.dtype) for value in scalars]
        + [
            pltpu.VMEM(inner_moved.shape, F32),
            pltpu.VMEM(inner_moved.shape, F32),
            pltpu.VMEM((round_up(inner_moved.shape[0], LANES), LANES), F32),
            pltpu.VMEM((slots, 2 * LANES), F32),
            pltpu.VMEM((rows, LANES), F32),
            pltpu.VMEM(gated.shape, BF16),
            pltpu.VMEM(inner.shape, BF16),
            pltpu.VMEM(group.shape, BF16),
            pltpu.VMEM((places,) + scan_next.shape[1:], BF16),
            pltpu.SemaphoreType.DMA((places,)),
            pltpu.SemaphoreType.DMA((3,)),
        ],
        input_output_aliases={len(scalars) + len(operands): 3},
        compiler_params=pltpu.CompilerParams(vmem_limit_bytes=limit),
        cost_estimate=pl.CostEstimate(
            flops=10_000_000, bytes_accessed=2_000_000, transcendentals=0
        ),
        name="advance_arrived",
    )(*scalars, *operands, scan_next, *arrived)


def swap_heads(value):
    return lax.ppermute(value, "head", [(0, 1), (1, 0)])


def exchange(replicas, blocks):
    rounds = rounds_of(replicas)
    if not rounds:
        return [lax.all_to_all(blocks[0], "dp", 0, 0, tiled=True)]
    return [
        lax.ppermute(block, "dp", [(source, source ^ mask) for source in range(replicas)])
        for mask, block in zip(rounds, blocks)
    ]


def per_device(
    replicas,
    tokens,
    inner_weight,
    gate_weight,
    group_weight,
    delta_weight,
    inner_taps,
    inner_offset,
    group_taps,
    group_offset,
    decay_log,
    delta_bias,
    skip_gain,
    inner_window,
    group_window,
    scan_state,
    send_list,
    receive_list,
    live_count,
):
    steps, slots, half = tokens.shape
    cap = send_list.shape[1] // replicas
    scan = jnp.transpose(scan_state, (0, 2, 1))
    inner = jnp.transpose(inner_window, (1, 0, 2))
    group = jnp.transpose(group_window, (1, 0, 2))
    own = tokens.reshape(steps * slots, half)

    group_weight = group_weight.T
    inner_offset = inner_offset[None]
    group_taps = jnp.concatenate([group_taps, group_offset[None]], axis=0)
    group_other = swap_heads(group)
    operands = (
        receive_list,
        live_count,
        decay_log,
        delta_bias,
        skip_gain,
        own,
        swap_heads(own),
        inner_weight,
        gate_weight,
        group_weight,
        swap_heads(group_weight),
        delta_weight.T,
        inner_taps,
        inner_offset,
        group_taps,
        swap_heads(group_taps),
        inner,
        group,
        group_other,
        scan,
    )
    blocks = pack(replicas, cap, send_list, scan, inner, group, group_other)
    arrived = exchange(replicas, blocks)
    light = [
        block for mask, block in zip(rounds_of(replicas), arrived) if mask < replicas // 2
    ]
    prepared = stay(replicas, cap, operands, light[:EARLIER])
    plan, gated, group_weights, inner_raw, both, *moved, scan_next = prepared
    gated, inner_next, group_next, scan_next = arrive(
        replicas,
        cap,
        (plan, live_count, skip_gain),
        (gated, group_weights, *moved, inner_raw, both, inner_taps, inner_offset, inner, group),
        scan_next,
        arrived,
    )
    return (
        gated,
        jnp.transpose(inner_next, (1, 0, 2)),
        jnp.transpose(group_next, (1, 0, 2)),
        jnp.transpose(scan_next, (0, 2, 1)),
    )


def solution(mesh):
    in_specs = (
        P(None, ("grp", "dp"), "head"),
        P(None, "head"),
        P(None, "head"),
        P(None, "head"),
        P(None, "head"),
        P(None, "head"),
        P("head"),
        P(None, "head"),
        P("head"),
        P("head"),
        P("head"),
        P("head"),
        P(("grp", "dp"), None, "head"),
        P(("grp", "dp"), None, "head"),
        P(("grp", "dp"), "head", None),
        P(("grp", "dp"), None),
        P(("grp", "dp"), None),
        P(("grp", "dp")),
    )
    out_specs = (
        P(None, ("grp", "dp"), "head"),
        P(("grp", "dp"), None, "head"),
        P(("grp", "dp"), None, "head"),
        P(("grp", "dp"), "head", None),
    )
    return jax.shard_map(
        functools.partial(per_device, mesh.shape["dp"]),
        mesh=mesh,
        in_specs=in_specs,
        out_specs=out_specs,
        check_vma=False,
    )
```

profile of v0, /device:TPU:22, one launch (start us, length us, event | category | flops | bytes accessed | tf_op | source)
XLA Modules:
  0.0 49.1 jit_solution(18239789429556713526)
XLA Ops:
  0.6 0.1 collective-permute-start.1
  0.7 0.5 %collective-permute-start = (bf16[112,2048]{1,0:T(8,128)(2,1)}, bf16[112,2048]{1,0:T(8,128)(2,1)S(1)}, u32[]{:S(2)}, u32[]{:S(2)}) collective-permute-start(bf16[112,2048]{1,0:T(8,128)(2,1)} %bitcast.25), channel_id=1, source_target_pairs={{0,1},{1,0},{2,3},{3,2},{4,5},{5,4},{6,7},{7,6},{8,9},{9,8},{10,11... | collective-permute-start | bytes 1376264 | tf_op jit(solution)/shard_map/ppermute | solution.py:692
  1.2 0.1 collective-permute-start.3
  1.3 2.2 %collective-permute-done.3.group_other.group_other_hbm = bf16[3,56,64]{2,1,0:T(8,128)(2,1)S(1)} collective-permute-done((bf16[3,56,64]{2,1,0:T(8,128)(2,1)}, bf16[3,56,64]{2,1,0:T(8,128)(2,1)S(1)}, u32[]{:S(2)}, u32[]{:S(2)}) %collective-permute-start.3) | collective-permute-done | bytes 21536 | tf_op jit(solution)/shard_map/ppermute | solution.py:692
  3.5 0.6 %copy-done.20 = bf16[3,56,64]{2,1,0:T(8,128)(2,1)} copy-done((bf16[3,56,64]{2,1,0:T(8,128)(2,1)}, bf16[3,56,64]{2,1,0:T(8,128)(2,1)S(1)}, u32[]{:S(2)}) %copy-start.20) | copy-done | bytes 21528
  4.2 3.3 %pack_leaving.1 = (bf16[1,496,128]{2,1,0:T(8,128)(2,1)}, bf16[1,496,128]{2,1,0:T(8,128)(2,1)}, bf16[1,496,128]{2,1,0:T(8,128)(2,1)}, bf16[1,496,128]{2,1,0:T(8,1...) custom-call(bf16[56,64,128]{2,1,0:T(8,128)(2,1)} %bitcast.20, ...), custom_call_target="tpu_custom_call" | custom-call | bytes 2000000 | tf_op jit(solution)/shard_map/pack_leaving/pallas_call | solution.py:156
  7.4 0.0 copy-start.23
  7.4 0.6 %collective-permute-start.4 = (bf16[1,496,128]{2,1,0:T(8,128)(2,1)}, bf16[1,496,128]{2,1,0:T(8,128)(2,1)S(1)}, u32[]{:S(2)}, u32[]{:S(2)}) collective-permute-start(bf16[1,496,128]{2,1,0:T(8,128)(2,1)} %get-tuple-element.26), channel_id=1, source_target_pairs={{0,2},{2,0},{4,6},{6,4},{8,10},{10,8},{12,14},{14,12},{1,3},{3,1},... | collective-permute-start | bytes 380936 | tf_op jit(solution)/shard_map/ppermute | solution.py:700
  8.0 1.6 %collective-permute-start.5 = (bf16[1,496,128]{2,1,0:T(8,128)(2,1)}, bf16[1,496,128]{2,1,0:T(8,128)(2,1)S(1)}, u32[]{:S(2)}, u32[]{:S(2)}) collective-permute-start(bf16[1,496,128]{2,1,0:T(8,128)(2,1)} %get-tuple-element.27), channel_id=1, source_target_pairs={{0,4},{2,6},{4,0},{6,2},{8,12},{10,14},{12,8},{14,10},{1,5},{3,7},... | collective-permute-start | bytes 380936 | tf_op jit(solution)/shard_map/ppermute | solution.py:700
  9.6 0.0 copy-done.23
  9.6 0.0 copy-done.24
  9.6 0.0 copy-start.21
  9.6 0.1 collective-permute-start.2
  9.7 1.2 %collective-permute-done.2.group_taps_other_hbm = f32[5,64]{1,0:T(8,128)S(1)} collective-permute-done((f32[5,64]{1,0:T(8,128)S(1)}, f32[5,64]{1,0:T(8,128)S(1)}, u32[]{:S(2)}, u32[]{:S(2)}) %collective-permute-start.2) | collective-permute-done | bytes 1312 | tf_op jit(solution)/shard_map/ppermute | solution.py:692
  10.9 0.3 collective-permute-start.6
  11.2 2.0 %collective-permute-done.4.refs_0_ = bf16[1,496,128]{2,1,0:T(8,128)(2,1)S(1)} collective-permute-done((bf16[1,496,128]{2,1,0:T(8,128)(2,1)}, bf16[1,496,128]{2,1,0:T(8,128)(2,1)S(1)}, u32[]{:S(2)}, u32[]{:S(2)}) %collective-permute-start.4) | collective-permute-done | bytes 127008 | tf_op jit(solution)/shard_map/ppermute | solution.py:700
  13.2 1.6 %collective-permute-start.7 = (bf16[1,496,128]{2,1,0:T(8,128)(2,1)}, bf16[1,496,128]{2,1,0:T(8,128)(2,1)S(1)}, u32[]{:S(2)}, u32[]{:S(2)}) collective-permute-start(bf16[1,496,128]{2,1,0:T(8,128)(2,1)} %get-tuple-element.40), channel_id=1, source_target_pairs={{0,10},{2,8},{4,14},{6,12},{8,2},{10,0},{12,6},{14,4},{1,11},{3,9}... | collective-permute-start | bytes 380936 | tf_op jit(solution)/shard_map/ppermute | solution.py:700
  14.8 0.0 collective-permute-done.5.refs_1_.refs_2_
  14.8 1.4 %collective-permute-start.8 = (bf16[1,496,128]{2,1,0:T(8,128)(2,1)}, bf16[1,496,128]{2,1,0:T(8,128)(2,1)S(1)}, u32[]{:S(2)}, u32[]{:S(2)}) collective-permute-start(bf16[1,496,128]{2,1,0:T(8,128)(2,1)} %get-tuple-element.41), channel_id=1, source_target_pairs={{0,12},{2,14},{4,8},{6,10},{8,4},{10,6},{12,0},{14,2},{1,13},{3,15... | collective-permute-start | bytes 380936 | tf_op jit(solution)/shard_map/ppermute | solution.py:700
  16.2 0.0 collective-permute-done.other_hbm
  16.2 1.0 %collective-permute-start.9 = (bf16[1,496,128]{2,1,0:T(8,128)(2,1)}, bf16[1,496,128]{2,1,0:T(8,128)(2,1)S(1)}, u32[]{:S(2)}, u32[]{:S(2)}) collective-permute-start(bf16[1,496,128]{2,1,0:T(8,128)(2,1)} %get-tuple-element.42), channel_id=1, source_target_pairs={{0,14},{2,12},{4,10},{6,8},{8,6},{10,4},{12,2},{14,0},{1,15},{3,13... | collective-permute-start | bytes 380936 | tf_op jit(solution)/shard_map/ppermute | solution.py:700
  17.2 0.0 collective-permute-done.1.group_weight_other
  17.2 0.0 copy-done.21
  17.2 0.0 copy-done.22
  17.2 3.0 %collective-permute-start.10 = (bf16[1,496,128]{2,1,0:T(8,128)(2,1)}, bf16[1,496,128]{2,1,0:T(8,128)(2,1)S(1)}, u32[]{:S(2)}, u32[]{:S(2)}) collective-permute-start(bf16[1,496,128]{2,1,0:T(8,128)(2,1)} %get-tuple-element.43), channel_id=1, source_target_pairs={{0,6},{2,4},{4,2},{6,0},{8,14},{10,12},{12,10},{14,8},{1,7},{3,5},... | collective-permute-start | bytes 380936 | tf_op jit(solution)/shard_map/ppermute | solution.py:700
  22.8 0.0 copy-done
  22.8 0.0 copy-start.4
  22.9 0.0 copy-start.5
  22.9 6.6 %advance_staying.1 = (s32[1,128]{1,0:T(1,128)}, f32[112,128]{1,0:T(8,128)}, f32[8,128]{1,0:T(8,128)}, f32[112,128]{1,0:T(8,128)}, f32[112,128]{1,0:T(8,128)}, /*...) custom-call(s32[1,56]{1,0:T(1,128)} %receive_hbm.1, ...), custom_call_target="tpu_custom_call" | custom-call | flops 300000000 | bytes 6000000 | tf_op jit(solution)/shard_map/advance_staying/pallas_call | solution.py:459
  29.5 0.0 collective-permute-done.6.refs_1_
  29.5 0.0 collective-permute-done.7.refs_3_
  29.5 4.3 %collective-permute-done.8.refs_4_ = bf16[1,496,128]{2,1,0:T(8,128)(2,1)S(1)} collective-permute-done((bf16[1,496,128]{2,1,0:T(8,128)(2,1)}, bf16[1,496,128]{2,1,0:T(8,128)(2,1)S(1)}, u32[]{:S(2)}, u32[]{:S(2)}) %collective-permute-start.8) | collective-permute-done | bytes 127008 | tf_op jit(solution)/shard_map/ppermute | solution.py:700
  33.8 2.9 %collective-permute-done.9.refs_5_ = bf16[1,496,128]{2,1,0:T(8,128)(2,1)S(1)} collective-permute-done((bf16[1,496,128]{2,1,0:T(8,128)(2,1)}, bf16[1,496,128]{2,1,0:T(8,128)(2,1)S(1)}, u32[]{:S(2)}, u32[]{:S(2)}) %collective-permute-start.9) | collective-permute-done | bytes 127008 | tf_op jit(solution)/shard_map/ppermute | solution.py:700
  36.7 0.0 collective-permute-done.10.refs_6_
  36.7 0.6 %copy-done.15 = f32[8,128]{1,0:T(8,128)S(1)} copy-done((f32[8,128]{1,0:T(8,128)S(1)}, f32[8,128]{1,0:T(8,128)}, u32[]{:S(2)}) %copy-start.15) | copy-done | bytes 4120
  37.4 0.0 copy-done.14
  37.4 0.0 copy-done.16
  37.4 0.9 %copy-done.1 = bf16[1,496,128]{2,1,0:T(8,128)(2,1)S(1)} copy-done((bf16[1,496,128]{2,1,0:T(8,128)(2,1)S(1)}, bf16[1,496,128]{2,1,0:T(8,128)(2,1)}, u32[]{:S(2)}) %copy-start.1) | copy-done | bytes 127000
  38.3 0.9 %copy-done.3 = bf16[1,496,128]{2,1,0:T(8,128)(2,1)S(1)} copy-done((bf16[1,496,128]{2,1,0:T(8,128)(2,1)S(1)}, bf16[1,496,128]{2,1,0:T(8,128)(2,1)}, u32[]{:S(2)}) %copy-start.3) | copy-done | bytes 127000
  39.2 0.8 %copy-done.6 = f32[112,128]{1,0:T(8,128)S(1)} copy-done((f32[112,128]{1,0:T(8,128)S(1)}, f32[112,128]{1,0:T(8,128)}, u32[]{:S(2)}) %copy-start.6) | copy-done | bytes 57368
  40.0 0.8 %copy-done.7 = f32[112,128]{1,0:T(8,128)S(1)} copy-done((f32[112,128]{1,0:T(8,128)S(1)}, f32[112,128]{1,0:T(8,128)}, u32[]{:S(2)}) %copy-start.7) | copy-done | bytes 57368
  40.8 0.8 %copy-done.8 = f32[112,128]{1,0:T(8,128)S(1)} copy-done((f32[112,128]{1,0:T(8,128)S(1)}, f32[112,128]{1,0:T(8,128)}, u32[]{:S(2)}) %copy-start.8) | copy-done | bytes 57368
  41.6 0.8 %copy-done.9 = f32[112,128]{1,0:T(8,128)S(1)} copy-done((f32[112,128]{1,0:T(8,128)S(1)}, f32[112,128]{1,0:T(8,128)}, u32[]{:S(2)}) %copy-start.9) | copy-done | bytes 57368
  42.5 0.8 %copy-done.10 = f32[112,128]{1,0:T(8,128)S(1)} copy-done((f32[112,128]{1,0:T(8,128)S(1)}, f32[112,128]{1,0:T(8,128)}, u32[]{:S(2)}) %copy-start.10) | copy-done | bytes 57368
  43.3 0.8 %copy-done.11 = f32[112,128]{1,0:T(8,128)S(1)} copy-done((f32[112,128]{1,0:T(8,128)S(1)}, f32[112,128]{1,0:T(8,128)}, u32[]{:S(2)}) %copy-start.11) | copy-done | bytes 57368
  44.1 0.8 %copy-done.12 = f32[112,128]{1,0:T(8,128)S(1)} copy-done((f32[112,128]{1,0:T(8,128)S(1)}, f32[112,128]{1,0:T(8,128)}, u32[]{:S(2)}) %copy-start.12) | copy-done | bytes 57368
  44.9 0.8 %copy-done.13 = f32[112,128]{1,0:T(8,128)S(1)} copy-done((f32[112,128]{1,0:T(8,128)S(1)}, f32[112,128]{1,0:T(8,128)}, u32[]{:S(2)}) %copy-start.13) | copy-done | bytes 57368
  45.7 3.3 %advance_arrived.1 = (bf16[2,56,128]{2,1,0:T(8,128)(2,1)}, bf16[3,56,128]{2,1,0:T(8,128)(2,1)}, bf16[3,56,64]{2,1,0:T(8,128)(2,1)}, bf16[56,64,128]{2,1,0:T(8,128)(2,1)}) custom-call(s32[1,128]{1,0:T(1,128)S(1)} %copy-done.17, s32[1]{0:T(128)S(6)} %copy.27.live_hbm, f32[1]{0:T(128)S(6)} %copy.26.skip_gain_hbm, ...), custom_call_target="tpu_custom_call", output_to_operand_aliasing={{3}: (16, {})} | custom-call | flops 10000000 | bytes 2000000 | tf_op jit(solution)/shard_map/advance_arrived/pallas_call | solution.py:658
  (28 shorter events, 0.1 us)
Async XLA Ops:
  0.6 16.6 %collective-permute-start.1 = (bf16[64,4096]{1,0:T(8,128)(2,1)}, bf16[64,4096]{1,0:T(8,128)(2,1)S(1)}, u32[]{:S(2)}, u32[]{:S(2)}) collective-permute-start(bf16[64,4096]{1,0:T(8,128)(2,1)} %bitcast.23), channel_id=1, source_target_pairs={{0,1},{1,0},{2,3},{3,2},{4,5},{5,4},{6,7},{7,6},{8,9},{9,8},{10,11... | collective-permute-start | bytes 1572872 | tf_op jit(solution)/shard_map/ppermute | solution.py:692
  0.7 15.5 %collective-permute-start = (bf16[112,2048]{1,0:T(8,128)(2,1)}, bf16[112,2048]{1,0:T(8,128)(2,1)S(1)}, u32[]{:S(2)}, u32[]{:S(2)}) collective-permute-start(bf16[112,2048]{1,0:T(8,128)(2,1)} %bitcast.25), channel_id=1, source_target_pairs={{0,1},{1,0},{2,3},{3,2},{4,5},{5,4},{6,7},{7,6},{8,9},{9,8},{10,11... | collective-permute-start | bytes 1376264 | tf_op jit(solution)/shard_map/ppermute | solution.py:692
  1.2 2.3 %collective-permute-start.3 = (bf16[3,56,64]{2,1,0:T(8,128)(2,1)}, bf16[3,56,64]{2,1,0:T(8,128)(2,1)S(1)}, u32[]{:S(2)}, u32[]{:S(2)}) collective-permute-start(bf16[3,56,64]{2,1,0:T(8,128)(2,1)} %bitcast.14), channel_id=1, source_target_pairs={{0,1},{1,0},{2,3},{3,2},{4,5},{5,4},{6,7},{7,6},{8,9},{9,8},{10,11... | collective-permute-start | bytes 64520 | tf_op jit(solution)/shard_map/ppermute | solution.py:692
  3.5 0.6 %copy-start.20 = (bf16[3,56,64]{2,1,0:T(8,128)(2,1)}, bf16[3,56,64]{2,1,0:T(8,128)(2,1)S(1)}, u32[]{:S(2)}) copy-start(bf16[3,56,64]{2,1,0:T(8,128)(2,1)S(1)} %collective-permute-done.3.group_other.group_other_hbm) | copy-start | bytes 64516
  7.4 2.2 %copy-start.23 = (f32[4,64]{1,0:T(4,128)S(1)}, f32[4,64]{1,0:T(4,128)}, u32[]{:S(2)}) copy-start(f32[4,64]{1,0:T(4,128)} %param.25) | copy-start | bytes 3076
  7.4 5.7 %collective-permute-start.4 = (bf16[1,496,128]{2,1,0:T(8,128)(2,1)}, bf16[1,496,128]{2,1,0:T(8,128)(2,1)S(1)}, u32[]{:S(2)}, u32[]{:S(2)}) collective-permute-start(bf16[1,496,128]{2,1,0:T(8,128)(2,1)} %get-tuple-element.26), channel_id=1, source_target_pairs={{0,2},{2,0},{4,6},{6,4},{8,10},{10,8},{12,14},{14,12},{1,3},{3,1},... | collective-permute-start | bytes 380936 | tf_op jit(solution)/shard_map/ppermute | solution.py:700
  8.0 1.6 %copy-start.24 = (f32[64]{0:T(128)S(1)}, f32[64]{0:T(128)}, u32[]{:S(2)}) copy-start(f32[64]{0:T(128)} %param.26) | copy-start | bytes 772
  8.0 6.7 %collective-permute-start.5 = (bf16[1,496,128]{2,1,0:T(8,128)(2,1)}, bf16[1,496,128]{2,1,0:T(8,128)(2,1)S(1)}, u32[]{:S(2)}, u32[]{:S(2)}) collective-permute-start(bf16[1,496,128]{2,1,0:T(8,128)(2,1)} %get-tuple-element.27), channel_id=1, source_target_pairs={{0,4},{2,6},{4,0},{6,2},{8,12},{10,14},{12,8},{14,10},{1,5},{3,7},... | collective-permute-start | bytes 380936 | tf_op jit(solution)/shard_map/ppermute | solution.py:700
  9.6 7.6 %copy-start.21 = (f32[5,64]{1,0:T(8,128)}, f32[5,64]{1,0:T(8,128)S(1)}, u32[]{:S(2)}) copy-start(f32[5,64]{1,0:T(8,128)S(1)} %pad_maximum_fusion.group_taps_hbm) | copy-start | bytes 3844
  9.6 1.2 %collective-permute-start.2 = (f32[5,64]{1,0:T(8,128)S(1)}, f32[5,64]{1,0:T(8,128)S(1)}, u32[]{:S(2)}, u32[]{:S(2)}) collective-permute-start(f32[5,64]{1,0:T(8,128)S(1)} %pad_maximum_fusion.group_taps_hbm), channel_id=1, source_target_pairs={{0,1},{1,0},{2,3},{3,2},{4,5},{5,4},{6,7},{7,6},{8,9},{9,8},{10,11... | collective-permute-start | bytes 3848 | tf_op jit(solution)/shard_map/ppermute | solution.py:692
  10.9 6.4 %copy-start.22 = (f32[5,64]{1,0:T(8,128)}, f32[5,64]{1,0:T(8,128)S(1)}, u32[]{:S(2)}) copy-start(f32[5,64]{1,0:T(8,128)S(1)} %collective-permute-done.2.group_taps_other_hbm) | copy-start | bytes 3844
  10.9 18.6 %collective-permute-start.6 = (bf16[1,496,128]{2,1,0:T(8,128)(2,1)}, bf16[1,496,128]{2,1,0:T(8,128)(2,1)S(1)}, u32[]{:S(2)}, u32[]{:S(2)}) collective-permute-start(bf16[1,496,128]{2,1,0:T(8,128)(2,1)} %get-tuple-element.39), channel_id=1, source_target_pairs={{0,8},{2,10},{4,12},{6,14},{8,0},{10,2},{12,4},{14,6},{1,9},{3,11}... | collective-permute-start | bytes 380936 | tf_op jit(solution)/shard_map/ppermute | solution.py:700
  13.2 9.6 %copy-start = (bf16[1,496,128]{2,1,0:T(8,128)(2,1)}, bf16[1,496,128]{2,1,0:T(8,128)(2,1)S(1)}, u32[]{:S(2)}) copy-start(bf16[1,496,128]{2,1,0:T(8,128)(2,1)S(1)} %collective-permute-done.4.refs_0_) | copy-start | bytes 380932
  13.2 16.3 %collective-permute-start.7 = (bf16[1,496,128]{2,1,0:T(8,128)(2,1)}, bf16[1,496,128]{2,1,0:T(8,128)(2,1)S(1)}, u32[]{:S(2)}, u32[]{:S(2)}) collective-permute-start(bf16[1,496,128]{2,1,0:T(8,128)(2,1)} %get-tuple-element.40), channel_id=1, source_target_pairs={{0,10},{2,8},{4,14},{6,12},{8,2},{10,0},{12,6},{14,4},{1,11},{3,9}... | collective-permute-start | bytes 380936 | tf_op jit(solution)/shard_map/ppermute | solution.py:700
  14.8 8.1 %copy-start.2 = (bf16[1,496,128]{2,1,0:T(8,128)(2,1)}, bf16[1,496,128]{2,1,0:T(8,128)(2,1)S(1)}, u32[]{:S(2)}) copy-start(bf16[1,496,128]{2,1,0:T(8,128)(2,1)S(1)} %collective-permute-done.5.refs_1_.refs_2_) | copy-start | bytes 380932
  14.8 19.0 %collective-permute-start.8 = (bf16[1,496,128]{2,1,0:T(8,128)(2,1)}, bf16[1,496,128]{2,1,0:T(8,128)(2,1)S(1)}, u32[]{:S(2)}, u32[]{:S(2)}) collective-permute-start(bf16[1,496,128]{2,1,0:T(8,128)(2,1)} %get-tuple-element.41), channel_id=1, source_target_pairs={{0,12},{2,14},{4,8},{6,10},{8,4},{10,6},{12,0},{14,2},{1,13},{3,15... | collective-permute-start | bytes 380936 | tf_op jit(solution)/shard_map/ppermute | solution.py:700
  16.2 6.6 %copy-start.19 = (bf16[112,2048]{1,0:T(8,128)(2,1)}, bf16[112,2048]{1,0:T(8,128)(2,1)S(1)}, u32[]{:S(2)}) copy-start(bf16[112,2048]{1,0:T(8,128)(2,1)S(1)} %collective-permute-done.other_hbm) | copy-start | bytes 1376260
  16.2 20.5 %collective-permute-start.9 = (bf16[1,496,128]{2,1,0:T(8,128)(2,1)}, bf16[1,496,128]{2,1,0:T(8,128)(2,1)S(1)}, u32[]{:S(2)}, u32[]{:S(2)}) collective-permute-start(bf16[1,496,128]{2,1,0:T(8,128)(2,1)} %get-tuple-element.42), channel_id=1, source_target_pairs={{0,14},{2,12},{4,10},{6,8},{8,6},{10,4},{12,2},{14,0},{1,15},{3,13... | collective-permute-start | bytes 380936 | tf_op jit(solution)/shard_map/ppermute | solution.py:700
  17.2 5.6 %copy-start.18 = (bf16[64,4096]{1,0:T(8,128)(2,1)}, bf16[64,4096]{1,0:T(8,128)(2,1)S(1)}, u32[]{:S(2)}) copy-start(bf16[64,4096]{1,0:T(8,128)(2,1)S(1)} %collective-permute-done.1.group_weight_other) | copy-start | bytes 1572868
  17.2 19.5 %collective-permute-start.10 = (bf16[1,496,128]{2,1,0:T(8,128)(2,1)}, bf16[1,496,128]{2,1,0:T(8,128)(2,1)S(1)}, u32[]{:S(2)}, u32[]{:S(2)}) collective-permute-start(bf16[1,496,128]{2,1,0:T(8,128)(2,1)} %get-tuple-element.43), channel_id=1, source_target_pairs={{0,6},{2,4},{4,2},{6,0},{8,14},{10,12},{12,10},{14,8},{1,7},{3,5},... | collective-permute-start | bytes 380936 | tf_op jit(solution)/shard_map/ppermute | solution.py:700
  22.8 13.9 %copy-start.4 = (bf16[56,3,128]{2,0,1:T(8,128)(2,1)S(1)}, bf16[56,3,128]{2,0,1:T(8,128)(2,1)}, u32[]{:S(2)}) copy-start(bf16[56,3,128]{2,0,1:T(8,128)(2,1)} %param.30) | copy-start | bytes 129028
  22.9 13.9 %copy-start.5 = (bf16[56,3,64]{2,0,1:T(8,128)(2,1)S(1)}, bf16[56,3,64]{2,0,1:T(8,128)(2,1)}, u32[]{:S(2)}) copy-start(bf16[56,3,64]{2,0,1:T(8,128)(2,1)} %param.31) | copy-start | bytes 64516
  36.7 0.7 %copy-start.15 = (f32[8,128]{1,0:T(8,128)S(1)}, f32[8,128]{1,0:T(8,128)}, u32[]{:S(2)}) copy-start(f32[8,128]{1,0:T(8,128)} %get-tuple-element.30.group_weights) | copy-start | bytes 12292
  36.7 0.7 %copy-start.14 = (f32[4,128]{1,0:T(4,128)S(1)}, f32[4,128]{1,0:T(4,128)}, u32[]{:S(2)}) copy-start(f32[4,128]{1,0:T(4,128)} %inner_taps.1) | copy-start | bytes 6148
  36.7 0.7 %copy-start.16 = (f32[128]{0:T(128)S(1)}, f32[128]{0:T(128)}, u32[]{:S(2)}) copy-start(f32[128]{0:T(128)} %param.24) | copy-start | bytes 1540
  36.7 0.7 %copy-start.17 = (s32[1,128]{1,0:T(1,128)S(1)}, s32[1,128]{1,0:T(1,128)}, u32[]{:S(2)}) copy-start(s32[1,128]{1,0:T(1,128)} %get-tuple-element.28.plan_hbm) | copy-start | bytes 1540
  37.4 0.9 %copy-start.1 = (bf16[1,496,128]{2,1,0:T(8,128)(2,1)S(1)}, bf16[1,496,128]{2,1,0:T(8,128)(2,1)}, u32[]{:S(2)}) copy-start(bf16[1,496,128]{2,1,0:T(8,128)(2,1)} %copy-done) | copy-start | bytes 380932
  38.3 0.9 %copy-start.3 = (bf16[1,496,128]{2,1,0:T(8,128)(2,1)S(1)}, bf16[1,496,128]{2,1,0:T(8,128)(2,1)}, u32[]{:S(2)}) copy-start(bf16[1,496,128]{2,1,0:T(8,128)(2,1)} %copy-done.2) | copy-start | bytes 380932
  39.2 0.8 %copy-start.6 = (f32[112,128]{1,0:T(8,128)S(1)}, f32[112,128]{1,0:T(8,128)}, u32[]{:S(2)}) copy-start(f32[112,128]{1,0:T(8,128)} %get-tuple-element.29.gated_in) | copy-start | bytes 172036
  40.0 0.8 %copy-start.7 = (f32[112,128]{1,0:T(8,128)S(1)}, f32[112,128]{1,0:T(8,128)}, u32[]{:S(2)}) copy-start(f32[112,128]{1,0:T(8,128)} %get-tuple-element.36.inner_raw) | copy-start | bytes 172036
  40.8 0.8 %copy-start.8 = (f32[112,128]{1,0:T(8,128)S(1)}, f32[112,128]{1,0:T(8,128)}, u32[]{:S(2)}) copy-start(f32[112,128]{1,0:T(8,128)} %get-tuple-element.37.both) | copy-start | bytes 172036
  41.6 0.8 %copy-start.9 = (f32[112,128]{1,0:T(8,128)S(1)}, f32[112,128]{1,0:T(8,128)}, u32[]{:S(2)}) copy-start(f32[112,128]{1,0:T(8,128)} %get-tuple-element.31.inner_moved) | copy-start | bytes 172036
  42.5 0.8 %copy-start.10 = (f32[112,128]{1,0:T(8,128)S(1)}, f32[112,128]{1,0:T(8,128)}, u32[]{:S(2)}) copy-start(f32[112,128]{1,0:T(8,128)} %get-tuple-element.32.group_moved) | copy-start | bytes 172036
  43.3 0.8 %copy-start.11 = (f32[112,128]{1,0:T(8,128)S(1)}, f32[112,128]{1,0:T(8,128)}, u32[]{:S(2)}) copy-start(f32[112,128]{1,0:T(8,128)} %get-tuple-element.33.gate_moved) | copy-start | bytes 172036
  44.1 0.8 %copy-start.12 = (f32[112,128]{1,0:T(8,128)S(1)}, f32[112,128]{1,0:T(8,128)}, u32[]{:S(2)}) copy-start(f32[112,128]{1,0:T(8,128)} %get-tuple-element.34.delta_moved) | copy-start | bytes 172036
  44.9 0.8 %copy-start.13 = (f32[112,128]{1,0:T(8,128)S(1)}, f32[112,128]{1,0:T(8,128)}, u32[]{:S(2)}) copy-start(f32[112,128]{1,0:T(8,128)} %get-tuple-element.35.decay_moved) | copy-start | bytes 172036
where the time goes:
time: 49.8 us; the launch traced here: 49.1 us
  Pallas kernels  13.2 us (27%)
  waiting for transfers between devices  12.6 us (25%)
  starting transfers between devices  10.2 us (20%)
  local copies, waits for them, and re-layouts  9.67 us (19%)
  between operations  3.4 us (7%)
    unnamed x50, local copies, waits for them, and re-layouts  9.67 us
    ppermute x7, starting transfers between devices, exchange(): lax.ppermute(block, 'dp', [(source, source ^ mask) for source in range(re...  9.51 us
    ppermute x7, waiting for transfers between devices, exchange(): lax.ppermute(block, 'dp', [(source, source ^ mask) for source in range(re...  9.18 us
    pallas_call x1, Pallas kernels, stay(): pl.pallas_call(functools.partial(stay_kernel, replicas, cap), out_shape=[...  6.59 us
    ppermute x4, waiting for transfers between devices, swap_heads(): return lax.ppermute(value, 'head', [(0, 1), (1, 0)])  3.4 us
    pallas_call x1, Pallas kernels, arrive(): pl.pallas_call(functools.partial(arrive_kernel, replicas, cap), out_shape...  3.33 us
    pallas_call x1, Pallas kernels, pack(): pl.pallas_call(functools.partial(pack_kernel, replicas, cap), out_shape=[...  3.27 us
  transfers between devices with their start and end apart: 11, of which 5 were waited for; matrix products, arithmetic and copies ran while one was open for 0% of the time, Pallas kernels for 20%

commit v1 on v0

--- a/solution.py
+++ b/solution.py
@@ -10,9 +10,9 @@
 F32 = jnp.float32
 BF16 = jnp.bfloat16
 SMALL_LIMIT = 8 * 1024 * 1024
+MEDIUM_LIMIT = 32 * 1024 * 1024
 LARGE_LIMIT = 60 * 1024 * 1024
 MAX_ROUNDS = 16
-EARLIER = 2
 LANES = 128
 ROWS = 8
 MAX_SETS = 64
@@ -41,7 +41,7 @@
     heavy = list(range(replicas // 2, replicas))
     order = []
     while light or heavy:
-        order += light[:1] + heavy[:1] if len(order) < 4 else heavy[:1] or light[:1]
+        order += light[:1] + heavy[:2] if len(order) < 2 else light[:1] + heavy[:1]
         light = [mask for mask in light if mask not in order]
         heavy = [mask for mask in heavy if mask not in order]
     return order
@@ -61,9 +61,9 @@
 def pack_kernel(replicas, cap, scan, send, inner, group, group_other, *refs):
     rounds = rounds_of(replicas)
     count = max(1, len(rounds))
-    outs = refs[:count]
-    (indices, inner_in, mine_in, theirs_in, held, table, picked, cast) = refs[count : count + 8]
-    load_sem, in_sem, out_sem, window_sem = refs[count + 8 :]
+    outs = refs[-12 - count : -12]
+    (indices, inner_in, mine_in, theirs_in, held, table, picked, cast) = refs[-12:-4]
+    load_sem, in_sem, out_sem, window_sem = refs[-4:]
     loads = [
         pltpu.make_async_copy(source, target, load_sem.at[place])
         for place, (source, target) in enumerate(
@@ -144,7 +144,7 @@
         window.wait()
 
 
-def pack(replicas, cap, send_list, scan, inner, group, group_other):
+def pack(replicas, cap, send_list, scan, inner, group, group_other, swapped):
     rounds = rounds_of(replicas)
     count = max(1, len(rounds))
     per_block = 1 if rounds else replicas
@@ -156,7 +156,7 @@
     return pl.pallas_call(
         functools.partial(pack_kernel, replicas, cap),
         out_shape=[jax.ShapeDtypeStruct((per_block, rows, LANES), BF16)] * count,
-        in_specs=[HBM] * 5,
+        in_specs=[HBM] * (5 + len(swapped)),
         out_specs=[HBM] * count,
         scratch_shapes=[
             pltpu.SMEM(send_list.shape, jnp.int32),
@@ -175,7 +175,7 @@
         compiler_params=pltpu.CompilerParams(vmem_limit_bytes=LARGE_LIMIT),
         cost_estimate=pl.CostEstimate(flops=0, bytes_accessed=2_000_000, transcendentals=0),
         name="pack_leaving",
-    )(scan, send_list, inner, group, group_other)
+    )(scan, send_list, inner, group, group_other, *swapped)
 
 
 def sources_of(replicas):
@@ -236,10 +236,6 @@
     replicas,
     cap,
     receive_hbm,
-    live_hbm,
-    decay_log_hbm,
-    delta_bias_hbm,
-    skip_gain_hbm,
     own_hbm,
     other_hbm,
     inner_weight,
@@ -249,8 +245,8 @@
     delta_weight,
     inner_taps_hbm,
     inner_offset_hbm,
-    group_taps_hbm,
-    group_taps_other_hbm,
+    small_hbm,
+    small_other_hbm,
     inner_hbm,
     group_hbm,
     group_other_hbm,
@@ -270,10 +266,6 @@
         decay_moved,
         scan_next,
         receive,
-        live,
-        decay_log,
-        delta_bias,
-        skip_gain,
         own,
         other,
         wide,
@@ -281,8 +273,8 @@
         delta_row,
         inner_taps,
         inner_offset,
-        group_taps,
-        group_taps_other,
+        small,
+        small_other,
         inner,
         group,
         group_other,
@@ -299,7 +291,7 @@
         done,
         sem,
         load_sem,
-    ) = refs[-41:]
+    ) = refs[-37:]
     taps, slots, _ = inner.shape
     rows, half = own.shape
     steps = rows // slots
@@ -320,14 +312,10 @@
         (other_hbm, other),
         (group_weight, band(head)),
         (group_weight_other, band(1 - head)),
-        (live_hbm, live),
-        (decay_log_hbm, decay_log),
-        (delta_bias_hbm, delta_bias),
-        (skip_gain_hbm, skip_gain),
         (inner_taps_hbm, inner_taps),
         (inner_offset_hbm, inner_offset),
-        (group_taps_hbm, group_taps),
-        (group_taps_other_hbm, group_taps_other),
+        (small_hbm, small),
+        (small_other_hbm, small_other),
         (inner_hbm, inner),
         (group_hbm, group),
         (group_other_hbm, group_other),
@@ -361,11 +349,21 @@
     inner_raw[...] = rounded(flat[:, :LANES])
     gate[...] = silu(rounded(flat[:, LANES:]))
     both[...] = rounded(deep[:, :first])
-    shifted = rounded(jnp.broadcast_to(deep[:, first : first + 1], (rows, LANES))) + delta_bias[0]
+    count = taps + 2
+
+    def full_row(number):
+        value = small[count + number : count + number + 1, :]
+        return jnp.concatenate([value, value], axis=1)
+
+    decay_log, delta_bias, skip_gain = (full_row(number) for number in range(3))
+    shifted = rounded(jnp.broadcast_to(deep[:, first : first + 1], (rows, LANES))) + delta_bias
     rate = jnp.maximum(shifted, 0.0) + jnp.log1p(jnp.exp(-jnp.abs(shifted)))
     delta[...] = rate
-    decay[...] = jnp.exp(-rate * jnp.exp(jnp.full((1, LANES), decay_log[0], F32)))
-    group_weights[: taps + 2, :] = both_halves(group_taps[...], group_taps_other[...])
+    decay[...] = jnp.exp(-rate * jnp.exp(decay_log))
+    group_weights[:count, :] = both_halves(small[:count, :], small_other[:count, :])
+    group_weights[count : count + 1, :] = skip_gain
+    live = small[count + 3, 0].astype(jnp.int32)
+    plan[0, plan.shape[1] - 1] = live
 
     def parts(ref):
         return [ref[step * slots : (step + 1) * slots, :] for step in range(steps)]
@@ -385,7 +383,7 @@
     for step in range(steps):
         part = slice(step * slots, (step + 1) * slots)
         driven[part, :] = delta[part, :] * inner_conv[step]
-        skipped[part, :] = inner_conv[step] * skip_gain[0]
+        skipped[part, :] = inner_conv[step] * skip_gain
         maps_in[part, :] = group_conv[step]
     sums[...] = jnp.zeros_like(sums)
     stride = ordered.shape[0] // steps
@@ -409,7 +407,7 @@
             maps,
             [step * stride + position for step in range(steps)],
         )
-        done[position] = jnp.where(slot < live[0], result, jnp.zeros_like(result))
+        done[position] = jnp.where(slot < live, result, jnp.zeros_like(result))
         copies.append(
             pltpu.make_async_copy(done.at[position], scan_next.at[slot], sem.at[position])
         )
@@ -439,8 +437,8 @@
         copy.wait()
 
 
-def stay(replicas, cap, operands, earlier):
-    scalars, arrays = operands[:5], operands[5:]
+def stay(replicas, cap, operands):
+    scalars, arrays = operands[:1], operands[1:]
     own, inner_weight, group_weight, delta_weight = arrays[0], arrays[2], arrays[4], arrays[6]
     inner, scan = arrays[-4], arrays[-1]
     taps, slots, _ = inner.shape
@@ -459,15 +457,15 @@
     return pl.pallas_call(
         functools.partial(stay_kernel, replicas, cap),
         out_shape=[
-            jax.ShapeDtypeStruct((1, round_up(moving + blocks * cap, LANES)), jnp.int32),
+            jax.ShapeDtypeStruct((1, round_up(moving + blocks * cap + 1, LANES)), jnp.int32),
             full,
-            jax.ShapeDtypeStruct((round_up(taps + 2, ROWS), LANES), F32),
+            jax.ShapeDtypeStruct((round_up(taps + 3, ROWS), LANES), F32),
             full,
             full,
         ]
         + [moved] * 5
         + [jax.ShapeDtypeStruct(scan.shape, BF16)],
-        in_specs=[HBM] * (len(operands) + len(earlier)),
+        in_specs=[HBM] * len(operands),
         out_specs=[SMEM] + [VMEM] * 9 + [HBM],
         scratch_shapes=[pltpu.SMEM(value.shape, value.dtype) for value in scalars]
         + [
@@ -484,22 +482,20 @@
             pltpu.VMEM((round_up(rows, LANES), LANES), F32),
             pltpu.VMEM((moving,) + scan.shape[1:], BF16),
             pltpu.SemaphoreType.DMA((moving,)),
-            pltpu.SemaphoreType.DMA((20,)),
+            pltpu.SemaphoreType.DMA((16,)),
         ],
-        compiler_params=pltpu.CompilerParams(vmem_limit_bytes=LARGE_LIMIT),
+        compiler_params=pltpu.CompilerParams(vmem_limit_bytes=MEDIUM_LIMIT),
         cost_estimate=pl.CostEstimate(
             flops=300_000_000, bytes_accessed=6_000_000, transcendentals=100_000
         ),
         name="advance_staying",
-    )(*operands, *earlier)
+    )(*operands)
 
 
 def arrive_kernel(
     replicas,
     cap,
     plan_hbm,
-    live_hbm,
-    skip_gain_hbm,
     gated_in,
     group_weights,
     inner_moved,
@@ -517,9 +513,8 @@
     *refs,
 ):
     del scan_in
-    arrived = refs[:-18]
-    gated_out, inner_next, group_next, scan_next = refs[-18:-14]
-    plan, live, skip_gain = refs[-14:-11]
+    arrived = refs[:-16]
+    gated_out, inner_next, group_next, scan_next, plan = refs[-16:-11]
     (driven, sums, ordered, table, gated, gated_cast, inner_out, group_out) = refs[-11:-3]
     done, sem, out_sem = refs[-3:]
     taps, slots, _ = inner.shape
@@ -528,14 +523,8 @@
     steps = inner_raw.shape[0] // slots
     width = group.shape[2]
     head = lax.axis_index("head")
-    loads = [
-        pltpu.make_async_copy(source, target, out_sem.at[place])
-        for place, (source, target) in enumerate(
-            [(plan_hbm, plan), (live_hbm, live), (skip_gain_hbm, skip_gain)]
-        )
-    ]
-    for load in loads:
-        load.start()
+    load = pltpu.make_async_copy(plan_hbm, plan, out_sem.at[0])
+    load.start()
     if rounds_of(replicas):
         blocks = [ref.at[0] for ref in arrived]
     else:
@@ -566,8 +555,8 @@
     stride = ordered.shape[0] // steps
     maps = transposed(group_conv, ordered, stride)
     sums[...] = jnp.zeros_like(sums)
-    for load in loads:
-        load.wait()
+    load.wait()
+    live = plan[0, plan.shape[1] - 1]
 
     def each(act):
         for block in range(len(blocks)):
@@ -595,11 +584,11 @@
             maps,
             [step * stride + place for step in range(steps)],
         )
-        done[block * cap + c] = jnp.where(slot < live[0], result, jnp.zeros_like(result))
+        done[block * cap + c] = jnp.where(slot < live, result, jnp.zeros_like(result))
         store(block, c, slot).start()
 
     each(advance)
-    living = lax.broadcasted_iota(jnp.int32, (slots, LANES), 0) < live[0]
+    living = lax.broadcasted_iota(jnp.int32, (slots, LANES), 0) < live
     for step in range(steps):
         part = slice(step * slots, (step + 1) * slots)
         tap = taps - steps + step
@@ -612,7 +601,7 @@
     gated[...] = gated_in[...]
     for step in range(steps):
         part = slice(step * moved_rows, (step + 1) * moved_rows)
-        skipped = inner_conv[step] * skip_gain[0]
+        skipped = inner_conv[step] * group_weights[taps + 2 : taps + 3, :]
         sums[part, :] = (sums[part, :] + skipped) * gate_moved[part, :]
     driven[:moved_rows, :] = windows[steps]
     driven[moved_rows : 2 * moved_rows, :] = windows[taps + steps]
@@ -647,7 +636,7 @@
         copy.wait()
 
 
-def arrive(replicas, cap, scalars, operands, scan_next, arrived):
+def arrive(replicas, cap, plan, operands, scan_next, arrived):
     inner_moved, inner_raw, inner, group = operands[2], operands[7], operands[-2], operands[-1]
     taps, slots, _ = inner.shape
     rows = inner_raw.shape[0]
@@ -663,10 +652,10 @@
             jax.ShapeDtypeStruct(group.shape, BF16),
             jax.ShapeDtypeStruct(scan_next.shape, BF16),
         ],
-        in_specs=[HBM] * len(scalars) + [VMEM] * len(operands) + [HBM] + [VMEM] * len(arrived),
+        in_specs=[HBM] + [VMEM] * len(operands) + [HBM] + [VMEM] * len(arrived),
         out_specs=[HBM] * 4,
-        scratch_shapes=[pltpu.SMEM(value.shape, value.dtype) for value in scalars]
-        + [
+        scratch_shapes=[
+            pltpu.SMEM(plan.shape, plan.dtype),
             pltpu.VMEM(inner_moved.shape, F32),
             pltpu.VMEM(inner_moved.shape, F32),
             pltpu.VMEM((round_up(inner_moved.shape[0], LANES), LANES), F32),
@@ -679,13 +668,13 @@
             pltpu.SemaphoreType.DMA((places,)),
             pltpu.SemaphoreType.DMA((3,)),
         ],
-        input_output_aliases={len(scalars) + len(operands): 3},
+        input_output_aliases={1 + len(operands): 3},
         compiler_params=pltpu.CompilerParams(vmem_limit_bytes=limit),
         cost_estimate=pl.CostEstimate(
             flops=10_000_000, bytes_accessed=2_000_000, transcendentals=0
         ),
         name="advance_arrived",
-    )(*scalars, *operands, scan_next, *arrived)
+    )(plan, *operands, scan_next, *arrived)
 
 
 def swap_heads(value):
@@ -732,41 +721,39 @@
 
     group_weight = group_weight.T
     inner_offset = inner_offset[None]
-    group_taps = jnp.concatenate([group_taps, group_offset[None]], axis=0)
+    numbers = jnp.concatenate([decay_log, delta_bias, skip_gain, live_count.astype(F32)])
+    numbers = jnp.broadcast_to(numbers[:, None], (numbers.shape[0], group_taps.shape[1]))
+    small = jnp.concatenate([group_taps, group_offset[None], numbers], axis=0)
     group_other = swap_heads(group)
-    operands = (
-        receive_list,
-        live_count,
-        decay_log,
-        delta_bias,
-        skip_gain,
-        own,
-        swap_heads(own),
-        inner_weight,
-        gate_weight,
-        group_weight,
-        swap_heads(group_weight),
-        delta_weight.T,
-        inner_taps,
-        inner_offset,
-        group_taps,
-        swap_heads(group_taps),
-        inner,
-        group,
-        group_other,
-        scan,
-    )
-    blocks = pack(replicas, cap, send_list, scan, inner, group, group_other)
+    swapped = [swap_heads(value) for value in (own, group_weight, small)]
+    blocks = pack(replicas, cap, send_list, scan, inner, group, group_other, swapped)
     arrived = exchange(replicas, blocks)
-    light = [
-        block for mask, block in zip(rounds_of(replicas), arrived) if mask < replicas // 2
-    ]
-    prepared = stay(replicas, cap, operands, light[:EARLIER])
-    plan, gated, group_weights, inner_raw, both, *moved, scan_next = prepared
+    plan, gated, group_weights, inner_raw, both, *moved, scan_next = stay(
+        replicas,
+        cap,
+        (
+            receive_list,
+            own,
+            swapped[0],
+            inner_weight,
+            gate_weight,
+            group_weight,
+            swapped[1],
+            delta_weight.T,
+            inner_taps,
+            inner_offset,
+            small,
+            swapped[2],
+            inner,
+            group,
+            group_other,
+            scan,
+        ),
+    )
     gated, inner_next, group_next, scan_next = arrive(
         replicas,
         cap,
-        (plan, live_count, skip_gain),
+        plan,
         (gated, group_weights, *moved, inner_raw, both, inner_taps, inner_offset, inner, group),
         scan_next,
         arrived,

time: 49.8 us -> 47.8 us (0.960)
  the two profiles are of different devices: /device:TPU:22 before, /device:TPU:0 now
where the time goes in v1:
time: 47.8 us; the launch traced here: 47.3 us
  starting transfers between devices  22 us (46%)
  Pallas kernels  12.3 us (26%)
  local copies, waits for them, and re-layouts  7.69 us (16%)
  between operations  3.39 us (7%)
  waiting for transfers between devices  1.12 us (2%)
  other arithmetic  0.85 us (2%)
    ppermute x7, starting transfers between devices, exchange(): lax.ppermute(block, 'dp', [(source, source ^ mask) for source in range(re...  20.9 us
    unnamed x38, local copies, waits for them, and re-layouts  7.69 us
    pallas_call x1, Pallas kernels, stay(): pl.pallas_call(functools.partial(stay_kernel, replicas, cap), out_shape=[...  5.59 us
    pallas_call x1, Pallas kernels, pack(): pl.pallas_call(functools.partial(pack_kernel, replicas, cap), out_shape=[...  3.43 us
    pallas_call x1, Pallas kernels, arrive(): pl.pallas_call(functools.partial(arrive_kernel, replicas, cap), out_shape...  3.26 us
    ppermute x4, starting transfers between devices, swap_heads(): return lax.ppermute(value, 'head', [(0, 1), (1, 0)])  1.11 us
    ppermute x4, waiting for transfers between devices, swap_heads(): return lax.ppermute(value, 'head', [(0, 1), (1, 0)])  1.1 us
  transfers between devices with their start and end apart: 11, of which 1 were waited for; matrix products, arithmetic and copies ran while one was open for 2% of the time, Pallas kernels for 12%

profile of v1, /device:TPU:0, one launch (start us, length us, event | category | flops | bytes accessed | tf_op | source)
XLA Modules:
  0.0 47.3 jit_solution(11653740849947566480)
XLA Ops:
  0.6 0.0 copy-start.5
  0.6 0.5 %collective-permute-start.1 = (bf16[64,4096]{1,0:T(8,128)(2,1)}, bf16[64,4096]{1,0:T(8,128)(2,1)S(1)}, u32[]{:S(2)}, u32[]{:S(2)}) collective-permute-start(bf16[64,4096]{1,0:T(8,128)(2,1)} %bitcast.13), channel_id=1, source_target_pairs={{0,1},{1,0},{2,3},{3,2},{4,5},{5,4},{6,7},{7,6},{8,9},{9,8},{10,11... | collective-permute-start | bytes 1572872 | tf_op jit(solution)/shard_map/ppermute | solution.py:681
  1.2 0.1 collective-permute-start
  1.2 0.4 collective-permute-start.3
  4.3 0.1 pad_maximum_fusion
  4.3 0.8 %maximum_maximum_fusion.small_hbm = f32[9,64]{1,0:T(8,128)S(1)} fusion(f32[1,64]{1,0:T(1,128)} %bitcast.28, f32[4,64]{1,0:T(4,128)} %param.25, f32[9]{0:T(128)S(1)} %pad_maximum_fusion), kind=kLoop, calls=%fused_computation | loop fusion | flops 1152 | bytes 3620 | tf_op jit(solution)/shard_map/concatenate | solution.py:726
  5.1 0.1 collective-permute-start.2
  5.2 1.1 %collective-permute-done.2.small_other_hbm.refs_2_ = f32[9,64]{1,0:T(8,128)S(1)} collective-permute-done((f32[9,64]{1,0:T(8,128)S(1)}, f32[9,64]{1,0:T(8,128)S(1)}, u32[]{:S(2)}, u32[]{:S(2)}) %collective-permute-start.2) | collective-permute-done | bytes 2336 | tf_op jit(solution)/shard_map/ppermute | solution.py:681
  6.3 0.0 collective-permute-done.3.group_other_hbm.group_other
  6.3 0.0 collective-permute-done.other_hbm.refs_0_
  6.3 0.0 copy-start.3
  6.3 0.0 collective-permute-done.1.group_weight_other.refs_1_
  6.3 0.0 copy-start.1
  6.3 0.6 %copy-done.13 = f32[9,64]{1,0:T(8,128)} copy-done((f32[9,64]{1,0:T(8,128)}, f32[9,64]{1,0:T(8,128)S(1)}, u32[]{:S(2)}) %copy-start.13) | copy-done | bytes 2328
  6.9 0.0 copy-done.11
  6.9 0.2 copy-done.3
  7.1 0.2 copy-done.1
  7.3 3.4 %pack_leaving.1 = (bf16[1,496,128]{2,1,0:T(8,128)(2,1)}, bf16[1,496,128]{2,1,0:T(8,128)(2,1)}, bf16[1,496,128]{2,1,0:T(8,128)(2,1)}, bf16[1,496,128]{2,1,0:T(8,1...) custom-call(bf16[56,64,128]{2,1,0:T(8,128)(2,1)} %bitcast.11, ...), custom_call_target="tpu_custom_call" | custom-call | bytes 2000000 | tf_op jit(solution)/shard_map/pack_leaving/pallas_call | solution.py:156
  10.7 0.0 copy-start.14
  10.7 5.7 %collective-permute-start.10 = (bf16[1,496,128]{2,1,0:T(8,128)(2,1)}, bf16[1,496,128]{2,1,0:T(8,128)(2,1)S(1)}, u32[]{:S(2)}, u32[]{:S(2)}) collective-permute-start(bf16[1,496,128]{2,1,0:T(8,128)(2,1)} %get-tuple-element.43), channel_id=1, source_target_pairs={{0,14},{2,12},{4,10},{6,8},{8,6},{10,4},{12,2},{14,0},{1,15},{3,13... | collective-permute-start | bytes 380936 | tf_op jit(solution)/shard_map/ppermute | solution.py:689
  16.4 0.5 %collective-permute-start.4 = (bf16[1,496,128]{2,1,0:T(8,128)(2,1)}, bf16[1,496,128]{2,1,0:T(8,128)(2,1)S(1)}, u32[]{:S(2)}, u32[]{:S(2)}) collective-permute-start(bf16[1,496,128]{2,1,0:T(8,128)(2,1)} %get-tuple-element.37), channel_id=1, source_target_pairs={{0,2},{2,0},{4,6},{6,4},{8,10},{10,8},{12,14},{14,12},{1,3},{3,1},... | collective-permute-start | bytes 380936 | tf_op jit(solution)/shard_map/ppermute | solution.py:689
  17.0 0.0 collective-permute-start.5
  17.0 3.8 %collective-permute-start.6 = (bf16[1,496,128]{2,1,0:T(8,128)(2,1)}, bf16[1,496,128]{2,1,0:T(8,128)(2,1)S(1)}, u32[]{:S(2)}, u32[]{:S(2)}) collective-permute-start(bf16[1,496,128]{2,1,0:T(8,128)(2,1)} %get-tuple-element.39), channel_id=1, source_target_pairs={{0,10},{2,8},{4,14},{6,12},{8,2},{10,0},{12,6},{14,4},{1,11},{3,9}... | collective-permute-start | bytes 380936 | tf_op jit(solution)/shard_map/ppermute | solution.py:689
  20.8 0.0 collective-permute-start.7
  20.8 0.0 collective-permute-done.10.refs_6_
  20.8 3.9 %collective-permute-start.8 = (bf16[1,496,128]{2,1,0:T(8,128)(2,1)}, bf16[1,496,128]{2,1,0:T(8,128)(2,1)S(1)}, u32[]{:S(2)}, u32[]{:S(2)}) collective-permute-start(bf16[1,496,128]{2,1,0:T(8,128)(2,1)} %get-tuple-element.41), channel_id=1, source_target_pairs={{0,12},{2,14},{4,8},{6,10},{8,4},{10,6},{12,0},{14,2},{1,13},{3,15... | collective-permute-start | bytes 380936 | tf_op jit(solution)/shard_map/ppermute | solution.py:689
  24.8 0.0 collective-permute-done.4.refs_0_
  24.8 6.8 %collective-permute-start.9 = (bf16[1,496,128]{2,1,0:T(8,128)(2,1)}, bf16[1,496,128]{2,1,0:T(8,128)(2,1)S(1)}, u32[]{:S(2)}, u32[]{:S(2)}) collective-permute-start(bf16[1,496,128]{2,1,0:T(8,128)(2,1)} %get-tuple-element.42), channel_id=1, source_target_pairs={{0,6},{2,4},{4,2},{6,0},{8,14},{10,12},{12,10},{14,8},{1,7},{3,5},... | collective-permute-start | bytes 380936 | tf_op jit(solution)/shard_map/ppermute | solution.py:689
  31.6 0.0 copy-done.5
  31.6 0.0 copy-done
  31.6 0.0 copy-done.9
  31.6 0.0 copy-done.10
  31.6 0.0 copy-done.15
  31.6 0.6 %copy-done.17 = f32[128]{0:T(128)S(1)} copy-done((f32[128]{0:T(128)S(1)}, f32[128]{0:T(128)}, u32[]{:S(2)}) %copy-start.17) | copy-done | bytes 536
  32.2 0.0 copy-done.18
  32.3 1.0 %copy-done.2 = bf16[64,4096]{1,0:T(8,128)(2,1)S(1)} copy-done((bf16[64,4096]{1,0:T(8,128)(2,1)S(1)}, bf16[64,4096]{1,0:T(8,128)(2,1)}, u32[]{:S(2)}) %copy-start.2) | copy-done | bytes 524312
  33.3 1.0 %copy-done.4 = bf16[112,2048]{1,0:T(8,128)(2,1)S(1)} copy-done((bf16[112,2048]{1,0:T(8,128)(2,1)S(1)}, bf16[112,2048]{1,0:T(8,128)(2,1)}, u32[]{:S(2)}) %copy-start.4) | copy-done | bytes 458776
  34.3 1.2 %copy-done.6 = bf16[4096,128]{1,0:T(8,128)(2,1)S(1)} copy-done((bf16[4096,128]{1,0:T(8,128)(2,1)S(1)}, bf16[4096,128]{1,0:T(8,128)(2,1)}, u32[]{:S(2)}) %copy-start.6) | copy-done | bytes 1048600
  35.5 1.0 %copy-done.7 = bf16[4096,64]{0,1:T(8,128)(2,1)S(1)} copy-done((bf16[4096,64]{0,1:T(8,128)(2,1)S(1)}, bf16[4096,64]{0,1:T(8,128)(2,1)}, u32[]{:S(2)}) %copy-start.7) | copy-done | bytes 524312
  36.6 1.0 %copy-done.8 = bf16[2,56,2048]{2,1,0:T(8,128)(2,1)S(1)} copy-done((bf16[2,56,2048]{2,1,0:T(8,128)(2,1)S(1)}, bf16[2,56,2048]{2,1,0:T(8,128)(2,1)}, u32[]{:S(2)}) %copy-start.8) | copy-done | bytes 458776
  37.6 0.8 %copy-done.12 = bf16[3,56,64]{2,1,0:T(8,128)(2,1)S(1)} copy-done((bf16[3,56,64]{2,1,0:T(8,128)(2,1)S(1)}, bf16[3,56,64]{2,1,0:T(8,128)(2,1)}, u32[]{:S(2)}) %copy-start.12) | copy-done | bytes 21528
  38.4 5.6 %advance_staying.1 = (s32[1,128]{1,0:T(1,128)S(1)}, f32[112,128]{1,0:T(8,128)S(1)}, f32[8,128]{1,0:T(8,128)S(1)}, f32[112,128]{1,0:T(8,128)S(1)}, f32[112,128]{1...) custom-call(s32[1,56]{1,0:T(1,128)S(1)} %copy-done.18, ...), custom_call_target="tpu_custom_call" | custom-call | flops 300000000 | bytes 6000000 | tf_op jit(solution)/shard_map/advance_staying/pallas_call | solution.py:457
  44.0 0.0 collective-permute-done.5.refs_1_
  44.0 0.0 collective-permute-done.6.refs_2_
  44.0 0.0 collective-permute-done.7.refs_3_
  44.0 0.0 collective-permute-done.8.refs_4_
  44.0 0.0 collective-permute-done.9.refs_5_
  44.0 3.3 %advance_arrived.1 = (bf16[2,56,128]{2,1,0:T(8,128)(2,1)}, bf16[3,56,128]{2,1,0:T(8,128)(2,1)}, bf16[3,56,64]{2,1,0:T(8,128)(2,1)}, bf16[56,64,128]{2,1,0:T(8,128)(2,1)}) custom-call(s32[1,128]{1,0:T(1,128)S(1)} %get-tuple-element.26.plan_hbm, f32[112,128]{1,0:T(8,128)S(1)} %get-tuple-element.27.gated_in, ...), custom_call_target="tpu_custom_call", output_to_operand_aliasing={{3}: (14, {})} | custom-call | flops 10000000 | bytes 2000000 | tf_op jit(solution)/shard_map/advance_arrived/pallas_call | solution.py:647
  (17 shorter events, 0.0 us)
Async XLA Ops:
  0.6 31.0 %copy-start.5 = (bf16[4096,128]{1,0:T(8,128)(2,1)S(1)}, bf16[4096,128]{1,0:T(8,128)(2,1)}, u32[]{:S(2)}) copy-start(bf16[4096,128]{1,0:T(8,128)(2,1)} %inner_weight.1) | copy-start | bytes 3145732
  0.6 5.7 %collective-permute-start.1 = (bf16[64,4096]{1,0:T(8,128)(2,1)}, bf16[64,4096]{1,0:T(8,128)(2,1)S(1)}, u32[]{:S(2)}, u32[]{:S(2)}) collective-permute-start(bf16[64,4096]{1,0:T(8,128)(2,1)} %bitcast.13), channel_id=1, source_target_pairs={{0,1},{1,0},{2,3},{3,2},{4,5},{5,4},{6,7},{7,6},{8,9},{9,8},{10,11... | collective-permute-start | bytes 1572872 | tf_op jit(solution)/shard_map/ppermute | solution.py:681
  1.2 5.1 %collective-permute-start = (bf16[112,2048]{1,0:T(8,128)(2,1)}, bf16[112,2048]{1,0:T(8,128)(2,1)S(1)}, u32[]{:S(2)}, u32[]{:S(2)}) collective-permute-start(bf16[112,2048]{1,0:T(8,128)(2,1)} %bitcast.15), channel_id=1, source_target_pairs={{0,1},{1,0},{2,3},{3,2},{4,5},{5,4},{6,7},{7,6},{8,9},{9,8},{10,11... | collective-permute-start | bytes 1376264 | tf_op jit(solution)/shard_map/ppermute | solution.py:681
  1.2 5.0 %collective-permute-start.3 = (bf16[3,56,64]{2,1,0:T(8,128)(2,1)}, bf16[3,56,64]{2,1,0:T(8,128)(2,1)S(1)}, u32[]{:S(2)}, u32[]{:S(2)}) collective-permute-start(bf16[3,56,64]{2,1,0:T(8,128)(2,1)} %bitcast.20), channel_id=1, source_target_pairs={{0,1},{1,0},{2,3},{3,2},{4,5},{5,4},{6,7},{7,6},{8,9},{9,8},{10,11... | collective-permute-start | bytes 64520 | tf_op jit(solution)/shard_map/ppermute | solution.py:681
  5.1 1.2 %collective-permute-start.2 = (f32[9,64]{1,0:T(8,128)S(1)}, f32[9,64]{1,0:T(8,128)S(1)}, u32[]{:S(2)}, u32[]{:S(2)}) collective-permute-start(f32[9,64]{1,0:T(8,128)S(1)} %maximum_maximum_fusion.small_hbm), channel_id=1, source_target_pairs={{0,1},{1,0},{2,3},{3,2},{4,5},{5,4},{6,7},{7,6},{8,9},{9,8},{10,11... | collective-permute-start | bytes 6920 | tf_op jit(solution)/shard_map/ppermute | solution.py:681
  6.3 0.6 %copy-start.13 = (f32[9,64]{1,0:T(8,128)}, f32[9,64]{1,0:T(8,128)S(1)}, u32[]{:S(2)}) copy-start(f32[9,64]{1,0:T(8,128)S(1)} %collective-permute-done.2.small_other_hbm.refs_2_) | copy-start | bytes 6916
  6.3 0.6 %copy-start.11 = (bf16[3,56,64]{2,1,0:T(8,128)(2,1)}, bf16[3,56,64]{2,1,0:T(8,128)(2,1)S(1)}, u32[]{:S(2)}) copy-start(bf16[3,56,64]{2,1,0:T(8,128)(2,1)S(1)} %collective-permute-done.3.group_other_hbm.group_other) | copy-start | bytes 64516
  6.3 0.8 %copy-start.3 = (bf16[112,2048]{1,0:T(8,128)(2,1)}, bf16[112,2048]{1,0:T(8,128)(2,1)S(1)}, u32[]{:S(2)}) copy-start(bf16[112,2048]{1,0:T(8,128)(2,1)S(1)} %collective-permute-done.other_hbm.refs_0_) | copy-start | bytes 1376260
  6.3 0.9 %copy-start.1 = (bf16[64,4096]{1,0:T(8,128)(2,1)}, bf16[64,4096]{1,0:T(8,128)(2,1)S(1)}, u32[]{:S(2)}) copy-start(bf16[64,4096]{1,0:T(8,128)(2,1)S(1)} %collective-permute-done.1.group_weight_other.refs_1_) | copy-start | bytes 1572868
  7.3 24.3 %copy-start = (bf16[56,128,64]{1,2,0:T(8,128)(2,1)S(1)}, bf16[56,128,64]{1,2,0:T(8,128)(2,1)}, u32[]{:S(2)}) copy-start(bf16[56,128,64]{1,2,0:T(8,128)(2,1)} %param.32) | copy-start | bytes 2752516
  7.3 24.3 %copy-start.9 = (bf16[56,3,128]{2,0,1:T(8,128)(2,1)S(1)}, bf16[56,3,128]{2,0,1:T(8,128)(2,1)}, u32[]{:S(2)}) copy-start(bf16[56,3,128]{2,0,1:T(8,128)(2,1)} %param.30) | copy-start | bytes 129028
  7.3 24.4 %copy-start.10 = (bf16[56,3,64]{2,0,1:T(8,128)(2,1)S(1)}, bf16[56,3,64]{2,0,1:T(8,128)(2,1)}, u32[]{:S(2)}) copy-start(bf16[56,3,64]{2,0,1:T(8,128)(2,1)} %param.31) | copy-start | bytes 64516
  7.3 24.4 %copy-start.15 = (bf16[4096,1]{0,1:T(2,128)(2,1)S(1)}, bf16[4096,1]{0,1:T(2,128)(2,1)}, u32[]{:S(2)}) copy-start(bf16[4096,1]{0,1:T(2,128)(2,1)} %param.22) | copy-start | bytes 24580
  10.7 20.9 %copy-start.14 = (f32[9,64]{1,0:T(8,128)S(1)}, f32[9,64]{1,0:T(8,128)}, u32[]{:S(2)}) copy-start(f32[9,64]{1,0:T(8,128)} %copy-done.13) | copy-start | bytes 6916
  10.7 10.1 %collective-permute-start.10 = (bf16[1,496,128]{2,1,0:T(8,128)(2,1)}, bf16[1,496,128]{2,1,0:T(8,128)(2,1)S(1)}, u32[]{:S(2)}, u32[]{:S(2)}) collective-permute-start(bf16[1,496,128]{2,1,0:T(8,128)(2,1)} %get-tuple-element.43), channel_id=1, source_target_pairs={{0,14},{2,12},{4,10},{6,8},{8,6},{10,4},{12,2},{14,0},{1,15},{3,13... | collective-permute-start | bytes 380936 | tf_op jit(solution)/shard_map/ppermute | solution.py:689
  16.4 8.3 %collective-permute-start.4 = (bf16[1,496,128]{2,1,0:T(8,128)(2,1)}, bf16[1,496,128]{2,1,0:T(8,128)(2,1)S(1)}, u32[]{:S(2)}, u32[]{:S(2)}) collective-permute-start(bf16[1,496,128]{2,1,0:T(8,128)(2,1)} %get-tuple-element.37), channel_id=1, source_target_pairs={{0,2},{2,0},{4,6},{6,4},{8,10},{10,8},{12,14},{14,12},{1,3},{3,1},... | collective-permute-start | bytes 380936 | tf_op jit(solution)/shard_map/ppermute | solution.py:689
  17.0 27.0 %collective-permute-start.5 = (bf16[1,496,128]{2,1,0:T(8,128)(2,1)}, bf16[1,496,128]{2,1,0:T(8,128)(2,1)S(1)}, u32[]{:S(2)}, u32[]{:S(2)}) collective-permute-start(bf16[1,496,128]{2,1,0:T(8,128)(2,1)} %get-tuple-element.38), channel_id=1, source_target_pairs={{0,8},{2,10},{4,12},{6,14},{8,0},{10,2},{12,4},{14,6},{1,9},{3,11}... | collective-permute-start | bytes 380936 | tf_op jit(solution)/shard_map/ppermute | solution.py:689
  17.0 27.0 %collective-permute-start.6 = (bf16[1,496,128]{2,1,0:T(8,128)(2,1)}, bf16[1,496,128]{2,1,0:T(8,128)(2,1)S(1)}, u32[]{:S(2)}, u32[]{:S(2)}) collective-permute-start(bf16[1,496,128]{2,1,0:T(8,128)(2,1)} %get-tuple-element.39), channel_id=1, source_target_pairs={{0,10},{2,8},{4,14},{6,12},{8,2},{10,0},{12,6},{14,4},{1,11},{3,9}... | collective-permute-start | bytes 380936 | tf_op jit(solution)/shard_map/ppermute | solution.py:689
  20.8 23.2 %collective-permute-start.7 = (bf16[1,496,128]{2,1,0:T(8,128)(2,1)}, bf16[1,496,128]{2,1,0:T(8,128)(2,1)S(1)}, u32[]{:S(2)}, u32[]{:S(2)}) collective-permute-start(bf16[1,496,128]{2,1,0:T(8,128)(2,1)} %get-tuple-element.40), channel_id=1, source_target_pairs={{0,4},{2,6},{4,0},{6,2},{8,12},{10,14},{12,8},{14,10},{1,5},{3,7},... | collective-permute-start | bytes 380936 | tf_op jit(solution)/shard_map/ppermute | solution.py:689
  20.8 23.2 %collective-permute-start.8 = (bf16[1,496,128]{2,1,0:T(8,128)(2,1)}, bf16[1,496,128]{2,1,0:T(8,128)(2,1)S(1)}, u32[]{:S(2)}, u32[]{:S(2)}) collective-permute-start(bf16[1,496,128]{2,1,0:T(8,128)(2,1)} %get-tuple-element.41), channel_id=1, source_target_pairs={{0,12},{2,14},{4,8},{6,10},{8,4},{10,6},{12,0},{14,2},{1,13},{3,15... | collective-permute-start | bytes 380936 | tf_op jit(solution)/shard_map/ppermute | solution.py:689
  24.8 6.9 %copy-start.16 = (f32[4,128]{1,0:T(4,128)S(1)}, f32[4,128]{1,0:T(4,128)}, u32[]{:S(2)}) copy-start(f32[4,128]{1,0:T(4,128)} %inner_taps.1) | copy-start | bytes 6148
  24.8 19.3 %collective-permute-start.9 = (bf16[1,496,128]{2,1,0:T(8,128)(2,1)}, bf16[1,496,128]{2,1,0:T(8,128)(2,1)S(1)}, u32[]{:S(2)}, u32[]{:S(2)}) collective-permute-start(bf16[1,496,128]{2,1,0:T(8,128)(2,1)} %get-tuple-element.42), channel_id=1, source_target_pairs={{0,6},{2,4},{4,2},{6,0},{8,14},{10,12},{12,10},{14,8},{1,7},{3,5},... | collective-permute-start | bytes 380936 | tf_op jit(solution)/shard_map/ppermute | solution.py:689
  31.6 0.7 %copy-start.17 = (f32[128]{0:T(128)S(1)}, f32[128]{0:T(128)}, u32[]{:S(2)}) copy-start(f32[128]{0:T(128)} %param.24) | copy-start | bytes 1540
  31.6 0.7 %copy-start.18 = (s32[1,56]{1,0:T(1,128)S(1)}, s32[1,56]{1,0:T(1,128)}, u32[]{:S(2)}) copy-start(s32[1,56]{1,0:T(1,128)} %receive_hbm.1) | copy-start | bytes 676
  32.3 1.0 %copy-start.2 = (bf16[64,4096]{1,0:T(8,128)(2,1)S(1)}, bf16[64,4096]{1,0:T(8,128)(2,1)}, u32[]{:S(2)}) copy-start(bf16[64,4096]{1,0:T(8,128)(2,1)} %copy-done.1) | copy-start | bytes 1572868
  33.3 1.0 %copy-start.4 = (bf16[112,2048]{1,0:T(8,128)(2,1)S(1)}, bf16[112,2048]{1,0:T(8,128)(2,1)}, u32[]{:S(2)}) copy-start(bf16[112,2048]{1,0:T(8,128)(2,1)} %copy-done.3) | copy-start | bytes 1376260
  34.3 1.2 %copy-start.6 = (bf16[4096,128]{1,0:T(8,128)(2,1)S(1)}, bf16[4096,128]{1,0:T(8,128)(2,1)}, u32[]{:S(2)}) copy-start(bf16[4096,128]{1,0:T(8,128)(2,1)} %gate_weight.1) | copy-start | bytes 3145732
  35.5 1.0 %copy-start.7 = (bf16[4096,64]{0,1:T(8,128)(2,1)S(1)}, bf16[4096,64]{0,1:T(8,128)(2,1)}, u32[]{:S(2)}) copy-start(bf16[4096,64]{0,1:T(8,128)(2,1)} %param.21) | copy-start | bytes 1572868
  36.6 1.0 %copy-start.8 = (bf16[2,56,2048]{2,1,0:T(8,128)(2,1)S(1)}, bf16[2,56,2048]{2,1,0:T(8,128)(2,1)}, u32[]{:S(2)}) copy-start(bf16[2,56,2048]{2,1,0:T(8,128)(2,1)} %param.18) | copy-start | bytes 1376260
  37.6 0.8 %copy-start.12 = (bf16[3,56,64]{2,1,0:T(8,128)(2,1)S(1)}, bf16[3,56,64]{2,1,0:T(8,128)(2,1)}, u32[]{:S(2)}) copy-start(bf16[3,56,64]{2,1,0:T(8,128)(2,1)} %copy-done.11) | copy-start | bytes 64516

commit v2 on v1

--- a/solution.py
+++ b/solution.py
@@ -10,9 +10,10 @@
 F32 = jnp.float32
 BF16 = jnp.bfloat16
 SMALL_LIMIT = 8 * 1024 * 1024
-MEDIUM_LIMIT = 32 * 1024 * 1024
-LARGE_LIMIT = 60 * 1024 * 1024
+MEDIUM_LIMIT = 16 * 1024 * 1024
+LARGE_LIMIT = 48 * 1024 * 1024
 MAX_ROUNDS = 16
+EARLIER = 3
 LANES = 128
 ROWS = 8
 MAX_SETS = 64
@@ -20,6 +21,10 @@
 VMEM = pl.BlockSpec(memory_space=pltpu.VMEM)
 SMEM = pl.BlockSpec(memory_space=pltpu.SMEM)
 HBM = pl.BlockSpec(memory_space=pl.ANY)
+
+
+def in_hbm(value):
+    return pltpu.with_memory_space_constraint(value, pltpu.HBM)
 
 
 def round_up(value, step):
@@ -39,12 +44,7 @@
         return []
     light = list(range(1, replicas // 2))
     heavy = list(range(replicas // 2, replicas))
-    order = []
-    while light or heavy:
-        order += light[:1] + heavy[:2] if len(order) < 2 else light[:1] + heavy[:1]
-        light = [mask for mask in light if mask not in order]
-        heavy = [mask for mask in heavy if mask not in order]
-    return order
+    return heavy[:1] + light[:2] + heavy[1:] + light[2:]
 
 
 def partner(replicas, mask):
@@ -61,87 +61,60 @@
 def pack_kernel(replicas, cap, scan, send, inner, group, group_other, *refs):
     rounds = rounds_of(replicas)
     count = max(1, len(rounds))
-    outs = refs[-12 - count : -12]
-    (indices, inner_in, mine_in, theirs_in, held, table, picked, cast) = refs[-12:-4]
-    load_sem, in_sem, out_sem, window_sem = refs[-4:]
+    outs = refs[-8 - count : -8]
+    indices, inner_in, group_in, table, picked, load_sem, list_sem, sem = refs[-8:]
+    load_list = pltpu.make_async_copy(send, indices, list_sem)
+    load_list.start()
     loads = [
         pltpu.make_async_copy(source, target, load_sem.at[place])
-        for place, (source, target) in enumerate(
-            [(send, indices), (inner, inner_in), (group, mine_in), (group_other, theirs_in)]
-        )
+        for place, (source, target) in enumerate([(inner, inner_in), (group, group_in)])
     ]
     for load in loads:
         load.start()
-    taps = inner_in.shape[0]
     state_rows = scan.shape[1]
-    blocks = []
     if rounds:
-        for ref, mask in zip(outs, rounds):
-            blocks.append((ref.at[0], partner(replicas, mask)))
+        blocks = [(ref.at[0], partner(replicas, mask)) for ref, mask in zip(outs, rounds)]
     else:
         blocks = [(outs[0].at[target], target) for target in range(replicas)]
-    loads[0].wait()
+    load_list.wait()
 
     plan = []
     for block, (ref, target) in enumerate(blocks):
         for c in range(cap):
             plan.append((block, ref, c, indices[0, target * cap + c]))
 
-    def fetch(place, index):
-        return pltpu.make_async_copy(scan.at[index], held.at[place], in_sem.at[place])
-
-    def store(place, ref, c):
-        return pltpu.make_async_copy(
-            held.at[place], ref.at[pl.ds(c * state_rows, state_rows)], out_sem.at[place]
-        )
-
-    for place, (_, _, _, index) in enumerate(plan):
-
-        @pl.when(index >= 0)
-        def _():
-            fetch(place, index).start()
-
-    for load in loads[1:]:
+    def each(act):
+        for place, (_, ref, c, index) in enumerate(plan):
+
+            @pl.when(index >= 0)
+            def _():
+                act(
+                    pltpu.make_async_copy(
+                        scan.at[index],
+                        ref.at[pl.ds(c * state_rows, state_rows)],
+                        sem.at[place],
+                    )
+                )
+
+    each(lambda copy: copy.start())
+    for load in loads:
         load.wait()
+    taps = inner_in.shape[0]
     for tap in range(taps):
         table[:, tap * LANES : (tap + 1) * LANES] = inner_in[tap].astype(F32)
         table[:, (taps + tap) * LANES : (taps + tap + 1) * LANES] = both_halves(
-            mine_in[tap].astype(F32), theirs_in[tap].astype(F32)
+            group_in[tap].astype(F32), group_other[tap].astype(F32)
         )
     picked[...] = jnp.zeros_like(picked)
-    for place, (block, _, c, index) in enumerate(plan):
+    for block, _, c, index in plan:
         row = table[pl.ds(jnp.maximum(index, 0), 1), :]
         for kind in range(2 * taps):
             picked[block, kind * ROWS + c : kind * ROWS + c + 1, :] = row[
                 :, kind * LANES : (kind + 1) * LANES
             ]
-    windows = []
     for block, (ref, _) in enumerate(blocks):
-        cast[block] = picked[block].astype(BF16)
-        windows.append(
-            pltpu.make_async_copy(
-                cast.at[block],
-                ref.at[pl.ds(cap * state_rows, cast.shape[1])],
-                window_sem.at[block],
-            )
-        )
-        windows[-1].start()
-
-    for place, (_, ref, c, index) in enumerate(plan):
-
-        @pl.when(index >= 0)
-        def _():
-            fetch(place, index).wait()
-            store(place, ref, c).start()
-
-    for place, (_, ref, c, index) in enumerate(plan):
-
-        @pl.when(index >= 0)
-        def _():
-            store(place, ref, c).wait()
-
-    for window in windows:
-        window.wait()
+        ref[cap * state_rows :, :] = picked[block].astype(BF16)
+    each(lambda copy: copy.wait())
 
 
 def pack(replicas, cap, send_list, scan, inner, group, group_other, swapped):
@@ -152,30 +125,25 @@
     window_rows = 2 * taps * ROWS
     rows = cap * scan.shape[1] + window_rows
     blocks = count * per_block
-    places = blocks * cap
     return pl.pallas_call(
         functools.partial(pack_kernel, replicas, cap),
-        out_shape=[jax.ShapeDtypeStruct((per_block, rows, LANES), BF16)] * count,
-        in_specs=[HBM] * (5 + len(swapped)),
-        out_specs=[HBM] * count,
+        out_shape=[pltpu.VMEM((per_block, rows, LANES), BF16)] * count,
+        in_specs=[HBM] * 4 + [VMEM] + [HBM] * len(swapped),
+        out_specs=[VMEM] * count,
         scratch_shapes=[
             pltpu.SMEM(send_list.shape, jnp.int32),
             pltpu.VMEM(inner.shape, BF16),
             pltpu.VMEM(group.shape, BF16),
-            pltpu.VMEM(group.shape, BF16),
-            pltpu.VMEM((places,) + scan.shape[1:], BF16),
             pltpu.VMEM((slots, 2 * taps * LANES), F32),
             pltpu.VMEM((blocks, window_rows, LANES), F32),
-            pltpu.VMEM((blocks, window_rows, LANES), BF16),
-            pltpu.SemaphoreType.DMA((4,)),
-            pltpu.SemaphoreType.DMA((places,)),
-            pltpu.SemaphoreType.DMA((places,)),
-            pltpu.SemaphoreType.DMA((blocks,)),
+            pltpu.SemaphoreType.DMA((2,)),
+            pltpu.SemaphoreType.DMA,
+            pltpu.SemaphoreType.DMA((blocks * cap,)),
         ],
-        compiler_params=pltpu.CompilerParams(vmem_limit_bytes=LARGE_LIMIT),
+        compiler_params=pltpu.CompilerParams(vmem_limit_bytes=SMALL_LIMIT),
         cost_estimate=pl.CostEstimate(flops=0, bytes_accessed=2_000_000, transcendentals=0),
         name="pack_leaving",
-    )(scan, send_list, inner, group, group_other, *swapped)
+    )(in_hbm(scan), in_hbm(send_list), in_hbm(inner), in_hbm(group), group_other, *swapped)
 
 
 def sources_of(replicas):
@@ -235,26 +203,30 @@
 def stay_kernel(
     replicas,
     cap,
+    decay_log,
+    delta_bias,
+    skip_gain,
+    live,
     receive_hbm,
     own_hbm,
-    other_hbm,
     inner_weight,
     gate_weight,
     group_weight,
-    group_weight_other,
     delta_weight,
     inner_taps_hbm,
     inner_offset_hbm,
-    small_hbm,
-    small_other_hbm,
     inner_hbm,
     group_hbm,
-    group_other_hbm,
     scan_hbm,
+    other,
+    group_weight_other,
+    small,
+    small_other,
+    group_other,
     *refs,
 ):
     (
-        plan,
+        plan_out,
         gated,
         group_weights,
         inner_raw,
@@ -265,19 +237,16 @@
         delta_moved,
         decay_moved,
         scan_next,
+        plan,
         receive,
         own,
-        other,
         wide,
         tall,
         delta_row,
         inner_taps,
         inner_offset,
-        small,
-        small_other,
         inner,
         group,
-        group_other,
         scan,
         inverse,
         gate,
@@ -291,7 +260,7 @@
         done,
         sem,
         load_sem,
-    ) = refs[-37:]
+    ) = refs[-34:]
     taps, slots, _ = inner.shape
     rows, half = own.shape
     steps = rows // slots
@@ -309,16 +278,12 @@
         (own_hbm, own),
         (inner_weight, wide.at[:, pl.ds(0, LANES)]),
         (gate_weight, wide.at[:, pl.ds(LANES, LANES)]),
-        (other_hbm, other),
         (group_weight, band(head)),
         (group_weight_other, band(1 - head)),
         (inner_taps_hbm, inner_taps),
         (inner_offset_hbm, inner_offset),
-        (small_hbm, small),
-        (small_other_hbm, small_other),
         (inner_hbm, inner),
         (group_hbm, group),
-        (group_other_hbm, group_other),
         (scan_hbm, scan),
     ]
     loads = [
@@ -349,21 +314,17 @@
     inner_raw[...] = rounded(flat[:, :LANES])
     gate[...] = silu(rounded(flat[:, LANES:]))
     both[...] = rounded(deep[:, :first])
-    count = taps + 2
-
-    def full_row(number):
-        value = small[count + number : count + number + 1, :]
-        return jnp.concatenate([value, value], axis=1)
-
-    decay_log, delta_bias, skip_gain = (full_row(number) for number in range(3))
-    shifted = rounded(jnp.broadcast_to(deep[:, first : first + 1], (rows, LANES))) + delta_bias
+    shifted = rounded(jnp.broadcast_to(deep[:, first : first + 1], (rows, LANES)))
+    shifted = shifted + delta_bias[0]
     rate = jnp.maximum(shifted, 0.0) + jnp.log1p(jnp.exp(-jnp.abs(shifted)))
     delta[...] = rate
-    decay[...] = jnp.exp(-rate * jnp.exp(decay_log))
-    group_weights[:count, :] = both_halves(small[:count, :], small_other[:count, :])
-    group_weights[count : count + 1, :] = skip_gain
-    live = small[count + 3, 0].astype(jnp.int32)
-    plan[0, plan.shape[1] - 1] = live
+    decay[...] = jnp.exp(-rate * jnp.exp(jnp.full((1, LANES), decay_log[0], F32)))
+    count = taps + 2
+    group_weights[:count, :] = both_halves(small[...], small_other[...])
+    group_weights[count : count + 1, :] = jnp.full((1, LANES), skip_gain[0], F32)
+    plan[0, plan.shape[1] - 1] = live[0]
+    save_plan = pltpu.make_async_copy(plan, plan_out, load_sem.at[0])
+    save_plan.start()
 
     def parts(ref):
         return [ref[step * slots : (step + 1) * slots, :] for step in range(steps)]
@@ -383,7 +344,7 @@
     for step in range(steps):
         part = slice(step * slots, (step + 1) * slots)
         driven[part, :] = delta[part, :] * inner_conv[step]
-        skipped[part, :] = inner_conv[step] * skip_gain
+        skipped[part, :] = inner_conv[step] * skip_gain[0]
         maps_in[part, :] = group_conv[step]
     sums[...] = jnp.zeros_like(sums)
     stride = ordered.shape[0] // steps
@@ -407,7 +368,7 @@
             maps,
             [step * stride + position for step in range(steps)],
         )
-        done[position] = jnp.where(slot < live, result, jnp.zeros_like(result))
+        done[position] = jnp.where(slot < live[0], result, jnp.zeros_like(result))
         copies.append(
             pltpu.make_async_copy(done.at[position], scan_next.at[slot], sem.at[position])
         )
@@ -435,12 +396,12 @@
 
     for copy in copies:
         copy.wait()
-
-
-def stay(replicas, cap, operands):
-    scalars, arrays = operands[:1], operands[1:]
-    own, inner_weight, group_weight, delta_weight = arrays[0], arrays[2], arrays[4], arrays[6]
-    inner, scan = arrays[-4], arrays[-1]
+    save_plan.wait()
+
+
+def stay(replicas, cap, scalars, arrays, near, earlier):
+    receive, own, group_weight, delta_weight = arrays[0], arrays[1], arrays[4], arrays[5]
+    inner, scan = arrays[-3], arrays[-1]
     taps, slots, _ = inner.shape
     rows = own.shape[0]
     steps = rows // slots
@@ -448,34 +409,39 @@
     blocks = len(sources_of(replicas))
     moved_rows = blocks * ROWS
     width, features = group_weight.shape
-    full = jax.ShapeDtypeStruct((rows, LANES), F32)
-    moved = jax.ShapeDtypeStruct((steps * moved_rows, LANES), F32)
+    full = pltpu.VMEM((rows, LANES), F32)
+    moved = pltpu.VMEM((steps * moved_rows, LANES), F32)
+    plan_shape = (1, round_up(moving + blocks * cap + 1, LANES))
 
     def like(value):
         return pltpu.VMEM(value.shape, value.dtype)
 
+    far = [in_hbm(value) for value in arrays]
     return pl.pallas_call(
         functools.partial(stay_kernel, replicas, cap),
         out_shape=[
-            jax.ShapeDtypeStruct((1, round_up(moving + blocks * cap + 1, LANES)), jnp.int32),
+            pltpu.VMEM(plan_shape, jnp.int32),
             full,
-            jax.ShapeDtypeStruct((round_up(taps + 3, ROWS), LANES), F32),
+            pltpu.VMEM((round_up(taps + 3, ROWS), LANES), F32),
             full,
             full,
         ]
         + [moved] * 5
         + [jax.ShapeDtypeStruct(scan.shape, BF16)],
-        in_specs=[HBM] * len(operands),
-        out_specs=[SMEM] + [VMEM] * 9 + [HBM],
-        scratch_shapes=[pltpu.SMEM(value.shape, value.dtype) for value in scalars]
-        + [
-            like(own),
+        in_specs=[SMEM] * len(scalars)
+        + [HBM] * len(far)
+        + [VMEM] * len(near)
+        + [HBM] * len(earlier),
+        out_specs=[VMEM] * 10 + [HBM],
+        scratch_shapes=[
+            pltpu.SMEM(plan_shape, jnp.int32),
+            pltpu.SMEM(receive.shape, jnp.int32),
             like(own),
             pltpu.VMEM((features, 2 * LANES), BF16),
             pltpu.VMEM((2 * width + 2 * ROWS, features), BF16),
             like(delta_weight),
         ]
-        + [like(value) for value in arrays[7:]]
+        + [like(value) for value in arrays[6:]]
         + [pltpu.SMEM((replicas * cap + 1,), jnp.int32)]
         + [pltpu.VMEM((rows, LANES), F32)] * 7
         + [
@@ -489,7 +455,7 @@
             flops=300_000_000, bytes_accessed=6_000_000, transcendentals=100_000
         ),
         name="advance_staying",
-    )(*operands)
+    )(*scalars, *far, *near, *earlier)
 
 
 def arrive_kernel(
@@ -721,9 +687,7 @@
 
     group_weight = group_weight.T
     inner_offset = inner_offset[None]
-    numbers = jnp.concatenate([decay_log, delta_bias, skip_gain, live_count.astype(F32)])
-    numbers = jnp.broadcast_to(numbers[:, None], (numbers.shape[0], group_taps.shape[1]))
-    small = jnp.concatenate([group_taps, group_offset[None], numbers], axis=0)
+    small = jnp.concatenate([group_taps, group_offset[None]], axis=0)
     group_other = swap_heads(group)
     swapped = [swap_heads(value) for value in (own, group_weight, small)]
     blocks = pack(replicas, cap, send_list, scan, inner, group, group_other, swapped)
@@ -731,24 +695,22 @@
     plan, gated, group_weights, inner_raw, both, *moved, scan_next = stay(
         replicas,
         cap,
+        (decay_log, delta_bias, skip_gain, live_count),
         (
             receive_list,
             own,
-            swapped[0],
             inner_weight,
             gate_weight,
             group_weight,
-            swapped[1],
             delta_weight.T,
             inner_taps,
             inner_offset,
-            small,
-            swapped[2],
             inner,
             group,
-            group_other,
             scan,
         ),
+        (swapped[0], swapped[1], small, swapped[2], group_other),
+        arrived[:EARLIER] if rounds_of(replicas) else [],
     )
     gated, inner_next, group_next, scan_next = arrive(
         replicas,

time: 47.8 us -> 36.7 us (0.77)
  the two profiles are of different devices: /device:TPU:0 before, /device:TPU:17 now
where the time goes in v2:
time: 36.7 us; the launch traced here: 36.4 us
  starting transfers between devices  12.8 us (35%)
  Pallas kernels  11 us (30%)
  waiting for transfers between devices  8.42 us (23%)
  between operations  3.3 us (9%)
  local copies, waits for them, and re-layouts  0.91 us (2%)
    ppermute x7, starting transfers between devices, exchange(): lax.ppermute(block, 'dp', [(source, source ^ mask) for source in range(re...  11.1 us
    ppermute x7, waiting for transfers between devices, exchange(): lax.ppermute(block, 'dp', [(source, source ^ mask) for source in range(re...  7.12 us
    pallas_call x1, Pallas kernels, stay(): pl.pallas_call(functools.partial(stay_kernel, replicas, cap), out_shape=[...  5.47 us
    pallas_call x1, Pallas kernels, arrive(): pl.pallas_call(functools.partial(arrive_kernel, replicas, cap), out_shape...  3.26 us
    pallas_call x1, Pallas kernels, pack(): pl.pallas_call(functools.partial(pack_kernel, replicas, cap), out_shape=[...  2.27 us
    ppermute x4, starting transfers between devices, swap_heads(): return lax.ppermute(value, 'head', [(0, 1), (1, 0)])  1.67 us
    ppermute x4, waiting for transfers between devices, swap_heads(): return lax.ppermute(value, 'head', [(0, 1), (1, 0)])  1.3 us
    unnamed x12, local copies, waits for them, and re-layouts  0.91 us
  transfers between devices with their start and end apart: 11, of which 5 were waited for; matrix products, arithmetic and copies ran while one was open for 0% of the time, Pallas kernels for 15%

profile of v2, /device:TPU:17, one launch (start us, length us, event | category | flops | bytes accessed | tf_op | source)
XLA Modules:
  0.0 36.4 jit_solution(240016177742868362)
XLA Ops:
  0.6 0.7 %collective-permute-start.1 = (bf16[64,4096]{1,0:T(8,128)(2,1)}, bf16[64,4096]{1,0:T(8,128)(2,1)S(1)}, u32[]{:S(2)}, u32[]{:S(2)}) collective-permute-start(bf16[64,4096]{1,0:T(8,128)(2,1)} %bitcast.23), channel_id=1, source_target_pairs={{0,1},{1,0},{2,3},{3,2},{4,5},{5,4},{6,7},{7,6},{8,9},{9,8},{10,11... | collective-permute-start | bytes 1572872 | tf_op jit(solution)/shard_map/ppermute | solution.py:647
  1.4 0.0 copy-start.4
  1.4 0.1 collective-permute-start
  1.5 0.0 copy-start.5
  1.5 0.4 %collective-permute-start.3 = (bf16[3,56,64]{2,1,0:T(8,128)(2,1)}, bf16[3,56,64]{2,1,0:T(8,128)(2,1)S(1)}, u32[]{:S(2)}, u32[]{:S(2)}) collective-permute-start(bf16[3,56,64]{2,1,0:T(8,128)(2,1)} %bitcast.14), channel_id=1, source_target_pairs={{0,1},{1,0},{2,3},{3,2},{4,5},{5,4},{6,7},{7,6},{8,9},{9,8},{10,11... | collective-permute-start | bytes 64520 | tf_op jit(solution)/shard_map/ppermute | solution.py:647
  1.9 0.2 copy-done.4
  2.1 0.1 copy-done.5
  2.1 0.4 %collective-permute-start.2 = (f32[5,64]{1,0:T(8,128)S(1)}, f32[5,64]{1,0:T(8,128)S(1)}, u32[]{:S(2)}, u32[]{:S(2)}) collective-permute-start(f32[5,64]{1,0:T(8,128)S(1)} %pad_maximum_fusion.small), channel_id=1, source_target_pairs={{0,1},{1,0},{2,3},{3,2},{4,5},{5,4},{6,7},{7,6},{8,9},{9,8},{10,11... | collective-permute-start | bytes 3848 | tf_op jit(solution)/shard_map/ppermute | solution.py:647
  2.5 1.0 %collective-permute-done.2.refs_2_.small_other = f32[5,64]{1,0:T(8,128)S(1)} collective-permute-done((f32[5,64]{1,0:T(8,128)S(1)}, f32[5,64]{1,0:T(8,128)S(1)}, u32[]{:S(2)}, u32[]{:S(2)}) %collective-permute-start.2) | collective-permute-done | bytes 1312 | tf_op jit(solution)/shard_map/ppermute | solution.py:647
  3.6 0.3 collective-permute-done.3.group_other
  3.8 0.0 collective-permute-done.refs_0_.other
  3.8 0.0 collective-permute-done.1.refs_1_.group_weight_other
  3.8 2.3 %pack_leaving.1 = (bf16[1,496,128]{2,1,0:T(8,128)(2,1)S(1)}, bf16[1,496,128]{2,1,0:T(8,128)(2,1)S(1)}, bf16[1,496,128]{2,1,0:T(8,128)(2,1)S(1)}, bf16[1,496,128]...) custom-call(bf16[56,64,128]{2,1,0:T(8,128)(2,1)} %bitcast.20, ...), custom_call_target="tpu_custom_call" | custom-call | bytes 2000000 | tf_op jit(solution)/shard_map/pack_leaving/pallas_call | solution.py:128
  6.1 0.1 collective-permute-start.4
  6.2 1.3 %collective-permute-start.5 = (bf16[1,496,128]{2,1,0:T(8,128)(2,1)S(1)}, bf16[1,496,128]{2,1,0:T(8,128)(2,1)S(1)}, u32[]{:S(2)}, u32[]{:S(2)}) collective-permute-start(bf16[1,496,128]{2,1,0:T(8,128)(2,1)S(1)} %get-tuple-element.27), channel_id=1, source_target_pairs={{0,2},{2,0},{4,6},{6,4},{8,10},{10,8},{12,14},{14,12},{1,3},{3,1},... | collective-permute-start | bytes 380936 | tf_op jit(solution)/shard_map/ppermute | solution.py:655
  7.5 1.3 %collective-permute-start.6 = (bf16[1,496,128]{2,1,0:T(8,128)(2,1)S(1)}, bf16[1,496,128]{2,1,0:T(8,128)(2,1)S(1)}, u32[]{:S(2)}, u32[]{:S(2)}) collective-permute-start(bf16[1,496,128]{2,1,0:T(8,128)(2,1)S(1)} %get-tuple-element.28), channel_id=1, source_target_pairs={{0,4},{2,6},{4,0},{6,2},{8,12},{10,14},{12,8},{14,10},{1,5},{3,7},... | collective-permute-start | bytes 380936 | tf_op jit(solution)/shard_map/ppermute | solution.py:655
  8.8 2.3 %collective-permute-start.7 = (bf16[1,496,128]{2,1,0:T(8,128)(2,1)S(1)}, bf16[1,496,128]{2,1,0:T(8,128)(2,1)S(1)}, u32[]{:S(2)}, u32[]{:S(2)}) collective-permute-start(bf16[1,496,128]{2,1,0:T(8,128)(2,1)S(1)} %get-tuple-element.40), channel_id=1, source_target_pairs={{0,10},{2,8},{4,14},{6,12},{8,2},{10,0},{12,6},{14,4},{1,11},{3,9}... | collective-permute-start | bytes 380936 | tf_op jit(solution)/shard_map/ppermute | solution.py:655
  11.0 0.0 collective-permute-start.8
  11.0 0.7 %collective-permute-done.4.refs_0_ = bf16[1,496,128]{2,1,0:T(8,128)(2,1)S(1)} collective-permute-done((bf16[1,496,128]{2,1,0:T(8,128)(2,1)S(1)}, bf16[1,496,128]{2,1,0:T(8,128)(2,1)S(1)}, u32[]{:S(2)}, u32[]{:S(2)}) %collective-permute-start.4) | collective-permute-done | bytes 127008 | tf_op jit(solution)/shard_map/ppermute | solution.py:655
  11.8 3.8 %collective-permute-start.9 = (bf16[1,496,128]{2,1,0:T(8,128)(2,1)S(1)}, bf16[1,496,128]{2,1,0:T(8,128)(2,1)S(1)}, u32[]{:S(2)}, u32[]{:S(2)}) collective-permute-start(bf16[1,496,128]{2,1,0:T(8,128)(2,1)S(1)} %get-tuple-element.42), channel_id=1, source_target_pairs={{0,14},{2,12},{4,10},{6,8},{8,6},{10,4},{12,2},{14,0},{1,15},{3,13... | collective-permute-start | bytes 380936 | tf_op jit(solution)/shard_map/ppermute | solution.py:655
  15.5 0.0 collective-permute-done.5.refs_1_
  15.5 2.4 %collective-permute-start.10 = (bf16[1,496,128]{2,1,0:T(8,128)(2,1)S(1)}, bf16[1,496,128]{2,1,0:T(8,128)(2,1)S(1)}, u32[]{:S(2)}, u32[]{:S(2)}) collective-permute-start(bf16[1,496,128]{2,1,0:T(8,128)(2,1)S(1)} %get-tuple-element.43), channel_id=1, source_target_pairs={{0,6},{2,4},{4,2},{6,0},{8,14},{10,12},{12,10},{14,8},{1,7},{3,5},... | collective-permute-start | bytes 380936 | tf_op jit(solution)/shard_map/ppermute | solution.py:655
  20.6 0.0 collective-permute-done.6.refs_2_
  20.6 0.0 copy-start
  20.6 0.0 copy-start.1
  20.6 5.5 %advance_staying.1 = (s32[1,128]{1,0:T(1,128)S(1)}, f32[112,128]{1,0:T(8,128)S(1)}, f32[8,128]{1,0:T(8,128)S(1)}, f32[112,128]{1,0:T(8,128)S(1)}, f32[112,128]{1...) custom-call(f32[1]{0:T(128)S(6)} %copy.24.decay_log, ...), custom_call_target="tpu_custom_call" | custom-call | flops 300000000 | bytes 6000000 | tf_op jit(solution)/shard_map/advance_staying/pallas_call | solution.py:420
  26.1 0.0 collective-permute-done.7.refs_3_
  26.1 2.7 %collective-permute-done.8.refs_4_ = bf16[1,496,128]{2,1,0:T(8,128)(2,1)S(1)} collective-permute-done((bf16[1,496,128]{2,1,0:T(8,128)(2,1)S(1)}, bf16[1,496,128]{2,1,0:T(8,128)(2,1)S(1)}, u32[]{:S(2)}, u32[]{:S(2)}) %collective-permute-start.8) | collective-permute-done | bytes 127008 | tf_op jit(solution)/shard_map/ppermute | solution.py:655
  28.8 3.6 %collective-permute-done.9.refs_5_ = bf16[1,496,128]{2,1,0:T(8,128)(2,1)S(1)} collective-permute-done((bf16[1,496,128]{2,1,0:T(8,128)(2,1)S(1)}, bf16[1,496,128]{2,1,0:T(8,128)(2,1)S(1)}, u32[]{:S(2)}, u32[]{:S(2)}) %collective-permute-start.9) | collective-permute-done | bytes 127008 | tf_op jit(solution)/shard_map/ppermute | solution.py:655
  32.5 0.0 collective-permute-done.10.refs_6_
  32.5 0.0 copy-start.2
  32.5 0.0 copy-start.3
  32.5 0.0 copy-done
  32.5 0.0 copy-done.1
  32.5 0.7 %copy-done.2 = f32[4,128]{1,0:T(4,128)S(1)} copy-done((f32[4,128]{1,0:T(4,128)S(1)}, f32[4,128]{1,0:T(4,128)}, u32[]{:S(2)}) %copy-start.2) | copy-done | bytes 2072
  33.1 0.0 copy-done.3
  33.1 3.3 %advance_arrived.1 = (bf16[2,56,128]{2,1,0:T(8,128)(2,1)}, bf16[3,56,128]{2,1,0:T(8,128)(2,1)}, bf16[3,56,64]{2,1,0:T(8,128)(2,1)}, bf16[56,64,128]{2,1,0:T(8,128)(2,1)}) custom-call(s32[1,128]{1,0:T(1,128)S(1)} %get-tuple-element.29.plan_hbm, f32[112,128]{1,0:T(8,128)S(1)} %get-tuple-element.30.gated_in, ...), custom_call_target="tpu_custom_call", output_to_operand_aliasing={{3}: (14, {})} | custom-call | flops 10000000 | bytes 2000000 | tf_op jit(solution)/shard_map/advance_arrived/pallas_call | solution.py:613
  (1 shorter events, 0.0 us)
Async XLA Ops:
  0.6 3.2 %collective-permute-start.1 = (bf16[64,4096]{1,0:T(8,128)(2,1)}, bf16[64,4096]{1,0:T(8,128)(2,1)S(1)}, u32[]{:S(2)}, u32[]{:S(2)}) collective-permute-start(bf16[64,4096]{1,0:T(8,128)(2,1)} %bitcast.23), channel_id=1, source_target_pairs={{0,1},{1,0},{2,3},{3,2},{4,5},{5,4},{6,7},{7,6},{8,9},{9,8},{10,11... | collective-permute-start | bytes 1572872 | tf_op jit(solution)/shard_map/ppermute | solution.py:647
  1.4 0.7 %copy-start.4 = (f32[4,64]{1,0:T(4,128)S(1)}, f32[4,64]{1,0:T(4,128)}, u32[]{:S(2)}) copy-start(f32[4,64]{1,0:T(4,128)} %param.25) | copy-start | bytes 3076
  1.4 2.5 %collective-permute-start = (bf16[112,2048]{1,0:T(8,128)(2,1)}, bf16[112,2048]{1,0:T(8,128)(2,1)S(1)}, u32[]{:S(2)}, u32[]{:S(2)}) collective-permute-start(bf16[112,2048]{1,0:T(8,128)(2,1)} %bitcast.25), channel_id=1, source_target_pairs={{0,1},{1,0},{2,3},{3,2},{4,5},{5,4},{6,7},{7,6},{8,9},{9,8},{10,11... | collective-permute-start | bytes 1376264 | tf_op jit(solution)/shard_map/ppermute | solution.py:647
  1.5 0.7 %copy-start.5 = (f32[64]{0:T(128)S(1)}, f32[64]{0:T(128)}, u32[]{:S(2)}) copy-start(f32[64]{0:T(128)} %param.26) | copy-start | bytes 772
  1.5 2.4 %collective-permute-start.3 = (bf16[3,56,64]{2,1,0:T(8,128)(2,1)}, bf16[3,56,64]{2,1,0:T(8,128)(2,1)S(1)}, u32[]{:S(2)}, u32[]{:S(2)}) collective-permute-start(bf16[3,56,64]{2,1,0:T(8,128)(2,1)} %bitcast.14), channel_id=1, source_target_pairs={{0,1},{1,0},{2,3},{3,2},{4,5},{5,4},{6,7},{7,6},{8,9},{9,8},{10,11... | collective-permute-start | bytes 64520 | tf_op jit(solution)/shard_map/ppermute | solution.py:647
  2.1 1.4 %collective-permute-start.2 = (f32[5,64]{1,0:T(8,128)S(1)}, f32[5,64]{1,0:T(8,128)S(1)}, u32[]{:S(2)}, u32[]{:S(2)}) collective-permute-start(f32[5,64]{1,0:T(8,128)S(1)} %pad_maximum_fusion.small), channel_id=1, source_target_pairs={{0,1},{1,0},{2,3},{3,2},{4,5},{5,4},{6,7},{7,6},{8,9},{9,8},{10,11... | collective-permute-start | bytes 3848 | tf_op jit(solution)/shard_map/ppermute | solution.py:647
  6.1 5.6 %collective-permute-start.4 = (bf16[1,496,128]{2,1,0:T(8,128)(2,1)S(1)}, bf16[1,496,128]{2,1,0:T(8,128)(2,1)S(1)}, u32[]{:S(2)}, u32[]{:S(2)}) collective-permute-start(bf16[1,496,128]{2,1,0:T(8,128)(2,1)S(1)} %get-tuple-element.26), channel_id=1, source_target_pairs={{0,8},{2,10},{4,12},{6,14},{8,0},{10,2},{12,4},{14,6},{1,9},{3,11}... | collective-permute-start | bytes 380936 | tf_op jit(solution)/shard_map/ppermute | solution.py:655
  6.2 9.3 %collective-permute-start.5 = (bf16[1,496,128]{2,1,0:T(8,128)(2,1)S(1)}, bf16[1,496,128]{2,1,0:T(8,128)(2,1)S(1)}, u32[]{:S(2)}, u32[]{:S(2)}) collective-permute-start(bf16[1,496,128]{2,1,0:T(8,128)(2,1)S(1)} %get-tuple-element.27), channel_id=1, source_target_pairs={{0,2},{2,0},{4,6},{6,4},{8,10},{10,8},{12,14},{14,12},{1,3},{3,1},... | collective-permute-start | bytes 380936 | tf_op jit(solution)/shard_map/ppermute | solution.py:655
  7.5 13.1 %collective-permute-start.6 = (bf16[1,496,128]{2,1,0:T(8,128)(2,1)S(1)}, bf16[1,496,128]{2,1,0:T(8,128)(2,1)S(1)}, u32[]{:S(2)}, u32[]{:S(2)}) collective-permute-start(bf16[1,496,128]{2,1,0:T(8,128)(2,1)S(1)} %get-tuple-element.28), channel_id=1, source_target_pairs={{0,4},{2,6},{4,0},{6,2},{8,12},{10,14},{12,8},{14,10},{1,5},{3,7},... | collective-permute-start | bytes 380936 | tf_op jit(solution)/shard_map/ppermute | solution.py:655
  8.8 17.3 %collective-permute-start.7 = (bf16[1,496,128]{2,1,0:T(8,128)(2,1)S(1)}, bf16[1,496,128]{2,1,0:T(8,128)(2,1)S(1)}, u32[]{:S(2)}, u32[]{:S(2)}) collective-permute-start(bf16[1,496,128]{2,1,0:T(8,128)(2,1)S(1)} %get-tuple-element.40), channel_id=1, source_target_pairs={{0,10},{2,8},{4,14},{6,12},{8,2},{10,0},{12,6},{14,4},{1,11},{3,9}... | collective-permute-start | bytes 380936 | tf_op jit(solution)/shard_map/ppermute | solution.py:655
  11.0 17.8 %collective-permute-start.8 = (bf16[1,496,128]{2,1,0:T(8,128)(2,1)S(1)}, bf16[1,496,128]{2,1,0:T(8,128)(2,1)S(1)}, u32[]{:S(2)}, u32[]{:S(2)}) collective-permute-start(bf16[1,496,128]{2,1,0:T(8,128)(2,1)S(1)} %get-tuple-element.41), channel_id=1, source_target_pairs={{0,12},{2,14},{4,8},{6,10},{8,4},{10,6},{12,0},{14,2},{1,13},{3,15... | collective-permute-start | bytes 380936 | tf_op jit(solution)/shard_map/ppermute | solution.py:655
  11.8 20.7 %collective-permute-start.9 = (bf16[1,496,128]{2,1,0:T(8,128)(2,1)S(1)}, bf16[1,496,128]{2,1,0:T(8,128)(2,1)S(1)}, u32[]{:S(2)}, u32[]{:S(2)}) collective-permute-start(bf16[1,496,128]{2,1,0:T(8,128)(2,1)S(1)} %get-tuple-element.42), channel_id=1, source_target_pairs={{0,14},{2,12},{4,10},{6,8},{8,6},{10,4},{12,2},{14,0},{1,15},{3,13... | collective-permute-start | bytes 380936 | tf_op jit(solution)/shard_map/ppermute | solution.py:655
  15.5 16.9 %collective-permute-start.10 = (bf16[1,496,128]{2,1,0:T(8,128)(2,1)S(1)}, bf16[1,496,128]{2,1,0:T(8,128)(2,1)S(1)}, u32[]{:S(2)}, u32[]{:S(2)}) collective-permute-start(bf16[1,496,128]{2,1,0:T(8,128)(2,1)S(1)} %get-tuple-element.43), channel_id=1, source_target_pairs={{0,6},{2,4},{4,2},{6,0},{8,14},{10,12},{12,10},{14,8},{1,7},{3,5},... | collective-permute-start | bytes 380936 | tf_op jit(solution)/shard_map/ppermute | solution.py:655
  20.6 11.9 %copy-start = (bf16[56,3,128]{2,0,1:T(8,128)(2,1)S(1)}, bf16[56,3,128]{2,0,1:T(8,128)(2,1)}, u32[]{:S(2)}) copy-start(bf16[56,3,128]{2,0,1:T(8,128)(2,1)} %param.30) | copy-start | bytes 129028
  20.6 11.9 %copy-start.1 = (bf16[56,3,64]{2,0,1:T(8,128)(2,1)S(1)}, bf16[56,3,64]{2,0,1:T(8,128)(2,1)}, u32[]{:S(2)}) copy-start(bf16[56,3,64]{2,0,1:T(8,128)(2,1)} %param.31) | copy-start | bytes 64516
  32.5 0.7 %copy-start.2 = (f32[4,128]{1,0:T(4,128)S(1)}, f32[4,128]{1,0:T(4,128)}, u32[]{:S(2)}) copy-start(f32[4,128]{1,0:T(4,128)} %inner_taps.1) | copy-start | bytes 6148
  32.5 0.7 %copy-start.3 = (f32[128]{0:T(128)S(1)}, f32[128]{0:T(128)}, u32[]{:S(2)}) copy-start(f32[128]{0:T(128)} %param.24) | copy-start | bytes 1540

commit v3 on v2

--- a/solution.py
+++ b/solution.py
@@ -14,6 +14,7 @@
 LARGE_LIMIT = 48 * 1024 * 1024
 MAX_ROUNDS = 16
 EARLIER = 3
+LAST = 2
 LANES = 128
 ROWS = 8
 MAX_SETS = 64
@@ -25,6 +26,10 @@
 
 def in_hbm(value):
     return pltpu.with_memory_space_constraint(value, pltpu.HBM)
+
+
+def in_vmem(value):
+    return pltpu.with_memory_space_constraint(value, pltpu.VMEM)
 
 
 def round_up(value, step):
@@ -44,7 +49,7 @@
         return []
     light = list(range(1, replicas // 2))
     heavy = list(range(replicas // 2, replicas))
-    return heavy[:1] + light[:2] + heavy[1:] + light[2:]
+    return heavy[:1] + light[:2] + heavy[1:2] + light[2:] + heavy[2:]
 
 
 def partner(replicas, mask):
@@ -58,26 +63,27 @@
     )
 
 
-def pack_kernel(replicas, cap, scan, send, inner, group, group_other, *refs):
+def destinations(replicas, outs):
     rounds = rounds_of(replicas)
-    count = max(1, len(rounds))
-    outs = refs[-8 - count : -8]
-    indices, inner_in, group_in, table, picked, load_sem, list_sem, sem = refs[-8:]
+    if rounds:
+        return [(ref.at[0], partner(replicas, mask)) for ref, mask in zip(outs, rounds)]
+    return [(outs[0].at[target], target) for target in range(replicas)]
+
+
+def states_kernel(replicas, cap, scan, send, inner, group, *refs):
+    outs, (picked, group_out, indices_out) = refs[:-11], refs[-11:-8]
+    indices, inner_in, table, load_sem, group_sem, list_sem, save_sem, sem = refs[-8:]
     load_list = pltpu.make_async_copy(send, indices, list_sem)
     load_list.start()
-    loads = [
-        pltpu.make_async_copy(source, target, load_sem.at[place])
-        for place, (source, target) in enumerate([(inner, inner_in), (group, group_in)])
-    ]
-    for load in loads:
-        load.start()
+    load = pltpu.make_async_copy(inner, inner_in, load_sem)
+    load.start()
+    load_group = pltpu.make_async_copy(group, group_out, group_sem)
+    load_group.start()
     state_rows = scan.shape[1]
-    if rounds:
-        blocks = [(ref.at[0], partner(replicas, mask)) for ref, mask in zip(outs, rounds)]
-    else:
-        blocks = [(outs[0].at[target], target) for target in range(replicas)]
+    blocks = destinations(replicas, outs)
     load_list.wait()
-
+    save = pltpu.make_async_copy(indices, indices_out, save_sem)
+    save.start()
     plan = []
     for block, (ref, target) in enumerate(blocks):
         for c in range(cap):
@@ -97,24 +103,46 @@
                 )
 
     each(lambda copy: copy.start())
-    for load in loads:
-        load.wait()
+    load.wait()
     taps = inner_in.shape[0]
     for tap in range(taps):
         table[:, tap * LANES : (tap + 1) * LANES] = inner_in[tap].astype(F32)
-        table[:, (taps + tap) * LANES : (taps + tap + 1) * LANES] = both_halves(
-            group_in[tap].astype(F32), group_other[tap].astype(F32)
-        )
     picked[...] = jnp.zeros_like(picked)
     for block, _, c, index in plan:
         row = table[pl.ds(jnp.maximum(index, 0), 1), :]
-        for kind in range(2 * taps):
-            picked[block, kind * ROWS + c : kind * ROWS + c + 1, :] = row[
-                :, kind * LANES : (kind + 1) * LANES
+        for tap in range(taps):
+            picked[block, tap * ROWS + c : tap * ROWS + c + 1, :] = row[
+                :, tap * LANES : (tap + 1) * LANES
             ]
-    for block, (ref, _) in enumerate(blocks):
-        ref[cap * state_rows :, :] = picked[block].astype(BF16)
+    load_group.wait()
+    save.wait()
     each(lambda copy: copy.wait())
+
+
+def windows_kernel(replicas, cap, state_rows, indices_in, group, group_other, picked_in, *refs):
+    count = max(1, len(rounds_of(replicas)))
+    outs = refs[-4 - count : -4]
+    indices, table, picked, sem = refs[-4:]
+    load = pltpu.make_async_copy(indices_in, indices, sem)
+    load.start()
+    taps = group.shape[0]
+    for tap in range(taps):
+        table[:, tap * LANES : (tap + 1) * LANES] = both_halves(
+            group[tap].astype(F32), group_other[tap].astype(F32)
+        )
+    picked[...] = jnp.zeros_like(picked)
+    load.wait()
+    for block, (ref, target) in enumerate(destinations(replicas, outs)):
+        for c in range(cap):
+            index = jnp.maximum(indices[0, target * cap + c], 0)
+            row = table[pl.ds(index, 1), :]
+            for tap in range(taps):
+                picked[block, tap * ROWS + c : tap * ROWS + c + 1, :] = row[
+                    :, tap * LANES : (tap + 1) * LANES
+                ]
+        ref[cap * state_rows :, :] = jnp.concatenate(
+            [picked_in[block], picked[block]], axis=0
+        ).astype(BF16)
 
 
 def pack(replicas, cap, send_list, scan, inner, group, group_other, swapped):
@@ -122,28 +150,52 @@
     count = max(1, len(rounds))
     per_block = 1 if rounds else replicas
     taps, slots, _ = inner.shape
-    window_rows = 2 * taps * ROWS
-    rows = cap * scan.shape[1] + window_rows
+    rows = cap * scan.shape[1] + 2 * taps * ROWS
     blocks = count * per_block
+    shapes = [pltpu.VMEM((per_block, rows, LANES), BF16)] * count
+    half = (blocks, taps * ROWS, LANES)
+    limit = SMALL_LIMIT if rounds else MEDIUM_LIMIT
+    *states, picked, group_near, indices = pl.pallas_call(
+        functools.partial(states_kernel, replicas, cap),
+        out_shape=shapes
+        + [
+            pltpu.VMEM(half, F32),
+            pltpu.VMEM(group.shape, BF16),
+            pltpu.VMEM(send_list.shape, jnp.int32),
+        ],
+        in_specs=[HBM] * 4,
+        out_specs=[VMEM] * (count + 3),
+        scratch_shapes=[
+            pltpu.SMEM(send_list.shape, jnp.int32),
+            pltpu.VMEM(inner.shape, BF16),
+            pltpu.VMEM((slots, taps * LANES), F32),
+            pltpu.SemaphoreType.DMA,
+            pltpu.SemaphoreType.DMA,
+            pltpu.SemaphoreType.DMA,
+            pltpu.SemaphoreType.DMA,
+            pltpu.SemaphoreType.DMA((blocks * cap,)),
+        ],
+        compiler_params=pltpu.CompilerParams(vmem_limit_bytes=limit),
+        cost_estimate=pl.CostEstimate(flops=0, bytes_accessed=2_000_000, transcendentals=0),
+        name="pack_states",
+    )(in_hbm(scan), in_hbm(send_list), in_hbm(inner), in_hbm(group))
+    near = [in_vmem(value) for value in states]
     return pl.pallas_call(
-        functools.partial(pack_kernel, replicas, cap),
-        out_shape=[pltpu.VMEM((per_block, rows, LANES), BF16)] * count,
-        in_specs=[HBM] * 4 + [VMEM] + [HBM] * len(swapped),
+        functools.partial(windows_kernel, replicas, cap, scan.shape[1]),
+        out_shape=shapes,
+        in_specs=[VMEM] * (4 + count) + [HBM] * len(swapped),
         out_specs=[VMEM] * count,
         scratch_shapes=[
             pltpu.SMEM(send_list.shape, jnp.int32),
-            pltpu.VMEM(inner.shape, BF16),
-            pltpu.VMEM(group.shape, BF16),
-            pltpu.VMEM((slots, 2 * taps * LANES), F32),
-            pltpu.VMEM((blocks, window_rows, LANES), F32),
-            pltpu.SemaphoreType.DMA((2,)),
+            pltpu.VMEM((slots, taps * LANES), F32),
+            pltpu.VMEM(half, F32),
             pltpu.SemaphoreType.DMA,
-            pltpu.SemaphoreType.DMA((blocks * cap,)),
         ],
-        compiler_params=pltpu.CompilerParams(vmem_limit_bytes=SMALL_LIMIT),
-        cost_estimate=pl.CostEstimate(flops=0, bytes_accessed=2_000_000, transcendentals=0),
-        name="pack_leaving",
-    )(in_hbm(scan), in_hbm(send_list), in_hbm(inner), in_hbm(group), group_other, *swapped)
+        input_output_aliases={4 + place: place for place in range(count)},
+        compiler_params=pltpu.CompilerParams(vmem_limit_bytes=limit),
+        cost_estimate=pl.CostEstimate(flops=0, bytes_accessed=500_000, transcendentals=0),
+        name="pack_windows",
+    )(indices, group_near, group_other, picked, *near, *swapped)
 
 
 def sources_of(replicas):
@@ -187,13 +239,13 @@
     return [scratch[first : first + LANES].T for first in range(0, scratch.shape[0], LANES)]
 
 
-def advance_slot(state, rows, driven, decay, sums, maps, lanes):
+def advance_slot(state, rows, driven, decays, sums, maps, lanes):
     hidden = state.astype(F32)
     width = state.shape[0]
-    for row, lane in zip(rows, lanes):
+    for row, decay, lane in zip(rows, decays, lanes):
         piece = maps[lane // LANES]
         column = piece[:, lane % LANES : lane % LANES + 1]
-        hidden = decay[row, :] * hidden + driven[row, :] * column[:width]
+        hidden = decay * hidden + driven[row, :] * column[:width]
         sums[row, :] = jnp.sum(hidden * column[width:], axis=0, keepdims=True)
         result = hidden.astype(BF16)
         hidden = result.astype(F32)
@@ -228,9 +280,10 @@
     (
         plan_out,
         gated,
-        group_weights,
-        inner_raw,
-        both,
+        weights,
+        base,
+        inner_part,
+        group_part,
         inner_moved,
         group_moved,
         gate_moved,
@@ -249,6 +302,8 @@
         group,
         scan,
         inverse,
+        inner_raw,
+        both,
         gate,
         delta,
         decay,
@@ -260,7 +315,7 @@
         done,
         sem,
         load_sem,
-    ) = refs[-34:]
+    ) = refs[-37:]
     taps, slots, _ = inner.shape
     rows, half = own.shape
     steps = rows // slots
@@ -320,8 +375,11 @@
     delta[...] = rate
     decay[...] = jnp.exp(-rate * jnp.exp(jnp.full((1, LANES), decay_log[0], F32)))
     count = taps + 2
-    group_weights[:count, :] = both_halves(small[...], small_other[...])
-    group_weights[count : count + 1, :] = jnp.full((1, LANES), skip_gain[0], F32)
+    weights[:count, :] = both_halves(small[...], small_other[...])
+    weights[count : count + 1, :] = jnp.full((1, LANES), skip_gain[0], F32)
+    later = round_up(count + 1, ROWS)
+    weights[later : later + taps + 1, :] = inner_taps[...]
+    weights[later + taps + 1 : later + taps + 2, :] = inner_offset[...]
     plan[0, plan.shape[1] - 1] = live[0]
     save_plan = pltpu.make_async_copy(plan, plan_out, load_sem.at[0])
     save_plan.start()
@@ -338,8 +396,8 @@
     group_conv = convolve(
         [both_halves(group[tap].astype(F32), group_other[tap].astype(F32)) for tap in range(taps)],
         parts(both),
-        group_weights[: taps + 1, :],
-        group_weights[taps + 1 : taps + 2, :],
+        weights[: taps + 1, :],
+        weights[taps + 1 : taps + 2, :],
     )
     for step in range(steps):
         part = slice(step * slots, (step + 1) * slots)
@@ -363,7 +421,7 @@
             scan[slot],
             [pl.ds(step * slots + slot, 1) for step in range(steps)],
             driven,
-            decay,
+            [decay[pl.ds(step * slots + slot, 1), :] for step in range(steps)],
             sums,
             maps,
             [step * stride + position for step in range(steps)],
@@ -383,6 +441,15 @@
     )
     for _, target in pairs:
         target[...] = jnp.zeros_like(target)
+    living = lax.broadcasted_iota(jnp.int32, (slots, LANES), 0) < live[0]
+    for step in range(steps):
+        part = slice(step * slots, (step + 1) * slots)
+        inner_part[step] = jnp.where(living, inner_raw[part, :], 0.0).astype(BF16)
+        raw = jnp.where(head == 0, both[part, :width], both[part, width:])
+        group_part[step] = jnp.where(living[:, :width], raw, 0.0).astype(BF16)
+    base[:, :LANES] = inner[steps].astype(F32)
+    group_own = group[steps].astype(F32)
+    base[:, LANES:] = jnp.concatenate([group_own, group_own], axis=1)
     for block in range(moved_rows // ROWS):
 
         @pl.when(plan[0, moving + block * cap] >= 0)
@@ -422,9 +489,10 @@
         out_shape=[
             pltpu.VMEM(plan_shape, jnp.int32),
             full,
-            pltpu.VMEM((round_up(taps + 3, ROWS), LANES), F32),
-            full,
-            full,
+            pltpu.VMEM((2 * round_up(taps + 3, ROWS), LANES), F32),
+            pltpu.VMEM((slots, 2 * LANES), F32),
+            pltpu.VMEM((steps, slots, LANES), BF16),
+            pltpu.VMEM((steps, slots, width), BF16),
         ]
         + [moved] * 5
         + [jax.ShapeDtypeStruct(scan.shape, BF16)],
@@ -432,7 +500,7 @@
         + [HBM] * len(far)
         + [VMEM] * len(near)
         + [HBM] * len(earlier),
-        out_specs=[VMEM] * 10 + [HBM],
+        out_specs=[VMEM] * 11 + [HBM],
         scratch_shapes=[
             pltpu.SMEM(plan_shape, jnp.int32),
             pltpu.SMEM(receive.shape, jnp.int32),
@@ -443,7 +511,7 @@
         ]
         + [like(value) for value in arrays[6:]]
         + [pltpu.SMEM((replicas * cap + 1,), jnp.int32)]
-        + [pltpu.VMEM((rows, LANES), F32)] * 7
+        + [pltpu.VMEM((rows, LANES), F32)] * 9
         + [
             pltpu.VMEM((round_up(rows, LANES), LANES), F32),
             pltpu.VMEM((moving,) + scan.shape[1:], BF16),
@@ -461,41 +529,61 @@
 def arrive_kernel(
     replicas,
     cap,
-    plan_hbm,
-    gated_in,
-    group_weights,
+    first,
+    last,
+    plan_near,
+    weights,
     inner_moved,
     group_moved,
     gate_moved,
     delta_moved,
     decay_moved,
-    inner_raw,
-    both,
-    inner_taps,
-    inner_offset,
-    inner,
-    group,
+    gated_in,
+    table_in,
+    inner_part,
+    group_part,
     scan_in,
     *refs,
 ):
     del scan_in
-    arrived = refs[:-16]
-    gated_out, inner_next, group_next, scan_next, plan = refs[-16:-11]
-    (driven, sums, ordered, table, gated, gated_cast, inner_out, group_out) = refs[-11:-3]
-    done, sem, out_sem = refs[-3:]
-    taps, slots, _ = inner.shape
+    if last:
+        arrived = refs[:-15]
+        gated_out, inner_next, group_next, scan_next = refs[-15:-11]
+        gated, table = refs[-11:-9]
+        gated_cast, inner_cast, group_cast = refs[-9:-6]
+    else:
+        arrived = refs[:-9]
+        gated, table, scan_next = refs[-9:-6]
+    plan, driven, sums, ordered, done, sem = refs[-6:]
+    steps, slots, width = group_part.shape
+    taps = steps + 1
     moving = slots // 2
     state_rows = scan_next.shape[1]
-    steps = inner_raw.shape[0] // slots
-    width = group.shape[2]
     head = lax.axis_index("head")
-    load = pltpu.make_async_copy(plan_hbm, plan, out_sem.at[0])
+    load = pltpu.make_async_copy(plan_near, plan, sem.at[0])
     load.start()
     if rounds_of(replicas):
         blocks = [ref.at[0] for ref in arrived]
     else:
         blocks = [arrived[0].at[source] for source in range(replicas)]
+    stored = inner_moved.shape[0] // steps
     moved_rows = len(blocks) * ROWS
+    if last:
+        copies = [
+            pltpu.make_async_copy(source, target, sem.at[1 + place])
+            for place, (source, target) in enumerate(
+                [
+                    (inner_part, inner_next.at[pl.ds(1, steps)]),
+                    (group_part, group_next.at[pl.ds(1, steps)]),
+                ]
+            )
+        ]
+        for copy in copies:
+            copy.start()
+
+    def parts(ref):
+        starts = [step * stored + first * ROWS for step in range(steps)]
+        return [ref[start : start + moved_rows, :] for start in starts]
 
     kinds = [[] for _ in range(2 * taps)]
     for ref in blocks:
@@ -503,49 +591,53 @@
         for kind in range(2 * taps):
             kinds[kind].append(block[kind * ROWS : (kind + 1) * ROWS])
     windows = [jnp.concatenate(kind, axis=0) for kind in kinds]
-
-    def parts(ref):
-        return [ref[step * moved_rows : (step + 1) * moved_rows, :] for step in range(steps)]
-
+    later = round_up(taps + 3, ROWS)
     inner_conv = convolve(
-        windows[:taps], parts(inner_moved), inner_taps[...], inner_offset[...]
+        windows[:taps],
+        parts(inner_moved),
+        weights[later : later + taps + 1, :],
+        weights[later + taps + 1 : later + taps + 2, :],
     )
     group_conv = convolve(
         windows[taps:],
         parts(group_moved),
-        group_weights[: taps + 1, :],
-        group_weights[taps + 1 : taps + 2, :],
+        weights[: taps + 1, :],
+        weights[taps + 1 : taps + 2, :],
     )
     for step, delta in enumerate(parts(delta_moved)):
         driven[step * moved_rows : (step + 1) * moved_rows, :] = delta * inner_conv[step]
     stride = ordered.shape[0] // steps
     maps = transposed(group_conv, ordered, stride)
     sums[...] = jnp.zeros_like(sums)
+    gated[...] = gated_in[...]
+    table[...] = table_in[...]
     load.wait()
     live = plan[0, plan.shape[1] - 1]
 
     def each(act):
         for block in range(len(blocks)):
-
-            @pl.when(plan[0, moving + block * cap] >= 0)
+            entry = moving + (first + block) * cap
+
+            @pl.when(plan[0, entry] >= 0)
             def _():
                 for c in range(cap):
-                    act(block, c, plan[0, moving + block * cap + c])
+                    act(block, c, plan[0, entry + c])
 
     def store(block, c, slot):
         place = block * cap + c
-        return pltpu.make_async_copy(done.at[place], scan_next.at[slot], sem.at[place])
+        return pltpu.make_async_copy(done.at[place], scan_next.at[slot], sem.at[4 + place])
 
     def advance(block, c, slot):
         place = block * ROWS + c
+        rows = [step * moved_rows + place for step in range(steps)]
         result = advance_slot(
             blocks[block][c * state_rows : (c + 1) * state_rows, :],
+            [slice(row, row + 1) for row in rows],
+            driven,
             [
-                slice(step * moved_rows + place, step * moved_rows + place + 1)
-                for step in range(steps)
+                decay_moved[row : row + 1, :]
+                for row in (step * stored + first * ROWS + place for step in range(steps))
             ],
-            driven,
-            decay_moved,
             sums,
             maps,
             [step * stride + place for step in range(steps)],
@@ -554,23 +646,12 @@
         store(block, c, slot).start()
 
     each(advance)
-    living = lax.broadcasted_iota(jnp.int32, (slots, LANES), 0) < live
-    for step in range(steps):
-        part = slice(step * slots, (step + 1) * slots)
-        tap = taps - steps + step
-        inner_out[tap] = jnp.where(living, inner_raw[part, :], 0.0).astype(BF16)
-        raw = jnp.where(head == 0, both[part, :width], both[part, width:])
-        group_out[tap] = jnp.where(living[:, :width], raw, 0.0).astype(BF16)
-    table[:, :LANES] = inner[steps].astype(F32)
-    group_own = group[steps].astype(F32)
-    table[:, LANES:] = jnp.concatenate([group_own, group_own], axis=1)
-    gated[...] = gated_in[...]
-    for step in range(steps):
+    for step, gate in enumerate(parts(gate_moved)):
         part = slice(step * moved_rows, (step + 1) * moved_rows)
-        skipped = inner_conv[step] * group_weights[taps + 2 : taps + 3, :]
-        sums[part, :] = (sums[part, :] + skipped) * gate_moved[part, :]
-    driven[:moved_rows, :] = windows[steps]
-    driven[moved_rows : 2 * moved_rows, :] = windows[taps + steps]
+        skipped = inner_conv[step] * weights[taps + 2 : taps + 3, :]
+        sums[part, :] = (sums[part, :] + skipped) * gate
+    driven[:moved_rows, :] = windows[taps - 1]
+    driven[moved_rows : 2 * moved_rows, :] = windows[2 * taps - 1]
 
     def scatter(block, c, slot):
         place = block * ROWS + c
@@ -583,64 +664,75 @@
         )
 
     each(scatter)
-    for step in range(steps):
-        part = slice(step * slots, (step + 1) * slots)
-        gated_cast[step] = jnp.where(living, gated[part, :], 0.0).astype(BF16)
-    inner_out[0] = jnp.where(living, table[:, :LANES], 0.0).astype(BF16)
-    carried = jnp.where(head == 0, table[:, LANES : LANES + width], table[:, LANES + width :])
-    group_out[0] = jnp.where(living[:, :width], carried, 0.0).astype(BF16)
-    copies = [
-        pltpu.make_async_copy(source, target, out_sem.at[place])
-        for place, (source, target) in enumerate(
-            [(inner_out, inner_next), (gated_cast, gated_out), (group_out, group_next)]
-        )
-    ]
-    for copy in copies:
-        copy.start()
+    if last:
+        living = lax.broadcasted_iota(jnp.int32, (slots, LANES), 0) < live
+        for step in range(steps):
+            part = slice(step * slots, (step + 1) * slots)
+            gated_cast[step] = jnp.where(living, gated[part, :], 0.0).astype(BF16)
+        inner_cast[0] = jnp.where(living, table[:, :LANES], 0.0).astype(BF16)
+        carried = jnp.where(head == 0, table[:, LANES : LANES + width], table[:, LANES + width :])
+        group_cast[0] = jnp.where(living[:, :width], carried, 0.0).astype(BF16)
+        ends = [
+            pltpu.make_async_copy(source, target, semaphore)
+            for source, target, semaphore in (
+                (gated_cast, gated_out, sem.at[0]),
+                (inner_cast, inner_next.at[pl.ds(0, 1)], sem.at[3]),
+                (group_cast, group_next.at[pl.ds(0, 1)], sem.at[sem.shape[0] - 1]),
+            )
+        ]
+        for copy in ends:
+            copy.start()
+        for copy in copies + ends:
+            copy.wait()
     each(lambda block, c, slot: store(block, c, slot).wait())
-    for copy in copies:
-        copy.wait()
-
-
-def arrive(replicas, cap, plan, operands, scan_next, arrived):
-    inner_moved, inner_raw, inner, group = operands[2], operands[7], operands[-2], operands[-1]
-    taps, slots, _ = inner.shape
-    rows = inner_raw.shape[0]
-    steps = rows // slots
-    places = len(sources_of(replicas)) * cap
-    gated = jax.ShapeDtypeStruct((steps, slots, LANES), BF16)
-    limit = SMALL_LIMIT if rounds_of(replicas) else LARGE_LIMIT
+
+
+def arrive(replicas, cap, first, last, operands, scan_next, arrived):
+    inner_moved, gated, table, inner_part, group_part = operands[2], *operands[7:]
+    steps, slots, width = group_part.shape
+    blocks = len(arrived) if rounds_of(replicas) else replicas
+    moved = (steps * blocks * ROWS, LANES)
+    carried = [pltpu.VMEM(value.shape, F32) for value in (gated, table)]
+    scan_shape = jax.ShapeDtypeStruct(scan_next.shape, BF16)
+    if last:
+        outs = [
+            jax.ShapeDtypeStruct((steps, slots, LANES), BF16),
+            jax.ShapeDtypeStruct((steps + 1, slots, LANES), BF16),
+            jax.ShapeDtypeStruct((steps + 1, slots, width), BF16),
+            scan_shape,
+        ]
+        scratch = carried + [
+            pltpu.VMEM((steps, slots, LANES), BF16),
+            pltpu.VMEM((1, slots, LANES), BF16),
+            pltpu.VMEM((1, slots, width), BF16),
+        ]
+        specs = [HBM] * 4
+    else:
+        outs, scratch, specs = carried + [scan_shape], [], [VMEM, VMEM, HBM]
+    plan = operands[0]
     return pl.pallas_call(
-        functools.partial(arrive_kernel, replicas, cap),
-        out_shape=[
-            gated,
-            jax.ShapeDtypeStruct(inner.shape, BF16),
-            jax.ShapeDtypeStruct(group.shape, BF16),
-            jax.ShapeDtypeStruct(scan_next.shape, BF16),
+        functools.partial(arrive_kernel, replicas, cap, first, last),
+        out_shape=outs,
+        in_specs=[VMEM] * len(operands) + [HBM] + [VMEM] * len(arrived),
+        out_specs=specs,
+        scratch_shapes=scratch
+        + [
+            pltpu.SMEM(plan.shape, plan.dtype),
+            pltpu.VMEM(moved, F32),
+            pltpu.VMEM(moved, F32),
+            pltpu.VMEM((round_up(moved[0], LANES), LANES), F32),
+            pltpu.VMEM((blocks * cap,) + scan_next.shape[1:], BF16),
+            pltpu.SemaphoreType.DMA((blocks * cap + 5,)),
         ],
-        in_specs=[HBM] + [VMEM] * len(operands) + [HBM] + [VMEM] * len(arrived),
-        out_specs=[HBM] * 4,
-        scratch_shapes=[
-            pltpu.SMEM(plan.shape, plan.dtype),
-            pltpu.VMEM(inner_moved.shape, F32),
-            pltpu.VMEM(inner_moved.shape, F32),
-            pltpu.VMEM((round_up(inner_moved.shape[0], LANES), LANES), F32),
-            pltpu.VMEM((slots, 2 * LANES), F32),
-            pltpu.VMEM((rows, LANES), F32),
-            pltpu.VMEM(gated.shape, BF16),
-            pltpu.VMEM(inner.shape, BF16),
-            pltpu.VMEM(group.shape, BF16),
-            pltpu.VMEM((places,) + scan_next.shape[1:], BF16),
-            pltpu.SemaphoreType.DMA((places,)),
-            pltpu.SemaphoreType.DMA((3,)),
-        ],
-        input_output_aliases={1 + len(operands): 3},
-        compiler_params=pltpu.CompilerParams(vmem_limit_bytes=limit),
+        input_output_aliases={len(operands): len(outs) - 1},
+        compiler_params=pltpu.CompilerParams(
+            vmem_limit_bytes=SMALL_LIMIT if rounds_of(replicas) else LARGE_LIMIT
+        ),
         cost_estimate=pl.CostEstimate(
             flops=10_000_000, bytes_accessed=2_000_000, transcendentals=0
         ),
-        name="advance_arrived",
-    )(plan, *operands, scan_next, *arrived)
+        name="advance_last" if last else "advance_arrived",
+    )(*operands, scan_next, *arrived)
 
 
 def swap_heads(value):
@@ -692,7 +784,7 @@
     swapped = [swap_heads(value) for value in (own, group_weight, small)]
     blocks = pack(replicas, cap, send_list, scan, inner, group, group_other, swapped)
     arrived = exchange(replicas, blocks)
-    plan, gated, group_weights, inner_raw, both, *moved, scan_next = stay(
+    plan, gated, weights, table, inner_part, group_part, *moved, scan_next = stay(
         replicas,
         cap,
         (decay_log, delta_bias, skip_gain, live_count),
@@ -712,13 +804,15 @@
         (swapped[0], swapped[1], small, swapped[2], group_other),
         arrived[:EARLIER] if rounds_of(replicas) else [],
     )
+    first = max(0, len(arrived) - LAST)
+    if first:
+        operands = (plan, weights, *moved, gated, table, inner_part, group_part)
+        gated, table, scan_next = arrive(
+            replicas, cap, 0, False, operands, scan_next, arrived[:first]
+        )
+    operands = (plan, weights, *moved, gated, table, inner_part, group_part)
     gated, inner_next, group_next, scan_next = arrive(
-        replicas,
-        cap,
-        plan,
-        (gated, group_weights, *moved, inner_raw, both, inner_taps, inner_offset, inner, group),
-        scan_next,
-        arrived,
+        replicas, cap, first, True, operands, scan_next, arrived[first:]
     )
     return (
         gated,

time: 36.7 us -> 34.1 us (0.929)
  the two profiles are of different devices: /device:TPU:17 before, /device:TPU:0 now
where the time goes in v3:
time: 34.1 us; the launch traced here: 33.7 us
  starting transfers between devices  15.1 us (44%)
  Pallas kernels  12.7 us (37%)
  between operations  3.33 us (10%)
  waiting for transfers between devices  2.34 us (7%)
    ppermute x7, starting transfers between devices, exchange(): lax.ppermute(block, 'dp', [(source, source ^ mask) for source in range(re...  13.6 us
    pallas_call x1, Pallas kernels, stay(): pl.pallas_call(functools.partial(stay_kernel, replicas, cap), out_shape=[...  5.5 us
    pallas_call x2, Pallas kernels, arrive(): pl.pallas_call(functools.partial(arrive_kernel, replicas, cap, first, las...  4.32 us
    ppermute x7, waiting for transfers between devices, exchange(): lax.ppermute(block, 'dp', [(source, source ^ mask) for source in range(re...  2.33 us
    pallas_call x1, Pallas kernels, pack(): pl.pallas_call(functools.partial(states_kernel, replicas, cap), out_shape...  2.15 us
    ppermute x4, starting transfers between devices, swap_heads(): return lax.ppermute(value, 'head', [(0, 1), (1, 0)])  1.45 us
    pallas_call x1, Pallas kernels, pack(): pl.pallas_call(functools.partial(windows_kernel, replicas, cap, scan.shap...  0.7 us
  transfers between devices with their start and end apart: 11, of which 1 were waited for; matrix products, arithmetic and copies ran while one was open for 0% of the time, Pallas kernels for 31%

profile of v3, /device:TPU:0, one launch (start us, length us, event | category | flops | bytes accessed | tf_op | source)
XLA Modules:
  0.0 33.7 jit_solution(17984509908982308161)
XLA Ops:
  0.6 0.5 %collective-permute-start.1 = (bf16[64,4096]{1,0:T(8,128)(2,1)}, bf16[64,4096]{1,0:T(8,128)(2,1)S(1)}, u32[]{:S(2)}, u32[]{:S(2)}) collective-permute-start(bf16[64,4096]{1,0:T(8,128)(2,1)} %bitcast.14), channel_id=1, source_target_pairs={{0,1},{1,0},{2,3},{3,2},{4,5},{5,4},{6,7},{7,6},{8,9},{9,8},{10,11... | collective-permute-start | bytes 1572872 | tf_op jit(solution)/shard_map/ppermute | solution.py:739
  1.1 0.0 copy-start
  1.2 0.1 collective-permute-start
  1.2 0.0 copy-start.1
  1.2 0.4 %collective-permute-start.3 = (bf16[3,56,64]{2,1,0:T(8,128)(2,1)}, bf16[3,56,64]{2,1,0:T(8,128)(2,1)S(1)}, u32[]{:S(2)}, u32[]{:S(2)}) collective-permute-start(bf16[3,56,64]{2,1,0:T(8,128)(2,1)} %bitcast.20), channel_id=1, source_target_pairs={{0,1},{1,0},{2,3},{3,2},{4,5},{5,4},{6,7},{7,6},{8,9},{9,8},{10,11... | collective-permute-start | bytes 64520 | tf_op jit(solution)/shard_map/ppermute | solution.py:739
  1.7 0.2 copy-done
  1.8 0.1 copy-done.1
  1.9 0.4 %collective-permute-start.2 = (f32[5,64]{1,0:T(8,128)S(1)}, f32[5,64]{1,0:T(8,128)S(1)}, u32[]{:S(2)}, u32[]{:S(2)}) collective-permute-start(f32[5,64]{1,0:T(8,128)S(1)} %pad_maximum_fusion.small), channel_id=1, source_target_pairs={{0,1},{1,0},{2,3},{3,2},{4,5},{5,4},{6,7},{7,6},{8,9},{9,8},{10,11... | collective-permute-start | bytes 3848 | tf_op jit(solution)/shard_map/ppermute | solution.py:739
  2.3 2.1 %pack_states.1 = (bf16[1,496,128]{2,1,0:T(8,128)(2,1)S(1)}, bf16[1,496,128]{2,1,0:T(8,128)(2,1)S(1)}, bf16[1,496,128]{2,1,0:T(8,128)(2,1)S(1)}, bf16[1,496,128]{...) custom-call(bf16[56,64,128]{2,1,0:T(8,128)(2,1)} %bitcast.11, ...), custom_call_target="tpu_custom_call" | custom-call | bytes 2000000 | tf_op jit(solution)/shard_map/pack_states/pallas_call | solution.py:158
  4.5 0.0 collective-permute-done.2.refs_9_.small_other
  4.5 0.0 collective-permute-done.3.group_other
  4.5 0.0 collective-permute-done.refs_7_.other
  4.5 0.0 collective-permute-done.1.refs_8_.group_weight_other
  4.5 0.7 %pack_windows.1 = (bf16[1,496,128]{2,1,0:T(8,128)(2,1)S(1)}, bf16[1,496,128]{2,1,0:T(8,128)(2,1)S(1)}, bf16[1,496,128]{2,1,0:T(8,128)(2,1)S(1)}, bf16[1,496,128]...) custom-call(s32[1,56]{1,0:T(1,128)S(1)} %get-tuple-element.40.indice, ...), custom_call_target="tpu_custom_call", output_to_operand_aliasing={{0}: (4, {}), {1}: (5, {}), {2}: (6, {}), {3}: (7, {}), {4}... | custom-call | bytes 500000 | tf_op jit(solution)/shard_map/pack_windows/pallas_call | solution.py:183
  5.2 3.8 %collective-permute-start.4 = (bf16[1,496,128]{2,1,0:T(8,128)(2,1)S(1)}, bf16[1,496,128]{2,1,0:T(8,128)(2,1)S(1)}, u32[]{:S(2)}, u32[]{:S(2)}) collective-permute-start(bf16[1,496,128]{2,1,0:T(8,128)(2,1)S(1)} %get-tuple-element.50), channel_id=1, source_target_pairs={{0,8},{2,10},{4,12},{6,14},{8,0},{10,2},{12,4},{14,6},{1,9},{3,11}... | collective-permute-start | bytes 380936 | tf_op jit(solution)/shard_map/ppermute | solution.py:747
  9.0 1.5 %collective-permute-start.5 = (bf16[1,496,128]{2,1,0:T(8,128)(2,1)S(1)}, bf16[1,496,128]{2,1,0:T(8,128)(2,1)S(1)}, u32[]{:S(2)}, u32[]{:S(2)}) collective-permute-start(bf16[1,496,128]{2,1,0:T(8,128)(2,1)S(1)} %get-tuple-element.51), channel_id=1, source_target_pairs={{0,2},{2,0},{4,6},{6,4},{8,10},{10,8},{12,14},{14,12},{1,3},{3,1},... | collective-permute-start | bytes 380936 | tf_op jit(solution)/shard_map/ppermute | solution.py:747
  10.5 1.6 %collective-permute-start.6 = (bf16[1,496,128]{2,1,0:T(8,128)(2,1)S(1)}, bf16[1,496,128]{2,1,0:T(8,128)(2,1)S(1)}, u32[]{:S(2)}, u32[]{:S(2)}) collective-permute-start(bf16[1,496,128]{2,1,0:T(8,128)(2,1)S(1)} %get-tuple-element.52), channel_id=1, source_target_pairs={{0,4},{2,6},{4,0},{6,2},{8,12},{10,14},{12,8},{14,10},{1,5},{3,7},... | collective-permute-start | bytes 380936 | tf_op jit(solution)/shard_map/ppermute | solution.py:747
  12.1 0.3 collective-permute-start.7
  12.4 1.4 %collective-permute-start.8 = (bf16[1,496,128]{2,1,0:T(8,128)(2,1)S(1)}, bf16[1,496,128]{2,1,0:T(8,128)(2,1)S(1)}, u32[]{:S(2)}, u32[]{:S(2)}) collective-permute-start(bf16[1,496,128]{2,1,0:T(8,128)(2,1)S(1)} %get-tuple-element.66), channel_id=1, source_target_pairs={{0,6},{2,4},{4,2},{6,0},{8,14},{10,12},{12,10},{14,8},{1,7},{3,5},... | collective-permute-start | bytes 380936 | tf_op jit(solution)/shard_map/ppermute | solution.py:747
  13.8 2.3 %collective-permute-done.4.refs_0_ = bf16[1,496,128]{2,1,0:T(8,128)(2,1)S(1)} collective-permute-done((bf16[1,496,128]{2,1,0:T(8,128)(2,1)S(1)}, bf16[1,496,128]{2,1,0:T(8,128)(2,1)S(1)}, u32[]{:S(2)}, u32[]{:S(2)}) %collective-permute-start.4) | collective-permute-done | bytes 127008 | tf_op jit(solution)/shard_map/ppermute | solution.py:747
  16.1 4.2 %collective-permute-start.9 = (bf16[1,496,128]{2,1,0:T(8,128)(2,1)S(1)}, bf16[1,496,128]{2,1,0:T(8,128)(2,1)S(1)}, u32[]{:S(2)}, u32[]{:S(2)}) collective-permute-start(bf16[1,496,128]{2,1,0:T(8,128)(2,1)S(1)} %get-tuple-element.70), channel_id=1, source_target_pairs={{0,12},{2,14},{4,8},{6,10},{8,4},{10,6},{12,0},{14,2},{1,13},{3,15... | collective-permute-start | bytes 380936 | tf_op jit(solution)/shard_map/ppermute | solution.py:747
  20.2 0.0 collective-permute-done.5.refs_1_
  20.2 0.9 %collective-permute-start.10 = (bf16[1,496,128]{2,1,0:T(8,128)(2,1)S(1)}, bf16[1,496,128]{2,1,0:T(8,128)(2,1)S(1)}, u32[]{:S(2)}, u32[]{:S(2)}) collective-permute-start(bf16[1,496,128]{2,1,0:T(8,128)(2,1)S(1)} %get-tuple-element.71), channel_id=1, source_target_pairs={{0,14},{2,12},{4,10},{6,8},{8,6},{10,4},{12,2},{14,0},{1,15},{3,13... | collective-permute-start | bytes 380936 | tf_op jit(solution)/shard_map/ppermute | solution.py:747
  23.8 0.0 collective-permute-done.6.refs_2_
  23.8 5.5 %advance_staying.1 = (s32[1,128]{1,0:T(1,128)S(1)}, f32[112,128]{1,0:T(8,128)S(1)}, f32[16,128]{1,0:T(8,128)S(1)}, f32[56,256]{1,0:T(8,128)S(1)}, bf16[2,56,128]...) custom-call(f32[1]{0:T(128)S(6)} %copy.40.decay_log, ...), custom_call_target="tpu_custom_call" | custom-call | flops 300000000 | bytes 6000000 | tf_op jit(solution)/shard_map/advance_staying/pallas_call | solution.py:487
  29.3 0.0 collective-permute-done.7.refs_3_
  29.3 0.0 collective-permute-done.8.refs_4_
  29.3 2.9 %advance_arrived.1 = (f32[112,128]{1,0:T(8,128)S(1)}, f32[56,256]{1,0:T(8,128)S(1)}, bf16[56,64,128]{2,1,0:T(8,128)(2,1)}) custom-call(s32[1,128]{1,0:T(1,128)S(1)} %get-tuple-element.53.plan_near, f32[16,128]{1,0:T(8,128)S(1)} %get-tuple-element.54.weights, f32[112,128]{1,0:T(8,128)S(1)} %get-tuple-element.55.inner_moved, ...), custom_call_target="tpu_custom_call", output_to_operand_aliasing={{2}: (11, {})} | custom-call | flops 10000000 | bytes 2000000 | tf_op jit(solution)/shard_map/advance_arrived/pallas_call | solution.py:713
  32.2 0.0 collective-permute-done.9.refs_0_
  32.2 0.0 collective-permute-done.10.refs_1_
  32.2 1.4 %advance_last.1 = (bf16[2,56,128]{2,1,0:T(8,128)(2,1)}, bf16[3,56,128]{2,1,0:T(8,128)(2,1)}, bf16[3,56,64]{2,1,0:T(8,128)(2,1)}, bf16[56,64,128]{2,1,0:T(8,128)(2,1)}) custom-call(s32[1,128]{1,0:T(1,128)S(1)} %get-tuple-element.53.plan_near, f32[16,128]{1,0:T(8,128)S(1)} %get-tuple-element.54.weights, ...), custom_call_target="tpu_custom_call", output_to_operand_aliasing={{3}: (11, {})} | custom-call | flops 10000000 | bytes 2000000 | tf_op jit(solution)/shard_map/advance_last/pallas_call | solution.py:713
  (1 shorter events, 0.0 us)
Async XLA Ops:
  0.6 3.9 %collective-permute-start.1 = (bf16[64,4096]{1,0:T(8,128)(2,1)}, bf16[64,4096]{1,0:T(8,128)(2,1)S(1)}, u32[]{:S(2)}, u32[]{:S(2)}) collective-permute-start(bf16[64,4096]{1,0:T(8,128)(2,1)} %bitcast.14), channel_id=1, source_target_pairs={{0,1},{1,0},{2,3},{3,2},{4,5},{5,4},{6,7},{7,6},{8,9},{9,8},{10,11... | collective-permute-start | bytes 1572872 | tf_op jit(solution)/shard_map/ppermute | solution.py:739
  1.1 0.7 %copy-start = (f32[4,64]{1,0:T(4,128)S(1)}, f32[4,64]{1,0:T(4,128)}, u32[]{:S(2)}) copy-start(f32[4,64]{1,0:T(4,128)} %param.25) | copy-start | bytes 3076
  1.2 3.4 %collective-permute-start = (bf16[112,2048]{1,0:T(8,128)(2,1)}, bf16[112,2048]{1,0:T(8,128)(2,1)S(1)}, u32[]{:S(2)}, u32[]{:S(2)}) collective-permute-start(bf16[112,2048]{1,0:T(8,128)(2,1)} %bitcast.16), channel_id=1, source_target_pairs={{0,1},{1,0},{2,3},{3,2},{4,5},{5,4},{6,7},{7,6},{8,9},{9,8},{10,11... | collective-permute-start | bytes 1376264 | tf_op jit(solution)/shard_map/ppermute | solution.py:739
  1.2 0.7 %copy-start.1 = (f32[64]{0:T(128)S(1)}, f32[64]{0:T(128)}, u32[]{:S(2)}) copy-start(f32[64]{0:T(128)} %param.26) | copy-start | bytes 772
  1.2 3.3 %collective-permute-start.3 = (bf16[3,56,64]{2,1,0:T(8,128)(2,1)}, bf16[3,56,64]{2,1,0:T(8,128)(2,1)S(1)}, u32[]{:S(2)}, u32[]{:S(2)}) collective-permute-start(bf16[3,56,64]{2,1,0:T(8,128)(2,1)} %bitcast.20), channel_id=1, source_target_pairs={{0,1},{1,0},{2,3},{3,2},{4,5},{5,4},{6,7},{7,6},{8,9},{9,8},{10,11... | collective-permute-start | bytes 64520 | tf_op jit(solution)/shard_map/ppermute | solution.py:739
  1.9 2.6 %collective-permute-start.2 = (f32[5,64]{1,0:T(8,128)S(1)}, f32[5,64]{1,0:T(8,128)S(1)}, u32[]{:S(2)}, u32[]{:S(2)}) collective-permute-start(f32[5,64]{1,0:T(8,128)S(1)} %pad_maximum_fusion.small), channel_id=1, source_target_pairs={{0,1},{1,0},{2,3},{3,2},{4,5},{5,4},{6,7},{7,6},{8,9},{9,8},{10,11... | collective-permute-start | bytes 3848 | tf_op jit(solution)/shard_map/ppermute | solution.py:739
  5.2 10.9 %collective-permute-start.4 = (bf16[1,496,128]{2,1,0:T(8,128)(2,1)S(1)}, bf16[1,496,128]{2,1,0:T(8,128)(2,1)S(1)}, u32[]{:S(2)}, u32[]{:S(2)}) collective-permute-start(bf16[1,496,128]{2,1,0:T(8,128)(2,1)S(1)} %get-tuple-element.50), channel_id=1, source_target_pairs={{0,8},{2,10},{4,12},{6,14},{8,0},{10,2},{12,4},{14,6},{1,9},{3,11}... | collective-permute-start | bytes 380936 | tf_op jit(solution)/shard_map/ppermute | solution.py:747
  9.0 11.2 %collective-permute-start.5 = (bf16[1,496,128]{2,1,0:T(8,128)(2,1)S(1)}, bf16[1,496,128]{2,1,0:T(8,128)(2,1)S(1)}, u32[]{:S(2)}, u32[]{:S(2)}) collective-permute-start(bf16[1,496,128]{2,1,0:T(8,128)(2,1)S(1)} %get-tuple-element.51), channel_id=1, source_target_pairs={{0,2},{2,0},{4,6},{6,4},{8,10},{10,8},{12,14},{14,12},{1,3},{3,1},... | collective-permute-start | bytes 380936 | tf_op jit(solution)/shard_map/ppermute | solution.py:747
  10.5 13.3 %collective-permute-start.6 = (bf16[1,496,128]{2,1,0:T(8,128)(2,1)S(1)}, bf16[1,496,128]{2,1,0:T(8,128)(2,1)S(1)}, u32[]{:S(2)}, u32[]{:S(2)}) collective-permute-start(bf16[1,496,128]{2,1,0:T(8,128)(2,1)S(1)} %get-tuple-element.52), channel_id=1, source_target_pairs={{0,4},{2,6},{4,0},{6,2},{8,12},{10,14},{12,8},{14,10},{1,5},{3,7},... | collective-permute-start | bytes 380936 | tf_op jit(solution)/shard_map/ppermute | solution.py:747
  12.1 17.2 %collective-permute-start.7 = (bf16[1,496,128]{2,1,0:T(8,128)(2,1)S(1)}, bf16[1,496,128]{2,1,0:T(8,128)(2,1)S(1)}, u32[]{:S(2)}, u32[]{:S(2)}) collective-permute-start(bf16[1,496,128]{2,1,0:T(8,128)(2,1)S(1)} %get-tuple-element.65), channel_id=1, source_target_pairs={{0,10},{2,8},{4,14},{6,12},{8,2},{10,0},{12,6},{14,4},{1,11},{3,9}... | collective-permute-start | bytes 380936 | tf_op jit(solution)/shard_map/ppermute | solution.py:747
  12.4 16.9 %collective-permute-start.8 = (bf16[1,496,128]{2,1,0:T(8,128)(2,1)S(1)}, bf16[1,496,128]{2,1,0:T(8,128)(2,1)S(1)}, u32[]{:S(2)}, u32[]{:S(2)}) collective-permute-start(bf16[1,496,128]{2,1,0:T(8,128)(2,1)S(1)} %get-tuple-element.66), channel_id=1, source_target_pairs={{0,6},{2,4},{4,2},{6,0},{8,14},{10,12},{12,10},{14,8},{1,7},{3,5},... | collective-permute-start | bytes 380936 | tf_op jit(solution)/shard_map/ppermute | solution.py:747
  16.1 16.1 %collective-permute-start.9 = (bf16[1,496,128]{2,1,0:T(8,128)(2,1)S(1)}, bf16[1,496,128]{2,1,0:T(8,128)(2,1)S(1)}, u32[]{:S(2)}, u32[]{:S(2)}) collective-permute-start(bf16[1,496,128]{2,1,0:T(8,128)(2,1)S(1)} %get-tuple-element.70), channel_id=1, source_target_pairs={{0,12},{2,14},{4,8},{6,10},{8,4},{10,6},{12,0},{14,2},{1,13},{3,15... | collective-permute-start | bytes 380936 | tf_op jit(solution)/shard_map/ppermute | solution.py:747
  20.2 12.0 %collective-permute-start.10 = (bf16[1,496,128]{2,1,0:T(8,128)(2,1)S(1)}, bf16[1,496,128]{2,1,0:T(8,128)(2,1)S(1)}, u32[]{:S(2)}, u32[]{:S(2)}) collective-permute-start(bf16[1,496,128]{2,1,0:T(8,128)(2,1)S(1)} %get-tuple-element.71), channel_id=1, source_target_pairs={{0,14},{2,12},{4,10},{6,8},{8,6},{10,4},{12,2},{14,0},{1,15},{3,13... | collective-permute-start | bytes 380936 | tf_op jit(solution)/shard_map/ppermute | solution.py:747

commit v4 on v3

--- a/solution.py
+++ b/solution.py
@@ -13,7 +13,7 @@
 MEDIUM_LIMIT = 16 * 1024 * 1024
 LARGE_LIMIT = 48 * 1024 * 1024
 MAX_ROUNDS = 16
-EARLIER = 3
+EARLIER = 2
 LAST = 2
 LANES = 128
 ROWS = 8
@@ -49,7 +49,7 @@
         return []
     light = list(range(1, replicas // 2))
     heavy = list(range(replicas // 2, replicas))
-    return heavy[:1] + light[:2] + heavy[1:2] + light[2:] + heavy[2:]
+    return light[:1] + heavy[:2] + light[1:] + heavy[2:]
 
 
 def partner(replicas, mask):

time: 34.1 us -> 36.1 us (1.059)
  starting transfers between devices: 15.1 us -> 16.3 us
  waiting for transfers between devices: 2.34 us -> 3.28 us
    ppermute x7, starting transfers between devices: 13.6 us -> 14.8 us  [exchange(): lax.ppermute(block, 'dp', [(source, source ^ mask) for source in range(re...]
    ppermute x7, waiting for transfers between devices: 2.33 us -> 3.27 us  [exchange(): lax.ppermute(block, 'dp', [(source, source ^ mask) for source in range(re...]
  transfers between devices with their start and end apart: 11 -> 11, of which waited for: 1 -> 1; matrix products, arithmetic and copies ran while one was open for 0% -> 0% of each run, Pallas kernels for 31% -> 27%
where the time goes in v4:
time: 36.1 us; the launch traced here: 35.8 us
  starting transfers between devices  16.3 us (45%)
  Pallas kernels  12.7 us (35%)
  between operations  3.33 us (9%)
  waiting for transfers between devices  3.28 us (9%)
    ppermute x7, starting transfers between devices, exchange(): lax.ppermute(block, 'dp', [(source, source ^ mask) for source in range(re...  14.8 us
    pallas_call x1, Pallas kernels, stay(): pl.pallas_call(functools.partial(stay_kernel, replicas, cap), out_shape=[...  5.5 us
    pallas_call x2, Pallas kernels, arrive(): pl.pallas_call(functools.partial(arrive_kernel, replicas, cap, first, las...  4.35 us
    ppermute x7, waiting for transfers between devices, exchange(): lax.ppermute(block, 'dp', [(source, source ^ mask) for source in range(re...  3.27 us
    pallas_call x1, Pallas kernels, pack(): pl.pallas_call(functools.partial(states_kernel, replicas, cap), out_shape...  2.12 us
    ppermute x4, starting transfers between devices, swap_heads(): return lax.ppermute(value, 'head', [(0, 1), (1, 0)])  1.45 us
  transfers between devices with their start and end apart: 11, of which 1 were waited for; matrix products, arithmetic and copies ran while one was open for 0% of the time, Pallas kernels for 27%

profile of v4, /device:TPU:0, one launch (start us, length us, event | category | flops | bytes accessed | tf_op | source)
XLA Modules:
  0.0 35.8 jit_solution(14179992922385277341)
XLA Ops:
  0.6 0.5 %collective-permute-start.1 = (bf16[64,4096]{1,0:T(8,128)(2,1)}, bf16[64,4096]{1,0:T(8,128)(2,1)S(1)}, u32[]{:S(2)}, u32[]{:S(2)}) collective-permute-start(bf16[64,4096]{1,0:T(8,128)(2,1)} %bitcast.14), channel_id=1, source_target_pairs={{0,1},{1,0},{2,3},{3,2},{4,5},{5,4},{6,7},{7,6},{8,9},{9,8},{10,11... | collective-permute-start | bytes 1572872 | tf_op jit(solution)/shard_map/ppermute | solution.py:739
  1.1 0.0 copy-start
  1.2 0.1 collective-permute-start
  1.2 0.0 copy-start.1
  1.2 0.4 %collective-permute-start.3 = (bf16[3,56,64]{2,1,0:T(8,128)(2,1)}, bf16[3,56,64]{2,1,0:T(8,128)(2,1)S(1)}, u32[]{:S(2)}, u32[]{:S(2)}) collective-permute-start(bf16[3,56,64]{2,1,0:T(8,128)(2,1)} %bitcast.20), channel_id=1, source_target_pairs={{0,1},{1,0},{2,3},{3,2},{4,5},{5,4},{6,7},{7,6},{8,9},{9,8},{10,11... | collective-permute-start | bytes 64520 | tf_op jit(solution)/shard_map/ppermute | solution.py:739
  1.7 0.2 copy-done
  1.8 0.1 copy-done.1
  1.9 0.4 %collective-permute-start.2 = (f32[5,64]{1,0:T(8,128)S(1)}, f32[5,64]{1,0:T(8,128)S(1)}, u32[]{:S(2)}, u32[]{:S(2)}) collective-permute-start(f32[5,64]{1,0:T(8,128)S(1)} %pad_maximum_fusion.small), channel_id=1, source_target_pairs={{0,1},{1,0},{2,3},{3,2},{4,5},{5,4},{6,7},{7,6},{8,9},{9,8},{10,11... | collective-permute-start | bytes 3848 | tf_op jit(solution)/shard_map/ppermute | solution.py:739
  2.3 2.1 %pack_states.1 = (bf16[1,496,128]{2,1,0:T(8,128)(2,1)S(1)}, bf16[1,496,128]{2,1,0:T(8,128)(2,1)S(1)}, bf16[1,496,128]{2,1,0:T(8,128)(2,1)S(1)}, bf16[1,496,128]{...) custom-call(bf16[56,64,128]{2,1,0:T(8,128)(2,1)} %bitcast.12, ...), custom_call_target="tpu_custom_call" | custom-call | bytes 2000000 | tf_op jit(solution)/shard_map/pack_states/pallas_call | solution.py:158
  4.5 0.0 collective-permute-done.2.refs_9_.small_other
  4.5 0.0 collective-permute-done.3.group_other
  4.5 0.0 collective-permute-done.refs_7_.other
  4.5 0.0 collective-permute-done.1.refs_8_.group_weight_other
  4.5 0.7 %pack_windows.1 = (bf16[1,496,128]{2,1,0:T(8,128)(2,1)S(1)}, bf16[1,496,128]{2,1,0:T(8,128)(2,1)S(1)}, bf16[1,496,128]{2,1,0:T(8,128)(2,1)S(1)}, bf16[1,496,128]...) custom-call(s32[1,56]{1,0:T(1,128)S(1)} %get-tuple-element.40.indice, ...), custom_call_target="tpu_custom_call", output_to_operand_aliasing={{0}: (4, {}), {1}: (5, {}), {2}: (6, {}), {3}: (7, {}), {4}... | custom-call | bytes 500000 | tf_op jit(solution)/shard_map/pack_windows/pallas_call | solution.py:183
  5.2 2.7 %collective-permute-start.4 = (bf16[1,496,128]{2,1,0:T(8,128)(2,1)S(1)}, bf16[1,496,128]{2,1,0:T(8,128)(2,1)S(1)}, u32[]{:S(2)}, u32[]{:S(2)}) collective-permute-start(bf16[1,496,128]{2,1,0:T(8,128)(2,1)S(1)} %get-tuple-element.50), channel_id=1, source_target_pairs={{0,2},{2,0},{4,6},{6,4},{8,10},{10,8},{12,14},{14,12},{1,3},{3,1},... | collective-permute-start | bytes 380936 | tf_op jit(solution)/shard_map/ppermute | solution.py:747
  7.9 2.6 %collective-permute-start.5 = (bf16[1,496,128]{2,1,0:T(8,128)(2,1)S(1)}, bf16[1,496,128]{2,1,0:T(8,128)(2,1)S(1)}, u32[]{:S(2)}, u32[]{:S(2)}) collective-permute-start(bf16[1,496,128]{2,1,0:T(8,128)(2,1)S(1)} %get-tuple-element.51), channel_id=1, source_target_pairs={{0,8},{2,10},{4,12},{6,14},{8,0},{10,2},{12,4},{14,6},{1,9},{3,11}... | collective-permute-start | bytes 380936 | tf_op jit(solution)/shard_map/ppermute | solution.py:747
  10.5 0.0 collective-permute-start.6
  10.5 1.9 %collective-permute-start.7 = (bf16[1,496,128]{2,1,0:T(8,128)(2,1)S(1)}, bf16[1,496,128]{2,1,0:T(8,128)(2,1)S(1)}, u32[]{:S(2)}, u32[]{:S(2)}) collective-permute-start(bf16[1,496,128]{2,1,0:T(8,128)(2,1)S(1)} %get-tuple-element.65), channel_id=1, source_target_pairs={{0,4},{2,6},{4,0},{6,2},{8,12},{10,14},{12,8},{14,10},{1,5},{3,7},... | collective-permute-start | bytes 380936 | tf_op jit(solution)/shard_map/ppermute | solution.py:747
  12.4 1.4 %collective-permute-start.8 = (bf16[1,496,128]{2,1,0:T(8,128)(2,1)S(1)}, bf16[1,496,128]{2,1,0:T(8,128)(2,1)S(1)}, u32[]{:S(2)}, u32[]{:S(2)}) collective-permute-start(bf16[1,496,128]{2,1,0:T(8,128)(2,1)S(1)} %get-tuple-element.66), channel_id=1, source_target_pairs={{0,6},{2,4},{4,2},{6,0},{8,14},{10,12},{12,10},{14,8},{1,7},{3,5},... | collective-permute-start | bytes 380936 | tf_op jit(solution)/shard_map/ppermute | solution.py:747
  13.8 0.0 collective-permute-done.4.refs_0_
  13.8 3.6 %collective-permute-start.9 = (bf16[1,496,128]{2,1,0:T(8,128)(2,1)S(1)}, bf16[1,496,128]{2,1,0:T(8,128)(2,1)S(1)}, u32[]{:S(2)}, u32[]{:S(2)}) collective-permute-start(bf16[1,496,128]{2,1,0:T(8,128)(2,1)S(1)} %get-tuple-element.70), channel_id=1, source_target_pairs={{0,12},{2,14},{4,8},{6,10},{8,4},{10,6},{12,0},{14,2},{1,13},{3,15... | collective-permute-start | bytes 380936 | tf_op jit(solution)/shard_map/ppermute | solution.py:747
  17.4 3.3 %collective-permute-done.5.refs_1_ = bf16[1,496,128]{2,1,0:T(8,128)(2,1)S(1)} collective-permute-done((bf16[1,496,128]{2,1,0:T(8,128)(2,1)S(1)}, bf16[1,496,128]{2,1,0:T(8,128)(2,1)S(1)}, u32[]{:S(2)}, u32[]{:S(2)}) %collective-permute-start.5) | collective-permute-done | bytes 127008 | tf_op jit(solution)/shard_map/ppermute | solution.py:747
  20.6 2.7 %collective-permute-start.10 = (bf16[1,496,128]{2,1,0:T(8,128)(2,1)S(1)}, bf16[1,496,128]{2,1,0:T(8,128)(2,1)S(1)}, u32[]{:S(2)}, u32[]{:S(2)}) collective-permute-start(bf16[1,496,128]{2,1,0:T(8,128)(2,1)S(1)} %get-tuple-element.71), channel_id=1, source_target_pairs={{0,14},{2,12},{4,10},{6,8},{8,6},{10,4},{12,2},{14,0},{1,15},{3,13... | collective-permute-start | bytes 380936 | tf_op jit(solution)/shard_map/ppermute | solution.py:747
  25.9 5.5 %advance_staying.1 = (s32[1,128]{1,0:T(1,128)S(1)}, f32[112,128]{1,0:T(8,128)S(1)}, f32[16,128]{1,0:T(8,128)S(1)}, f32[56,256]{1,0:T(8,128)S(1)}, bf16[2,56,128]...) custom-call(f32[1]{0:T(128)S(6)} %copy.40.decay_log, ...), custom_call_target="tpu_custom_call" | custom-call | flops 300000000 | bytes 6000000 | tf_op jit(solution)/shard_map/advance_staying/pallas_call | solution.py:487
  31.4 0.0 collective-permute-done.6.refs_2_
  31.4 0.0 collective-permute-done.7.refs_3_
  31.4 0.0 collective-permute-done.8.refs_4_
  31.4 2.2 %advance_arrived.1 = (f32[112,128]{1,0:T(8,128)S(1)}, f32[56,256]{1,0:T(8,128)S(1)}, bf16[56,64,128]{2,1,0:T(8,128)(2,1)}) custom-call(s32[1,128]{1,0:T(1,128)S(1)} %get-tuple-element.52.plan_near, f32[16,128]{1,0:T(8,128)S(1)} %get-tuple-element.53.weights, f32[112,128]{1,0:T(8,128)S(1)} %get-tuple-element.54.inner_moved, ...), custom_call_target="tpu_custom_call", output_to_operand_aliasing={{2}: (11, {})} | custom-call | flops 10000000 | bytes 2000000 | tf_op jit(solution)/shard_map/advance_arrived/pallas_call | solution.py:713
  33.6 0.0 collective-permute-done.9.refs_0_
  33.6 0.0 collective-permute-done.10.refs_1_
  33.6 2.2 %advance_last.1 = (bf16[2,56,128]{2,1,0:T(8,128)(2,1)}, bf16[3,56,128]{2,1,0:T(8,128)(2,1)}, bf16[3,56,64]{2,1,0:T(8,128)(2,1)}, bf16[56,64,128]{2,1,0:T(8,128)(2,1)}) custom-call(s32[1,128]{1,0:T(1,128)S(1)} %get-tuple-element.52.plan_near, f32[16,128]{1,0:T(8,128)S(1)} %get-tuple-element.53.weights, ...), custom_call_target="tpu_custom_call", output_to_operand_aliasing={{3}: (11, {})} | custom-call | flops 10000000 | bytes 2000000 | tf_op jit(solution)/shard_map/advance_last/pallas_call | solution.py:713
  (1 shorter events, 0.0 us)
Async XLA Ops:
  0.6 3.9 %collective-permute-start.1 = (bf16[64,4096]{1,0:T(8,128)(2,1)}, bf16[64,4096]{1,0:T(8,128)(2,1)S(1)}, u32[]{:S(2)}, u32[]{:S(2)}) collective-permute-start(bf16[64,4096]{1,0:T(8,128)(2,1)} %bitcast.14), channel_id=1, source_target_pairs={{0,1},{1,0},{2,3},{3,2},{4,5},{5,4},{6,7},{7,6},{8,9},{9,8},{10,11... | collective-permute-start | bytes 1572872 | tf_op jit(solution)/shard_map/ppermute | solution.py:739
  1.1 0.7 %copy-start = (f32[4,64]{1,0:T(4,128)S(1)}, f32[4,64]{1,0:T(4,128)}, u32[]{:S(2)}) copy-start(f32[4,64]{1,0:T(4,128)} %param.25) | copy-start | bytes 3076
  1.2 3.3 %collective-permute-start = (bf16[112,2048]{1,0:T(8,128)(2,1)}, bf16[112,2048]{1,0:T(8,128)(2,1)S(1)}, u32[]{:S(2)}, u32[]{:S(2)}) collective-permute-start(bf16[112,2048]{1,0:T(8,128)(2,1)} %bitcast.16), channel_id=1, source_target_pairs={{0,1},{1,0},{2,3},{3,2},{4,5},{5,4},{6,7},{7,6},{8,9},{9,8},{10,11... | collective-permute-start | bytes 1376264 | tf_op jit(solution)/shard_map/ppermute | solution.py:739
  1.2 0.7 %copy-start.1 = (f32[64]{0:T(128)S(1)}, f32[64]{0:T(128)}, u32[]{:S(2)}) copy-start(f32[64]{0:T(128)} %param.26) | copy-start | bytes 772
  1.2 3.2 %collective-permute-start.3 = (bf16[3,56,64]{2,1,0:T(8,128)(2,1)}, bf16[3,56,64]{2,1,0:T(8,128)(2,1)S(1)}, u32[]{:S(2)}, u32[]{:S(2)}) collective-permute-start(bf16[3,56,64]{2,1,0:T(8,128)(2,1)} %bitcast.20), channel_id=1, source_target_pairs={{0,1},{1,0},{2,3},{3,2},{4,5},{5,4},{6,7},{7,6},{8,9},{9,8},{10,11... | collective-permute-start | bytes 64520 | tf_op jit(solution)/shard_map/ppermute | solution.py:739
  1.9 2.6 %collective-permute-start.2 = (f32[5,64]{1,0:T(8,128)S(1)}, f32[5,64]{1,0:T(8,128)S(1)}, u32[]{:S(2)}, u32[]{:S(2)}) collective-permute-start(f32[5,64]{1,0:T(8,128)S(1)} %pad_maximum_fusion.small), channel_id=1, source_target_pairs={{0,1},{1,0},{2,3},{3,2},{4,5},{5,4},{6,7},{7,6},{8,9},{9,8},{10,11... | collective-permute-start | bytes 3848 | tf_op jit(solution)/shard_map/ppermute | solution.py:739
  5.2 8.6 %collective-permute-start.4 = (bf16[1,496,128]{2,1,0:T(8,128)(2,1)S(1)}, bf16[1,496,128]{2,1,0:T(8,128)(2,1)S(1)}, u32[]{:S(2)}, u32[]{:S(2)}) collective-permute-start(bf16[1,496,128]{2,1,0:T(8,128)(2,1)S(1)} %get-tuple-element.50), channel_id=1, source_target_pairs={{0,2},{2,0},{4,6},{6,4},{8,10},{10,8},{12,14},{14,12},{1,3},{3,1},... | collective-permute-start | bytes 380936 | tf_op jit(solution)/shard_map/ppermute | solution.py:747
  7.9 12.7 %collective-permute-start.5 = (bf16[1,496,128]{2,1,0:T(8,128)(2,1)S(1)}, bf16[1,496,128]{2,1,0:T(8,128)(2,1)S(1)}, u32[]{:S(2)}, u32[]{:S(2)}) collective-permute-start(bf16[1,496,128]{2,1,0:T(8,128)(2,1)S(1)} %get-tuple-element.51), channel_id=1, source_target_pairs={{0,8},{2,10},{4,12},{6,14},{8,0},{10,2},{12,4},{14,6},{1,9},{3,11}... | collective-permute-start | bytes 380936 | tf_op jit(solution)/shard_map/ppermute | solution.py:747
  10.5 20.9 %collective-permute-start.6 = (bf16[1,496,128]{2,1,0:T(8,128)(2,1)S(1)}, bf16[1,496,128]{2,1,0:T(8,128)(2,1)S(1)}, u32[]{:S(2)}, u32[]{:S(2)}) collective-permute-start(bf16[1,496,128]{2,1,0:T(8,128)(2,1)S(1)} %get-tuple-element.64), channel_id=1, source_target_pairs={{0,10},{2,8},{4,14},{6,12},{8,2},{10,0},{12,6},{14,4},{1,11},{3,9}... | collective-permute-start | bytes 380936 | tf_op jit(solution)/shard_map/ppermute | solution.py:747
  10.5 20.9 %collective-permute-start.7 = (bf16[1,496,128]{2,1,0:T(8,128)(2,1)S(1)}, bf16[1,496,128]{2,1,0:T(8,128)(2,1)S(1)}, u32[]{:S(2)}, u32[]{:S(2)}) collective-permute-start(bf16[1,496,128]{2,1,0:T(8,128)(2,1)S(1)} %get-tuple-element.65), channel_id=1, source_target_pairs={{0,4},{2,6},{4,0},{6,2},{8,12},{10,14},{12,8},{14,10},{1,5},{3,7},... | collective-permute-start | bytes 380936 | tf_op jit(solution)/shard_map/ppermute | solution.py:747
  12.4 19.0 %collective-permute-start.8 = (bf16[1,496,128]{2,1,0:T(8,128)(2,1)S(1)}, bf16[1,496,128]{2,1,0:T(8,128)(2,1)S(1)}, u32[]{:S(2)}, u32[]{:S(2)}) collective-permute-start(bf16[1,496,128]{2,1,0:T(8,128)(2,1)S(1)} %get-tuple-element.66), channel_id=1, source_target_pairs={{0,6},{2,4},{4,2},{6,0},{8,14},{10,12},{12,10},{14,8},{1,7},{3,5},... | collective-permute-start | bytes 380936 | tf_op jit(solution)/shard_map/ppermute | solution.py:747
  13.8 19.8 %collective-permute-start.9 = (bf16[1,496,128]{2,1,0:T(8,128)(2,1)S(1)}, bf16[1,496,128]{2,1,0:T(8,128)(2,1)S(1)}, u32[]{:S(2)}, u32[]{:S(2)}) collective-permute-start(bf16[1,496,128]{2,1,0:T(8,128)(2,1)S(1)} %get-tuple-element.70), channel_id=1, source_target_pairs={{0,12},{2,14},{4,8},{6,10},{8,4},{10,6},{12,0},{14,2},{1,13},{3,15... | collective-permute-start | bytes 380936 | tf_op jit(solution)/shard_map/ppermute | solution.py:747
  20.6 13.0 %collective-permute-start.10 = (bf16[1,496,128]{2,1,0:T(8,128)(2,1)S(1)}, bf16[1,496,128]{2,1,0:T(8,128)(2,1)S(1)}, u32[]{:S(2)}, u32[]{:S(2)}) collective-permute-start(bf16[1,496,128]{2,1,0:T(8,128)(2,1)S(1)} %get-tuple-element.71), channel_id=1, source_target_pairs={{0,14},{2,12},{4,10},{6,8},{8,6},{10,4},{12,2},{14,0},{1,15},{3,13... | collective-permute-start | bytes 380936 | tf_op jit(solution)/shard_map/ppermute | solution.py:747

commit v5 on v4

--- a/solution.py
+++ b/solution.py
@@ -49,7 +49,7 @@
         return []
     light = list(range(1, replicas // 2))
     heavy = list(range(replicas // 2, replicas))
-    return light[:1] + heavy[:2] + light[1:] + heavy[2:]
+    return light[:2] + heavy[:2] + light[2:] + heavy[2:]
 
 
 def partner(replicas, mask):
@@ -329,10 +329,10 @@
 
     pairs = [
         (receive_hbm, receive),
-        (delta_weight, delta_row),
         (own_hbm, own),
         (inner_weight, wide.at[:, pl.ds(0, LANES)]),
         (gate_weight, wide.at[:, pl.ds(LANES, LANES)]),
+        (delta_weight, delta_row),
         (group_weight, band(head)),
         (group_weight_other, band(1 - head)),
         (inner_taps_hbm, inner_taps),
@@ -349,16 +349,17 @@
         load.start()
     loads[0].wait()
     make_plan(replicas, cap, receive, slots, plan, inverse)
-    loads[1].wait()
-    first = 2 * width
-    tall[first:, :] = jnp.broadcast_to(delta_row[...], (tall.shape[0] - first, 2 * half))
-    for load in loads[2:]:
+    for load in loads[1:4]:
         load.wait()
     mine = pl.ds(pl.multiple_of(head * half, half), half)
     theirs = pl.ds(pl.multiple_of((1 - head) * half, half), half)
     flat = jnp.dot(own[...], wide[mine, :], preferred_element_type=F32) + jnp.dot(
         other[...], wide[theirs, :], preferred_element_type=F32
     )
+    for load in loads[4:]:
+        load.wait()
+    first = 2 * width
+    tall[first:, :] = jnp.broadcast_to(delta_row[...], (tall.shape[0] - first, 2 * half))
 
     def across(tokens, part):
         return lax.dot_general(

time: 36.1 us -> 34.6 us (0.958)
  the two profiles are of different devices: /device:TPU:0 before, /device:TPU:18 now
where the time goes in v5:
time: 34.6 us; the launch traced here: 34.2 us
  Pallas kernels  12.8 us (37%)
  starting transfers between devices  9.77 us (28%)
  waiting for transfers between devices  7.76 us (22%)
  between operations  3.33 us (10%)
  local copies, waits for them, and re-layouts  0.57 us (2%)
    ppermute x7, starting transfers between devices, exchange(): lax.ppermute(block, 'dp', [(source, source ^ mask) for source in range(re...  8.99 us
    ppermute x7, waiting for transfers between devices, exchange(): lax.ppermute(block, 'dp', [(source, source ^ mask) for source in range(re...  7.75 us
    pallas_call x1, Pallas kernels, stay(): pl.pallas_call(functools.partial(stay_kernel, replicas, cap), out_shape=[...  5.64 us
    pallas_call x2, Pallas kernels, arrive(): pl.pallas_call(functools.partial(arrive_kernel, replicas, cap, first, las...  4.36 us
    pallas_call x1, Pallas kernels, pack(): pl.pallas_call(functools.partial(states_kernel, replicas, cap), out_shape...  2.11 us
    ppermute x4, starting transfers between devices, swap_heads(): return lax.ppermute(value, 'head', [(0, 1), (1, 0)])  0.78 us
    pallas_call x1, Pallas kernels, pack(): pl.pallas_call(functools.partial(windows_kernel, replicas, cap, scan.shap...  0.7 us
  transfers between devices with their start and end apart: 11, of which 3 were waited for; matrix products, arithmetic and copies ran while one was open for 0% of the time, Pallas kernels for 29%

profile of v5, /device:TPU:18, one launch (start us, length us, event | category | flops | bytes accessed | tf_op | source)
XLA Modules:
  0.0 34.2 jit_solution(11575138683273343202)
XLA Ops:
  0.6 0.1 collective-permute-start.1
  0.7 0.0 copy-start
  0.7 0.5 %collective-permute-start = (bf16[112,2048]{1,0:T(8,128)(2,1)}, bf16[112,2048]{1,0:T(8,128)(2,1)S(1)}, u32[]{:S(2)}, u32[]{:S(2)}) collective-permute-start(bf16[112,2048]{1,0:T(8,128)(2,1)} %bitcast.16), channel_id=1, source_target_pairs={{0,1},{1,0},{2,3},{3,2},{4,5},{5,4},{6,7},{7,6},{8,9},{9,8},{10,11... | collective-permute-start | bytes 1376264 | tf_op jit(solution)/shard_map/ppermute | solution.py:740
  1.2 0.0 copy-start.1
  1.2 0.1 collective-permute-start.3
  1.3 0.1 copy-done
  1.4 0.5 %copy-done.1 = f32[64]{0:T(128)S(1)} copy-done((f32[64]{0:T(128)S(1)}, f32[64]{0:T(128)}, u32[]{:S(2)}) %copy-start.1) | copy-done | bytes 280
  1.9 0.1 collective-permute-start.2
  2.0 2.1 %pack_states.1 = (bf16[1,496,128]{2,1,0:T(8,128)(2,1)S(1)}, bf16[1,496,128]{2,1,0:T(8,128)(2,1)S(1)}, bf16[1,496,128]{2,1,0:T(8,128)(2,1)S(1)}, bf16[1,496,128]{...) custom-call(bf16[56,64,128]{2,1,0:T(8,128)(2,1)} %bitcast.12, ...), custom_call_target="tpu_custom_call" | custom-call | bytes 2000000 | tf_op jit(solution)/shard_map/pack_states/pallas_call | solution.py:158
  4.1 0.0 collective-permute-done.2.refs_9_.small_other
  4.1 0.0 collective-permute-done.3.group_other
  4.1 0.0 collective-permute-done.refs_7_.other
  4.2 0.0 collective-permute-done.1.refs_8_.group_weight_other
  4.2 0.7 %pack_windows.1 = (bf16[1,496,128]{2,1,0:T(8,128)(2,1)S(1)}, bf16[1,496,128]{2,1,0:T(8,128)(2,1)S(1)}, bf16[1,496,128]{2,1,0:T(8,128)(2,1)S(1)}, bf16[1,496,128]...) custom-call(s32[1,56]{1,0:T(1,128)S(1)} %get-tuple-element.40.indice, ...), custom_call_target="tpu_custom_call", output_to_operand_aliasing={{0}: (4, {}), {1}: (5, {}), {2}: (6, {}), {3}: (7, {}), {4}... | custom-call | bytes 500000 | tf_op jit(solution)/shard_map/pack_windows/pallas_call | solution.py:183
  4.9 0.6 %collective-permute-start.4 = (bf16[1,496,128]{2,1,0:T(8,128)(2,1)S(1)}, bf16[1,496,128]{2,1,0:T(8,128)(2,1)S(1)}, u32[]{:S(2)}, u32[]{:S(2)}) collective-permute-start(bf16[1,496,128]{2,1,0:T(8,128)(2,1)S(1)} %get-tuple-element.50), channel_id=1, source_target_pairs={{0,2},{2,0},{4,6},{6,4},{8,10},{10,8},{12,14},{14,12},{1,3},{3,1},... | collective-permute-start | bytes 380936 | tf_op jit(solution)/shard_map/ppermute | solution.py:748
  5.5 1.6 %collective-permute-start.5 = (bf16[1,496,128]{2,1,0:T(8,128)(2,1)S(1)}, bf16[1,496,128]{2,1,0:T(8,128)(2,1)S(1)}, u32[]{:S(2)}, u32[]{:S(2)}) collective-permute-start(bf16[1,496,128]{2,1,0:T(8,128)(2,1)S(1)} %get-tuple-element.51), channel_id=1, source_target_pairs={{0,4},{2,6},{4,0},{6,2},{8,12},{10,14},{12,8},{14,10},{1,5},{3,7},... | collective-permute-start | bytes 380936 | tf_op jit(solution)/shard_map/ppermute | solution.py:748
  7.1 0.3 collective-permute-start.6
  7.5 3.5 %collective-permute-start.7 = (bf16[1,496,128]{2,1,0:T(8,128)(2,1)S(1)}, bf16[1,496,128]{2,1,0:T(8,128)(2,1)S(1)}, u32[]{:S(2)}, u32[]{:S(2)}) collective-permute-start(bf16[1,496,128]{2,1,0:T(8,128)(2,1)S(1)} %get-tuple-element.65), channel_id=1, source_target_pairs={{0,10},{2,8},{4,14},{6,12},{8,2},{10,0},{12,6},{14,4},{1,11},{3,9}... | collective-permute-start | bytes 380936 | tf_op jit(solution)/shard_map/ppermute | solution.py:748
  11.0 0.4 %collective-permute-start.8 = (bf16[1,496,128]{2,1,0:T(8,128)(2,1)S(1)}, bf16[1,496,128]{2,1,0:T(8,128)(2,1)S(1)}, u32[]{:S(2)}, u32[]{:S(2)}) collective-permute-start(bf16[1,496,128]{2,1,0:T(8,128)(2,1)S(1)} %get-tuple-element.66), channel_id=1, source_target_pairs={{0,6},{2,4},{4,2},{6,0},{8,14},{10,12},{12,10},{14,8},{1,7},{3,5},... | collective-permute-start | bytes 380936 | tf_op jit(solution)/shard_map/ppermute | solution.py:748
  11.4 0.0 collective-permute-done.4.refs_0_
  11.4 0.5 %collective-permute-start.9 = (bf16[1,496,128]{2,1,0:T(8,128)(2,1)S(1)}, bf16[1,496,128]{2,1,0:T(8,128)(2,1)S(1)}, u32[]{:S(2)}, u32[]{:S(2)}) collective-permute-start(bf16[1,496,128]{2,1,0:T(8,128)(2,1)S(1)} %get-tuple-element.70), channel_id=1, source_target_pairs={{0,12},{2,14},{4,8},{6,10},{8,4},{10,6},{12,0},{14,2},{1,13},{3,15... | collective-permute-start | bytes 380936 | tf_op jit(solution)/shard_map/ppermute | solution.py:748
  11.8 0.4 %collective-permute-done.5.refs_1_ = bf16[1,496,128]{2,1,0:T(8,128)(2,1)S(1)} collective-permute-done((bf16[1,496,128]{2,1,0:T(8,128)(2,1)S(1)}, bf16[1,496,128]{2,1,0:T(8,128)(2,1)S(1)}, u32[]{:S(2)}, u32[]{:S(2)}) %collective-permute-start.5) | collective-permute-done | bytes 127008 | tf_op jit(solution)/shard_map/ppermute | solution.py:748
  12.3 2.0 %collective-permute-start.10 = (bf16[1,496,128]{2,1,0:T(8,128)(2,1)S(1)}, bf16[1,496,128]{2,1,0:T(8,128)(2,1)S(1)}, u32[]{:S(2)}, u32[]{:S(2)}) collective-permute-start(bf16[1,496,128]{2,1,0:T(8,128)(2,1)S(1)} %get-tuple-element.71), channel_id=1, source_target_pairs={{0,14},{2,12},{4,10},{6,8},{8,6},{10,4},{12,2},{14,0},{1,15},{3,13... | collective-permute-start | bytes 380936 | tf_op jit(solution)/shard_map/ppermute | solution.py:748
  16.9 5.6 %advance_staying.1 = (s32[1,128]{1,0:T(1,128)S(1)}, f32[112,128]{1,0:T(8,128)S(1)}, f32[16,128]{1,0:T(8,128)S(1)}, f32[56,256]{1,0:T(8,128)S(1)}, bf16[2,56,128]...) custom-call(f32[1]{0:T(128)S(6)} %copy.40.decay_log, ...), custom_call_target="tpu_custom_call" | custom-call | flops 300000000 | bytes 6000000 | tf_op jit(solution)/shard_map/advance_staying/pallas_call | solution.py:488
  22.5 0.0 collective-permute-done.6.refs_2_
  22.6 0.0 collective-permute-done.7.refs_3_
  22.6 0.0 collective-permute-done.8.refs_4_
  22.6 2.2 %advance_arrived.1 = (f32[112,128]{1,0:T(8,128)S(1)}, f32[56,256]{1,0:T(8,128)S(1)}, bf16[56,64,128]{2,1,0:T(8,128)(2,1)}) custom-call(s32[1,128]{1,0:T(1,128)S(1)} %get-tuple-element.52.plan_near, f32[16,128]{1,0:T(8,128)S(1)} %get-tuple-element.53.weights, f32[112,128]{1,0:T(8,128)S(1)} %get-tuple-element.54.inner_moved, ...), custom_call_target="tpu_custom_call", output_to_operand_aliasing={{2}: (11, {})} | custom-call | flops 10000000 | bytes 2000000 | tf_op jit(solution)/shard_map/advance_arrived/pallas_call | solution.py:714
  24.8 4.8 %collective-permute-done.9.refs_0_ = bf16[1,496,128]{2,1,0:T(8,128)(2,1)S(1)} collective-permute-done((bf16[1,496,128]{2,1,0:T(8,128)(2,1)S(1)}, bf16[1,496,128]{2,1,0:T(8,128)(2,1)S(1)}, u32[]{:S(2)}, u32[]{:S(2)}) %collective-permute-start.9) | collective-permute-done | bytes 127008 | tf_op jit(solution)/shard_map/ppermute | solution.py:748
  29.6 2.5 %collective-permute-done.10.refs_1_ = bf16[1,496,128]{2,1,0:T(8,128)(2,1)S(1)} collective-permute-done((bf16[1,496,128]{2,1,0:T(8,128)(2,1)S(1)}, bf16[1,496,128]{2,1,0:T(8,128)(2,1)S(1)}, u32[]{:S(2)}, u32[]{:S(2)}) %collective-permute-start.10) | collective-permute-done | bytes 127008 | tf_op jit(solution)/shard_map/ppermute | solution.py:748
  32.1 2.2 %advance_last.1 = (bf16[2,56,128]{2,1,0:T(8,128)(2,1)}, bf16[3,56,128]{2,1,0:T(8,128)(2,1)}, bf16[3,56,64]{2,1,0:T(8,128)(2,1)}, bf16[56,64,128]{2,1,0:T(8,128)(2,1)}) custom-call(s32[1,128]{1,0:T(1,128)S(1)} %get-tuple-element.52.plan_near, f32[16,128]{1,0:T(8,128)S(1)} %get-tuple-element.53.weights, ...), custom_call_target="tpu_custom_call", output_to_operand_aliasing={{3}: (11, {})} | custom-call | flops 10000000 | bytes 2000000 | tf_op jit(solution)/shard_map/advance_last/pallas_call | solution.py:714
  (1 shorter events, 0.0 us)
Async XLA Ops:
  0.6 3.5 %collective-permute-start.1 = (bf16[64,4096]{1,0:T(8,128)(2,1)}, bf16[64,4096]{1,0:T(8,128)(2,1)S(1)}, u32[]{:S(2)}, u32[]{:S(2)}) collective-permute-start(bf16[64,4096]{1,0:T(8,128)(2,1)} %bitcast.14), channel_id=1, source_target_pairs={{0,1},{1,0},{2,3},{3,2},{4,5},{5,4},{6,7},{7,6},{8,9},{9,8},{10,11... | collective-permute-start | bytes 1572872 | tf_op jit(solution)/shard_map/ppermute | solution.py:740
  0.7 0.7 %copy-start = (f32[4,64]{1,0:T(4,128)S(1)}, f32[4,64]{1,0:T(4,128)}, u32[]{:S(2)}) copy-start(f32[4,64]{1,0:T(4,128)} %param.25) | copy-start | bytes 3076
  0.7 3.4 %collective-permute-start = (bf16[112,2048]{1,0:T(8,128)(2,1)}, bf16[112,2048]{1,0:T(8,128)(2,1)S(1)}, u32[]{:S(2)}, u32[]{:S(2)}) collective-permute-start(bf16[112,2048]{1,0:T(8,128)(2,1)} %bitcast.16), channel_id=1, source_target_pairs={{0,1},{1,0},{2,3},{3,2},{4,5},{5,4},{6,7},{7,6},{8,9},{9,8},{10,11... | collective-permute-start | bytes 1376264 | tf_op jit(solution)/shard_map/ppermute | solution.py:740
  1.2 0.7 %copy-start.1 = (f32[64]{0:T(128)S(1)}, f32[64]{0:T(128)}, u32[]{:S(2)}) copy-start(f32[64]{0:T(128)} %param.26) | copy-start | bytes 772
  1.2 2.9 %collective-permute-start.3 = (bf16[3,56,64]{2,1,0:T(8,128)(2,1)}, bf16[3,56,64]{2,1,0:T(8,128)(2,1)S(1)}, u32[]{:S(2)}, u32[]{:S(2)}) collective-permute-start(bf16[3,56,64]{2,1,0:T(8,128)(2,1)} %bitcast.20), channel_id=1, source_target_pairs={{0,1},{1,0},{2,3},{3,2},{4,5},{5,4},{6,7},{7,6},{8,9},{9,8},{10,11... | collective-permute-start | bytes 64520 | tf_op jit(solution)/shard_map/ppermute | solution.py:740
  1.9 2.3 %collective-permute-start.2 = (f32[5,64]{1,0:T(8,128)S(1)}, f32[5,64]{1,0:T(8,128)S(1)}, u32[]{:S(2)}, u32[]{:S(2)}) collective-permute-start(f32[5,64]{1,0:T(8,128)S(1)} %pad_maximum_fusion.small), channel_id=1, source_target_pairs={{0,1},{1,0},{2,3},{3,2},{4,5},{5,4},{6,7},{7,6},{8,9},{9,8},{10,11... | collective-permute-start | bytes 3848 | tf_op jit(solution)/shard_map/ppermute | solution.py:740
  4.9 6.5 %collective-permute-start.4 = (bf16[1,496,128]{2,1,0:T(8,128)(2,1)S(1)}, bf16[1,496,128]{2,1,0:T(8,128)(2,1)S(1)}, u32[]{:S(2)}, u32[]{:S(2)}) collective-permute-start(bf16[1,496,128]{2,1,0:T(8,128)(2,1)S(1)} %get-tuple-element.50), channel_id=1, source_target_pairs={{0,2},{2,0},{4,6},{6,4},{8,10},{10,8},{12,14},{14,12},{1,3},{3,1},... | collective-permute-start | bytes 380936 | tf_op jit(solution)/shard_map/ppermute | solution.py:748
  5.5 6.8 %collective-permute-start.5 = (bf16[1,496,128]{2,1,0:T(8,128)(2,1)S(1)}, bf16[1,496,128]{2,1,0:T(8,128)(2,1)S(1)}, u32[]{:S(2)}, u32[]{:S(2)}) collective-permute-start(bf16[1,496,128]{2,1,0:T(8,128)(2,1)S(1)} %get-tuple-element.51), channel_id=1, source_target_pairs={{0,4},{2,6},{4,0},{6,2},{8,12},{10,14},{12,8},{14,10},{1,5},{3,7},... | collective-permute-start | bytes 380936 | tf_op jit(solution)/shard_map/ppermute | solution.py:748
  7.1 15.4 %collective-permute-start.6 = (bf16[1,496,128]{2,1,0:T(8,128)(2,1)S(1)}, bf16[1,496,128]{2,1,0:T(8,128)(2,1)S(1)}, u32[]{:S(2)}, u32[]{:S(2)}) collective-permute-start(bf16[1,496,128]{2,1,0:T(8,128)(2,1)S(1)} %get-tuple-element.64), channel_id=1, source_target_pairs={{0,8},{2,10},{4,12},{6,14},{8,0},{10,2},{12,4},{14,6},{1,9},{3,11}... | collective-permute-start | bytes 380936 | tf_op jit(solution)/shard_map/ppermute | solution.py:748
  7.5 15.1 %collective-permute-start.7 = (bf16[1,496,128]{2,1,0:T(8,128)(2,1)S(1)}, bf16[1,496,128]{2,1,0:T(8,128)(2,1)S(1)}, u32[]{:S(2)}, u32[]{:S(2)}) collective-permute-start(bf16[1,496,128]{2,1,0:T(8,128)(2,1)S(1)} %get-tuple-element.65), channel_id=1, source_target_pairs={{0,10},{2,8},{4,14},{6,12},{8,2},{10,0},{12,6},{14,4},{1,11},{3,9}... | collective-permute-start | bytes 380936 | tf_op jit(solution)/shard_map/ppermute | solution.py:748
  11.0 11.6 %collective-permute-start.8 = (bf16[1,496,128]{2,1,0:T(8,128)(2,1)S(1)}, bf16[1,496,128]{2,1,0:T(8,128)(2,1)S(1)}, u32[]{:S(2)}, u32[]{:S(2)}) collective-permute-start(bf16[1,496,128]{2,1,0:T(8,128)(2,1)S(1)} %get-tuple-element.66), channel_id=1, source_target_pairs={{0,6},{2,4},{4,2},{6,0},{8,14},{10,12},{12,10},{14,8},{1,7},{3,5},... | collective-permute-start | bytes 380936 | tf_op jit(solution)/shard_map/ppermute | solution.py:748
  11.4 18.2 %collective-permute-start.9 = (bf16[1,496,128]{2,1,0:T(8,128)(2,1)S(1)}, bf16[1,496,128]{2,1,0:T(8,128)(2,1)S(1)}, u32[]{:S(2)}, u32[]{:S(2)}) collective-permute-start(bf16[1,496,128]{2,1,0:T(8,128)(2,1)S(1)} %get-tuple-element.70), channel_id=1, source_target_pairs={{0,12},{2,14},{4,8},{6,10},{8,4},{10,6},{12,0},{14,2},{1,13},{3,15... | collective-permute-start | bytes 380936 | tf_op jit(solution)/shard_map/ppermute | solution.py:748
  12.3 19.8 %collective-permute-start.10 = (bf16[1,496,128]{2,1,0:T(8,128)(2,1)S(1)}, bf16[1,496,128]{2,1,0:T(8,128)(2,1)S(1)}, u32[]{:S(2)}, u32[]{:S(2)}) collective-permute-start(bf16[1,496,128]{2,1,0:T(8,128)(2,1)S(1)} %get-tuple-element.71), channel_id=1, source_target_pairs={{0,14},{2,12},{4,10},{6,8},{8,6},{10,4},{12,2},{14,0},{1,15},{3,13... | collective-permute-start | bytes 380936 | tf_op jit(solution)/shard_map/ppermute | solution.py:748

commit v6 on v5

--- a/solution.py
+++ b/solution.py
@@ -12,8 +12,7 @@
 SMALL_LIMIT = 8 * 1024 * 1024
 MEDIUM_LIMIT = 16 * 1024 * 1024
 LARGE_LIMIT = 48 * 1024 * 1024
-MAX_ROUNDS = 16
-EARLIER = 2
+MAX_HALVES = 16
 LAST = 2
 LANES = 128
 ROWS = 8
@@ -44,16 +43,31 @@
     return value.astype(BF16).astype(F32)
 
 
-def rounds_of(replicas):
-    if replicas > MAX_ROUNDS or replicas & (replicas - 1):
+def masks_of(replicas):
+    if replicas > MAX_HALVES or replicas & (replicas - 1) or replicas < 4:
         return []
-    light = list(range(1, replicas // 2))
-    heavy = list(range(replicas // 2, replicas))
-    return light[:2] + heavy[:2] + light[2:] + heavy[2:]
-
-
-def partner(replicas, mask):
-    return jnp.bitwise_xor(lax.axis_index("dp"), mask)
+    return list(range(replicas // 2, replicas))
+
+
+def peers_of(replicas):
+    masks = masks_of(replicas)
+    if not masks:
+        return [list(range(replicas))]
+    me = lax.axis_index("dp")
+    half = replicas // 2
+    first = me // half * half
+    return [[first + place for place in range(half)]] + [
+        [jnp.bitwise_xor(me, mask)] for mask in masks
+    ]
+
+
+def block_counts(replicas):
+    masks = masks_of(replicas)
+    return [replicas // 2] + [1] * len(masks) if masks else [replicas]
+
+
+def blocks_of(refs):
+    return [ref.at[place] for ref in refs for place in range(ref.shape[0])]
 
 
 def both_halves(mine, theirs):
@@ -63,11 +77,12 @@
     )
 
 
-def destinations(replicas, outs):
-    rounds = rounds_of(replicas)
-    if rounds:
-        return [(ref.at[0], partner(replicas, mask)) for ref, mask in zip(outs, rounds)]
-    return [(outs[0].at[target], target) for target in range(replicas)]
+def pack_plan(replicas, cap, refs, indices):
+    plan = []
+    for block, (ref, peer) in enumerate(zip(blocks_of(refs), sum(peers_of(replicas), []))):
+        for c in range(cap):
+            plan.append((block, ref, c, indices[0, peer * cap + c]))
+    return plan
 
 
 def states_kernel(replicas, cap, scan, send, inner, group, *refs):
@@ -80,14 +95,10 @@
     load_group = pltpu.make_async_copy(group, group_out, group_sem)
     load_group.start()
     state_rows = scan.shape[1]
-    blocks = destinations(replicas, outs)
     load_list.wait()
     save = pltpu.make_async_copy(indices, indices_out, save_sem)
     save.start()
-    plan = []
-    for block, (ref, target) in enumerate(blocks):
-        for c in range(cap):
-            plan.append((block, ref, c, indices[0, target * cap + c]))
+    plan = pack_plan(replicas, cap, outs, indices)
 
     def each(act):
         for place, (_, ref, c, index) in enumerate(plan):
@@ -119,12 +130,22 @@
     each(lambda copy: copy.wait())
 
 
-def windows_kernel(replicas, cap, state_rows, indices_in, group, group_other, picked_in, *refs):
-    count = max(1, len(rounds_of(replicas)))
-    outs = refs[-4 - count : -4]
-    indices, table, picked, sem = refs[-4:]
+def windows_kernel(replicas, cap, indices_in, group, group_other, picked_in, near_in, *refs):
+    count = len(block_counts(replicas))
+    outs = refs[-5 - count : -5]
+    indices, table, picked, sem, near_sem = refs[-5:]
     load = pltpu.make_async_copy(indices_in, indices, sem)
     load.start()
+    copies = [
+        pltpu.make_async_copy(
+            near_in.at[place],
+            outs[0].at[place, pl.ds(0, near_in.shape[1])],
+            near_sem.at[place],
+        )
+        for place in range(near_in.shape[0])
+    ]
+    for copy in copies:
+        copy.start()
     taps = group.shape[0]
     for tap in range(taps):
         table[:, tap * LANES : (tap + 1) * LANES] = both_halves(
@@ -132,32 +153,33 @@
         )
     picked[...] = jnp.zeros_like(picked)
     load.wait()
-    for block, (ref, target) in enumerate(destinations(replicas, outs)):
-        for c in range(cap):
-            index = jnp.maximum(indices[0, target * cap + c], 0)
-            row = table[pl.ds(index, 1), :]
-            for tap in range(taps):
-                picked[block, tap * ROWS + c : tap * ROWS + c + 1, :] = row[
-                    :, tap * LANES : (tap + 1) * LANES
-                ]
-        ref[cap * state_rows :, :] = jnp.concatenate(
-            [picked_in[block], picked[block]], axis=0
-        ).astype(BF16)
+    for block, ref, c, index in pack_plan(replicas, cap, outs, indices):
+        row = table[pl.ds(jnp.maximum(index, 0), 1), :]
+        for tap in range(taps):
+            picked[block, tap * ROWS + c : tap * ROWS + c + 1, :] = row[
+                :, tap * LANES : (tap + 1) * LANES
+            ]
+        if c == cap - 1:
+            ref[near_in.shape[1] :, :] = jnp.concatenate(
+                [picked_in[block], picked[block]], axis=0
+            ).astype(BF16)
+    for copy in copies:
+        copy.wait()
 
 
 def pack(replicas, cap, send_list, scan, inner, group, group_other, swapped):
-    rounds = rounds_of(replicas)
-    count = max(1, len(rounds))
-    per_block = 1 if rounds else replicas
+    counts = block_counts(replicas)
+    count, blocks = len(counts), sum(counts)
     taps, slots, _ = inner.shape
-    rows = cap * scan.shape[1] + 2 * taps * ROWS
-    blocks = count * per_block
-    shapes = [pltpu.VMEM((per_block, rows, LANES), BF16)] * count
+    state_rows = cap * scan.shape[1]
+    rows = state_rows + 2 * taps * ROWS
+    shapes = [pltpu.VMEM((number, rows, LANES), BF16) for number in counts]
     half = (blocks, taps * ROWS, LANES)
-    limit = SMALL_LIMIT if rounds else MEDIUM_LIMIT
-    *states, picked, group_near, indices = pl.pallas_call(
+    limit = SMALL_LIMIT if masks_of(replicas) else MEDIUM_LIMIT
+    near, *states, picked, group_near, indices = pl.pallas_call(
         functools.partial(states_kernel, replicas, cap),
-        out_shape=shapes
+        out_shape=[pltpu.VMEM((counts[0], state_rows, LANES), BF16)]
+        + shapes[1:]
         + [
             pltpu.VMEM(half, F32),
             pltpu.VMEM(group.shape, BF16),
@@ -179,30 +201,24 @@
         cost_estimate=pl.CostEstimate(flops=0, bytes_accessed=2_000_000, transcendentals=0),
         name="pack_states",
     )(in_hbm(scan), in_hbm(send_list), in_hbm(inner), in_hbm(group))
-    near = [in_vmem(value) for value in states]
+    states = [in_vmem(value) for value in states]
     return pl.pallas_call(
-        functools.partial(windows_kernel, replicas, cap, scan.shape[1]),
+        functools.partial(windows_kernel, replicas, cap),
         out_shape=shapes,
-        in_specs=[VMEM] * (4 + count) + [HBM] * len(swapped),
+        in_specs=[VMEM] * (5 + len(states)) + [HBM] * len(swapped),
         out_specs=[VMEM] * count,
         scratch_shapes=[
             pltpu.SMEM(send_list.shape, jnp.int32),
             pltpu.VMEM((slots, taps * LANES), F32),
             pltpu.VMEM(half, F32),
             pltpu.SemaphoreType.DMA,
+            pltpu.SemaphoreType.DMA((counts[0],)),
         ],
-        input_output_aliases={4 + place: place for place in range(count)},
+        input_output_aliases={5 + place: 1 + place for place in range(len(states))},
         compiler_params=pltpu.CompilerParams(vmem_limit_bytes=limit),
         cost_estimate=pl.CostEstimate(flops=0, bytes_accessed=500_000, transcendentals=0),
         name="pack_windows",
-    )(indices, group_near, group_other, picked, *near, *swapped)
-
-
-def sources_of(replicas):
-    rounds = rounds_of(replicas)
-    if rounds:
-        return [partner(replicas, mask) for mask in rounds]
-    return list(range(replicas))
+    )(indices, group_near, group_other, picked, near, *states, *swapped)
 
 
 def make_plan(replicas, cap, receive, slots, plan, inverse):
@@ -216,7 +232,7 @@
         plan[0, jnp.where(stays, kept, moving)] = slot
         inverse[jnp.where(stays, replicas * cap, entry)] = slot
         kept = kept + jnp.where(stays, 1, 0)
-    for block, source in enumerate(sources_of(replicas)):
+    for block, source in enumerate(sum(peers_of(replicas), [])):
         for c in range(cap):
             plan[0, moving + block * cap + c] = inverse[source * cap + c]
 
@@ -467,14 +483,14 @@
     save_plan.wait()
 
 
-def stay(replicas, cap, scalars, arrays, near, earlier):
+def stay(replicas, cap, scalars, arrays, near):
     receive, own, group_weight, delta_weight = arrays[0], arrays[1], arrays[4], arrays[5]
     inner, scan = arrays[-3], arrays[-1]
     taps, slots, _ = inner.shape
     rows = own.shape[0]
     steps = rows // slots
     moving = slots // 2
-    blocks = len(sources_of(replicas))
+    blocks = sum(block_counts(replicas))
     moved_rows = blocks * ROWS
     width, features = group_weight.shape
     full = pltpu.VMEM((rows, LANES), F32)
@@ -497,10 +513,7 @@
         ]
         + [moved] * 5
         + [jax.ShapeDtypeStruct(scan.shape, BF16)],
-        in_specs=[SMEM] * len(scalars)
-        + [HBM] * len(far)
-        + [VMEM] * len(near)
-        + [HBM] * len(earlier),
+        in_specs=[SMEM] * len(scalars) + [HBM] * len(far) + [VMEM] * len(near),
         out_specs=[VMEM] * 11 + [HBM],
         scratch_shapes=[
             pltpu.SMEM(plan_shape, jnp.int32),
@@ -524,7 +537,7 @@
             flops=300_000_000, bytes_accessed=6_000_000, transcendentals=100_000
         ),
         name="advance_staying",
-    )(*scalars, *far, *near, *earlier)
+    )(*scalars, *far, *near)
 
 
 def arrive_kernel(
@@ -563,10 +576,7 @@
     head = lax.axis_index("head")
     load = pltpu.make_async_copy(plan_near, plan, sem.at[0])
     load.start()
-    if rounds_of(replicas):
-        blocks = [ref.at[0] for ref in arrived]
-    else:
-        blocks = [arrived[0].at[source] for source in range(replicas)]
+    blocks = blocks_of(arrived)
     stored = inner_moved.shape[0] // steps
     moved_rows = len(blocks) * ROWS
     if last:
@@ -691,7 +701,7 @@
 def arrive(replicas, cap, first, last, operands, scan_next, arrived):
     inner_moved, gated, table, inner_part, group_part = operands[2], *operands[7:]
     steps, slots, width = group_part.shape
-    blocks = len(arrived) if rounds_of(replicas) else replicas
+    blocks = sum(value.shape[0] for value in arrived)
     moved = (steps * blocks * ROWS, LANES)
     carried = [pltpu.VMEM(value.shape, F32) for value in (gated, table)]
     scan_shape = jax.ShapeDtypeStruct(scan_next.shape, BF16)
@@ -727,7 +737,7 @@
         ],
         input_output_aliases={len(operands): len(outs) - 1},
         compiler_params=pltpu.CompilerParams(
-            vmem_limit_bytes=SMALL_LIMIT if rounds_of(replicas) else LARGE_LIMIT
+            vmem_limit_bytes=SMALL_LIMIT if masks_of(replicas) else LARGE_LIMIT
         ),
         cost_estimate=pl.CostEstimate(
             flops=10_000_000, bytes_accessed=2_000_000, transcendentals=0
@@ -740,14 +750,18 @@
     return lax.ppermute(value, "head", [(0, 1), (1, 0)])
 
 
-def exchange(replicas, blocks):
-    rounds = rounds_of(replicas)
-    if not rounds:
-        return [lax.all_to_all(blocks[0], "dp", 0, 0, tiled=True)]
-    return [
-        lax.ppermute(block, "dp", [(source, source ^ mask) for source in range(replicas)])
-        for mask, block in zip(rounds, blocks)
+def exchange(replicas, arrays):
+    masks = masks_of(replicas)
+    if not masks:
+        return [lax.all_to_all(arrays[0], "dp", 0, 0, tiled=True)]
+    moved = [
+        lax.ppermute(array, "dp", [(source, source ^ mask) for source in range(replicas)])
+        for mask, array in zip(masks, arrays[1:])
     ]
+    half = replicas // 2
+    halves = [list(range(half)), list(range(half, replicas))]
+    within = lax.all_to_all(arrays[0], "dp", 0, 0, axis_index_groups=halves, tiled=True)
+    return [within] + moved
 
 
 def per_device(
@@ -803,17 +817,17 @@
             scan,
         ),
         (swapped[0], swapped[1], small, swapped[2], group_other),
-        arrived[:EARLIER] if rounds_of(replicas) else [],
-    )
-    first = max(0, len(arrived) - LAST)
-    if first:
+    )
+    split = max(0, len(arrived) - LAST)
+    first = sum(value.shape[0] for value in arrived[:split])
+    if split:
         operands = (plan, weights, *moved, gated, table, inner_part, group_part)
         gated, table, scan_next = arrive(
-            replicas, cap, 0, False, operands, scan_next, arrived[:first]
+            replicas, cap, 0, False, operands, scan_next, arrived[:split]
         )
     operands = (plan, weights, *moved, gated, table, inner_part, group_part)
     gated, inner_next, group_next, scan_next = arrive(
-        replicas, cap, first, True, operands, scan_next, arrived[first:]
+        replicas, cap, first, True, operands, scan_next, arrived[split:]
     )
     return (
         gated,

time: 34.6 us -> 38.6 us (1.12)
  the two profiles are of different devices: /device:TPU:18 before, /device:TPU:20 now
where the time goes in v6:
time: 38.6 us; the launch traced here: 38.2 us
  Pallas kernels  14 us (36%)
  starting transfers between devices  10.4 us (27%)
  waiting for transfers between devices  9.86 us (26%)
  between operations  3.32 us (9%)
  local copies, waits for them, and re-layouts  0.57 us (1%)
    ppermute x4, waiting for transfers between devices, exchange(): lax.ppermute(array, 'dp', [(source, source ^ mask) for source in range(re...  9.85 us
    ppermute x4, starting transfers between devices, exchange(): lax.ppermute(array, 'dp', [(source, source ^ mask) for source in range(re...  5.85 us
    pallas_call x1, Pallas kernels, stay(): pl.pallas_call(functools.partial(stay_kernel, replicas, cap), out_shape=[...  5.64 us
    pallas_call x2, Pallas kernels, arrive(): pl.pallas_call(functools.partial(arrive_kernel, replicas, cap, first, las...  4.4 us
    all_to_all x1, starting transfers between devices, exchange(): lax.all_to_all(arrays[0], 'dp', 0, 0, axis_index_groups=halves, tiled=True)  3.81 us
    pallas_call x1, Pallas kernels, pack(): pl.pallas_call(functools.partial(states_kernel, replicas, cap), out_shape...  2.23 us
    pallas_call x1, Pallas kernels, pack(): pl.pallas_call(functools.partial(windows_kernel, replicas, cap), out_shap...  1.74 us
    ppermute x4, starting transfers between devices, swap_heads(): return lax.ppermute(value, 'head', [(0, 1), (1, 0)])  0.78 us
  transfers between devices with their start and end apart: 9, of which 3 were waited for; matrix products, arithmetic and copies ran while one was open for 0% of the time, Pallas kernels for 27%

profile of v6, /device:TPU:20, one launch (start us, length us, event | category | flops | bytes accessed | tf_op | source)
XLA Modules:
  0.0 38.2 jit_solution(10773327007267339065)
XLA Ops:
  0.6 0.1 collective-permute-start.1
  0.7 0.0 copy-start
  0.7 0.5 %collective-permute-start = (bf16[112,2048]{1,0:T(8,128)(2,1)}, bf16[112,2048]{1,0:T(8,128)(2,1)S(1)}, u32[]{:S(2)}, u32[]{:S(2)}) collective-permute-start(bf16[112,2048]{1,0:T(8,128)(2,1)} %bitcast.16), channel_id=1, source_target_pairs={{0,1},{1,0},{2,3},{3,2},{4,5},{5,4},{6,7},{7,6},{8,9},{9,8},{10,11... | collective-permute-start | bytes 1376264 | tf_op jit(solution)/shard_map/ppermute | solution.py:750
  1.2 0.0 copy-start.1
  1.2 0.1 collective-permute-start.3
  1.3 0.1 copy-done
  1.4 0.5 %copy-done.1 = f32[64]{0:T(128)S(1)} copy-done((f32[64]{0:T(128)S(1)}, f32[64]{0:T(128)}, u32[]{:S(2)}) %copy-start.1) | copy-done | bytes 280
  1.9 0.1 collective-permute-start.2
  2.0 2.2 %pack_states.1 = (bf16[4,448,128]{2,1,0:T(8,128)(2,1)S(1)}, bf16[1,496,128]{2,1,0:T(8,128)(2,1)S(1)}, bf16[1,496,128]{2,1,0:T(8,128)(2,1)S(1)}, bf16[1,496,128]{...) custom-call(bf16[56,64,128]{2,1,0:T(8,128)(2,1)} %bitcast.12, ...), custom_call_target="tpu_custom_call" | custom-call | bytes 2000000 | tf_op jit(solution)/shard_map/pack_states/pallas_call | solution.py:179
  4.2 0.0 collective-permute-done.2.small_other.refs_6_
  4.3 0.0 collective-permute-done.3.group_other
  4.3 0.0 collective-permute-done.other.refs_4_
  4.3 0.0 collective-permute-done.1.group_weight_other.refs_5_
  4.3 1.7 %pack_windows.1 = (bf16[4,496,128]{2,1,0:T(8,128)(2,1)}, bf16[1,496,128]{2,1,0:T(8,128)(2,1)S(1)}, bf16[1,496,128]{2,1,0:T(8,128)(2,1)S(1)}, bf16[1,496,128]{2,1,0:T(8,128)(2,1)S(1)}, bf16[1,496,128]{2,1,0:T(8,128)(2,1)S(1)}) custom-call(s32[1,56]{1,0:T(1,128)S(1)} %get-tuple-element.48.indice, ...), custom_call_target="tpu_custom_call", output_to_operand_aliasing={{1}: (5, {}), {2}: (6, {}), {3}: (7, {}), {4}: (8, {})} | custom-call | bytes 500000 | tf_op jit(solution)/shard_map/pack_windows/pallas_call | solution.py:205
  6.0 3.8 %all-to-all-start = ((bf16[4,496,128]{2,1,0:T(8,128)(2,1)}), bf16[4,496,128]{2,1,0:T(8,128)(2,1)S(1)}, u32[]{:S(2)}, u32[]{:S(2)}) async-start(bf16[4,496,128]{2,1,0:T(8,128)(2,1)} %get-tuple-element.56), calls=%async_computation | async-start | bytes 1015808 | tf_op jit(solution)/shard_map/all_to_all | solution.py:763
  9.8 0.3 collective-permute-start.4
  10.2 4.0 %collective-permute-start.5 = (bf16[1,496,128]{2,1,0:T(8,128)(2,1)S(1)}, bf16[1,496,128]{2,1,0:T(8,128)(2,1)S(1)}, u32[]{:S(2)}, u32[]{:S(2)}) collective-permute-start(bf16[1,496,128]{2,1,0:T(8,128)(2,1)S(1)} %get-tuple-element.58), channel_id=1, source_target_pairs={{0,10},{2,8},{4,14},{6,12},{8,2},{10,0},{12,6},{14,4},{1,11},{3,9}... | collective-permute-start | bytes 380936 | tf_op jit(solution)/shard_map/ppermute | solution.py:758
  14.2 0.3 collective-permute-start.6
  14.6 1.1 %collective-permute-start.7 = (bf16[1,496,128]{2,1,0:T(8,128)(2,1)S(1)}, bf16[1,496,128]{2,1,0:T(8,128)(2,1)S(1)}, u32[]{:S(2)}, u32[]{:S(2)}) collective-permute-start(bf16[1,496,128]{2,1,0:T(8,128)(2,1)S(1)} %get-tuple-element.63), channel_id=1, source_target_pairs={{0,14},{2,12},{4,10},{6,8},{8,6},{10,4},{12,2},{14,0},{1,15},{3,13... | collective-permute-start | bytes 380936 | tf_op jit(solution)/shard_map/ppermute | solution.py:758
  18.3 5.6 %advance_staying.1 = (s32[1,128]{1,0:T(1,128)S(1)}, f32[112,128]{1,0:T(8,128)S(1)}, f32[16,128]{1,0:T(8,128)S(1)}, f32[56,256]{1,0:T(8,128)S(1)}, bf16[2,56,128]...) custom-call(f32[1]{0:T(128)S(6)} %copy.34.decay_log, ...), custom_call_target="tpu_custom_call" | custom-call | flops 300000000 | bytes 6000000 | tf_op jit(solution)/shard_map/advance_staying/pallas_call | solution.py:504
  23.9 0.0 collective-permute-done.4.refs_1_
  23.9 5.0 %collective-permute-done.5.refs_2_ = bf16[1,496,128]{2,1,0:T(8,128)(2,1)S(1)} collective-permute-done((bf16[1,496,128]{2,1,0:T(8,128)(2,1)S(1)}, bf16[1,496,128]{2,1,0:T(8,128)(2,1)S(1)}, u32[]{:S(2)}, u32[]{:S(2)}) %collective-permute-start.5) | collective-permute-done | bytes 127008 | tf_op jit(solution)/shard_map/ppermute | solution.py:758
  29.0 0.0 all-to-all-done.refs_0_
  29.0 2.6 %advance_arrived.1 = (f32[112,128]{1,0:T(8,128)S(1)}, f32[56,256]{1,0:T(8,128)S(1)}, bf16[56,64,128]{2,1,0:T(8,128)(2,1)}) custom-call(s32[1,128]{1,0:T(1,128)S(1)} %get-tuple-element.36.plan_near, f32[16,128]{1,0:T(8,128)S(1)} %get-tuple-element.37.weights, f32[128,128]{1,0:T(8,128)S(1)} %get-tuple-element.38.inner_moved, ...), custom_call_target="tpu_custom_call", output_to_operand_aliasing={{2}: (11, {})} | custom-call | flops 10000000 | bytes 2000000 | tf_op jit(solution)/shard_map/advance_arrived/pallas_call | solution.py:724
  31.6 2.3 %collective-permute-done.6.refs_0_ = bf16[1,496,128]{2,1,0:T(8,128)(2,1)S(1)} collective-permute-done((bf16[1,496,128]{2,1,0:T(8,128)(2,1)S(1)}, bf16[1,496,128]{2,1,0:T(8,128)(2,1)S(1)}, u32[]{:S(2)}, u32[]{:S(2)}) %collective-permute-start.6) | collective-permute-done | bytes 127008 | tf_op jit(solution)/shard_map/ppermute | solution.py:758
  33.9 2.5 %collective-permute-done.7.refs_1_ = bf16[1,496,128]{2,1,0:T(8,128)(2,1)S(1)} collective-permute-done((bf16[1,496,128]{2,1,0:T(8,128)(2,1)S(1)}, bf16[1,496,128]{2,1,0:T(8,128)(2,1)S(1)}, u32[]{:S(2)}, u32[]{:S(2)}) %collective-permute-start.7) | collective-permute-done | bytes 127008 | tf_op jit(solution)/shard_map/ppermute | solution.py:758
  36.4 1.8 %advance_last.1 = (bf16[2,56,128]{2,1,0:T(8,128)(2,1)}, bf16[3,56,128]{2,1,0:T(8,128)(2,1)}, bf16[3,56,64]{2,1,0:T(8,128)(2,1)}, bf16[56,64,128]{2,1,0:T(8,128)(2,1)}) custom-call(s32[1,128]{1,0:T(1,128)S(1)} %get-tuple-element.36.plan_near, f32[16,128]{1,0:T(8,128)S(1)} %get-tuple-element.37.weights, ...), custom_call_target="tpu_custom_call", output_to_operand_aliasing={{3}: (11, {})} | custom-call | flops 10000000 | bytes 2000000 | tf_op jit(solution)/shard_map/advance_last/pallas_call | solution.py:724
  (1 shorter events, 0.0 us)
Async XLA Ops:
  0.6 3.6 %collective-permute-start.1 = (bf16[64,4096]{1,0:T(8,128)(2,1)}, bf16[64,4096]{1,0:T(8,128)(2,1)S(1)}, u32[]{:S(2)}, u32[]{:S(2)}) collective-permute-start(bf16[64,4096]{1,0:T(8,128)(2,1)} %bitcast.14), channel_id=1, source_target_pairs={{0,1},{1,0},{2,3},{3,2},{4,5},{5,4},{6,7},{7,6},{8,9},{9,8},{10,11... | collective-permute-start | bytes 1572872 | tf_op jit(solution)/shard_map/ppermute | solution.py:750
  0.7 0.7 %copy-start = (f32[4,64]{1,0:T(4,128)S(1)}, f32[4,64]{1,0:T(4,128)}, u32[]{:S(2)}) copy-start(f32[4,64]{1,0:T(4,128)} %param.25) | copy-start | bytes 3076
  0.7 3.5 %collective-permute-start = (bf16[112,2048]{1,0:T(8,128)(2,1)}, bf16[112,2048]{1,0:T(8,128)(2,1)S(1)}, u32[]{:S(2)}, u32[]{:S(2)}) collective-permute-start(bf16[112,2048]{1,0:T(8,128)(2,1)} %bitcast.16), channel_id=1, source_target_pairs={{0,1},{1,0},{2,3},{3,2},{4,5},{5,4},{6,7},{7,6},{8,9},{9,8},{10,11... | collective-permute-start | bytes 1376264 | tf_op jit(solution)/shard_map/ppermute | solution.py:750
  1.2 0.7 %copy-start.1 = (f32[64]{0:T(128)S(1)}, f32[64]{0:T(128)}, u32[]{:S(2)}) copy-start(f32[64]{0:T(128)} %param.26) | copy-start | bytes 772
  1.2 3.0 %collective-permute-start.3 = (bf16[3,56,64]{2,1,0:T(8,128)(2,1)}, bf16[3,56,64]{2,1,0:T(8,128)(2,1)S(1)}, u32[]{:S(2)}, u32[]{:S(2)}) collective-permute-start(bf16[3,56,64]{2,1,0:T(8,128)(2,1)} %bitcast.20), channel_id=1, source_target_pairs={{0,1},{1,0},{2,3},{3,2},{4,5},{5,4},{6,7},{7,6},{8,9},{9,8},{10,11... | collective-permute-start | bytes 64520 | tf_op jit(solution)/shard_map/ppermute | solution.py:750
  1.9 2.4 %collective-permute-start.2 = (f32[5,64]{1,0:T(8,128)S(1)}, f32[5,64]{1,0:T(8,128)S(1)}, u32[]{:S(2)}, u32[]{:S(2)}) collective-permute-start(f32[5,64]{1,0:T(8,128)S(1)} %pad_maximum_fusion.small), channel_id=1, source_target_pairs={{0,1},{1,0},{2,3},{3,2},{4,5},{5,4},{6,7},{7,6},{8,9},{9,8},{10,11... | collective-permute-start | bytes 3848 | tf_op jit(solution)/shard_map/ppermute | solution.py:750
  6.0 22.9 %all-to-all-start = ((bf16[4,496,128]{2,1,0:T(8,128)(2,1)}), bf16[4,496,128]{2,1,0:T(8,128)(2,1)S(1)}, u32[]{:S(2)}, u32[]{:S(2)}) async-start(bf16[4,496,128]{2,1,0:T(8,128)(2,1)} %get-tuple-element.56), calls=%async_computation | async-start | bytes 1015808 | tf_op jit(solution)/shard_map/all_to_all | solution.py:763
  9.8 14.1 %collective-permute-start.4 = (bf16[1,496,128]{2,1,0:T(8,128)(2,1)S(1)}, bf16[1,496,128]{2,1,0:T(8,128)(2,1)S(1)}, u32[]{:S(2)}, u32[]{:S(2)}) collective-permute-start(bf16[1,496,128]{2,1,0:T(8,128)(2,1)S(1)} %get-tuple-element.57), channel_id=1, source_target_pairs={{0,8},{2,10},{4,12},{6,14},{8,0},{10,2},{12,4},{14,6},{1,9},{3,11}... | collective-permute-start | bytes 380936 | tf_op jit(solution)/shard_map/ppermute | solution.py:758
  10.2 18.8 %collective-permute-start.5 = (bf16[1,496,128]{2,1,0:T(8,128)(2,1)S(1)}, bf16[1,496,128]{2,1,0:T(8,128)(2,1)S(1)}, u32[]{:S(2)}, u32[]{:S(2)}) collective-permute-start(bf16[1,496,128]{2,1,0:T(8,128)(2,1)S(1)} %get-tuple-element.58), channel_id=1, source_target_pairs={{0,10},{2,8},{4,14},{6,12},{8,2},{10,0},{12,6},{14,4},{1,11},{3,9}... | collective-permute-start | bytes 380936 | tf_op jit(solution)/shard_map/ppermute | solution.py:758
  14.2 19.7 %collective-permute-start.6 = (bf16[1,496,128]{2,1,0:T(8,128)(2,1)S(1)}, bf16[1,496,128]{2,1,0:T(8,128)(2,1)S(1)}, u32[]{:S(2)}, u32[]{:S(2)}) collective-permute-start(bf16[1,496,128]{2,1,0:T(8,128)(2,1)S(1)} %get-tuple-element.62), channel_id=1, source_target_pairs={{0,12},{2,14},{4,8},{6,10},{8,4},{10,6},{12,0},{14,2},{1,13},{3,15... | collective-permute-start | bytes 380936 | tf_op jit(solution)/shard_map/ppermute | solution.py:758
  14.6 21.8 %collective-permute-start.7 = (bf16[1,496,128]{2,1,0:T(8,128)(2,1)S(1)}, bf16[1,496,128]{2,1,0:T(8,128)(2,1)S(1)}, u32[]{:S(2)}, u32[]{:S(2)}) collective-permute-start(bf16[1,496,128]{2,1,0:T(8,128)(2,1)S(1)} %get-tuple-element.63), channel_id=1, source_target_pairs={{0,14},{2,12},{4,10},{6,8},{8,6},{10,4},{12,2},{14,0},{1,15},{3,13... | collective-permute-start | bytes 380936 | tf_op jit(solution)/shard_map/ppermute | solution.py:758

commit v7 on v5

--- a/solution.py
+++ b/solution.py
@@ -13,8 +13,7 @@
 MEDIUM_LIMIT = 16 * 1024 * 1024
 LARGE_LIMIT = 48 * 1024 * 1024
 MAX_ROUNDS = 16
-EARLIER = 2
-LAST = 2
+LAST = 5
 LANES = 128
 ROWS = 8
 MAX_SETS = 64
@@ -49,7 +48,7 @@
         return []
     light = list(range(1, replicas // 2))
     heavy = list(range(replicas // 2, replicas))
-    return light[:2] + heavy[:2] + light[2:] + heavy[2:]
+    return heavy + light
 
 
 def partner(replicas, mask):
@@ -277,6 +276,9 @@
     group_other,
     *refs,
 ):
+    count = (len(refs) - 38) // 2
+    light_in = refs[:count]
+    light_out = refs[count + 12 : 2 * count + 12]
     (
         plan_out,
         gated,
@@ -290,6 +292,8 @@
         delta_moved,
         decay_moved,
         scan_next,
+    ) = refs[count : count + 12]
+    (
         plan,
         receive,
         own,
@@ -315,7 +319,14 @@
         done,
         sem,
         load_sem,
-    ) = refs[-37:]
+        light_sem,
+    ) = refs[-26:]
+    passed = [
+        pltpu.make_async_copy(source, target, light_sem.at[place])
+        for place, (source, target) in enumerate(zip(light_in, light_out))
+    ]
+    for copy in passed:
+        copy.start()
     taps, slots, _ = inner.shape
     rows, half = own.shape
     steps = rows // slots
@@ -465,9 +476,11 @@
     for copy in copies:
         copy.wait()
     save_plan.wait()
-
-
-def stay(replicas, cap, scalars, arrays, near, earlier):
+    for copy in passed:
+        copy.wait()
+
+
+def stay(replicas, cap, scalars, arrays, near, light):
     receive, own, group_weight, delta_weight = arrays[0], arrays[1], arrays[4], arrays[5]
     inner, scan = arrays[-3], arrays[-1]
     taps, slots, _ = inner.shape
@@ -496,12 +509,12 @@
             pltpu.VMEM((steps, slots, width), BF16),
         ]
         + [moved] * 5
-        + [jax.ShapeDtypeStruct(scan.shape, BF16)],
+        + [jax.ShapeDtypeStruct(scan.shape, BF16)]
+        + [pltpu.VMEM(value.shape, BF16) for value in light],
         in_specs=[SMEM] * len(scalars)
         + [HBM] * len(far)
-        + [VMEM] * len(near)
-        + [HBM] * len(earlier),
-        out_specs=[VMEM] * 11 + [HBM],
+        + [VMEM] * (len(near) + len(light)),
+        out_specs=[VMEM] * 11 + [HBM] + [VMEM] * len(light),
         scratch_shapes=[
             pltpu.SMEM(plan_shape, jnp.int32),
             pltpu.SMEM(receive.shape, jnp.int32),
@@ -518,13 +531,14 @@
             pltpu.VMEM((moving,) + scan.shape[1:], BF16),
             pltpu.SemaphoreType.DMA((moving,)),
             pltpu.SemaphoreType.DMA((16,)),
+            pltpu.SemaphoreType.DMA((max(1, len(light)),)),
         ],
         compiler_params=pltpu.CompilerParams(vmem_limit_bytes=MEDIUM_LIMIT),
         cost_estimate=pl.CostEstimate(
             flops=300_000_000, bytes_accessed=6_000_000, transcendentals=100_000
         ),
         name="advance_staying",
-    )(*scalars, *far, *near, *earlier)
+    )(*scalars, *far, *near, *light)
 
 
 def arrive_kernel(
@@ -783,9 +797,10 @@
     small = jnp.concatenate([group_taps, group_offset[None]], axis=0)
     group_other = swap_heads(group)
     swapped = [swap_heads(value) for value in (own, group_weight, small)]
-    blocks = pack(replicas, cap, send_list, scan, inner, group, group_other, swapped)
-    arrived = exchange(replicas, blocks)
-    plan, gated, weights, table, inner_part, group_part, *moved, scan_next = stay(
+    blocks = list(pack(replicas, cap, send_list, scan, inner, group, group_other, swapped))
+    rounds = rounds_of(replicas)
+    delayed = [place for place, mask in enumerate(rounds) if mask < replicas // 2]
+    plan, gated, weights, table, inner_part, group_part, *moved = stay(
         replicas,
         cap,
         (decay_log, delta_bias, skip_gain, live_count),
@@ -803,8 +818,12 @@
             scan,
         ),
         (swapped[0], swapped[1], small, swapped[2], group_other),
-        arrived[:EARLIER] if rounds_of(replicas) else [],
-    )
+        [blocks[place] for place in delayed],
+    )
+    moved, scan_next, light = moved[:5], moved[5], moved[6:]
+    for place, block in zip(delayed, light):
+        blocks[place] = block
+    arrived = exchange(replicas, blocks)
     first = max(0, len(arrived) - LAST)
     if first:
         operands = (plan, weights, *moved, gated, table, inner_part, group_part)

time: 34.6 us -> 37 us (1.069)
  the two profiles are of different devices: /device:TPU:18 before, /device:TPU:0 now
where the time goes in v7:
time: 37 us; the launch traced here: 36.7 us
  Pallas kernels  13.3 us (36%)
  starting transfers between devices  12.4 us (34%)
  waiting for transfers between devices  7.46 us (20%)
  between operations  3.31 us (9%)
    ppermute x7, starting transfers between devices, exchange(): lax.ppermute(block, 'dp', [(source, source ^ mask) for source in range(re...  10.9 us
    ppermute x7, waiting for transfers between devices, exchange(): lax.ppermute(block, 'dp', [(source, source ^ mask) for source in range(re...  7.45 us
    pallas_call x1, Pallas kernels, stay(): pl.pallas_call(functools.partial(stay_kernel, replicas, cap), out_shape=[...  6.04 us
    pallas_call x2, Pallas kernels, arrive(): pl.pallas_call(functools.partial(arrive_kernel, replicas, cap, first, las...  4.42 us
    pallas_call x1, Pallas kernels, pack(): pl.pallas_call(functools.partial(states_kernel, replicas, cap), out_shape...  2.13 us
    ppermute x4, starting transfers between devices, swap_heads(): return lax.ppermute(value, 'head', [(0, 1), (1, 0)])  1.45 us
  transfers between devices with their start and end apart: 11, of which 2 were waited for; matrix products, arithmetic and copies ran while one was open for 0% of the time, Pallas kernels for 27%

profile of v7, /device:TPU:0, one launch (start us, length us, event | category | flops | bytes accessed | tf_op | source)
XLA Modules:
  0.0 36.7 jit_solution(3809269446038105620)
XLA Ops:
  0.6 0.5 %collective-permute-start.1 = (bf16[64,4096]{1,0:T(8,128)(2,1)}, bf16[64,4096]{1,0:T(8,128)(2,1)S(1)}, u32[]{:S(2)}, u32[]{:S(2)}) collective-permute-start(bf16[64,4096]{1,0:T(8,128)(2,1)} %bitcast.14), channel_id=1, source_target_pairs={{0,1},{1,0},{2,3},{3,2},{4,5},{5,4},{6,7},{7,6},{8,9},{9,8},{10,11... | collective-permute-start | bytes 1572872 | tf_op jit(solution)/shard_map/ppermute | solution.py:754
  1.1 0.0 copy-start
  1.2 0.1 collective-permute-start
  1.2 0.0 copy-start.1
  1.2 0.4 %collective-permute-start.3 = (bf16[3,56,64]{2,1,0:T(8,128)(2,1)}, bf16[3,56,64]{2,1,0:T(8,128)(2,1)S(1)}, u32[]{:S(2)}, u32[]{:S(2)}) collective-permute-start(bf16[3,56,64]{2,1,0:T(8,128)(2,1)} %bitcast.20), channel_id=1, source_target_pairs={{0,1},{1,0},{2,3},{3,2},{4,5},{5,4},{6,7},{7,6},{8,9},{9,8},{10,11... | collective-permute-start | bytes 64520 | tf_op jit(solution)/shard_map/ppermute | solution.py:754
  1.7 0.2 copy-done
  1.8 0.1 copy-done.1
  1.9 0.4 %collective-permute-start.2 = (f32[5,64]{1,0:T(8,128)S(1)}, f32[5,64]{1,0:T(8,128)S(1)}, u32[]{:S(2)}, u32[]{:S(2)}) collective-permute-start(f32[5,64]{1,0:T(8,128)S(1)} %pad_maximum_fusion.small), channel_id=1, source_target_pairs={{0,1},{1,0},{2,3},{3,2},{4,5},{5,4},{6,7},{7,6},{8,9},{9,8},{10,11... | collective-permute-start | bytes 3848 | tf_op jit(solution)/shard_map/ppermute | solution.py:754
  2.3 2.1 %pack_states.1 = (bf16[1,496,128]{2,1,0:T(8,128)(2,1)S(1)}, bf16[1,496,128]{2,1,0:T(8,128)(2,1)S(1)}, bf16[1,496,128]{2,1,0:T(8,128)(2,1)S(1)}, bf16[1,496,128]{...) custom-call(bf16[56,64,128]{2,1,0:T(8,128)(2,1)} %bitcast.11, ...), custom_call_target="tpu_custom_call" | custom-call | bytes 2000000 | tf_op jit(solution)/shard_map/pack_states/pallas_call | solution.py:157
  4.5 0.0 collective-permute-done.2.refs_9_.small_other
  4.5 0.0 collective-permute-done.3.group_other
  4.5 0.0 collective-permute-done.refs_7_.other
  4.5 0.0 collective-permute-done.1.refs_8_.group_weight_other
  4.5 0.7 %pack_windows.1 = (bf16[1,496,128]{2,1,0:T(8,128)(2,1)S(1)}, bf16[1,496,128]{2,1,0:T(8,128)(2,1)S(1)}, bf16[1,496,128]{2,1,0:T(8,128)(2,1)S(1)}, bf16[1,496,128]...) custom-call(s32[1,56]{1,0:T(1,128)S(1)} %get-tuple-element.43.indice, ...), custom_call_target="tpu_custom_call", output_to_operand_aliasing={{0}: (4, {}), {1}: (5, {}), {2}: (6, {}), {3}: (7, {}), {4}... | custom-call | bytes 500000 | tf_op jit(solution)/shard_map/pack_windows/pallas_call | solution.py:182
  5.2 3.8 %collective-permute-start.4 = (bf16[1,496,128]{2,1,0:T(8,128)(2,1)S(1)}, bf16[1,496,128]{2,1,0:T(8,128)(2,1)S(1)}, u32[]{:S(2)}, u32[]{:S(2)}) collective-permute-start(bf16[1,496,128]{2,1,0:T(8,128)(2,1)S(1)} %get-tuple-element.68), channel_id=1, source_target_pairs={{0,8},{2,10},{4,12},{6,14},{8,0},{10,2},{12,4},{14,6},{1,9},{3,11}... | collective-permute-start | bytes 380936 | tf_op jit(solution)/shard_map/ppermute | solution.py:762
  9.0 1.3 %collective-permute-start.5 = (bf16[1,496,128]{2,1,0:T(8,128)(2,1)S(1)}, bf16[1,496,128]{2,1,0:T(8,128)(2,1)S(1)}, u32[]{:S(2)}, u32[]{:S(2)}) collective-permute-start(bf16[1,496,128]{2,1,0:T(8,128)(2,1)S(1)} %get-tuple-element.69), channel_id=1, source_target_pairs={{0,10},{2,8},{4,14},{6,12},{8,2},{10,0},{12,6},{14,4},{1,11},{3,9}... | collective-permute-start | bytes 380936 | tf_op jit(solution)/shard_map/ppermute | solution.py:762
  12.9 3.7 %collective-permute-start.6 = (bf16[1,496,128]{2,1,0:T(8,128)(2,1)S(1)}, bf16[1,496,128]{2,1,0:T(8,128)(2,1)S(1)}, u32[]{:S(2)}, u32[]{:S(2)}) collective-permute-start(bf16[1,496,128]{2,1,0:T(8,128)(2,1)S(1)} %get-tuple-element.73), channel_id=1, source_target_pairs={{0,12},{2,14},{4,8},{6,10},{8,4},{10,6},{12,0},{14,2},{1,13},{3,15... | collective-permute-start | bytes 380936 | tf_op jit(solution)/shard_map/ppermute | solution.py:762
  16.5 0.1 collective-permute-start.7
  16.6 6.0 %advance_staying.1 = (s32[1,128]{1,0:T(1,128)S(1)}, f32[112,128]{1,0:T(8,128)S(1)}, f32[16,128]{1,0:T(8,128)S(1)}, f32[56,256]{1,0:T(8,128)S(1)}, bf16[2,56,128]...) custom-call(f32[1]{0:T(128)S(6)} %copy.40.decay_log, ...), custom_call_target="tpu_custom_call" | custom-call | flops 300000000 | bytes 6000000 | tf_op jit(solution)/shard_map/advance_staying/pallas_call | solution.py:501
  22.6 1.7 %collective-permute-start.8 = (bf16[1,496,128]{2,1,0:T(8,128)(2,1)S(1)}, bf16[1,496,128]{2,1,0:T(8,128)(2,1)S(1)}, u32[]{:S(2)}, u32[]{:S(2)}) collective-permute-start(bf16[1,496,128]{2,1,0:T(8,128)(2,1)S(1)} %get-tuple-element.75), channel_id=1, source_target_pairs={{0,2},{2,0},{4,6},{6,4},{8,10},{10,8},{12,14},{14,12},{1,3},{3,1},... | collective-permute-start | bytes 380936 | tf_op jit(solution)/shard_map/ppermute | solution.py:762
  24.3 0.0 collective-permute-done.4.refs_0_
  24.3 0.3 collective-permute-start.9
  24.6 3.5 %collective-permute-done.5.refs_1_ = bf16[1,496,128]{2,1,0:T(8,128)(2,1)S(1)} collective-permute-done((bf16[1,496,128]{2,1,0:T(8,128)(2,1)S(1)}, bf16[1,496,128]{2,1,0:T(8,128)(2,1)S(1)}, u32[]{:S(2)}, u32[]{:S(2)}) %collective-permute-start.5) | collective-permute-done | bytes 127008 | tf_op jit(solution)/shard_map/ppermute | solution.py:762
  28.1 0.2 collective-permute-start.10
  28.3 1.7 %advance_arrived.1 = (f32[112,128]{1,0:T(8,128)S(1)}, f32[56,256]{1,0:T(8,128)S(1)}, bf16[56,64,128]{2,1,0:T(8,128)(2,1)}) custom-call(s32[1,128]{1,0:T(1,128)S(1)} %get-tuple-element.56.plan_near, f32[16,128]{1,0:T(8,128)S(1)} %get-tuple-element.57.weights, f32[112,128]{1,0:T(8,128)S(1)} %get-tuple-element.58.inner_moved, ...), custom_call_target="tpu_custom_call", output_to_operand_aliasing={{2}: (11, {})} | custom-call | flops 10000000 | bytes 2000000 | tf_op jit(solution)/shard_map/advance_arrived/pallas_call | solution.py:728
  29.9 0.0 collective-permute-done.6.refs_0_
  29.9 0.0 collective-permute-done.7.refs_1_
  29.9 0.0 collective-permute-done.8.refs_2_
  30.0 0.0 collective-permute-done.9.refs_3_
  30.0 3.9 %collective-permute-done.10.refs_4_ = bf16[1,496,128]{2,1,0:T(8,128)(2,1)S(1)} collective-permute-done((bf16[1,496,128]{2,1,0:T(8,128)(2,1)S(1)}, bf16[1,496,128]{2,1,0:T(8,128)(2,1)S(1)}, u32[]{:S(2)}, u32[]{:S(2)}) %collective-permute-start.10) | collective-permute-done | bytes 127008 | tf_op jit(solution)/shard_map/ppermute | solution.py:762
  33.9 2.8 %advance_last.1 = (bf16[2,56,128]{2,1,0:T(8,128)(2,1)}, bf16[3,56,128]{2,1,0:T(8,128)(2,1)}, bf16[3,56,64]{2,1,0:T(8,128)(2,1)}, bf16[56,64,128]{2,1,0:T(8,128)(2,1)}) custom-call(s32[1,128]{1,0:T(1,128)S(1)} %get-tuple-element.56.plan_near, f32[16,128]{1,0:T(8,128)S(1)} %get-tuple-element.57.weights, ...), custom_call_target="tpu_custom_call", output_to_operand_aliasing={{3}: (11, {})} | custom-call | flops 10000000 | bytes 2000000 | tf_op jit(solution)/shard_map/advance_last/pallas_call | solution.py:728
  (1 shorter events, 0.0 us)
Async XLA Ops:
  0.6 3.9 %collective-permute-start.1 = (bf16[64,4096]{1,0:T(8,128)(2,1)}, bf16[64,4096]{1,0:T(8,128)(2,1)S(1)}, u32[]{:S(2)}, u32[]{:S(2)}) collective-permute-start(bf16[64,4096]{1,0:T(8,128)(2,1)} %bitcast.14), channel_id=1, source_target_pairs={{0,1},{1,0},{2,3},{3,2},{4,5},{5,4},{6,7},{7,6},{8,9},{9,8},{10,11... | collective-permute-start | bytes 1572872 | tf_op jit(solution)/shard_map/ppermute | solution.py:754
  1.1 0.7 %copy-start = (f32[4,64]{1,0:T(4,128)S(1)}, f32[4,64]{1,0:T(4,128)}, u32[]{:S(2)}) copy-start(f32[4,64]{1,0:T(4,128)} %param.25) | copy-start | bytes 3076
  1.2 3.3 %collective-permute-start = (bf16[112,2048]{1,0:T(8,128)(2,1)}, bf16[112,2048]{1,0:T(8,128)(2,1)S(1)}, u32[]{:S(2)}, u32[]{:S(2)}) collective-permute-start(bf16[112,2048]{1,0:T(8,128)(2,1)} %bitcast.16), channel_id=1, source_target_pairs={{0,1},{1,0},{2,3},{3,2},{4,5},{5,4},{6,7},{7,6},{8,9},{9,8},{10,11... | collective-permute-start | bytes 1376264 | tf_op jit(solution)/shard_map/ppermute | solution.py:754
  1.2 0.7 %copy-start.1 = (f32[64]{0:T(128)S(1)}, f32[64]{0:T(128)}, u32[]{:S(2)}) copy-start(f32[64]{0:T(128)} %param.26) | copy-start | bytes 772
  1.2 3.2 %collective-permute-start.3 = (bf16[3,56,64]{2,1,0:T(8,128)(2,1)}, bf16[3,56,64]{2,1,0:T(8,128)(2,1)S(1)}, u32[]{:S(2)}, u32[]{:S(2)}) collective-permute-start(bf16[3,56,64]{2,1,0:T(8,128)(2,1)} %bitcast.20), channel_id=1, source_target_pairs={{0,1},{1,0},{2,3},{3,2},{4,5},{5,4},{6,7},{7,6},{8,9},{9,8},{10,11... | collective-permute-start | bytes 64520 | tf_op jit(solution)/shard_map/ppermute | solution.py:754
  1.9 2.6 %collective-permute-start.2 = (f32[5,64]{1,0:T(8,128)S(1)}, f32[5,64]{1,0:T(8,128)S(1)}, u32[]{:S(2)}, u32[]{:S(2)}) collective-permute-start(f32[5,64]{1,0:T(8,128)S(1)} %pad_maximum_fusion.small), channel_id=1, source_target_pairs={{0,1},{1,0},{2,3},{3,2},{4,5},{5,4},{6,7},{7,6},{8,9},{9,8},{10,11... | collective-permute-start | bytes 3848 | tf_op jit(solution)/shard_map/ppermute | solution.py:754
  5.2 19.1 %collective-permute-start.4 = (bf16[1,496,128]{2,1,0:T(8,128)(2,1)S(1)}, bf16[1,496,128]{2,1,0:T(8,128)(2,1)S(1)}, u32[]{:S(2)}, u32[]{:S(2)}) collective-permute-start(bf16[1,496,128]{2,1,0:T(8,128)(2,1)S(1)} %get-tuple-element.68), channel_id=1, source_target_pairs={{0,8},{2,10},{4,12},{6,14},{8,0},{10,2},{12,4},{14,6},{1,9},{3,11}... | collective-permute-start | bytes 380936 | tf_op jit(solution)/shard_map/ppermute | solution.py:762
  9.0 19.1 %collective-permute-start.5 = (bf16[1,496,128]{2,1,0:T(8,128)(2,1)S(1)}, bf16[1,496,128]{2,1,0:T(8,128)(2,1)S(1)}, u32[]{:S(2)}, u32[]{:S(2)}) collective-permute-start(bf16[1,496,128]{2,1,0:T(8,128)(2,1)S(1)} %get-tuple-element.69), channel_id=1, source_target_pairs={{0,10},{2,8},{4,14},{6,12},{8,2},{10,0},{12,6},{14,4},{1,11},{3,9}... | collective-permute-start | bytes 380936 | tf_op jit(solution)/shard_map/ppermute | solution.py:762
  12.9 17.1 %collective-permute-start.6 = (bf16[1,496,128]{2,1,0:T(8,128)(2,1)S(1)}, bf16[1,496,128]{2,1,0:T(8,128)(2,1)S(1)}, u32[]{:S(2)}, u32[]{:S(2)}) collective-permute-start(bf16[1,496,128]{2,1,0:T(8,128)(2,1)S(1)} %get-tuple-element.73), channel_id=1, source_target_pairs={{0,12},{2,14},{4,8},{6,10},{8,4},{10,6},{12,0},{14,2},{1,13},{3,15... | collective-permute-start | bytes 380936 | tf_op jit(solution)/shard_map/ppermute | solution.py:762
  16.5 13.4 %collective-permute-start.7 = (bf16[1,496,128]{2,1,0:T(8,128)(2,1)S(1)}, bf16[1,496,128]{2,1,0:T(8,128)(2,1)S(1)}, u32[]{:S(2)}, u32[]{:S(2)}) collective-permute-start(bf16[1,496,128]{2,1,0:T(8,128)(2,1)S(1)} %get-tuple-element.74), channel_id=1, source_target_pairs={{0,14},{2,12},{4,10},{6,8},{8,6},{10,4},{12,2},{14,0},{1,15},{3,13... | collective-permute-start | bytes 380936 | tf_op jit(solution)/shard_map/ppermute | solution.py:762
  22.6 7.3 %collective-permute-start.8 = (bf16[1,496,128]{2,1,0:T(8,128)(2,1)S(1)}, bf16[1,496,128]{2,1,0:T(8,128)(2,1)S(1)}, u32[]{:S(2)}, u32[]{:S(2)}) collective-permute-start(bf16[1,496,128]{2,1,0:T(8,128)(2,1)S(1)} %get-tuple-element.75), channel_id=1, source_target_pairs={{0,2},{2,0},{4,6},{6,4},{8,10},{10,8},{12,14},{14,12},{1,3},{3,1},... | collective-permute-start | bytes 380936 | tf_op jit(solution)/shard_map/ppermute | solution.py:762
  24.3 5.6 %collective-permute-start.9 = (bf16[1,496,128]{2,1,0:T(8,128)(2,1)S(1)}, bf16[1,496,128]{2,1,0:T(8,128)(2,1)S(1)}, u32[]{:S(2)}, u32[]{:S(2)}) collective-permute-start(bf16[1,496,128]{2,1,0:T(8,128)(2,1)S(1)} %get-tuple-element.76), channel_id=1, source_target_pairs={{0,4},{2,6},{4,0},{6,2},{8,12},{10,14},{12,8},{14,10},{1,5},{3,7},... | collective-permute-start | bytes 380936 | tf_op jit(solution)/shard_map/ppermute | solution.py:762
  28.1 5.8 %collective-permute-start.10 = (bf16[1,496,128]{2,1,0:T(8,128)(2,1)S(1)}, bf16[1,496,128]{2,1,0:T(8,128)(2,1)S(1)}, u32[]{:S(2)}, u32[]{:S(2)}) collective-permute-start(bf16[1,496,128]{2,1,0:T(8,128)(2,1)S(1)} %get-tuple-element.77), channel_id=1, source_target_pairs={{0,6},{2,4},{4,2},{6,0},{8,14},{10,12},{12,10},{14,8},{1,7},{3,5},... | collective-permute-start | bytes 380936 | tf_op jit(solution)/shard_map/ppermute | solution.py:762

commit v8 on v5

--- a/solution.py
+++ b/solution.py
@@ -48,7 +48,7 @@
     if replicas > MAX_ROUNDS or replicas & (replicas - 1):
         return []
     light = list(range(1, replicas // 2))
-    heavy = list(range(replicas // 2, replicas))
+    heavy = list(range(3 * replicas // 4, replicas)) + list(range(replicas // 2, 3 * replicas // 4))
     return light[:2] + heavy[:2] + light[2:] + heavy[2:]
 
 

time: 34.6 us -> 36.6 us (1.058)
  the two profiles are of different devices: /device:TPU:18 before, /device:TPU:0 now
where the time goes in v8:
time: 36.6 us; the launch traced here: 36.1 us
  starting transfers between devices  13.5 us (37%)
  Pallas kernels  12.8 us (35%)
  waiting for transfers between devices  6.24 us (17%)
  between operations  3.32 us (9%)
    ppermute x7, starting transfers between devices, exchange(): lax.ppermute(block, 'dp', [(source, source ^ mask) for source in range(re...  12.1 us
    ppermute x7, waiting for transfers between devices, exchange(): lax.ppermute(block, 'dp', [(source, source ^ mask) for source in range(re...  6.23 us
    pallas_call x1, Pallas kernels, stay(): pl.pallas_call(functools.partial(stay_kernel, replicas, cap), out_shape=[...  5.64 us
    pallas_call x2, Pallas kernels, arrive(): pl.pallas_call(functools.partial(arrive_kernel, replicas, cap, first, las...  4.3 us
    pallas_call x1, Pallas kernels, pack(): pl.pallas_call(functools.partial(states_kernel, replicas, cap), out_shape...  2.14 us
    ppermute x4, starting transfers between devices, swap_heads(): return lax.ppermute(value, 'head', [(0, 1), (1, 0)])  1.45 us
  transfers between devices with their start and end apart: 11, of which 2 were waited for; matrix products, arithmetic and copies ran while one was open for 0% of the time, Pallas kernels for 29%

profile of v8, /device:TPU:0, one launch (start us, length us, event | category | flops | bytes accessed | tf_op | source)
XLA Modules:
  0.0 36.1 jit_solution(16984288474542833093)
XLA Ops:
  0.6 0.5 %collective-permute-start.1 = (bf16[64,4096]{1,0:T(8,128)(2,1)}, bf16[64,4096]{1,0:T(8,128)(2,1)S(1)}, u32[]{:S(2)}, u32[]{:S(2)}) collective-permute-start(bf16[64,4096]{1,0:T(8,128)(2,1)} %bitcast.14), channel_id=1, source_target_pairs={{0,1},{1,0},{2,3},{3,2},{4,5},{5,4},{6,7},{7,6},{8,9},{9,8},{10,11... | collective-permute-start | bytes 1572872 | tf_op jit(solution)/shard_map/ppermute | solution.py:740
  1.1 0.0 copy-start
  1.2 0.1 collective-permute-start
  1.2 0.0 copy-start.1
  1.2 0.4 %collective-permute-start.3 = (bf16[3,56,64]{2,1,0:T(8,128)(2,1)}, bf16[3,56,64]{2,1,0:T(8,128)(2,1)S(1)}, u32[]{:S(2)}, u32[]{:S(2)}) collective-permute-start(bf16[3,56,64]{2,1,0:T(8,128)(2,1)} %bitcast.20), channel_id=1, source_target_pairs={{0,1},{1,0},{2,3},{3,2},{4,5},{5,4},{6,7},{7,6},{8,9},{9,8},{10,11... | collective-permute-start | bytes 64520 | tf_op jit(solution)/shard_map/ppermute | solution.py:740
  1.7 0.2 copy-done
  1.8 0.1 copy-done.1
  1.9 0.4 %collective-permute-start.2 = (f32[5,64]{1,0:T(8,128)S(1)}, f32[5,64]{1,0:T(8,128)S(1)}, u32[]{:S(2)}, u32[]{:S(2)}) collective-permute-start(f32[5,64]{1,0:T(8,128)S(1)} %pad_maximum_fusion.small), channel_id=1, source_target_pairs={{0,1},{1,0},{2,3},{3,2},{4,5},{5,4},{6,7},{7,6},{8,9},{9,8},{10,11... | collective-permute-start | bytes 3848 | tf_op jit(solution)/shard_map/ppermute | solution.py:740
  2.3 2.1 %pack_states.1 = (bf16[1,496,128]{2,1,0:T(8,128)(2,1)S(1)}, bf16[1,496,128]{2,1,0:T(8,128)(2,1)S(1)}, bf16[1,496,128]{2,1,0:T(8,128)(2,1)S(1)}, bf16[1,496,128]{...) custom-call(bf16[56,64,128]{2,1,0:T(8,128)(2,1)} %bitcast.12, ...), custom_call_target="tpu_custom_call" | custom-call | bytes 2000000 | tf_op jit(solution)/shard_map/pack_states/pallas_call | solution.py:158
  4.5 0.0 collective-permute-done.2.refs_9_.small_other
  4.5 0.0 collective-permute-done.3.group_other
  4.5 0.0 collective-permute-done.refs_7_.other
  4.5 0.0 collective-permute-done.1.refs_8_.group_weight_other
  4.5 0.7 %pack_windows.1 = (bf16[1,496,128]{2,1,0:T(8,128)(2,1)S(1)}, bf16[1,496,128]{2,1,0:T(8,128)(2,1)S(1)}, bf16[1,496,128]{2,1,0:T(8,128)(2,1)S(1)}, bf16[1,496,128]...) custom-call(s32[1,56]{1,0:T(1,128)S(1)} %get-tuple-element.40.indice, ...), custom_call_target="tpu_custom_call", output_to_operand_aliasing={{0}: (4, {}), {1}: (5, {}), {2}: (6, {}), {3}: (7, {}), {4}... | custom-call | bytes 500000 | tf_op jit(solution)/shard_map/pack_windows/pallas_call | solution.py:183
  5.2 2.7 %collective-permute-start.4 = (bf16[1,496,128]{2,1,0:T(8,128)(2,1)S(1)}, bf16[1,496,128]{2,1,0:T(8,128)(2,1)S(1)}, u32[]{:S(2)}, u32[]{:S(2)}) collective-permute-start(bf16[1,496,128]{2,1,0:T(8,128)(2,1)S(1)} %get-tuple-element.50), channel_id=1, source_target_pairs={{0,2},{2,0},{4,6},{6,4},{8,10},{10,8},{12,14},{14,12},{1,3},{3,1},... | collective-permute-start | bytes 380936 | tf_op jit(solution)/shard_map/ppermute | solution.py:748
  7.9 1.6 %collective-permute-start.5 = (bf16[1,496,128]{2,1,0:T(8,128)(2,1)S(1)}, bf16[1,496,128]{2,1,0:T(8,128)(2,1)S(1)}, u32[]{:S(2)}, u32[]{:S(2)}) collective-permute-start(bf16[1,496,128]{2,1,0:T(8,128)(2,1)S(1)} %get-tuple-element.51), channel_id=1, source_target_pairs={{0,4},{2,6},{4,0},{6,2},{8,12},{10,14},{12,8},{14,10},{1,5},{3,7},... | collective-permute-start | bytes 380936 | tf_op jit(solution)/shard_map/ppermute | solution.py:748
  9.5 2.5 %collective-permute-start.6 = (bf16[1,496,128]{2,1,0:T(8,128)(2,1)S(1)}, bf16[1,496,128]{2,1,0:T(8,128)(2,1)S(1)}, u32[]{:S(2)}, u32[]{:S(2)}) collective-permute-start(bf16[1,496,128]{2,1,0:T(8,128)(2,1)S(1)} %get-tuple-element.64), channel_id=1, source_target_pairs={{0,12},{2,14},{4,8},{6,10},{8,4},{10,6},{12,0},{14,2},{1,13},{3,15... | collective-permute-start | bytes 380936 | tf_op jit(solution)/shard_map/ppermute | solution.py:748
  12.0 1.3 %collective-permute-start.7 = (bf16[1,496,128]{2,1,0:T(8,128)(2,1)S(1)}, bf16[1,496,128]{2,1,0:T(8,128)(2,1)S(1)}, u32[]{:S(2)}, u32[]{:S(2)}) collective-permute-start(bf16[1,496,128]{2,1,0:T(8,128)(2,1)S(1)} %get-tuple-element.65), channel_id=1, source_target_pairs={{0,14},{2,12},{4,10},{6,8},{8,6},{10,4},{12,2},{14,0},{1,15},{3,13... | collective-permute-start | bytes 380936 | tf_op jit(solution)/shard_map/ppermute | solution.py:748
  13.3 0.3 collective-permute-start.8
  13.6 0.0 collective-permute-done.4.refs_0_
  13.6 3.7 %collective-permute-start.9 = (bf16[1,496,128]{2,1,0:T(8,128)(2,1)S(1)}, bf16[1,496,128]{2,1,0:T(8,128)(2,1)S(1)}, u32[]{:S(2)}, u32[]{:S(2)}) collective-permute-start(bf16[1,496,128]{2,1,0:T(8,128)(2,1)S(1)} %get-tuple-element.70), channel_id=1, source_target_pairs={{0,8},{2,10},{4,12},{6,14},{8,0},{10,2},{12,4},{14,6},{1,9},{3,11}... | collective-permute-start | bytes 380936 | tf_op jit(solution)/shard_map/ppermute | solution.py:748
  17.3 0.0 collective-permute-done.5.refs_1_
  17.3 0.1 collective-permute-start.10
  19.9 5.6 %advance_staying.1 = (s32[1,128]{1,0:T(1,128)S(1)}, f32[112,128]{1,0:T(8,128)S(1)}, f32[16,128]{1,0:T(8,128)S(1)}, f32[56,256]{1,0:T(8,128)S(1)}, bf16[2,56,128]...) custom-call(f32[1]{0:T(128)S(6)} %copy.40.decay_log, ...), custom_call_target="tpu_custom_call" | custom-call | flops 300000000 | bytes 6000000 | tf_op jit(solution)/shard_map/advance_staying/pallas_call | solution.py:488
  25.5 0.0 collective-permute-done.6.refs_2_
  25.6 0.0 collective-permute-done.7.refs_3_
  25.6 0.0 collective-permute-done.8.refs_4_
  25.6 2.9 %advance_arrived.1 = (f32[112,128]{1,0:T(8,128)S(1)}, f32[56,256]{1,0:T(8,128)S(1)}, bf16[56,64,128]{2,1,0:T(8,128)(2,1)}) custom-call(s32[1,128]{1,0:T(1,128)S(1)} %get-tuple-element.52.plan_near, f32[16,128]{1,0:T(8,128)S(1)} %get-tuple-element.53.weights, f32[112,128]{1,0:T(8,128)S(1)} %get-tuple-element.54.inner_moved, ...), custom_call_target="tpu_custom_call", output_to_operand_aliasing={{2}: (11, {})} | custom-call | flops 10000000 | bytes 2000000 | tf_op jit(solution)/shard_map/advance_arrived/pallas_call | solution.py:714
  28.4 4.3 %collective-permute-done.9.refs_0_ = bf16[1,496,128]{2,1,0:T(8,128)(2,1)S(1)} collective-permute-done((bf16[1,496,128]{2,1,0:T(8,128)(2,1)S(1)}, bf16[1,496,128]{2,1,0:T(8,128)(2,1)S(1)}, u32[]{:S(2)}, u32[]{:S(2)}) %collective-permute-start.9) | collective-permute-done | bytes 127008 | tf_op jit(solution)/shard_map/ppermute | solution.py:748
  32.8 1.9 %collective-permute-done.10.refs_1_ = bf16[1,496,128]{2,1,0:T(8,128)(2,1)S(1)} collective-permute-done((bf16[1,496,128]{2,1,0:T(8,128)(2,1)S(1)}, bf16[1,496,128]{2,1,0:T(8,128)(2,1)S(1)}, u32[]{:S(2)}, u32[]{:S(2)}) %collective-permute-start.10) | collective-permute-done | bytes 127008 | tf_op jit(solution)/shard_map/ppermute | solution.py:748
  34.7 1.4 %advance_last.1 = (bf16[2,56,128]{2,1,0:T(8,128)(2,1)}, bf16[3,56,128]{2,1,0:T(8,128)(2,1)}, bf16[3,56,64]{2,1,0:T(8,128)(2,1)}, bf16[56,64,128]{2,1,0:T(8,128)(2,1)}) custom-call(s32[1,128]{1,0:T(1,128)S(1)} %get-tuple-element.52.plan_near, f32[16,128]{1,0:T(8,128)S(1)} %get-tuple-element.53.weights, ...), custom_call_target="tpu_custom_call", output_to_operand_aliasing={{3}: (11, {})} | custom-call | flops 10000000 | bytes 2000000 | tf_op jit(solution)/shard_map/advance_last/pallas_call | solution.py:714
  (1 shorter events, 0.0 us)
Async XLA Ops:
  0.6 3.9 %collective-permute-start.1 = (bf16[64,4096]{1,0:T(8,128)(2,1)}, bf16[64,4096]{1,0:T(8,128)(2,1)S(1)}, u32[]{:S(2)}, u32[]{:S(2)}) collective-permute-start(bf16[64,4096]{1,0:T(8,128)(2,1)} %bitcast.14), channel_id=1, source_target_pairs={{0,1},{1,0},{2,3},{3,2},{4,5},{5,4},{6,7},{7,6},{8,9},{9,8},{10,11... | collective-permute-start | bytes 1572872 | tf_op jit(solution)/shard_map/ppermute | solution.py:740
  1.1 0.7 %copy-start = (f32[4,64]{1,0:T(4,128)S(1)}, f32[4,64]{1,0:T(4,128)}, u32[]{:S(2)}) copy-start(f32[4,64]{1,0:T(4,128)} %param.25) | copy-start | bytes 3076
  1.2 3.3 %collective-permute-start = (bf16[112,2048]{1,0:T(8,128)(2,1)}, bf16[112,2048]{1,0:T(8,128)(2,1)S(1)}, u32[]{:S(2)}, u32[]{:S(2)}) collective-permute-start(bf16[112,2048]{1,0:T(8,128)(2,1)} %bitcast.16), channel_id=1, source_target_pairs={{0,1},{1,0},{2,3},{3,2},{4,5},{5,4},{6,7},{7,6},{8,9},{9,8},{10,11... | collective-permute-start | bytes 1376264 | tf_op jit(solution)/shard_map/ppermute | solution.py:740
  1.2 0.7 %copy-start.1 = (f32[64]{0:T(128)S(1)}, f32[64]{0:T(128)}, u32[]{:S(2)}) copy-start(f32[64]{0:T(128)} %param.26) | copy-start | bytes 772
  1.2 3.2 %collective-permute-start.3 = (bf16[3,56,64]{2,1,0:T(8,128)(2,1)}, bf16[3,56,64]{2,1,0:T(8,128)(2,1)S(1)}, u32[]{:S(2)}, u32[]{:S(2)}) collective-permute-start(bf16[3,56,64]{2,1,0:T(8,128)(2,1)} %bitcast.20), channel_id=1, source_target_pairs={{0,1},{1,0},{2,3},{3,2},{4,5},{5,4},{6,7},{7,6},{8,9},{9,8},{10,11... | collective-permute-start | bytes 64520 | tf_op jit(solution)/shard_map/ppermute | solution.py:740
  1.9 2.6 %collective-permute-start.2 = (f32[5,64]{1,0:T(8,128)S(1)}, f32[5,64]{1,0:T(8,128)S(1)}, u32[]{:S(2)}, u32[]{:S(2)}) collective-permute-start(f32[5,64]{1,0:T(8,128)S(1)} %pad_maximum_fusion.small), channel_id=1, source_target_pairs={{0,1},{1,0},{2,3},{3,2},{4,5},{5,4},{6,7},{7,6},{8,9},{9,8},{10,11... | collective-permute-start | bytes 3848 | tf_op jit(solution)/shard_map/ppermute | solution.py:740
  5.2 8.3 %collective-permute-start.4 = (bf16[1,496,128]{2,1,0:T(8,128)(2,1)S(1)}, bf16[1,496,128]{2,1,0:T(8,128)(2,1)S(1)}, u32[]{:S(2)}, u32[]{:S(2)}) collective-permute-start(bf16[1,496,128]{2,1,0:T(8,128)(2,1)S(1)} %get-tuple-element.50), channel_id=1, source_target_pairs={{0,2},{2,0},{4,6},{6,4},{8,10},{10,8},{12,14},{14,12},{1,3},{3,1},... | collective-permute-start | bytes 380936 | tf_op jit(solution)/shard_map/ppermute | solution.py:748
  7.9 9.3 %collective-permute-start.5 = (bf16[1,496,128]{2,1,0:T(8,128)(2,1)S(1)}, bf16[1,496,128]{2,1,0:T(8,128)(2,1)S(1)}, u32[]{:S(2)}, u32[]{:S(2)}) collective-permute-start(bf16[1,496,128]{2,1,0:T(8,128)(2,1)S(1)} %get-tuple-element.51), channel_id=1, source_target_pairs={{0,4},{2,6},{4,0},{6,2},{8,12},{10,14},{12,8},{14,10},{1,5},{3,7},... | collective-permute-start | bytes 380936 | tf_op jit(solution)/shard_map/ppermute | solution.py:748
  9.5 16.0 %collective-permute-start.6 = (bf16[1,496,128]{2,1,0:T(8,128)(2,1)S(1)}, bf16[1,496,128]{2,1,0:T(8,128)(2,1)S(1)}, u32[]{:S(2)}, u32[]{:S(2)}) collective-permute-start(bf16[1,496,128]{2,1,0:T(8,128)(2,1)S(1)} %get-tuple-element.64), channel_id=1, source_target_pairs={{0,12},{2,14},{4,8},{6,10},{8,4},{10,6},{12,0},{14,2},{1,13},{3,15... | collective-permute-start | bytes 380936 | tf_op jit(solution)/shard_map/ppermute | solution.py:748
  12.0 13.6 %collective-permute-start.7 = (bf16[1,496,128]{2,1,0:T(8,128)(2,1)S(1)}, bf16[1,496,128]{2,1,0:T(8,128)(2,1)S(1)}, u32[]{:S(2)}, u32[]{:S(2)}) collective-permute-start(bf16[1,496,128]{2,1,0:T(8,128)(2,1)S(1)} %get-tuple-element.65), channel_id=1, source_target_pairs={{0,14},{2,12},{4,10},{6,8},{8,6},{10,4},{12,2},{14,0},{1,15},{3,13... | collective-permute-start | bytes 380936 | tf_op jit(solution)/shard_map/ppermute | solution.py:748
  13.3 12.3 %collective-permute-start.8 = (bf16[1,496,128]{2,1,0:T(8,128)(2,1)S(1)}, bf16[1,496,128]{2,1,0:T(8,128)(2,1)S(1)}, u32[]{:S(2)}, u32[]{:S(2)}) collective-permute-start(bf16[1,496,128]{2,1,0:T(8,128)(2,1)S(1)} %get-tuple-element.66), channel_id=1, source_target_pairs={{0,6},{2,4},{4,2},{6,0},{8,14},{10,12},{12,10},{14,8},{1,7},{3,5},... | collective-permute-start | bytes 380936 | tf_op jit(solution)/shard_map/ppermute | solution.py:748
  13.6 19.2 %collective-permute-start.9 = (bf16[1,496,128]{2,1,0:T(8,128)(2,1)S(1)}, bf16[1,496,128]{2,1,0:T(8,128)(2,1)S(1)}, u32[]{:S(2)}, u32[]{:S(2)}) collective-permute-start(bf16[1,496,128]{2,1,0:T(8,128)(2,1)S(1)} %get-tuple-element.70), channel_id=1, source_target_pairs={{0,8},{2,10},{4,12},{6,14},{8,0},{10,2},{12,4},{14,6},{1,9},{3,11}... | collective-permute-start | bytes 380936 | tf_op jit(solution)/shard_map/ppermute | solution.py:748
  17.3 17.4 %collective-permute-start.10 = (bf16[1,496,128]{2,1,0:T(8,128)(2,1)S(1)}, bf16[1,496,128]{2,1,0:T(8,128)(2,1)S(1)}, u32[]{:S(2)}, u32[]{:S(2)}) collective-permute-start(bf16[1,496,128]{2,1,0:T(8,128)(2,1)S(1)} %get-tuple-element.71), channel_id=1, source_target_pairs={{0,10},{2,8},{4,14},{6,12},{8,2},{10,0},{12,6},{14,4},{1,11},{3,9}... | collective-permute-start | bytes 380936 | tf_op jit(solution)/shard_map/ppermute | solution.py:748

commit v9 on v3

--- a/solution.py
+++ b/solution.py
@@ -14,7 +14,7 @@
 LARGE_LIMIT = 48 * 1024 * 1024
 MAX_ROUNDS = 16
 EARLIER = 3
-LAST = 2
+LAST = 3
 LANES = 128
 ROWS = 8
 MAX_SETS = 64
@@ -49,7 +49,7 @@
         return []
     light = list(range(1, replicas // 2))
     heavy = list(range(replicas // 2, replicas))
-    return heavy[:1] + light[:2] + heavy[1:2] + light[2:] + heavy[2:]
+    return heavy[:1] + light[:2] + heavy[1:] + light[2:]
 
 
 def partner(replicas, mask):

time: 34.1 us -> 34.4 us (level)
  the two profiles are of different devices: /device:TPU:0 before, /device:TPU:17 now
where the time goes in v9:
time: 34.4 us; the launch traced here: 34.1 us
  Pallas kernels  12.7 us (37%)
  starting transfers between devices  12.3 us (36%)
  waiting for transfers between devices  5.49 us (16%)
  between operations  3.32 us (10%)
    ppermute x7, starting transfers between devices, exchange(): lax.ppermute(block, 'dp', [(source, source ^ mask) for source in range(re...  10.6 us
    pallas_call x1, Pallas kernels, stay(): pl.pallas_call(functools.partial(stay_kernel, replicas, cap), out_shape=[...  5.49 us
    ppermute x7, waiting for transfers between devices, exchange(): lax.ppermute(block, 'dp', [(source, source ^ mask) for source in range(re...  5.48 us
    pallas_call x2, Pallas kernels, arrive(): pl.pallas_call(functools.partial(arrive_kernel, replicas, cap, first, las...  4.37 us
    pallas_call x1, Pallas kernels, pack(): pl.pallas_call(functools.partial(states_kernel, replicas, cap), out_shape...  2.14 us
    ppermute x4, starting transfers between devices, swap_heads(): return lax.ppermute(value, 'head', [(0, 1), (1, 0)])  1.67 us
    pallas_call x1, Pallas kernels, pack(): pl.pallas_call(functools.partial(windows_kernel, replicas, cap, scan.shap...  0.7 us
  transfers between devices with their start and end apart: 11, of which 3 were waited for; matrix products, arithmetic and copies ran while one was open for 0% of the time, Pallas kernels for 29%

profile of v9, /device:TPU:17, one launch (start us, length us, event | category | flops | bytes accessed | tf_op | source)
XLA Modules:
  0.0 34.1 jit_solution(1279193626041974121)
XLA Ops:
  0.6 0.7 %collective-permute-start.1 = (bf16[64,4096]{1,0:T(8,128)(2,1)}, bf16[64,4096]{1,0:T(8,128)(2,1)S(1)}, u32[]{:S(2)}, u32[]{:S(2)}) collective-permute-start(bf16[64,4096]{1,0:T(8,128)(2,1)} %bitcast.14), channel_id=1, source_target_pairs={{0,1},{1,0},{2,3},{3,2},{4,5},{5,4},{6,7},{7,6},{8,9},{9,8},{10,11... | collective-permute-start | bytes 1572872 | tf_op jit(solution)/shard_map/ppermute | solution.py:739
  1.4 0.0 copy-start
  1.4 0.1 collective-permute-start
  1.5 0.0 copy-start.1
  1.5 0.4 %collective-permute-start.3 = (bf16[3,56,64]{2,1,0:T(8,128)(2,1)}, bf16[3,56,64]{2,1,0:T(8,128)(2,1)S(1)}, u32[]{:S(2)}, u32[]{:S(2)}) collective-permute-start(bf16[3,56,64]{2,1,0:T(8,128)(2,1)} %bitcast.20), channel_id=1, source_target_pairs={{0,1},{1,0},{2,3},{3,2},{4,5},{5,4},{6,7},{7,6},{8,9},{9,8},{10,11... | collective-permute-start | bytes 64520 | tf_op jit(solution)/shard_map/ppermute | solution.py:739
  1.9 0.2 copy-done
  2.1 0.1 copy-done.1
  2.1 0.4 %collective-permute-start.2 = (f32[5,64]{1,0:T(8,128)S(1)}, f32[5,64]{1,0:T(8,128)S(1)}, u32[]{:S(2)}, u32[]{:S(2)}) collective-permute-start(f32[5,64]{1,0:T(8,128)S(1)} %pad_maximum_fusion.small), channel_id=1, source_target_pairs={{0,1},{1,0},{2,3},{3,2},{4,5},{5,4},{6,7},{7,6},{8,9},{9,8},{10,11... | collective-permute-start | bytes 3848 | tf_op jit(solution)/shard_map/ppermute | solution.py:739
  2.5 2.1 %pack_states.1 = (bf16[1,496,128]{2,1,0:T(8,128)(2,1)S(1)}, bf16[1,496,128]{2,1,0:T(8,128)(2,1)S(1)}, bf16[1,496,128]{2,1,0:T(8,128)(2,1)S(1)}, bf16[1,496,128]{...) custom-call(bf16[56,64,128]{2,1,0:T(8,128)(2,1)} %bitcast.11, ...), custom_call_target="tpu_custom_call" | custom-call | bytes 2000000 | tf_op jit(solution)/shard_map/pack_states/pallas_call | solution.py:158
  4.7 0.0 collective-permute-done.2.refs_9_.small_other
  4.7 0.0 collective-permute-done.3.group_other
  4.7 0.0 collective-permute-done.refs_7_.other
  4.7 0.0 collective-permute-done.1.refs_8_.group_weight_other
  4.7 0.7 %pack_windows.1 = (bf16[1,496,128]{2,1,0:T(8,128)(2,1)S(1)}, bf16[1,496,128]{2,1,0:T(8,128)(2,1)S(1)}, bf16[1,496,128]{2,1,0:T(8,128)(2,1)S(1)}, bf16[1,496,128]...) custom-call(s32[1,56]{1,0:T(1,128)S(1)} %get-tuple-element.40.indice, ...), custom_call_target="tpu_custom_call", output_to_operand_aliasing={{0}: (4, {}), {1}: (5, {}), {2}: (6, {}), {3}: (7, {}), {4}... | custom-call | bytes 500000 | tf_op jit(solution)/shard_map/pack_windows/pallas_call | solution.py:183
  5.4 0.1 collective-permute-start.4
  5.5 1.3 %collective-permute-start.5 = (bf16[1,496,128]{2,1,0:T(8,128)(2,1)S(1)}, bf16[1,496,128]{2,1,0:T(8,128)(2,1)S(1)}, u32[]{:S(2)}, u32[]{:S(2)}) collective-permute-start(bf16[1,496,128]{2,1,0:T(8,128)(2,1)S(1)} %get-tuple-element.51), channel_id=1, source_target_pairs={{0,2},{2,0},{4,6},{6,4},{8,10},{10,8},{12,14},{14,12},{1,3},{3,1},... | collective-permute-start | bytes 380936 | tf_op jit(solution)/shard_map/ppermute | solution.py:747
  6.8 1.3 %collective-permute-start.6 = (bf16[1,496,128]{2,1,0:T(8,128)(2,1)S(1)}, bf16[1,496,128]{2,1,0:T(8,128)(2,1)S(1)}, u32[]{:S(2)}, u32[]{:S(2)}) collective-permute-start(bf16[1,496,128]{2,1,0:T(8,128)(2,1)S(1)} %get-tuple-element.52), channel_id=1, source_target_pairs={{0,4},{2,6},{4,0},{6,2},{8,12},{10,14},{12,8},{14,10},{1,5},{3,7},... | collective-permute-start | bytes 380936 | tf_op jit(solution)/shard_map/ppermute | solution.py:747
  8.1 2.3 %collective-permute-start.7 = (bf16[1,496,128]{2,1,0:T(8,128)(2,1)S(1)}, bf16[1,496,128]{2,1,0:T(8,128)(2,1)S(1)}, u32[]{:S(2)}, u32[]{:S(2)}) collective-permute-start(bf16[1,496,128]{2,1,0:T(8,128)(2,1)S(1)} %get-tuple-element.65), channel_id=1, source_target_pairs={{0,10},{2,8},{4,14},{6,12},{8,2},{10,0},{12,6},{14,4},{1,11},{3,9}... | collective-permute-start | bytes 380936 | tf_op jit(solution)/shard_map/ppermute | solution.py:747
  10.3 0.0 collective-permute-start.8
  10.3 1.0 %collective-permute-done.4.refs_0_ = bf16[1,496,128]{2,1,0:T(8,128)(2,1)S(1)} collective-permute-done((bf16[1,496,128]{2,1,0:T(8,128)(2,1)S(1)}, bf16[1,496,128]{2,1,0:T(8,128)(2,1)S(1)}, u32[]{:S(2)}, u32[]{:S(2)}) %collective-permute-start.4) | collective-permute-done | bytes 127008 | tf_op jit(solution)/shard_map/ppermute | solution.py:747
  11.3 3.3 %collective-permute-start.9 = (bf16[1,496,128]{2,1,0:T(8,128)(2,1)S(1)}, bf16[1,496,128]{2,1,0:T(8,128)(2,1)S(1)}, u32[]{:S(2)}, u32[]{:S(2)}) collective-permute-start(bf16[1,496,128]{2,1,0:T(8,128)(2,1)S(1)} %get-tuple-element.70), channel_id=1, source_target_pairs={{0,14},{2,12},{4,10},{6,8},{8,6},{10,4},{12,2},{14,0},{1,15},{3,13... | collective-permute-start | bytes 380936 | tf_op jit(solution)/shard_map/ppermute | solution.py:747
  14.7 0.0 collective-permute-done.5.refs_1_
  14.7 2.4 %collective-permute-start.10 = (bf16[1,496,128]{2,1,0:T(8,128)(2,1)S(1)}, bf16[1,496,128]{2,1,0:T(8,128)(2,1)S(1)}, u32[]{:S(2)}, u32[]{:S(2)}) collective-permute-start(bf16[1,496,128]{2,1,0:T(8,128)(2,1)S(1)} %get-tuple-element.71), channel_id=1, source_target_pairs={{0,6},{2,4},{4,2},{6,0},{8,14},{10,12},{12,10},{14,8},{1,7},{3,5},... | collective-permute-start | bytes 380936 | tf_op jit(solution)/shard_map/ppermute | solution.py:747
  19.7 0.0 collective-permute-done.6.refs_2_
  19.7 5.5 %advance_staying.1 = (s32[1,128]{1,0:T(1,128)S(1)}, f32[112,128]{1,0:T(8,128)S(1)}, f32[16,128]{1,0:T(8,128)S(1)}, f32[56,256]{1,0:T(8,128)S(1)}, bf16[2,56,128]...) custom-call(f32[1]{0:T(128)S(6)} %copy.40.decay_log, ...), custom_call_target="tpu_custom_call" | custom-call | flops 300000000 | bytes 6000000 | tf_op jit(solution)/shard_map/advance_staying/pallas_call | solution.py:487
  25.2 0.0 collective-permute-done.7.refs_3_
  25.2 2.1 %advance_arrived.1 = (f32[112,128]{1,0:T(8,128)S(1)}, f32[56,256]{1,0:T(8,128)S(1)}, bf16[56,64,128]{2,1,0:T(8,128)(2,1)}) custom-call(s32[1,128]{1,0:T(1,128)S(1)} %get-tuple-element.53.plan_near, f32[16,128]{1,0:T(8,128)S(1)} %get-tuple-element.54.weights, f32[112,128]{1,0:T(8,128)S(1)} %get-tuple-element.55.inner_moved, ...), custom_call_target="tpu_custom_call", output_to_operand_aliasing={{2}: (11, {})} | custom-call | flops 10000000 | bytes 2000000 | tf_op jit(solution)/shard_map/advance_arrived/pallas_call | solution.py:713
  27.3 0.9 %collective-permute-done.8.refs_0_ = bf16[1,496,128]{2,1,0:T(8,128)(2,1)S(1)} collective-permute-done((bf16[1,496,128]{2,1,0:T(8,128)(2,1)S(1)}, bf16[1,496,128]{2,1,0:T(8,128)(2,1)S(1)}, u32[]{:S(2)}, u32[]{:S(2)}) %collective-permute-start.8) | collective-permute-done | bytes 127008 | tf_op jit(solution)/shard_map/ppermute | solution.py:747
  28.2 3.6 %collective-permute-done.9.refs_1_ = bf16[1,496,128]{2,1,0:T(8,128)(2,1)S(1)} collective-permute-done((bf16[1,496,128]{2,1,0:T(8,128)(2,1)S(1)}, bf16[1,496,128]{2,1,0:T(8,128)(2,1)S(1)}, u32[]{:S(2)}, u32[]{:S(2)}) %collective-permute-start.9) | collective-permute-done | bytes 127008 | tf_op jit(solution)/shard_map/ppermute | solution.py:747
  31.8 0.0 collective-permute-done.10.refs_2_
  31.8 2.2 %advance_last.1 = (bf16[2,56,128]{2,1,0:T(8,128)(2,1)}, bf16[3,56,128]{2,1,0:T(8,128)(2,1)}, bf16[3,56,64]{2,1,0:T(8,128)(2,1)}, bf16[56,64,128]{2,1,0:T(8,128)(2,1)}) custom-call(s32[1,128]{1,0:T(1,128)S(1)} %get-tuple-element.53.plan_near, f32[16,128]{1,0:T(8,128)S(1)} %get-tuple-element.54.weights, ...), custom_call_target="tpu_custom_call", output_to_operand_aliasing={{3}: (11, {})} | custom-call | flops 10000000 | bytes 2000000 | tf_op jit(solution)/shard_map/advance_last/pallas_call | solution.py:713
  (1 shorter events, 0.0 us)
Async XLA Ops:
  0.6 4.1 %collective-permute-start.1 = (bf16[64,4096]{1,0:T(8,128)(2,1)}, bf16[64,4096]{1,0:T(8,128)(2,1)S(1)}, u32[]{:S(2)}, u32[]{:S(2)}) collective-permute-start(bf16[64,4096]{1,0:T(8,128)(2,1)} %bitcast.14), channel_id=1, source_target_pairs={{0,1},{1,0},{2,3},{3,2},{4,5},{5,4},{6,7},{7,6},{8,9},{9,8},{10,11... | collective-permute-start | bytes 1572872 | tf_op jit(solution)/shard_map/ppermute | solution.py:739
  1.4 0.7 %copy-start = (f32[4,64]{1,0:T(4,128)S(1)}, f32[4,64]{1,0:T(4,128)}, u32[]{:S(2)}) copy-start(f32[4,64]{1,0:T(4,128)} %param.25) | copy-start | bytes 3076
  1.4 3.4 %collective-permute-start = (bf16[112,2048]{1,0:T(8,128)(2,1)}, bf16[112,2048]{1,0:T(8,128)(2,1)S(1)}, u32[]{:S(2)}, u32[]{:S(2)}) collective-permute-start(bf16[112,2048]{1,0:T(8,128)(2,1)} %bitcast.16), channel_id=1, source_target_pairs={{0,1},{1,0},{2,3},{3,2},{4,5},{5,4},{6,7},{7,6},{8,9},{9,8},{10,11... | collective-permute-start | bytes 1376264 | tf_op jit(solution)/shard_map/ppermute | solution.py:739
  1.5 0.7 %copy-start.1 = (f32[64]{0:T(128)S(1)}, f32[64]{0:T(128)}, u32[]{:S(2)}) copy-start(f32[64]{0:T(128)} %param.26) | copy-start | bytes 772
  1.5 3.3 %collective-permute-start.3 = (bf16[3,56,64]{2,1,0:T(8,128)(2,1)}, bf16[3,56,64]{2,1,0:T(8,128)(2,1)S(1)}, u32[]{:S(2)}, u32[]{:S(2)}) collective-permute-start(bf16[3,56,64]{2,1,0:T(8,128)(2,1)} %bitcast.20), channel_id=1, source_target_pairs={{0,1},{1,0},{2,3},{3,2},{4,5},{5,4},{6,7},{7,6},{8,9},{9,8},{10,11... | collective-permute-start | bytes 64520 | tf_op jit(solution)/shard_map/ppermute | solution.py:739
  2.1 2.6 %collective-permute-start.2 = (f32[5,64]{1,0:T(8,128)S(1)}, f32[5,64]{1,0:T(8,128)S(1)}, u32[]{:S(2)}, u32[]{:S(2)}) collective-permute-start(f32[5,64]{1,0:T(8,128)S(1)} %pad_maximum_fusion.small), channel_id=1, source_target_pairs={{0,1},{1,0},{2,3},{3,2},{4,5},{5,4},{6,7},{7,6},{8,9},{9,8},{10,11... | collective-permute-start | bytes 3848 | tf_op jit(solution)/shard_map/ppermute | solution.py:739
  5.4 5.9 %collective-permute-start.4 = (bf16[1,496,128]{2,1,0:T(8,128)(2,1)S(1)}, bf16[1,496,128]{2,1,0:T(8,128)(2,1)S(1)}, u32[]{:S(2)}, u32[]{:S(2)}) collective-permute-start(bf16[1,496,128]{2,1,0:T(8,128)(2,1)S(1)} %get-tuple-element.50), channel_id=1, source_target_pairs={{0,8},{2,10},{4,12},{6,14},{8,0},{10,2},{12,4},{14,6},{1,9},{3,11}... | collective-permute-start | bytes 380936 | tf_op jit(solution)/shard_map/ppermute | solution.py:747
  5.5 9.1 %collective-permute-start.5 = (bf16[1,496,128]{2,1,0:T(8,128)(2,1)S(1)}, bf16[1,496,128]{2,1,0:T(8,128)(2,1)S(1)}, u32[]{:S(2)}, u32[]{:S(2)}) collective-permute-start(bf16[1,496,128]{2,1,0:T(8,128)(2,1)S(1)} %get-tuple-element.51), channel_id=1, source_target_pairs={{0,2},{2,0},{4,6},{6,4},{8,10},{10,8},{12,14},{14,12},{1,3},{3,1},... | collective-permute-start | bytes 380936 | tf_op jit(solution)/shard_map/ppermute | solution.py:747
  6.8 12.9 %collective-permute-start.6 = (bf16[1,496,128]{2,1,0:T(8,128)(2,1)S(1)}, bf16[1,496,128]{2,1,0:T(8,128)(2,1)S(1)}, u32[]{:S(2)}, u32[]{:S(2)}) collective-permute-start(bf16[1,496,128]{2,1,0:T(8,128)(2,1)S(1)} %get-tuple-element.52), channel_id=1, source_target_pairs={{0,4},{2,6},{4,0},{6,2},{8,12},{10,14},{12,8},{14,10},{1,5},{3,7},... | collective-permute-start | bytes 380936 | tf_op jit(solution)/shard_map/ppermute | solution.py:747
  8.1 17.1 %collective-permute-start.7 = (bf16[1,496,128]{2,1,0:T(8,128)(2,1)S(1)}, bf16[1,496,128]{2,1,0:T(8,128)(2,1)S(1)}, u32[]{:S(2)}, u32[]{:S(2)}) collective-permute-start(bf16[1,496,128]{2,1,0:T(8,128)(2,1)S(1)} %get-tuple-element.65), channel_id=1, source_target_pairs={{0,10},{2,8},{4,14},{6,12},{8,2},{10,0},{12,6},{14,4},{1,11},{3,9}... | collective-permute-start | bytes 380936 | tf_op jit(solution)/shard_map/ppermute | solution.py:747
  10.3 17.9 %collective-permute-start.8 = (bf16[1,496,128]{2,1,0:T(8,128)(2,1)S(1)}, bf16[1,496,128]{2,1,0:T(8,128)(2,1)S(1)}, u32[]{:S(2)}, u32[]{:S(2)}) collective-permute-start(bf16[1,496,128]{2,1,0:T(8,128)(2,1)S(1)} %get-tuple-element.69), channel_id=1, source_target_pairs={{0,12},{2,14},{4,8},{6,10},{8,4},{10,6},{12,0},{14,2},{1,13},{3,15... | collective-permute-start | bytes 380936 | tf_op jit(solution)/shard_map/ppermute | solution.py:747
  11.3 20.5 %collective-permute-start.9 = (bf16[1,496,128]{2,1,0:T(8,128)(2,1)S(1)}, bf16[1,496,128]{2,1,0:T(8,128)(2,1)S(1)}, u32[]{:S(2)}, u32[]{:S(2)}) collective-permute-start(bf16[1,496,128]{2,1,0:T(8,128)(2,1)S(1)} %get-tuple-element.70), channel_id=1, source_target_pairs={{0,14},{2,12},{4,10},{6,8},{8,6},{10,4},{12,2},{14,0},{1,15},{3,13... | collective-permute-start | bytes 380936 | tf_op jit(solution)/shard_map/ppermute | solution.py:747
  14.7 17.2 %collective-permute-start.10 = (bf16[1,496,128]{2,1,0:T(8,128)(2,1)S(1)}, bf16[1,496,128]{2,1,0:T(8,128)(2,1)S(1)}, u32[]{:S(2)}, u32[]{:S(2)}) collective-permute-start(bf16[1,496,128]{2,1,0:T(8,128)(2,1)S(1)} %get-tuple-element.71), channel_id=1, source_target_pairs={{0,6},{2,4},{4,2},{6,0},{8,14},{10,12},{12,10},{14,8},{1,7},{3,5},... | collective-permute-start | bytes 380936 | tf_op jit(solution)/shard_map/ppermute | solution.py:747

commit v10 on v3

--- a/solution.py
+++ b/solution.py
@@ -28,10 +28,6 @@
     return pltpu.with_memory_space_constraint(value, pltpu.HBM)
 
 
-def in_vmem(value):
-    return pltpu.with_memory_space_constraint(value, pltpu.VMEM)
-
-
 def round_up(value, step):
     return -(-value // step) * step
 
@@ -63,27 +59,26 @@
     )
 
 
-def destinations(replicas, outs):
+def pack_kernel(replicas, cap, scan, send, inner, group, group_other, *refs):
     rounds = rounds_of(replicas)
-    if rounds:
-        return [(ref.at[0], partner(replicas, mask)) for ref, mask in zip(outs, rounds)]
-    return [(outs[0].at[target], target) for target in range(replicas)]
-
-
-def states_kernel(replicas, cap, scan, send, inner, group, *refs):
-    outs, (picked, group_out, indices_out) = refs[:-11], refs[-11:-8]
-    indices, inner_in, table, load_sem, group_sem, list_sem, save_sem, sem = refs[-8:]
+    count = max(1, len(rounds))
+    outs = refs[-8 - count : -8]
+    indices, inner_in, group_in, table, picked, load_sem, list_sem, sem = refs[-8:]
     load_list = pltpu.make_async_copy(send, indices, list_sem)
     load_list.start()
-    load = pltpu.make_async_copy(inner, inner_in, load_sem)
-    load.start()
-    load_group = pltpu.make_async_copy(group, group_out, group_sem)
-    load_group.start()
+    loads = [
+        pltpu.make_async_copy(source, target, load_sem.at[place])
+        for place, (source, target) in enumerate([(inner, inner_in), (group, group_in)])
+    ]
+    for load in loads:
+        load.start()
     state_rows = scan.shape[1]
-    blocks = destinations(replicas, outs)
+    if rounds:
+        blocks = [(ref.at[0], partner(replicas, mask)) for ref, mask in zip(outs, rounds)]
+    else:
+        blocks = [(outs[0].at[target], target) for target in range(replicas)]
     load_list.wait()
-    save = pltpu.make_async_copy(indices, indices_out, save_sem)
-    save.start()
+
     plan = []
     for block, (ref, target) in enumerate(blocks):
         for c in range(cap):
@@ -103,46 +98,24 @@
                 )
 
     each(lambda copy: copy.start())
-    load.wait()
+    for load in loads:
+        load.wait()
     taps = inner_in.shape[0]
     for tap in range(taps):
         table[:, tap * LANES : (tap + 1) * LANES] = inner_in[tap].astype(F32)
+        table[:, (taps + tap) * LANES : (taps + tap + 1) * LANES] = both_halves(
+            group_in[tap].astype(F32), group_other[tap].astype(F32)
+        )
     picked[...] = jnp.zeros_like(picked)
     for block, _, c, index in plan:
         row = table[pl.ds(jnp.maximum(index, 0), 1), :]
-        for tap in range(taps):
-            picked[block, tap * ROWS + c : tap * ROWS + c + 1, :] = row[
-                :, tap * LANES : (tap + 1) * LANES
+        for kind in range(2 * taps):
+            picked[block, kind * ROWS + c : kind * ROWS + c + 1, :] = row[
+                :, kind * LANES : (kind + 1) * LANES
             ]
-    load_group.wait()
-    save.wait()
+    for block, (ref, _) in enumerate(blocks):
+        ref[cap * state_rows :, :] = picked[block].astype(BF16)
     each(lambda copy: copy.wait())
-
-
-def windows_kernel(replicas, cap, state_rows, indices_in, group, group_other, picked_in, *refs):
-    count = max(1, len(rounds_of(replicas)))
-    outs = refs[-4 - count : -4]
-    indices, table, picked, sem = refs[-4:]
-    load = pltpu.make_async_copy(indices_in, indices, sem)
-    load.start()
-    taps = group.shape[0]
-    for tap in range(taps):
-        table[:, tap * LANES : (tap + 1) * LANES] = both_halves(
-            group[tap].astype(F32), group_other[tap].astype(F32)
-        )
-    picked[...] = jnp.zeros_like(picked)
-    load.wait()
-    for block, (ref, target) in enumerate(destinations(replicas, outs)):
-        for c in range(cap):
-            index = jnp.maximum(indices[0, target * cap + c], 0)
-            row = table[pl.ds(index, 1), :]
-            for tap in range(taps):
-                picked[block, tap * ROWS + c : tap * ROWS + c + 1, :] = row[
-                    :, tap * LANES : (tap + 1) * LANES
-                ]
-        ref[cap * state_rows :, :] = jnp.concatenate(
-            [picked_in[block], picked[block]], axis=0
-        ).astype(BF16)
 
 
 def pack(replicas, cap, send_list, scan, inner, group, group_other, swapped):
@@ -150,52 +123,28 @@
     count = max(1, len(rounds))
     per_block = 1 if rounds else replicas
     taps, slots, _ = inner.shape
-    rows = cap * scan.shape[1] + 2 * taps * ROWS
+    window_rows = 2 * taps * ROWS
+    rows = cap * scan.shape[1] + window_rows
     blocks = count * per_block
-    shapes = [pltpu.VMEM((per_block, rows, LANES), BF16)] * count
-    half = (blocks, taps * ROWS, LANES)
-    limit = SMALL_LIMIT if rounds else MEDIUM_LIMIT
-    *states, picked, group_near, indices = pl.pallas_call(
-        functools.partial(states_kernel, replicas, cap),
-        out_shape=shapes
-        + [
-            pltpu.VMEM(half, F32),
-            pltpu.VMEM(group.shape, BF16),
-            pltpu.VMEM(send_list.shape, jnp.int32),
-        ],
-        in_specs=[HBM] * 4,
-        out_specs=[VMEM] * (count + 3),
+    return pl.pallas_call(
+        functools.partial(pack_kernel, replicas, cap),
+        out_shape=[pltpu.VMEM((per_block, rows, LANES), BF16)] * count,
+        in_specs=[HBM] * 4 + [VMEM] + [HBM] * len(swapped),
+        out_specs=[VMEM] * count,
         scratch_shapes=[
             pltpu.SMEM(send_list.shape, jnp.int32),
             pltpu.VMEM(inner.shape, BF16),
-            pltpu.VMEM((slots, taps * LANES), F32),
-            pltpu.SemaphoreType.DMA,
-            pltpu.SemaphoreType.DMA,
-            pltpu.SemaphoreType.DMA,
+            pltpu.VMEM(group.shape, BF16),
+            pltpu.VMEM((slots, 2 * taps * LANES), F32),
+            pltpu.VMEM((blocks, window_rows, LANES), F32),
+            pltpu.SemaphoreType.DMA((2,)),
             pltpu.SemaphoreType.DMA,
             pltpu.SemaphoreType.DMA((blocks * cap,)),
         ],
-        compiler_params=pltpu.CompilerParams(vmem_limit_bytes=limit),
+        compiler_params=pltpu.CompilerParams(vmem_limit_bytes=SMALL_LIMIT),
         cost_estimate=pl.CostEstimate(flops=0, bytes_accessed=2_000_000, transcendentals=0),
-        name="pack_states",
-    )(in_hbm(scan), in_hbm(send_list), in_hbm(inner), in_hbm(group))
-    near = [in_vmem(value) for value in states]
-    return pl.pallas_call(
-        functools.partial(windows_kernel, replicas, cap, scan.shape[1]),
-        out_shape=shapes,
-        in_specs=[VMEM] * (4 + count) + [HBM] * len(swapped),
-        out_specs=[VMEM] * count,
-        scratch_shapes=[
-            pltpu.SMEM(send_list.shape, jnp.int32),
-            pltpu.VMEM((slots, taps * LANES), F32),
-            pltpu.VMEM(half, F32),
-            pltpu.SemaphoreType.DMA,
-        ],
-        input_output_aliases={4 + place: place for place in range(count)},
-        compiler_params=pltpu.CompilerParams(vmem_limit_bytes=limit),
-        cost_estimate=pl.CostEstimate(flops=0, bytes_accessed=500_000, transcendentals=0),
-        name="pack_windows",
-    )(indices, group_near, group_other, picked, *near, *swapped)
+        name="pack_leaving",
+    )(in_hbm(scan), in_hbm(send_list), in_hbm(inner), in_hbm(group), group_other, *swapped)
 
 
 def sources_of(replicas):

time: 34.1 us -> 35 us (1.026)
  waiting for transfers between devices: 2.34 us -> 3.79 us
  Pallas kernels: 12.7 us -> 12.1 us
    ppermute x4, waiting for transfers between devices: 0.01 us -> 1.3 us  [swap_heads(): return lax.ppermute(value, 'head', [(0, 1), (1, 0)])]
    pallas_call x2 -> x1, Pallas kernels: 2.85 us -> 2.28 us  [pack(): pl.pallas_call(functools.partial(pack_kernel, replicas, cap), out_shape=[...]
  transfers between devices with their start and end apart: 11 -> 11, of which waited for: 1 -> 3; matrix products, arithmetic and copies ran while one was open for 0% -> 0% of each run, Pallas kernels for 31% -> 23%
where the time goes in v10:
time: 35 us; the launch traced here: 34.6 us
  starting transfers between devices  15.2 us (43%)
  Pallas kernels  12.1 us (35%)
  waiting for transfers between devices  3.79 us (11%)
  between operations  3.3 us (9%)
    ppermute x7, starting transfers between devices, exchange(): lax.ppermute(block, 'dp', [(source, source ^ mask) for source in range(re...  13.7 us
    pallas_call x1, Pallas kernels, stay(): pl.pallas_call(functools.partial(stay_kernel, replicas, cap), out_shape=[...  5.49 us
    pallas_call x2, Pallas kernels, arrive(): pl.pallas_call(functools.partial(arrive_kernel, replicas, cap, first, las...  4.33 us
    ppermute x7, waiting for transfers between devices, exchange(): lax.ppermute(block, 'dp', [(source, source ^ mask) for source in range(re...  2.49 us
    pallas_call x1, Pallas kernels, pack(): pl.pallas_call(functools.partial(pack_kernel, replicas, cap), out_shape=[...  2.28 us
    ppermute x4, starting transfers between devices, swap_heads(): return lax.ppermute(value, 'head', [(0, 1), (1, 0)])  1.45 us
    ppermute x4, waiting for transfers between devices, swap_heads(): return lax.ppermute(value, 'head', [(0, 1), (1, 0)])  1.3 us
  transfers between devices with their start and end apart: 11, of which 3 were waited for; matrix products, arithmetic and copies ran while one was open for 0% of the time, Pallas kernels for 23%

profile of v10, /device:TPU:0, one launch (start us, length us, event | category | flops | bytes accessed | tf_op | source)
XLA Modules:
  0.0 34.6 jit_solution(7502539200602614436)
XLA Ops:
  0.6 0.5 %collective-permute-start.1 = (bf16[64,4096]{1,0:T(8,128)(2,1)}, bf16[64,4096]{1,0:T(8,128)(2,1)S(1)}, u32[]{:S(2)}, u32[]{:S(2)}) collective-permute-start(bf16[64,4096]{1,0:T(8,128)(2,1)} %bitcast.14), channel_id=1, source_target_pairs={{0,1},{1,0},{2,3},{3,2},{4,5},{5,4},{6,7},{7,6},{8,9},{9,8},{10,11... | collective-permute-start | bytes 1572872 | tf_op jit(solution)/shard_map/ppermute | solution.py:688
  1.1 0.0 copy-start
  1.2 0.1 collective-permute-start
  1.2 0.0 copy-start.1
  1.2 0.4 %collective-permute-start.3 = (bf16[3,56,64]{2,1,0:T(8,128)(2,1)}, bf16[3,56,64]{2,1,0:T(8,128)(2,1)S(1)}, u32[]{:S(2)}, u32[]{:S(2)}) collective-permute-start(bf16[3,56,64]{2,1,0:T(8,128)(2,1)} %bitcast.20), channel_id=1, source_target_pairs={{0,1},{1,0},{2,3},{3,2},{4,5},{5,4},{6,7},{7,6},{8,9},{9,8},{10,11... | collective-permute-start | bytes 64520 | tf_op jit(solution)/shard_map/ppermute | solution.py:688
  1.7 0.2 copy-done
  1.8 0.1 copy-done.1
  1.9 0.4 %collective-permute-start.2 = (f32[5,64]{1,0:T(8,128)S(1)}, f32[5,64]{1,0:T(8,128)S(1)}, u32[]{:S(2)}, u32[]{:S(2)}) collective-permute-start(f32[5,64]{1,0:T(8,128)S(1)} %pad_maximum_fusion.small), channel_id=1, source_target_pairs={{0,1},{1,0},{2,3},{3,2},{4,5},{5,4},{6,7},{7,6},{8,9},{9,8},{10,11... | collective-permute-start | bytes 3848 | tf_op jit(solution)/shard_map/ppermute | solution.py:688
  2.3 1.0 %collective-permute-done.2.refs_2_.small_other = f32[5,64]{1,0:T(8,128)S(1)} collective-permute-done((f32[5,64]{1,0:T(8,128)S(1)}, f32[5,64]{1,0:T(8,128)S(1)}, u32[]{:S(2)}, u32[]{:S(2)}) %collective-permute-start.2) | collective-permute-done | bytes 1312 | tf_op jit(solution)/shard_map/ppermute | solution.py:688
  3.4 0.3 collective-permute-done.3.group_other
  3.6 0.0 collective-permute-done.refs_0_.other
  3.6 0.0 collective-permute-done.1.refs_1_.group_weight_other
  3.6 2.3 %pack_leaving.1 = (bf16[1,496,128]{2,1,0:T(8,128)(2,1)S(1)}, bf16[1,496,128]{2,1,0:T(8,128)(2,1)S(1)}, bf16[1,496,128]{2,1,0:T(8,128)(2,1)S(1)}, bf16[1,496,128]...) custom-call(bf16[56,64,128]{2,1,0:T(8,128)(2,1)} %bitcast.11, ...), custom_call_target="tpu_custom_call" | custom-call | bytes 2000000 | tf_op jit(solution)/shard_map/pack_leaving/pallas_call | solution.py:129
  5.9 4.0 %collective-permute-start.4 = (bf16[1,496,128]{2,1,0:T(8,128)(2,1)S(1)}, bf16[1,496,128]{2,1,0:T(8,128)(2,1)S(1)}, u32[]{:S(2)}, u32[]{:S(2)}) collective-permute-start(bf16[1,496,128]{2,1,0:T(8,128)(2,1)S(1)} %get-tuple-element.30), channel_id=1, source_target_pairs={{0,8},{2,10},{4,12},{6,14},{8,0},{10,2},{12,4},{14,6},{1,9},{3,11}... | collective-permute-start | bytes 380936 | tf_op jit(solution)/shard_map/ppermute | solution.py:696
  10.0 1.5 %collective-permute-start.5 = (bf16[1,496,128]{2,1,0:T(8,128)(2,1)S(1)}, bf16[1,496,128]{2,1,0:T(8,128)(2,1)S(1)}, u32[]{:S(2)}, u32[]{:S(2)}) collective-permute-start(bf16[1,496,128]{2,1,0:T(8,128)(2,1)S(1)} %get-tuple-element.31), channel_id=1, source_target_pairs={{0,2},{2,0},{4,6},{6,4},{8,10},{10,8},{12,14},{14,12},{1,3},{3,1},... | collective-permute-start | bytes 380936 | tf_op jit(solution)/shard_map/ppermute | solution.py:696
  11.4 1.6 %collective-permute-start.6 = (bf16[1,496,128]{2,1,0:T(8,128)(2,1)S(1)}, bf16[1,496,128]{2,1,0:T(8,128)(2,1)S(1)}, u32[]{:S(2)}, u32[]{:S(2)}) collective-permute-start(bf16[1,496,128]{2,1,0:T(8,128)(2,1)S(1)} %get-tuple-element.32), channel_id=1, source_target_pairs={{0,4},{2,6},{4,0},{6,2},{8,12},{10,14},{12,8},{14,10},{1,5},{3,7},... | collective-permute-start | bytes 380936 | tf_op jit(solution)/shard_map/ppermute | solution.py:696
  13.0 0.3 collective-permute-start.7
  13.3 1.3 %collective-permute-start.8 = (bf16[1,496,128]{2,1,0:T(8,128)(2,1)S(1)}, bf16[1,496,128]{2,1,0:T(8,128)(2,1)S(1)}, u32[]{:S(2)}, u32[]{:S(2)}) collective-permute-start(bf16[1,496,128]{2,1,0:T(8,128)(2,1)S(1)} %get-tuple-element.46), channel_id=1, source_target_pairs={{0,6},{2,4},{4,2},{6,0},{8,14},{10,12},{12,10},{14,8},{1,7},{3,5},... | collective-permute-start | bytes 380936 | tf_op jit(solution)/shard_map/ppermute | solution.py:696
  14.7 2.5 %collective-permute-done.4.refs_0_ = bf16[1,496,128]{2,1,0:T(8,128)(2,1)S(1)} collective-permute-done((bf16[1,496,128]{2,1,0:T(8,128)(2,1)S(1)}, bf16[1,496,128]{2,1,0:T(8,128)(2,1)S(1)}, u32[]{:S(2)}, u32[]{:S(2)}) %collective-permute-start.4) | collective-permute-done | bytes 127008 | tf_op jit(solution)/shard_map/ppermute | solution.py:696
  17.1 4.1 %collective-permute-start.9 = (bf16[1,496,128]{2,1,0:T(8,128)(2,1)S(1)}, bf16[1,496,128]{2,1,0:T(8,128)(2,1)S(1)}, u32[]{:S(2)}, u32[]{:S(2)}) collective-permute-start(bf16[1,496,128]{2,1,0:T(8,128)(2,1)S(1)} %get-tuple-element.50), channel_id=1, source_target_pairs={{0,12},{2,14},{4,8},{6,10},{8,4},{10,6},{12,0},{14,2},{1,13},{3,15... | collective-permute-start | bytes 380936 | tf_op jit(solution)/shard_map/ppermute | solution.py:696
  21.2 0.0 collective-permute-done.5.refs_1_
  21.2 0.9 %collective-permute-start.10 = (bf16[1,496,128]{2,1,0:T(8,128)(2,1)S(1)}, bf16[1,496,128]{2,1,0:T(8,128)(2,1)S(1)}, u32[]{:S(2)}, u32[]{:S(2)}) collective-permute-start(bf16[1,496,128]{2,1,0:T(8,128)(2,1)S(1)} %get-tuple-element.51), channel_id=1, source_target_pairs={{0,14},{2,12},{4,10},{6,8},{8,6},{10,4},{12,2},{14,0},{1,15},{3,13... | collective-permute-start | bytes 380936 | tf_op jit(solution)/shard_map/ppermute | solution.py:696
  24.7 0.0 collective-permute-done.6.refs_2_
  24.7 5.5 %advance_staying.1 = (s32[1,128]{1,0:T(1,128)S(1)}, f32[112,128]{1,0:T(8,128)S(1)}, f32[16,128]{1,0:T(8,128)S(1)}, f32[56,256]{1,0:T(8,128)S(1)}, bf16[2,56,128]...) custom-call(f32[1]{0:T(128)S(6)} %copy.26.decay_log, ...), custom_call_target="tpu_custom_call" | custom-call | flops 300000000 | bytes 6000000 | tf_op jit(solution)/shard_map/advance_staying/pallas_call | solution.py:436
  30.2 0.0 collective-permute-done.7.refs_3_
  30.3 0.0 collective-permute-done.8.refs_4_
  30.3 2.5 %advance_arrived.1 = (f32[112,128]{1,0:T(8,128)S(1)}, f32[56,256]{1,0:T(8,128)S(1)}, bf16[56,64,128]{2,1,0:T(8,128)(2,1)}) custom-call(s32[1,128]{1,0:T(1,128)S(1)} %get-tuple-element.33.plan_near, f32[16,128]{1,0:T(8,128)S(1)} %get-tuple-element.34.weights, f32[112,128]{1,0:T(8,128)S(1)} %get-tuple-element.35.inner_moved, ...), custom_call_target="tpu_custom_call", output_to_operand_aliasing={{2}: (11, {})} | custom-call | flops 10000000 | bytes 2000000 | tf_op jit(solution)/shard_map/advance_arrived/pallas_call | solution.py:662
  32.8 0.0 collective-permute-done.9.refs_0_
  32.8 0.0 collective-permute-done.10.refs_1_
  32.8 1.8 %advance_last.1 = (bf16[2,56,128]{2,1,0:T(8,128)(2,1)}, bf16[3,56,128]{2,1,0:T(8,128)(2,1)}, bf16[3,56,64]{2,1,0:T(8,128)(2,1)}, bf16[56,64,128]{2,1,0:T(8,128)(2,1)}) custom-call(s32[1,128]{1,0:T(1,128)S(1)} %get-tuple-element.33.plan_near, f32[16,128]{1,0:T(8,128)S(1)} %get-tuple-element.34.weights, ...), custom_call_target="tpu_custom_call", output_to_operand_aliasing={{3}: (11, {})} | custom-call | flops 10000000 | bytes 2000000 | tf_op jit(solution)/shard_map/advance_last/pallas_call | solution.py:662
  (1 shorter events, 0.0 us)
Async XLA Ops:
  0.6 3.0 %collective-permute-start.1 = (bf16[64,4096]{1,0:T(8,128)(2,1)}, bf16[64,4096]{1,0:T(8,128)(2,1)S(1)}, u32[]{:S(2)}, u32[]{:S(2)}) collective-permute-start(bf16[64,4096]{1,0:T(8,128)(2,1)} %bitcast.14), channel_id=1, source_target_pairs={{0,1},{1,0},{2,3},{3,2},{4,5},{5,4},{6,7},{7,6},{8,9},{9,8},{10,11... | collective-permute-start | bytes 1572872 | tf_op jit(solution)/shard_map/ppermute | solution.py:688
  1.1 0.7 %copy-start = (f32[4,64]{1,0:T(4,128)S(1)}, f32[4,64]{1,0:T(4,128)}, u32[]{:S(2)}) copy-start(f32[4,64]{1,0:T(4,128)} %param.25) | copy-start | bytes 3076
  1.2 2.5 %collective-permute-start = (bf16[112,2048]{1,0:T(8,128)(2,1)}, bf16[112,2048]{1,0:T(8,128)(2,1)S(1)}, u32[]{:S(2)}, u32[]{:S(2)}) collective-permute-start(bf16[112,2048]{1,0:T(8,128)(2,1)} %bitcast.16), channel_id=1, source_target_pairs={{0,1},{1,0},{2,3},{3,2},{4,5},{5,4},{6,7},{7,6},{8,9},{9,8},{10,11... | collective-permute-start | bytes 1376264 | tf_op jit(solution)/shard_map/ppermute | solution.py:688
  1.2 0.7 %copy-start.1 = (f32[64]{0:T(128)S(1)}, f32[64]{0:T(128)}, u32[]{:S(2)}) copy-start(f32[64]{0:T(128)} %param.26) | copy-start | bytes 772
  1.2 2.4 %collective-permute-start.3 = (bf16[3,56,64]{2,1,0:T(8,128)(2,1)}, bf16[3,56,64]{2,1,0:T(8,128)(2,1)S(1)}, u32[]{:S(2)}, u32[]{:S(2)}) collective-permute-start(bf16[3,56,64]{2,1,0:T(8,128)(2,1)} %bitcast.20), channel_id=1, source_target_pairs={{0,1},{1,0},{2,3},{3,2},{4,5},{5,4},{6,7},{7,6},{8,9},{9,8},{10,11... | collective-permute-start | bytes 64520 | tf_op jit(solution)/shard_map/ppermute | solution.py:688
  1.9 1.4 %collective-permute-start.2 = (f32[5,64]{1,0:T(8,128)S(1)}, f32[5,64]{1,0:T(8,128)S(1)}, u32[]{:S(2)}, u32[]{:S(2)}) collective-permute-start(f32[5,64]{1,0:T(8,128)S(1)} %pad_maximum_fusion.small), channel_id=1, source_target_pairs={{0,1},{1,0},{2,3},{3,2},{4,5},{5,4},{6,7},{7,6},{8,9},{9,8},{10,11... | collective-permute-start | bytes 3848 | tf_op jit(solution)/shard_map/ppermute | solution.py:688
  5.9 11.2 %collective-permute-start.4 = (bf16[1,496,128]{2,1,0:T(8,128)(2,1)S(1)}, bf16[1,496,128]{2,1,0:T(8,128)(2,1)S(1)}, u32[]{:S(2)}, u32[]{:S(2)}) collective-permute-start(bf16[1,496,128]{2,1,0:T(8,128)(2,1)S(1)} %get-tuple-element.30), channel_id=1, source_target_pairs={{0,8},{2,10},{4,12},{6,14},{8,0},{10,2},{12,4},{14,6},{1,9},{3,11}... | collective-permute-start | bytes 380936 | tf_op jit(solution)/shard_map/ppermute | solution.py:696
  10.0 11.3 %collective-permute-start.5 = (bf16[1,496,128]{2,1,0:T(8,128)(2,1)S(1)}, bf16[1,496,128]{2,1,0:T(8,128)(2,1)S(1)}, u32[]{:S(2)}, u32[]{:S(2)}) collective-permute-start(bf16[1,496,128]{2,1,0:T(8,128)(2,1)S(1)} %get-tuple-element.31), channel_id=1, source_target_pairs={{0,2},{2,0},{4,6},{6,4},{8,10},{10,8},{12,14},{14,12},{1,3},{3,1},... | collective-permute-start | bytes 380936 | tf_op jit(solution)/shard_map/ppermute | solution.py:696
  11.4 13.3 %collective-permute-start.6 = (bf16[1,496,128]{2,1,0:T(8,128)(2,1)S(1)}, bf16[1,496,128]{2,1,0:T(8,128)(2,1)S(1)}, u32[]{:S(2)}, u32[]{:S(2)}) collective-permute-start(bf16[1,496,128]{2,1,0:T(8,128)(2,1)S(1)} %get-tuple-element.32), channel_id=1, source_target_pairs={{0,4},{2,6},{4,0},{6,2},{8,12},{10,14},{12,8},{14,10},{1,5},{3,7},... | collective-permute-start | bytes 380936 | tf_op jit(solution)/shard_map/ppermute | solution.py:696
  13.0 17.3 %collective-permute-start.7 = (bf16[1,496,128]{2,1,0:T(8,128)(2,1)S(1)}, bf16[1,496,128]{2,1,0:T(8,128)(2,1)S(1)}, u32[]{:S(2)}, u32[]{:S(2)}) collective-permute-start(bf16[1,496,128]{2,1,0:T(8,128)(2,1)S(1)} %get-tuple-element.45), channel_id=1, source_target_pairs={{0,10},{2,8},{4,14},{6,12},{8,2},{10,0},{12,6},{14,4},{1,11},{3,9}... | collective-permute-start | bytes 380936 | tf_op jit(solution)/shard_map/ppermute | solution.py:696
  13.3 16.9 %collective-permute-start.8 = (bf16[1,496,128]{2,1,0:T(8,128)(2,1)S(1)}, bf16[1,496,128]{2,1,0:T(8,128)(2,1)S(1)}, u32[]{:S(2)}, u32[]{:S(2)}) collective-permute-start(bf16[1,496,128]{2,1,0:T(8,128)(2,1)S(1)} %get-tuple-element.46), channel_id=1, source_target_pairs={{0,6},{2,4},{4,2},{6,0},{8,14},{10,12},{12,10},{14,8},{1,7},{3,5},... | collective-permute-start | bytes 380936 | tf_op jit(solution)/shard_map/ppermute | solution.py:696
  17.1 15.7 %collective-permute-start.9 = (bf16[1,496,128]{2,1,0:T(8,128)(2,1)S(1)}, bf16[1,496,128]{2,1,0:T(8,128)(2,1)S(1)}, u32[]{:S(2)}, u32[]{:S(2)}) collective-permute-start(bf16[1,496,128]{2,1,0:T(8,128)(2,1)S(1)} %get-tuple-element.50), channel_id=1, source_target_pairs={{0,12},{2,14},{4,8},{6,10},{8,4},{10,6},{12,0},{14,2},{1,13},{3,15... | collective-permute-start | bytes 380936 | tf_op jit(solution)/shard_map/ppermute | solution.py:696
  21.2 11.6 %collective-permute-start.10 = (bf16[1,496,128]{2,1,0:T(8,128)(2,1)S(1)}, bf16[1,496,128]{2,1,0:T(8,128)(2,1)S(1)}, u32[]{:S(2)}, u32[]{:S(2)}) collective-permute-start(bf16[1,496,128]{2,1,0:T(8,128)(2,1)S(1)} %get-tuple-element.51), channel_id=1, source_target_pairs={{0,14},{2,12},{4,10},{6,8},{8,6},{10,4},{12,2},{14,0},{1,15},{3,13... | collective-permute-start | bytes 380936 | tf_op jit(solution)/shard_map/ppermute | solution.py:696

commit v11 on v3

--- a/solution.py
+++ b/solution.py
@@ -196,6 +196,94 @@
         cost_estimate=pl.CostEstimate(flops=0, bytes_accessed=500_000, transcendentals=0),
         name="pack_windows",
     )(indices, group_near, group_other, picked, *near, *swapped)
+
+
+def at_once_kernel(replicas, cap, scan, send, inner, group, group_other, *refs):
+    rounds = rounds_of(replicas)
+    count = max(1, len(rounds))
+    outs = refs[-8 - count : -8]
+    indices, inner_in, group_in, table, picked, load_sem, list_sem, sem = refs[-8:]
+    load_list = pltpu.make_async_copy(send, indices, list_sem)
+    load_list.start()
+    loads = [
+        pltpu.make_async_copy(source, target, load_sem.at[place])
+        for place, (source, target) in enumerate([(inner, inner_in), (group, group_in)])
+    ]
+    for load in loads:
+        load.start()
+    state_rows = scan.shape[1]
+    if rounds:
+        blocks = [(ref.at[0], partner(replicas, mask)) for ref, mask in zip(outs, rounds)]
+    else:
+        blocks = [(outs[0].at[target], target) for target in range(replicas)]
+    load_list.wait()
+
+    plan = []
+    for block, (ref, target) in enumerate(blocks):
+        for c in range(cap):
+            plan.append((block, ref, c, indices[0, target * cap + c]))
+
+    def each(act):
+        for place, (_, ref, c, index) in enumerate(plan):
+
+            @pl.when(index >= 0)
+            def _():
+                act(
+                    pltpu.make_async_copy(
+                        scan.at[index],
+                        ref.at[pl.ds(c * state_rows, state_rows)],
+                        sem.at[place],
+                    )
+                )
+
+    each(lambda copy: copy.start())
+    for load in loads:
+        load.wait()
+    taps = inner_in.shape[0]
+    for tap in range(taps):
+        table[:, tap * LANES : (tap + 1) * LANES] = inner_in[tap].astype(F32)
+        table[:, (taps + tap) * LANES : (taps + tap + 1) * LANES] = both_halves(
+            group_in[tap].astype(F32), group_other[tap].astype(F32)
+        )
+    picked[...] = jnp.zeros_like(picked)
+    for block, _, c, index in plan:
+        row = table[pl.ds(jnp.maximum(index, 0), 1), :]
+        for kind in range(2 * taps):
+            picked[block, kind * ROWS + c : kind * ROWS + c + 1, :] = row[
+                :, kind * LANES : (kind + 1) * LANES
+            ]
+    for block, (ref, _) in enumerate(blocks):
+        ref[cap * state_rows :, :] = picked[block].astype(BF16)
+    each(lambda copy: copy.wait())
+
+
+def pack_at_once(replicas, cap, send_list, scan, inner, group, group_other):
+    rounds = rounds_of(replicas)
+    count = max(1, len(rounds))
+    per_block = 1 if rounds else replicas
+    taps, slots, _ = inner.shape
+    window_rows = 2 * taps * ROWS
+    rows = cap * scan.shape[1] + window_rows
+    blocks = count * per_block
+    return pl.pallas_call(
+        functools.partial(at_once_kernel, replicas, cap),
+        out_shape=[jax.ShapeDtypeStruct((per_block, rows, LANES), BF16)] * count,
+        in_specs=[HBM] * 4 + [VMEM],
+        out_specs=[VMEM] * count,
+        scratch_shapes=[
+            pltpu.SMEM(send_list.shape, jnp.int32),
+            pltpu.VMEM(inner.shape, BF16),
+            pltpu.VMEM(group.shape, BF16),
+            pltpu.VMEM((slots, 2 * taps * LANES), F32),
+            pltpu.VMEM((blocks, window_rows, LANES), F32),
+            pltpu.SemaphoreType.DMA((2,)),
+            pltpu.SemaphoreType.DMA,
+            pltpu.SemaphoreType.DMA((blocks * cap,)),
+        ],
+        compiler_params=pltpu.CompilerParams(vmem_limit_bytes=LARGE_LIMIT),
+        cost_estimate=pl.CostEstimate(flops=0, bytes_accessed=2_000_000, transcendentals=0),
+        name="pack_leaving",
+    )(in_hbm(scan), in_hbm(send_list), in_hbm(inner), in_hbm(group), group_other)
 
 
 def sources_of(replicas):
@@ -782,7 +870,10 @@
     small = jnp.concatenate([group_taps, group_offset[None]], axis=0)
     group_other = swap_heads(group)
     swapped = [swap_heads(value) for value in (own, group_weight, small)]
-    blocks = pack(replicas, cap, send_list, scan, inner, group, group_other, swapped)
+    if rounds_of(replicas):
+        blocks = pack(replicas, cap, send_list, scan, inner, group, group_other, swapped)
+    else:
+        blocks = pack_at_once(replicas, cap, send_list, scan, inner, group, group_other)
     arrived = exchange(replicas, blocks)
     plan, gated, weights, table, inner_part, group_part, *moved, scan_next = stay(
         replicas,

time: 34.1 us -> 34.1 us (level)
  transfers between devices with their start and end apart: 11 -> 11, of which waited for: 1 -> 1; matrix products, arithmetic and copies ran while one was open for 0% -> 0% of each run, Pallas kernels for 31% -> 30%
where the time goes in v11:
time: 34.1 us; the launch traced here: 33.7 us
  starting transfers between devices  15.2 us (45%)
  Pallas kernels  12.6 us (37%)
  between operations  3.33 us (10%)
  waiting for transfers between devices  2.3 us (7%)
    ppermute x7, starting transfers between devices, exchange(): lax.ppermute(block, 'dp', [(source, source ^ mask) for source in range(re...  13.7 us
    pallas_call x1, Pallas kernels, stay(): pl.pallas_call(functools.partial(stay_kernel, replicas, cap), out_shape=[...  5.5 us
    pallas_call x2, Pallas kernels, arrive(): pl.pallas_call(functools.partial(arrive_kernel, replicas, cap, first, las...  4.34 us
    ppermute x7, waiting for transfers between devices, exchange(): lax.ppermute(block, 'dp', [(source, source ^ mask) for source in range(re...  2.29 us
    pallas_call x1, Pallas kernels, pack(): pl.pallas_call(functools.partial(states_kernel, replicas, cap), out_shape...  2.12 us
    ppermute x4, starting transfers between devices, swap_heads(): return lax.ppermute(value, 'head', [(0, 1), (1, 0)])  1.45 us
    pallas_call x1, Pallas kernels, pack(): pl.pallas_call(functools.partial(windows_kernel, replicas, cap, scan.shap...  0.7 us
  transfers between devices with their start and end apart: 11, of which 1 were waited for; matrix products, arithmetic and copies ran while one was open for 0% of the time, Pallas kernels for 30%

profile of v11, /device:TPU:0, one launch (start us, length us, event | category | flops | bytes accessed | tf_op | source)
XLA Modules:
  0.0 33.7 jit_solution(17984509908982308161)
XLA Ops:
  0.6 0.5 %collective-permute-start.1 = (bf16[64,4096]{1,0:T(8,128)(2,1)}, bf16[64,4096]{1,0:T(8,128)(2,1)S(1)}, u32[]{:S(2)}, u32[]{:S(2)}) collective-permute-start(bf16[64,4096]{1,0:T(8,128)(2,1)} %bitcast.14), channel_id=1, source_target_pairs={{0,1},{1,0},{2,3},{3,2},{4,5},{5,4},{6,7},{7,6},{8,9},{9,8},{10,11... | collective-permute-start | bytes 1572872 | tf_op jit(solution)/shard_map/ppermute | solution.py:827
  1.1 0.0 copy-start
  1.2 0.1 collective-permute-start
  1.2 0.0 copy-start.1
  1.2 0.4 %collective-permute-start.3 = (bf16[3,56,64]{2,1,0:T(8,128)(2,1)}, bf16[3,56,64]{2,1,0:T(8,128)(2,1)S(1)}, u32[]{:S(2)}, u32[]{:S(2)}) collective-permute-start(bf16[3,56,64]{2,1,0:T(8,128)(2,1)} %bitcast.20), channel_id=1, source_target_pairs={{0,1},{1,0},{2,3},{3,2},{4,5},{5,4},{6,7},{7,6},{8,9},{9,8},{10,11... | collective-permute-start | bytes 64520 | tf_op jit(solution)/shard_map/ppermute | solution.py:827
  1.7 0.2 copy-done
  1.8 0.1 copy-done.1
  1.9 0.4 %collective-permute-start.2 = (f32[5,64]{1,0:T(8,128)S(1)}, f32[5,64]{1,0:T(8,128)S(1)}, u32[]{:S(2)}, u32[]{:S(2)}) collective-permute-start(f32[5,64]{1,0:T(8,128)S(1)} %pad_maximum_fusion.small), channel_id=1, source_target_pairs={{0,1},{1,0},{2,3},{3,2},{4,5},{5,4},{6,7},{7,6},{8,9},{9,8},{10,11... | collective-permute-start | bytes 3848 | tf_op jit(solution)/shard_map/ppermute | solution.py:827
  2.3 2.1 %pack_states.1 = (bf16[1,496,128]{2,1,0:T(8,128)(2,1)S(1)}, bf16[1,496,128]{2,1,0:T(8,128)(2,1)S(1)}, bf16[1,496,128]{2,1,0:T(8,128)(2,1)S(1)}, bf16[1,496,128]{...) custom-call(bf16[56,64,128]{2,1,0:T(8,128)(2,1)} %bitcast.11, ...), custom_call_target="tpu_custom_call" | custom-call | bytes 2000000 | tf_op jit(solution)/shard_map/pack_states/pallas_call | solution.py:158
  4.5 0.0 collective-permute-done.2.refs_9_.small_other
  4.5 0.0 collective-permute-done.3.group_other
  4.5 0.0 collective-permute-done.refs_7_.other
  4.5 0.0 collective-permute-done.1.refs_8_.group_weight_other
  4.5 0.7 %pack_windows.1 = (bf16[1,496,128]{2,1,0:T(8,128)(2,1)S(1)}, bf16[1,496,128]{2,1,0:T(8,128)(2,1)S(1)}, bf16[1,496,128]{2,1,0:T(8,128)(2,1)S(1)}, bf16[1,496,128]...) custom-call(s32[1,56]{1,0:T(1,128)S(1)} %get-tuple-element.40.indice, ...), custom_call_target="tpu_custom_call", output_to_operand_aliasing={{0}: (4, {}), {1}: (5, {}), {2}: (6, {}), {3}: (7, {}), {4}... | custom-call | bytes 500000 | tf_op jit(solution)/shard_map/pack_windows/pallas_call | solution.py:183
  5.2 3.8 %collective-permute-start.4 = (bf16[1,496,128]{2,1,0:T(8,128)(2,1)S(1)}, bf16[1,496,128]{2,1,0:T(8,128)(2,1)S(1)}, u32[]{:S(2)}, u32[]{:S(2)}) collective-permute-start(bf16[1,496,128]{2,1,0:T(8,128)(2,1)S(1)} %get-tuple-element.50), channel_id=1, source_target_pairs={{0,8},{2,10},{4,12},{6,14},{8,0},{10,2},{12,4},{14,6},{1,9},{3,11}... | collective-permute-start | bytes 380936 | tf_op jit(solution)/shard_map/ppermute | solution.py:835
  9.0 1.5 %collective-permute-start.5 = (bf16[1,496,128]{2,1,0:T(8,128)(2,1)S(1)}, bf16[1,496,128]{2,1,0:T(8,128)(2,1)S(1)}, u32[]{:S(2)}, u32[]{:S(2)}) collective-permute-start(bf16[1,496,128]{2,1,0:T(8,128)(2,1)S(1)} %get-tuple-element.51), channel_id=1, source_target_pairs={{0,2},{2,0},{4,6},{6,4},{8,10},{10,8},{12,14},{14,12},{1,3},{3,1},... | collective-permute-start | bytes 380936 | tf_op jit(solution)/shard_map/ppermute | solution.py:835
  10.5 1.5 %collective-permute-start.6 = (bf16[1,496,128]{2,1,0:T(8,128)(2,1)S(1)}, bf16[1,496,128]{2,1,0:T(8,128)(2,1)S(1)}, u32[]{:S(2)}, u32[]{:S(2)}) collective-permute-start(bf16[1,496,128]{2,1,0:T(8,128)(2,1)S(1)} %get-tuple-element.52), channel_id=1, source_target_pairs={{0,4},{2,6},{4,0},{6,2},{8,12},{10,14},{12,8},{14,10},{1,5},{3,7},... | collective-permute-start | bytes 380936 | tf_op jit(solution)/shard_map/ppermute | solution.py:835
  12.1 0.3 collective-permute-start.7
  12.4 1.4 %collective-permute-start.8 = (bf16[1,496,128]{2,1,0:T(8,128)(2,1)S(1)}, bf16[1,496,128]{2,1,0:T(8,128)(2,1)S(1)}, u32[]{:S(2)}, u32[]{:S(2)}) collective-permute-start(bf16[1,496,128]{2,1,0:T(8,128)(2,1)S(1)} %get-tuple-element.66), channel_id=1, source_target_pairs={{0,6},{2,4},{4,2},{6,0},{8,14},{10,12},{12,10},{14,8},{1,7},{3,5},... | collective-permute-start | bytes 380936 | tf_op jit(solution)/shard_map/ppermute | solution.py:835
  13.8 2.3 %collective-permute-done.4.refs_0_ = bf16[1,496,128]{2,1,0:T(8,128)(2,1)S(1)} collective-permute-done((bf16[1,496,128]{2,1,0:T(8,128)(2,1)S(1)}, bf16[1,496,128]{2,1,0:T(8,128)(2,1)S(1)}, u32[]{:S(2)}, u32[]{:S(2)}) %collective-permute-start.4) | collective-permute-done | bytes 127008 | tf_op jit(solution)/shard_map/ppermute | solution.py:835
  16.1 4.2 %collective-permute-start.9 = (bf16[1,496,128]{2,1,0:T(8,128)(2,1)S(1)}, bf16[1,496,128]{2,1,0:T(8,128)(2,1)S(1)}, u32[]{:S(2)}, u32[]{:S(2)}) collective-permute-start(bf16[1,496,128]{2,1,0:T(8,128)(2,1)S(1)} %get-tuple-element.70), channel_id=1, source_target_pairs={{0,12},{2,14},{4,8},{6,10},{8,4},{10,6},{12,0},{14,2},{1,13},{3,15... | collective-permute-start | bytes 380936 | tf_op jit(solution)/shard_map/ppermute | solution.py:835
  20.2 0.0 collective-permute-done.5.refs_1_
  20.2 1.0 %collective-permute-start.10 = (bf16[1,496,128]{2,1,0:T(8,128)(2,1)S(1)}, bf16[1,496,128]{2,1,0:T(8,128)(2,1)S(1)}, u32[]{:S(2)}, u32[]{:S(2)}) collective-permute-start(bf16[1,496,128]{2,1,0:T(8,128)(2,1)S(1)} %get-tuple-element.71), channel_id=1, source_target_pairs={{0,14},{2,12},{4,10},{6,8},{8,6},{10,4},{12,2},{14,0},{1,15},{3,13... | collective-permute-start | bytes 380936 | tf_op jit(solution)/shard_map/ppermute | solution.py:835
  23.8 0.0 collective-permute-done.6.refs_2_
  23.8 5.5 %advance_staying.1 = (s32[1,128]{1,0:T(1,128)S(1)}, f32[112,128]{1,0:T(8,128)S(1)}, f32[16,128]{1,0:T(8,128)S(1)}, f32[56,256]{1,0:T(8,128)S(1)}, bf16[2,56,128]...) custom-call(f32[1]{0:T(128)S(6)} %copy.40.decay_log, ...), custom_call_target="tpu_custom_call" | custom-call | flops 300000000 | bytes 6000000 | tf_op jit(solution)/shard_map/advance_staying/pallas_call | solution.py:575
  29.3 0.0 collective-permute-done.7.refs_3_
  29.3 0.0 collective-permute-done.8.refs_4_
  29.3 2.5 %advance_arrived.1 = (f32[112,128]{1,0:T(8,128)S(1)}, f32[56,256]{1,0:T(8,128)S(1)}, bf16[56,64,128]{2,1,0:T(8,128)(2,1)}) custom-call(s32[1,128]{1,0:T(1,128)S(1)} %get-tuple-element.53.plan_near, f32[16,128]{1,0:T(8,128)S(1)} %get-tuple-element.54.weights, f32[112,128]{1,0:T(8,128)S(1)} %get-tuple-element.55.inner_moved, ...), custom_call_target="tpu_custom_call", output_to_operand_aliasing={{2}: (11, {})} | custom-call | flops 10000000 | bytes 2000000 | tf_op jit(solution)/shard_map/advance_arrived/pallas_call | solution.py:801
  31.9 0.0 collective-permute-done.9.refs_0_
  31.9 0.0 collective-permute-done.10.refs_1_
  31.9 1.8 %advance_last.1 = (bf16[2,56,128]{2,1,0:T(8,128)(2,1)}, bf16[3,56,128]{2,1,0:T(8,128)(2,1)}, bf16[3,56,64]{2,1,0:T(8,128)(2,1)}, bf16[56,64,128]{2,1,0:T(8,128)(2,1)}) custom-call(s32[1,128]{1,0:T(1,128)S(1)} %get-tuple-element.53.plan_near, f32[16,128]{1,0:T(8,128)S(1)} %get-tuple-element.54.weights, ...), custom_call_target="tpu_custom_call", output_to_operand_aliasing={{3}: (11, {})} | custom-call | flops 10000000 | bytes 2000000 | tf_op jit(solution)/shard_map/advance_last/pallas_call | solution.py:801
  (1 shorter events, 0.0 us)
Async XLA Ops:
  0.6 3.9 %collective-permute-start.1 = (bf16[64,4096]{1,0:T(8,128)(2,1)}, bf16[64,4096]{1,0:T(8,128)(2,1)S(1)}, u32[]{:S(2)}, u32[]{:S(2)}) collective-permute-start(bf16[64,4096]{1,0:T(8,128)(2,1)} %bitcast.14), channel_id=1, source_target_pairs={{0,1},{1,0},{2,3},{3,2},{4,5},{5,4},{6,7},{7,6},{8,9},{9,8},{10,11... | collective-permute-start | bytes 1572872 | tf_op jit(solution)/shard_map/ppermute | solution.py:827
  1.1 0.7 %copy-start = (f32[4,64]{1,0:T(4,128)S(1)}, f32[4,64]{1,0:T(4,128)}, u32[]{:S(2)}) copy-start(f32[4,64]{1,0:T(4,128)} %param.25) | copy-start | bytes 3076
  1.2 3.3 %collective-permute-start = (bf16[112,2048]{1,0:T(8,128)(2,1)}, bf16[112,2048]{1,0:T(8,128)(2,1)S(1)}, u32[]{:S(2)}, u32[]{:S(2)}) collective-permute-start(bf16[112,2048]{1,0:T(8,128)(2,1)} %bitcast.16), channel_id=1, source_target_pairs={{0,1},{1,0},{2,3},{3,2},{4,5},{5,4},{6,7},{7,6},{8,9},{9,8},{10,11... | collective-permute-start | bytes 1376264 | tf_op jit(solution)/shard_map/ppermute | solution.py:827
  1.2 0.7 %copy-start.1 = (f32[64]{0:T(128)S(1)}, f32[64]{0:T(128)}, u32[]{:S(2)}) copy-start(f32[64]{0:T(128)} %param.26) | copy-start | bytes 772
  1.2 3.2 %collective-permute-start.3 = (bf16[3,56,64]{2,1,0:T(8,128)(2,1)}, bf16[3,56,64]{2,1,0:T(8,128)(2,1)S(1)}, u32[]{:S(2)}, u32[]{:S(2)}) collective-permute-start(bf16[3,56,64]{2,1,0:T(8,128)(2,1)} %bitcast.20), channel_id=1, source_target_pairs={{0,1},{1,0},{2,3},{3,2},{4,5},{5,4},{6,7},{7,6},{8,9},{9,8},{10,11... | collective-permute-start | bytes 64520 | tf_op jit(solution)/shard_map/ppermute | solution.py:827
  1.9 2.5 %collective-permute-start.2 = (f32[5,64]{1,0:T(8,128)S(1)}, f32[5,64]{1,0:T(8,128)S(1)}, u32[]{:S(2)}, u32[]{:S(2)}) collective-permute-start(f32[5,64]{1,0:T(8,128)S(1)} %pad_maximum_fusion.small), channel_id=1, source_target_pairs={{0,1},{1,0},{2,3},{3,2},{4,5},{5,4},{6,7},{7,6},{8,9},{9,8},{10,11... | collective-permute-start | bytes 3848 | tf_op jit(solution)/shard_map/ppermute | solution.py:827
  5.2 10.9 %collective-permute-start.4 = (bf16[1,496,128]{2,1,0:T(8,128)(2,1)S(1)}, bf16[1,496,128]{2,1,0:T(8,128)(2,1)S(1)}, u32[]{:S(2)}, u32[]{:S(2)}) collective-permute-start(bf16[1,496,128]{2,1,0:T(8,128)(2,1)S(1)} %get-tuple-element.50), channel_id=1, source_target_pairs={{0,8},{2,10},{4,12},{6,14},{8,0},{10,2},{12,4},{14,6},{1,9},{3,11}... | collective-permute-start | bytes 380936 | tf_op jit(solution)/shard_map/ppermute | solution.py:835
  9.0 11.2 %collective-permute-start.5 = (bf16[1,496,128]{2,1,0:T(8,128)(2,1)S(1)}, bf16[1,496,128]{2,1,0:T(8,128)(2,1)S(1)}, u32[]{:S(2)}, u32[]{:S(2)}) collective-permute-start(bf16[1,496,128]{2,1,0:T(8,128)(2,1)S(1)} %get-tuple-element.51), channel_id=1, source_target_pairs={{0,2},{2,0},{4,6},{6,4},{8,10},{10,8},{12,14},{14,12},{1,3},{3,1},... | collective-permute-start | bytes 380936 | tf_op jit(solution)/shard_map/ppermute | solution.py:835
  10.5 13.3 %collective-permute-start.6 = (bf16[1,496,128]{2,1,0:T(8,128)(2,1)S(1)}, bf16[1,496,128]{2,1,0:T(8,128)(2,1)S(1)}, u32[]{:S(2)}, u32[]{:S(2)}) collective-permute-start(bf16[1,496,128]{2,1,0:T(8,128)(2,1)S(1)} %get-tuple-element.52), channel_id=1, source_target_pairs={{0,4},{2,6},{4,0},{6,2},{8,12},{10,14},{12,8},{14,10},{1,5},{3,7},... | collective-permute-start | bytes 380936 | tf_op jit(solution)/shard_map/ppermute | solution.py:835
  12.1 17.2 %collective-permute-start.7 = (bf16[1,496,128]{2,1,0:T(8,128)(2,1)S(1)}, bf16[1,496,128]{2,1,0:T(8,128)(2,1)S(1)}, u32[]{:S(2)}, u32[]{:S(2)}) collective-permute-start(bf16[1,496,128]{2,1,0:T(8,128)(2,1)S(1)} %get-tuple-element.65), channel_id=1, source_target_pairs={{0,10},{2,8},{4,14},{6,12},{8,2},{10,0},{12,6},{14,4},{1,11},{3,9}... | collective-permute-start | bytes 380936 | tf_op jit(solution)/shard_map/ppermute | solution.py:835
  12.4 16.9 %collective-permute-start.8 = (bf16[1,496,128]{2,1,0:T(8,128)(2,1)S(1)}, bf16[1,496,128]{2,1,0:T(8,128)(2,1)S(1)}, u32[]{:S(2)}, u32[]{:S(2)}) collective-permute-start(bf16[1,496,128]{2,1,0:T(8,128)(2,1)S(1)} %get-tuple-element.66), channel_id=1, source_target_pairs={{0,6},{2,4},{4,2},{6,0},{8,14},{10,12},{12,10},{14,8},{1,7},{3,5},... | collective-permute-start | bytes 380936 | tf_op jit(solution)/shard_map/ppermute | solution.py:835
  16.1 15.8 %collective-permute-start.9 = (bf16[1,496,128]{2,1,0:T(8,128)(2,1)S(1)}, bf16[1,496,128]{2,1,0:T(8,128)(2,1)S(1)}, u32[]{:S(2)}, u32[]{:S(2)}) collective-permute-start(bf16[1,496,128]{2,1,0:T(8,128)(2,1)S(1)} %get-tuple-element.70), channel_id=1, source_target_pairs={{0,12},{2,14},{4,8},{6,10},{8,4},{10,6},{12,0},{14,2},{1,13},{3,15... | collective-permute-start | bytes 380936 | tf_op jit(solution)/shard_map/ppermute | solution.py:835
  20.2 11.7 %collective-permute-start.10 = (bf16[1,496,128]{2,1,0:T(8,128)(2,1)S(1)}, bf16[1,496,128]{2,1,0:T(8,128)(2,1)S(1)}, u32[]{:S(2)}, u32[]{:S(2)}) collective-permute-start(bf16[1,496,128]{2,1,0:T(8,128)(2,1)S(1)} %get-tuple-element.71), channel_id=1, source_target_pairs={{0,14},{2,12},{4,10},{6,8},{8,6},{10,4},{12,2},{14,0},{1,15},{3,13... | collective-permute-start | bytes 380936 | tf_op jit(solution)/shard_map/ppermute | solution.py:835

commit v12 on v11

--- a/solution.py
+++ b/solution.py
@@ -49,6 +49,7 @@
         return []
     light = list(range(1, replicas // 2))
     heavy = list(range(replicas // 2, replicas))
+    heavy = heavy[::2] + heavy[1::2]
     return heavy[:1] + light[:2] + heavy[1:2] + light[2:] + heavy[2:]
 
 

time: 34.1 us -> 35.3 us (1.035)
  waiting for transfers between devices: 2.3 us -> 3.05 us
  starting transfers between devices: 15.2 us -> 15.7 us
    ppermute x7, waiting for transfers between devices: 2.29 us -> 3.04 us  [exchange(): lax.ppermute(block, 'dp', [(source, source ^ mask) for source in range(re...]
    ppermute x7, starting transfers between devices: 13.7 us -> 14.2 us  [exchange(): lax.ppermute(block, 'dp', [(source, source ^ mask) for source in range(re...]
  transfers between devices with their start and end apart: 11 -> 11, of which waited for: 1 -> 1; matrix products, arithmetic and copies ran while one was open for 0% -> 0% of each run, Pallas kernels for 30% -> 29%
where the time goes in v12:
time: 35.3 us; the launch traced here: 34.9 us
  starting transfers between devices  15.7 us (44%)
  Pallas kernels  12.6 us (36%)
  between operations  3.33 us (9%)
  waiting for transfers between devices  3.05 us (9%)
    ppermute x7, starting transfers between devices, exchange(): lax.ppermute(block, 'dp', [(source, source ^ mask) for source in range(re...  14.2 us
    pallas_call x1, Pallas kernels, stay(): pl.pallas_call(functools.partial(stay_kernel, replicas, cap), out_shape=[...  5.49 us
    pallas_call x2, Pallas kernels, arrive(): pl.pallas_call(functools.partial(arrive_kernel, replicas, cap, first, las...  4.34 us
    ppermute x7, waiting for transfers between devices, exchange(): lax.ppermute(block, 'dp', [(source, source ^ mask) for source in range(re...  3.04 us
    pallas_call x1, Pallas kernels, pack(): pl.pallas_call(functools.partial(states_kernel, replicas, cap), out_shape...  2.11 us
    ppermute x4, starting transfers between devices, swap_heads(): return lax.ppermute(value, 'head', [(0, 1), (1, 0)])  1.45 us
  transfers between devices with their start and end apart: 11, of which 1 were waited for; matrix products, arithmetic and copies ran while one was open for 0% of the time, Pallas kernels for 29%

profile of v12, /device:TPU:0, one launch (start us, length us, event | category | flops | bytes accessed | tf_op | source)
XLA Modules:
  0.0 34.9 jit_solution(3250858628582564719)
XLA Ops:
  0.6 0.5 %collective-permute-start.1 = (bf16[64,4096]{1,0:T(8,128)(2,1)}, bf16[64,4096]{1,0:T(8,128)(2,1)S(1)}, u32[]{:S(2)}, u32[]{:S(2)}) collective-permute-start(bf16[64,4096]{1,0:T(8,128)(2,1)} %bitcast.14), channel_id=1, source_target_pairs={{0,1},{1,0},{2,3},{3,2},{4,5},{5,4},{6,7},{7,6},{8,9},{9,8},{10,11... | collective-permute-start | bytes 1572872 | tf_op jit(solution)/shard_map/ppermute | solution.py:828
  1.1 0.0 copy-start
  1.2 0.1 collective-permute-start
  1.2 0.0 copy-start.1
  1.2 0.4 %collective-permute-start.3 = (bf16[3,56,64]{2,1,0:T(8,128)(2,1)}, bf16[3,56,64]{2,1,0:T(8,128)(2,1)S(1)}, u32[]{:S(2)}, u32[]{:S(2)}) collective-permute-start(bf16[3,56,64]{2,1,0:T(8,128)(2,1)} %bitcast.20), channel_id=1, source_target_pairs={{0,1},{1,0},{2,3},{3,2},{4,5},{5,4},{6,7},{7,6},{8,9},{9,8},{10,11... | collective-permute-start | bytes 64520 | tf_op jit(solution)/shard_map/ppermute | solution.py:828
  1.7 0.2 copy-done
  1.8 0.1 copy-done.1
  1.9 0.4 %collective-permute-start.2 = (f32[5,64]{1,0:T(8,128)S(1)}, f32[5,64]{1,0:T(8,128)S(1)}, u32[]{:S(2)}, u32[]{:S(2)}) collective-permute-start(f32[5,64]{1,0:T(8,128)S(1)} %pad_maximum_fusion.small), channel_id=1, source_target_pairs={{0,1},{1,0},{2,3},{3,2},{4,5},{5,4},{6,7},{7,6},{8,9},{9,8},{10,11... | collective-permute-start | bytes 3848 | tf_op jit(solution)/shard_map/ppermute | solution.py:828
  2.3 2.1 %pack_states.1 = (bf16[1,496,128]{2,1,0:T(8,128)(2,1)S(1)}, bf16[1,496,128]{2,1,0:T(8,128)(2,1)S(1)}, bf16[1,496,128]{2,1,0:T(8,128)(2,1)S(1)}, bf16[1,496,128]{...) custom-call(bf16[56,64,128]{2,1,0:T(8,128)(2,1)} %bitcast.11, ...), custom_call_target="tpu_custom_call" | custom-call | bytes 2000000 | tf_op jit(solution)/shard_map/pack_states/pallas_call | solution.py:159
  4.4 0.0 collective-permute-done.2.refs_9_.small_other
  4.5 0.0 collective-permute-done.3.group_other
  4.5 0.0 collective-permute-done.refs_7_.other
  4.5 0.0 collective-permute-done.1.refs_8_.group_weight_other
  4.5 0.7 %pack_windows.1 = (bf16[1,496,128]{2,1,0:T(8,128)(2,1)S(1)}, bf16[1,496,128]{2,1,0:T(8,128)(2,1)S(1)}, bf16[1,496,128]{2,1,0:T(8,128)(2,1)S(1)}, bf16[1,496,128]...) custom-call(s32[1,56]{1,0:T(1,128)S(1)} %get-tuple-element.40.indice, ...), custom_call_target="tpu_custom_call", output_to_operand_aliasing={{0}: (4, {}), {1}: (5, {}), {2}: (6, {}), {3}: (7, {}), {4}... | custom-call | bytes 500000 | tf_op jit(solution)/shard_map/pack_windows/pallas_call | solution.py:184
  5.2 3.8 %collective-permute-start.4 = (bf16[1,496,128]{2,1,0:T(8,128)(2,1)S(1)}, bf16[1,496,128]{2,1,0:T(8,128)(2,1)S(1)}, u32[]{:S(2)}, u32[]{:S(2)}) collective-permute-start(bf16[1,496,128]{2,1,0:T(8,128)(2,1)S(1)} %get-tuple-element.50), channel_id=1, source_target_pairs={{0,8},{2,10},{4,12},{6,14},{8,0},{10,2},{12,4},{14,6},{1,9},{3,11}... | collective-permute-start | bytes 380936 | tf_op jit(solution)/shard_map/ppermute | solution.py:836
  9.0 1.5 %collective-permute-start.5 = (bf16[1,496,128]{2,1,0:T(8,128)(2,1)S(1)}, bf16[1,496,128]{2,1,0:T(8,128)(2,1)S(1)}, u32[]{:S(2)}, u32[]{:S(2)}) collective-permute-start(bf16[1,496,128]{2,1,0:T(8,128)(2,1)S(1)} %get-tuple-element.51), channel_id=1, source_target_pairs={{0,2},{2,0},{4,6},{6,4},{8,10},{10,8},{12,14},{14,12},{1,3},{3,1},... | collective-permute-start | bytes 380936 | tf_op jit(solution)/shard_map/ppermute | solution.py:836
  10.5 1.6 %collective-permute-start.6 = (bf16[1,496,128]{2,1,0:T(8,128)(2,1)S(1)}, bf16[1,496,128]{2,1,0:T(8,128)(2,1)S(1)}, u32[]{:S(2)}, u32[]{:S(2)}) collective-permute-start(bf16[1,496,128]{2,1,0:T(8,128)(2,1)S(1)} %get-tuple-element.52), channel_id=1, source_target_pairs={{0,4},{2,6},{4,0},{6,2},{8,12},{10,14},{12,8},{14,10},{1,5},{3,7},... | collective-permute-start | bytes 380936 | tf_op jit(solution)/shard_map/ppermute | solution.py:836
  12.1 0.2 collective-permute-start.7
  12.3 0.7 %collective-permute-start.8 = (bf16[1,496,128]{2,1,0:T(8,128)(2,1)S(1)}, bf16[1,496,128]{2,1,0:T(8,128)(2,1)S(1)}, u32[]{:S(2)}, u32[]{:S(2)}) collective-permute-start(bf16[1,496,128]{2,1,0:T(8,128)(2,1)S(1)} %get-tuple-element.66), channel_id=1, source_target_pairs={{0,6},{2,4},{4,2},{6,0},{8,14},{10,12},{12,10},{14,8},{1,7},{3,5},... | collective-permute-start | bytes 380936 | tf_op jit(solution)/shard_map/ppermute | solution.py:836
  12.9 3.0 %collective-permute-done.4.refs_0_ = bf16[1,496,128]{2,1,0:T(8,128)(2,1)S(1)} collective-permute-done((bf16[1,496,128]{2,1,0:T(8,128)(2,1)S(1)}, bf16[1,496,128]{2,1,0:T(8,128)(2,1)S(1)}, u32[]{:S(2)}, u32[]{:S(2)}) %collective-permute-start.4) | collective-permute-done | bytes 127008 | tf_op jit(solution)/shard_map/ppermute | solution.py:836
  16.0 1.4 %collective-permute-start.9 = (bf16[1,496,128]{2,1,0:T(8,128)(2,1)S(1)}, bf16[1,496,128]{2,1,0:T(8,128)(2,1)S(1)}, u32[]{:S(2)}, u32[]{:S(2)}) collective-permute-start(bf16[1,496,128]{2,1,0:T(8,128)(2,1)S(1)} %get-tuple-element.70), channel_id=1, source_target_pairs={{0,10},{2,8},{4,14},{6,12},{8,2},{10,0},{12,6},{14,4},{1,11},{3,9}... | collective-permute-start | bytes 380936 | tf_op jit(solution)/shard_map/ppermute | solution.py:836
  17.4 0.0 collective-permute-done.5.refs_1_
  17.4 5.1 %collective-permute-start.10 = (bf16[1,496,128]{2,1,0:T(8,128)(2,1)S(1)}, bf16[1,496,128]{2,1,0:T(8,128)(2,1)S(1)}, u32[]{:S(2)}, u32[]{:S(2)}) collective-permute-start(bf16[1,496,128]{2,1,0:T(8,128)(2,1)S(1)} %get-tuple-element.71), channel_id=1, source_target_pairs={{0,14},{2,12},{4,10},{6,8},{8,6},{10,4},{12,2},{14,0},{1,15},{3,13... | collective-permute-start | bytes 380936 | tf_op jit(solution)/shard_map/ppermute | solution.py:836
  25.0 0.0 collective-permute-done.6.refs_2_
  25.0 5.5 %advance_staying.1 = (s32[1,128]{1,0:T(1,128)S(1)}, f32[112,128]{1,0:T(8,128)S(1)}, f32[16,128]{1,0:T(8,128)S(1)}, f32[56,256]{1,0:T(8,128)S(1)}, bf16[2,56,128]...) custom-call(f32[1]{0:T(128)S(6)} %copy.40.decay_log, ...), custom_call_target="tpu_custom_call" | custom-call | flops 300000000 | bytes 6000000 | tf_op jit(solution)/shard_map/advance_staying/pallas_call | solution.py:576
  30.5 0.0 collective-permute-done.7.refs_3_
  30.6 0.0 collective-permute-done.8.refs_4_
  30.6 2.5 %advance_arrived.1 = (f32[112,128]{1,0:T(8,128)S(1)}, f32[56,256]{1,0:T(8,128)S(1)}, bf16[56,64,128]{2,1,0:T(8,128)(2,1)}) custom-call(s32[1,128]{1,0:T(1,128)S(1)} %get-tuple-element.53.plan_near, f32[16,128]{1,0:T(8,128)S(1)} %get-tuple-element.54.weights, f32[112,128]{1,0:T(8,128)S(1)} %get-tuple-element.55.inner_moved, ...), custom_call_target="tpu_custom_call", output_to_operand_aliasing={{2}: (11, {})} | custom-call | flops 10000000 | bytes 2000000 | tf_op jit(solution)/shard_map/advance_arrived/pallas_call | solution.py:802
  33.1 0.0 collective-permute-done.9.refs_0_
  33.1 0.0 collective-permute-done.10.refs_1_
  33.1 1.8 %advance_last.1 = (bf16[2,56,128]{2,1,0:T(8,128)(2,1)}, bf16[3,56,128]{2,1,0:T(8,128)(2,1)}, bf16[3,56,64]{2,1,0:T(8,128)(2,1)}, bf16[56,64,128]{2,1,0:T(8,128)(2,1)}) custom-call(s32[1,128]{1,0:T(1,128)S(1)} %get-tuple-element.53.plan_near, f32[16,128]{1,0:T(8,128)S(1)} %get-tuple-element.54.weights, ...), custom_call_target="tpu_custom_call", output_to_operand_aliasing={{3}: (11, {})} | custom-call | flops 10000000 | bytes 2000000 | tf_op jit(solution)/shard_map/advance_last/pallas_call | solution.py:802
  (1 shorter events, 0.0 us)
Async XLA Ops:
  0.6 3.8 %collective-permute-start.1 = (bf16[64,4096]{1,0:T(8,128)(2,1)}, bf16[64,4096]{1,0:T(8,128)(2,1)S(1)}, u32[]{:S(2)}, u32[]{:S(2)}) collective-permute-start(bf16[64,4096]{1,0:T(8,128)(2,1)} %bitcast.14), channel_id=1, source_target_pairs={{0,1},{1,0},{2,3},{3,2},{4,5},{5,4},{6,7},{7,6},{8,9},{9,8},{10,11... | collective-permute-start | bytes 1572872 | tf_op jit(solution)/shard_map/ppermute | solution.py:828
  1.1 0.7 %copy-start = (f32[4,64]{1,0:T(4,128)S(1)}, f32[4,64]{1,0:T(4,128)}, u32[]{:S(2)}) copy-start(f32[4,64]{1,0:T(4,128)} %param.25) | copy-start | bytes 3076
  1.2 3.3 %collective-permute-start = (bf16[112,2048]{1,0:T(8,128)(2,1)}, bf16[112,2048]{1,0:T(8,128)(2,1)S(1)}, u32[]{:S(2)}, u32[]{:S(2)}) collective-permute-start(bf16[112,2048]{1,0:T(8,128)(2,1)} %bitcast.16), channel_id=1, source_target_pairs={{0,1},{1,0},{2,3},{3,2},{4,5},{5,4},{6,7},{7,6},{8,9},{9,8},{10,11... | collective-permute-start | bytes 1376264 | tf_op jit(solution)/shard_map/ppermute | solution.py:828
  1.2 0.7 %copy-start.1 = (f32[64]{0:T(128)S(1)}, f32[64]{0:T(128)}, u32[]{:S(2)}) copy-start(f32[64]{0:T(128)} %param.26) | copy-start | bytes 772
  1.2 3.2 %collective-permute-start.3 = (bf16[3,56,64]{2,1,0:T(8,128)(2,1)}, bf16[3,56,64]{2,1,0:T(8,128)(2,1)S(1)}, u32[]{:S(2)}, u32[]{:S(2)}) collective-permute-start(bf16[3,56,64]{2,1,0:T(8,128)(2,1)} %bitcast.20), channel_id=1, source_target_pairs={{0,1},{1,0},{2,3},{3,2},{4,5},{5,4},{6,7},{7,6},{8,9},{9,8},{10,11... | collective-permute-start | bytes 64520 | tf_op jit(solution)/shard_map/ppermute | solution.py:828
  1.9 2.5 %collective-permute-start.2 = (f32[5,64]{1,0:T(8,128)S(1)}, f32[5,64]{1,0:T(8,128)S(1)}, u32[]{:S(2)}, u32[]{:S(2)}) collective-permute-start(f32[5,64]{1,0:T(8,128)S(1)} %pad_maximum_fusion.small), channel_id=1, source_target_pairs={{0,1},{1,0},{2,3},{3,2},{4,5},{5,4},{6,7},{7,6},{8,9},{9,8},{10,11... | collective-permute-start | bytes 3848 | tf_op jit(solution)/shard_map/ppermute | solution.py:828
  5.2 10.8 %collective-permute-start.4 = (bf16[1,496,128]{2,1,0:T(8,128)(2,1)S(1)}, bf16[1,496,128]{2,1,0:T(8,128)(2,1)S(1)}, u32[]{:S(2)}, u32[]{:S(2)}) collective-permute-start(bf16[1,496,128]{2,1,0:T(8,128)(2,1)S(1)} %get-tuple-element.50), channel_id=1, source_target_pairs={{0,8},{2,10},{4,12},{6,14},{8,0},{10,2},{12,4},{14,6},{1,9},{3,11}... | collective-permute-start | bytes 380936 | tf_op jit(solution)/shard_map/ppermute | solution.py:836
  9.0 8.4 %collective-permute-start.5 = (bf16[1,496,128]{2,1,0:T(8,128)(2,1)S(1)}, bf16[1,496,128]{2,1,0:T(8,128)(2,1)S(1)}, u32[]{:S(2)}, u32[]{:S(2)}) collective-permute-start(bf16[1,496,128]{2,1,0:T(8,128)(2,1)S(1)} %get-tuple-element.51), channel_id=1, source_target_pairs={{0,2},{2,0},{4,6},{6,4},{8,10},{10,8},{12,14},{14,12},{1,3},{3,1},... | collective-permute-start | bytes 380936 | tf_op jit(solution)/shard_map/ppermute | solution.py:836
  10.5 14.6 %collective-permute-start.6 = (bf16[1,496,128]{2,1,0:T(8,128)(2,1)S(1)}, bf16[1,496,128]{2,1,0:T(8,128)(2,1)S(1)}, u32[]{:S(2)}, u32[]{:S(2)}) collective-permute-start(bf16[1,496,128]{2,1,0:T(8,128)(2,1)S(1)} %get-tuple-element.52), channel_id=1, source_target_pairs={{0,4},{2,6},{4,0},{6,2},{8,12},{10,14},{12,8},{14,10},{1,5},{3,7},... | collective-permute-start | bytes 380936 | tf_op jit(solution)/shard_map/ppermute | solution.py:836
  12.1 18.5 %collective-permute-start.7 = (bf16[1,496,128]{2,1,0:T(8,128)(2,1)S(1)}, bf16[1,496,128]{2,1,0:T(8,128)(2,1)S(1)}, u32[]{:S(2)}, u32[]{:S(2)}) collective-permute-start(bf16[1,496,128]{2,1,0:T(8,128)(2,1)S(1)} %get-tuple-element.65), channel_id=1, source_target_pairs={{0,12},{2,14},{4,8},{6,10},{8,4},{10,6},{12,0},{14,2},{1,13},{3,15... | collective-permute-start | bytes 380936 | tf_op jit(solution)/shard_map/ppermute | solution.py:836
  12.3 18.3 %collective-permute-start.8 = (bf16[1,496,128]{2,1,0:T(8,128)(2,1)S(1)}, bf16[1,496,128]{2,1,0:T(8,128)(2,1)S(1)}, u32[]{:S(2)}, u32[]{:S(2)}) collective-permute-start(bf16[1,496,128]{2,1,0:T(8,128)(2,1)S(1)} %get-tuple-element.66), channel_id=1, source_target_pairs={{0,6},{2,4},{4,2},{6,0},{8,14},{10,12},{12,10},{14,8},{1,7},{3,5},... | collective-permute-start | bytes 380936 | tf_op jit(solution)/shard_map/ppermute | solution.py:836
  16.0 17.2 %collective-permute-start.9 = (bf16[1,496,128]{2,1,0:T(8,128)(2,1)S(1)}, bf16[1,496,128]{2,1,0:T(8,128)(2,1)S(1)}, u32[]{:S(2)}, u32[]{:S(2)}) collective-permute-start(bf16[1,496,128]{2,1,0:T(8,128)(2,1)S(1)} %get-tuple-element.70), channel_id=1, source_target_pairs={{0,10},{2,8},{4,14},{6,12},{8,2},{10,0},{12,6},{14,4},{1,11},{3,9}... | collective-permute-start | bytes 380936 | tf_op jit(solution)/shard_map/ppermute | solution.py:836
  17.4 15.8 %collective-permute-start.10 = (bf16[1,496,128]{2,1,0:T(8,128)(2,1)S(1)}, bf16[1,496,128]{2,1,0:T(8,128)(2,1)S(1)}, u32[]{:S(2)}, u32[]{:S(2)}) collective-permute-start(bf16[1,496,128]{2,1,0:T(8,128)(2,1)S(1)} %get-tuple-element.71), channel_id=1, source_target_pairs={{0,14},{2,12},{4,10},{6,8},{8,6},{10,4},{12,2},{14,0},{1,15},{3,13... | collective-permute-start | bytes 380936 | tf_op jit(solution)/shard_map/ppermute | solution.py:836
